TPU v7x, 512 devices: a whole 4x4x16 slice. The times are simulated.
512 devices in a mesh: dp: 16 (over x, y), owner: 32 (over z, core).
Axes of the slice: x: 4, y: 4, z: 16, core: 2. Of those that a mesh axis runs over, the one named last changes fastest.
Arguments:
- grad_partial: bfloat16 [16, 160, 512, 512], P('dp', 'owner'), may hold values from -5 to 5
- statistics: float32 [16, 32, 2, 512, 512], P('dp', 'owner'), may hold values from -3072 to 3072, as said below
- owner_table: int32 [160, 2], replicated, may hold values from 0 to 511, as said below
Outputs:
- update: bfloat16 [160, 512, 512], P('owner', 'dp')
Inputs may be any that keep to these rules, and one draw needn't show every extreme that they name: `owner_table`: entry [b, s] names the device d * 32 + o (d its index along dp, o along owner) that keeps the statistic of side s of block b. Each device is named by at most 2 entries and some device by exactly 2; the entries naming a device, in increasing order of 2 b + s, use its slots 0, 1, ... of statistics, and its other slots are never read. The blocks b with b // 5 = c (block column c) name devices of any one owner index o at most 1 times, and some owner index is named exactly 1 times by every block column. Each statistics[d, o, q] is a symmetric positive definite matrix.
All inputs are finite; a program needn't handle non-finite values.
Results may differ from a plain program's by a relative error of at most 0.017.
Values may be sent and summed in bfloat16 or wider, within the bound.
No kernel may reach another device: no remote copies, remote signals or barrier semaphores. Data moves between devices by JAX's collectives and lax.ppermute only.
A program may use at most 64 MiB of HBM per device.

v0:
```python
import math

import jax
import jax.numpy as jnp
from jax import lax
from jax.sharding import PartitionSpec as P

decay_rate = 0.9
update_gain = 16.0
root_gain = 1.5
highest = lax.Precision.HIGHEST


def item_tables(owner_table, n_owner, blocks_col):
    device = owner_table.reshape(-1)
    numbers = jnp.arange(device.shape[0], dtype=jnp.int32)
    earlier = numbers[None, :] < numbers[:, None]
    slot_of = jnp.sum(((device[None, :] == device[:, None]) & earlier).astype(jnp.int32), axis=1)
    column = device % n_owner
    source = numbers // (2 * blocks_col)
    same_pair = (
        (column[None, :] == column[:, None]) & (source[None, :] == source[:, None]) & earlier
    )
    pair_copy = jnp.sum(same_pair.astype(jnp.int32), axis=1)
    return (device, slot_of, column, source, pair_copy, numbers)


def newton_roots(new_stat):
    order_n = new_stat.shape[-1]
    identity = jnp.eye(order_n, dtype=jnp.float32)
    frob_norm = jnp.sqrt(jnp.sum(new_stat * new_stat, axis=(1, 2)) + 1e-06)
    root_scale = (root_gain * math.sqrt(order_n) / frob_norm)[:, None, None]
    scaled_stat = root_scale * new_stat
    first_step = 1.25 * identity - 0.25 * scaled_stat
    squared = jnp.einsum("qij,qjk->qik", first_step, first_step, precision=highest)
    fourth = jnp.einsum("qij,qjk->qik", squared, squared, precision=highest)
    moved_stat = jnp.einsum("qij,qjk->qik", fourth, scaled_stat, precision=highest)
    second_step = 1.25 * identity - 0.25 * moved_stat
    return root_scale**0.25 * jnp.einsum("qij,qjk->qik", first_step, second_step, precision=highest)


def body(grad_partial, statistics, owner_table):
    n_dp = lax.axis_size("dp")
    n_owner = lax.axis_size("owner")
    blocks_col = grad_partial.shape[1]
    order_b = grad_partial.shape[3]
    slab_rows = order_b // n_dp
    slot_count = statistics.shape[2]
    pair_count = (2 * blocks_col + n_owner - 1) // n_owner
    lane_count = n_owner * pair_count
    item_width = 2 * blocks_col
    row_index = lax.axis_index("dp")
    col_index = lax.axis_index("owner")
    my_device = row_index * n_owner + col_index
    summed = lax.psum_scatter(
        grad_partial[0].astype(jnp.float32).astype(jnp.bfloat16),
        "dp",
        scatter_dimension=1,
        tiled=True,
    )
    device, slot_of, column, source, pair_copy, numbers = item_tables(
        owner_table, n_owner, blocks_col
    )
    mine_col = lax.dynamic_slice_in_dim(column, col_index * item_width, item_width)
    mine_copy = lax.dynamic_slice_in_dim(pair_copy, col_index * item_width, item_width)
    target = mine_col * pair_count + mine_copy
    lane_pick = (target[None, :] == jnp.arange(lane_count)[:, None]).astype(jnp.bfloat16)
    by_block = lane_pick.reshape(lane_count, blocks_col, 2).sum(axis=2)
    outgoing = jnp.dot(
        by_block,
        summed.reshape(blocks_col, slab_rows * order_b),
        preferred_element_type=jnp.float32,
    )
    outgoing = outgoing.astype(jnp.bfloat16).reshape(n_owner, pair_count, slab_rows, order_b)
    arrived = lax.all_to_all(outgoing, "owner", split_axis=0, concat_axis=0, tiled=True)
    in_column = column == col_index
    slot_row = slot_of * n_dp + device // n_owner
    lane_of = source * pair_count + pair_copy
    slot_hot = (
        (slot_row[:, None] == jnp.arange(slot_count * n_dp)[None, :]) & in_column[:, None]
    ).astype(jnp.float32)
    lane_hot = (lane_of[:, None] == jnp.arange(lane_count)[None, :]).astype(jnp.float32)
    route_table = jnp.einsum("ka,kb->ab", slot_hot, lane_hot).astype(jnp.bfloat16)
    forward = jnp.dot(
        route_table,
        arrived.reshape(lane_count, slab_rows * order_b),
        preferred_element_type=jnp.float32,
    )
    forward = forward.astype(jnp.bfloat16).reshape(slot_count, n_dp, slab_rows, order_b)
    owned = lax.all_to_all(forward, "dp", split_axis=1, concat_axis=1, tiled=True).reshape(
        slot_count, order_b, order_b
    )
    is_mine = device == my_device
    left_item = numbers % 2 == 0
    slot_ids = jnp.arange(slot_count)
    is_left = (
        jnp.sum(
            ((slot_of[:, None] == slot_ids[None, :]) & (is_mine & left_item)[:, None]).astype(
                jnp.int32
            ),
            axis=0,
        )
        > 0
    )
    left_mask = is_left[:, None, None]
    oriented = jnp.where(left_mask, owned, jnp.swapaxes(owned, 1, 2))
    gram_sum = jnp.einsum("qik,qjk->qij", oriented, oriented, preferred_element_type=jnp.float32)
    new_stat = decay_rate * statistics[0, 0] + (1.0 - decay_rate) * gram_sum
    inverse_roots = newton_roots(new_stat).astype(jnp.bfloat16)
    back_rows = lax.all_to_all(
        inverse_roots.reshape(slot_count, n_dp, slab_rows, order_b),
        "dp",
        split_axis=1,
        concat_axis=1,
        tiled=True,
    )
    returned = jnp.dot(
        route_table.T,
        back_rows.reshape(slot_count * n_dp, slab_rows * order_b),
        preferred_element_type=jnp.float32,
    )
    returned = returned.astype(jnp.bfloat16).reshape(n_owner, pair_count, slab_rows, order_b)
    home_rows = lax.all_to_all(returned, "owner", split_axis=0, concat_axis=0, tiled=True)
    item_rows = jnp.dot(
        lane_pick.T,
        home_rows.reshape(lane_count, slab_rows * order_b),
        preferred_element_type=jnp.float32,
    )
    item_rows = item_rows.astype(jnp.bfloat16).reshape(blocks_col, 2, slab_rows, order_b)
    left_rows = item_rows[:, 0]
    right_rows = item_rows[:, 1]
    columns = summed
    applied_rows = jnp.einsum(
        "jrk,jkc->jrc",
        columns,
        lax.all_gather(right_rows, "dp", axis=1, tiled=True),
        preferred_element_type=jnp.float32,
    ).astype(jnp.bfloat16)
    columns = left_rows
    combined = jnp.einsum(
        "jrk,jkc->jrc",
        columns,
        lax.all_gather(applied_rows, "dp", axis=1, tiled=True),
        preferred_element_type=jnp.float32,
    )
    return (update_gain * combined).astype(jnp.bfloat16)


def solution(mesh):
    in_specs = (P("dp", "owner", None, None), P("dp", "owner", None, None, None), P())
    out_specs = P("owner", "dp", None)
    return jax.shard_map(body, mesh=mesh, in_specs=in_specs, out_specs=out_specs, check_vma=False)
```

profile of v0, /device:TPU:1, one launch (start us, length us, event | category | flops | bytes accessed | tf_op | source)
XLA Modules:
  0.0 427.9 jit_solution(7372320996058796730)
XLA Ops:
  6.5 0.0 copy-start.1
  6.5 0.0 reduce-scatter.2.cloned.1.call-start
  6.5 0.7 reduce-scatter.2.cloned.1.call-update
  7.3 0.0 copy-done.1
  7.3 0.1 copy.29
  7.4 0.1 reshape.196
  7.6 0.2 convert_reduce_fusion.1
  7.8 0.1 dynamic-slice_add_fusion
  7.9 0.1 eq.166
  8.0 0.1 fusion.35
  8.1 97.6 %reduce-scatter.2.cloned.1.call-done = bf16[5,32,512]{2,1,0:T(8,128)(2,1)} async-done(((bf16[5,512,512]{2,1,0:T(8,128)(2,1)}), bf16[5,32,512]{2,1,0:T(8,128)(2,1)}) %reduce-scatter.2.cloned.1.call-update) | async-done | bytes 163856 | tf_op jit(solution)/shard_map/reduce_scatter | solution.py:55
  105.7 1.0 copy.41
  106.7 0.5 convolution_convert_fusion.2
  107.2 1.3 copy.42
  108.5 14.7 %all-to-all-start = ((bf16[32,1,32,512]{3,2,1,0:T(8,128)(2,1)}), bf16[32,1,32,512]{3,2,1,0:T(8,128)(2,1)S(1)}, u32[]{:S(2)}, u32[]{:S(2)}) async-start(bf16[32,1,32,512]{3,2,1,0:T(8,128)(2,1)} %bitcast.2), calls=%async_computation.1 | async-start | bytes 2097152 | tf_op jit(solution)/shard_map/all_to_all | solution.py:75
  123.2 0.2 convert_reduce_fusion
  123.5 0.3 convolution_convert_fusion.4
  123.8 55.1 %all-to-all-done = bf16[32,1,32,512]{3,2,1,0:T(8,128)(2,1)S(1)} async-done(((bf16[32,1,32,512]{3,2,1,0:T(8,128)(2,1)}), bf16[32,1,32,512]{3,2,1,0:T(8,128)(2,1)S(1)}, u32[]{:S(2)}, u32[]{:S(2)}) %all-to-all-start) | async-done | bytes 1048608 | tf_op jit(solution)/shard_map/all_to_all | solution.py:75
  179.0 0.6 copy.43
  179.6 0.4 convolution_convert_fusion.1
  180.0 0.3 copy.44
  180.3 1.1 copy.31
  181.4 4.5 %all-to-all-start.1 = ((bf16[2,16,32,512]{3,2,0,1:T(8,128)(2,1)}), bf16[2,16,32,512]{3,2,0,1:T(8,128)(2,1)S(1)}, u32[]{:S(2)}, u32[]{:S(2)}) async-start(bf16[2,16,32,512]{3,2,0,1:T(8,128)(2,1)} %copy.31), calls=%async_computation.2 | async-start | bytes 2097152 | tf_op jit(solution)/shard_map/all_to_all | solution.py:90
  185.9 0.0 all-gather.6.cloned.1.call-start
  185.9 0.1 fusion.34
  186.1 0.1 fusion.25
  186.2 14.9 %all-to-all-done.1 = bf16[2,16,32,512]{3,2,0,1:T(8,128)(2,1)S(1)} async-done(((bf16[2,16,32,512]{3,2,0,1:T(8,128)(2,1)}), bf16[2,16,32,512]{3,2,0,1:T(8,128)(2,1)S(1)}, u32[]{:S(2)}, u32[]{:S(2)}) %all-to-all-start.1) | async-done | bytes 1048608 | tf_op jit(solution)/shard_map/all_to_all | solution.py:90
  201.1 0.1 copy.32
  201.2 0.7 copy.33
  202.0 2.7 multiply_reduce_fusion
  204.7 4.1 fusion.7
  208.8 3.5 fusion.49
  212.3 3.7 fusion.5
  216.0 4.1 multiply_convert_fusion
  220.1 0.1 copy.34
  220.2 19.4 %all_to_all.20 = bf16[2,16,32,512]{3,2,0,1:T(8,128)(2,1)S(1)} all-to-all(bf16[2,16,32,512]{3,2,0,1:T(8,128)(2,1)S(1)} %copy.34), channel_id=1, replica_groups=mesh['dp'=16,'owner'=32] {'dp'}, dimensions={1} | all-to-all | bytes 2097152 | tf_op jit(solution)/shard_map/all_to_all | solution.py:110
  239.7 0.1 copy.35
  239.8 0.6 copy.45
  240.4 0.5 convolution_convert_fusion
  240.8 0.3 copy.46
  241.2 61.5 %all_to_all.21 = bf16[32,1,32,512]{3,2,1,0:T(8,128)(2,1)S(1)} all-to-all(bf16[32,1,32,512]{3,2,1,0:T(8,128)(2,1)S(1)} %bitcast.79), channel_id=1, replica_groups=mesh['dp'=16,'owner'=32] {'owner'}, dimensions={0} | all-to-all | bytes 2097152 | tf_op jit(solution)/shard_map/all_to_all | solution.py:123
  302.7 0.6 copy.47
  303.3 0.0 copy-start
  303.3 0.4 convolution_convert_fusion.3
  303.6 0.2 copy.48
  303.8 0.7 slice_bitcast_fusion
  304.5 0.0 all-gather.6.cloned.1.call-update
  304.5 0.0 all-gather.4.cloned.1.call-start
  304.6 49.7 %all-gather.6.cloned.1.call-done = bf16[5,1,512,512]{3,2,0,1:T(8,128)(2,1)} async-done(((bf16[5,1,32,512]{3,2,0,1:T(8,128)(2,1)}), bf16[5,1,512,512]{3,2,0,1:T(8,128)(2,1)}) %all-gather.6.cloned.1.call-update) | async-done | bytes 2621456 | tf_op jit(solution)/shard_map/all_gather | solution.py:136
  354.3 0.0 copy-done
  354.3 3.0 fusion.14
  357.3 0.0 all-gather.4.cloned.1.call-update
  357.3 61.2 %all-gather.4.cloned.1.call-done = bf16[5,512,512]{2,1,0:T(8,128)(2,1)} async-done(((bf16[5,32,512]{2,1,0:T(8,128)(2,1)}), bf16[5,512,512]{2,1,0:T(8,128)(2,1)}) %all-gather.4.cloned.1.call-update) | async-done | bytes 2621456 | tf_op jit(solution)/shard_map/all_gather | solution.py:143
  418.5 2.9 fusion.10
  (6 shorter events, 0.1 us)
Async XLA Ops:
  6.5 0.7 copy-start.1
  6.5 99.2 %reduce-scatter.2.cloned.1.call-start = ((), (), s32[]{:S(2)}) async-start(), calls=%async_computation.5 | async-start | bytes 2785280 | tf_op jit(solution)/shard_map/reduce_scatter | solution.py:55
  108.5 70.5 %all-to-all-start = ((bf16[32,1,32,512]{3,2,1,0:T(8,128)(2,1)}), bf16[32,1,32,512]{3,2,1,0:T(8,128)(2,1)S(1)}, u32[]{:S(2)}, u32[]{:S(2)}) async-start(bf16[32,1,32,512]{3,2,1,0:T(8,128)(2,1)} %bitcast.2), calls=%async_computation.1 | async-start | bytes 2097152 | tf_op jit(solution)/shard_map/all_to_all | solution.py:75
  181.4 19.8 %all-to-all-start.1 = ((bf16[2,16,32,512]{3,2,0,1:T(8,128)(2,1)}), bf16[2,16,32,512]{3,2,0,1:T(8,128)(2,1)S(1)}, u32[]{:S(2)}, u32[]{:S(2)}) async-start(bf16[2,16,32,512]{3,2,0,1:T(8,128)(2,1)} %copy.31), calls=%async_computation.2 | async-start | bytes 2097152 | tf_op jit(solution)/shard_map/all_to_all | solution.py:90
  185.9 168.4 %all-gather.6.cloned.1.call-start = ((), (), s32[]{:S(2)}) async-start(), calls=%async_computation.7 | async-start | bytes 2785280 | tf_op jit(solution)/shard_map/all_gather | solution.py:136
  303.3 51.1 %copy-start = (bf16[5,32,512]{2,1,0:T(8,128)(2,1)S(1)}, bf16[5,32,512]{2,1,0:T(8,128)(2,1)}, u32[]{:S(2)}) copy-start(bf16[5,32,512]{2,1,0:T(8,128)(2,1)} %reduce-scatter.2.cloned.1.call-done) | copy-start | bytes 491524
  304.5 113.9 %all-gather.4.cloned.1.call-start = ((), (), s32[]{:S(2)}) async-start(), calls=%async_computation.6 | async-start | bytes 2785280 | tf_op jit(solution)/shard_map/all_gather | solution.py:143
Sparse Core Ops, SparseCore 0:
  11.5 94.0 reduce-scatter.1
  304.6 49.6 all-gather.5
  357.4 61.0 all-gather.3
where the time goes:
time: 428 us
  waiting for transfers between devices  279 us (65%)
  blocking collectives  80.9 us (19%)
  matrix products  26.1 us (6%)
  starting transfers between devices  19.3 us (5%)
  between operations  13.3 us (3%)
  local copies, waits for them, and re-layouts  7.99 us (2%)
    reduce_scatter x1, waiting for transfers between devices, body(): lax.psum_scatter(grad_partial[0].astype(jnp.float32).astype(jnp.bfloat16)...  97.6 us
    all_to_all x1, blocking collectives, body(): lax.all_to_all(returned, 'owner', split_axis=0, concat_axis=0, tiled=True)  61.5 us
    all_gather x1, waiting for transfers between devices, body(): lax.all_gather(applied_rows, 'dp', axis=1, tiled=True)  61.2 us
    all_to_all x1, waiting for transfers between devices, body(): lax.all_to_all(outgoing, 'owner', split_axis=0, concat_axis=0, tiled=True)  55.1 us
    all_gather x1, waiting for transfers between devices, body(): lax.all_gather(right_rows, 'dp', axis=1, tiled=True)  49.7 us
    all_to_all x1, blocking collectives, body(): lax.all_to_all(inverse_roots.reshape(slot_count, n_dp, slab_rows, order_b...  19.4 us
    all_to_all x1, waiting for transfers between devices, body(): lax.all_to_all(forward, 'dp', split_axis=1, concat_axis=1, tiled=True)  14.9 us
    all_to_all x1, starting transfers between devices, body(): lax.all_to_all(outgoing, 'owner', split_axis=0, concat_axis=0, tiled=True)  14.7 us
  transfers between devices with their start and end apart: 5, of which 5 were waited for; matrix products, arithmetic and copies ran while one was open for 0% of the time, Pallas kernels for 0%

commit v1 on v0

v1 whole, which is shorter than its diff:
```python
import functools
import math

import jax
import jax.numpy as jnp
import numpy as np
from jax import lax
from jax.experimental import pallas as pl
from jax.experimental.pallas import tpu as pltpu
from jax.sharding import Mesh
from jax.sharding import PartitionSpec as P

decay_rate = 0.9
update_gain = 16.0
root_gain = 1.5

side_x = 4
chips = (
    ((0, 0), (0, 2), (2, 0), (1, 1), (3, 3)),
    ((1, 0), (1, 2), (3, 0), (2, 1), (0, 3)),
)
blocks_col = len(chips[0])
packed_rows = 72

VMEM = pl.BlockSpec(memory_space=pltpu.VMEM)
SMEM = pl.BlockSpec(memory_space=pltpu.SMEM)


def even(v):
    return v ^ 1


def odd(v):
    return side_x - 1 - v


def order(portion, core):
    first, later = (even, odd) if core == 0 else (odd, even)
    one, two = portion, 1 - portion
    return ((one, first), (one, later), (two, first), (two, later))


def pairs(portion, step):
    out = []
    for x in range(side_x):
        for y in range(side_x):
            for p in range(2):
                axis, pairing = order(portion, p)[step]
                to = (pairing(x), y) if axis == 0 else (x, pairing(y))
                out.append((2 * (side_x * x + y) + p, 2 * (side_x * to[0] + to[1]) + p))
    return out


def padded(items, count):
    assert len(items) <= count
    return (list(items) + [0] * count)[:count]


@functools.cache
def tree_tables():
    first, second, third = [], [], []
    for d in range(side_x * side_x):
        here = (d // side_x, d % side_x)
        for p in range(2):
            one, two, three = [], [], []
            for portion in range(2):
                steps = order(portion, p)
                axis, later = steps[1]
                at = [c[axis] for c in chips[p]]
                me = here[axis]
                kept = [j for j in range(blocks_col) if at[j] in (me, later(me))]
                one += padded([j for j in range(blocks_col) if j not in kept], 3)
                padded(kept, 3)
                go = [i for i, j in enumerate(kept) if at[j] == later(me)]
                stay = [i for i, j in enumerate(kept) if at[j] == me]
                for place in padded(go, 2) + padded(stay, 2):
                    two += [place, padded(kept, 3)[place]]
                mine = [kept[i] for i in stay]
                axis, later = steps[3]
                near = (here[axis], later(here[axis]))
                stay = [i for i, j in enumerate(mine) if chips[p][j][axis] in near]
                go = [i for i, j in enumerate(mine) if chips[p][j][axis] not in near]
                three += padded(go, 1) + padded(stay, 1)
            first.append(one)
            second.append(two)
            third.append(three)
    return [np.array(t, np.int32) for t in (first, second, third)]


@functools.cache
def home_tables():
    item = np.zeros((2, 2 * side_x * side_x), np.int32)
    rows = np.zeros((2, blocks_col), np.int32)
    for p in range(2):
        for j, (x, y) in enumerate(chips[p]):
            d = side_x * x + y
            rows[p, j] = d
            item[p, 2 * d : 2 * d + 2] = (2 * j, 2 * j + 1)
    return item, rows


def params(mib):
    return pltpu.CompilerParams(vmem_limit_bytes=mib * 1024 * 1024)


def add_rounded(a, b):
    return (a.astype(jnp.float32) + b.astype(jnp.float32)).astype(jnp.bfloat16)


def choose_kernel(table, source, s0, s1):
    height = s0.shape[1]
    for h, sent in enumerate((s0, s1)):
        for u in range(3):
            sent[u] = source[table[3 * h + u], h * height : (h + 1) * height, :]


def first_sum_kernel(table, source, r0, r1, s0, s1, kept):
    height = r0.shape[1]
    for h, (got, sent) in enumerate(((r0, s0), (r1, s1))):
        for u in range(4):
            place, block = table[8 * h + 2 * u], table[8 * h + 2 * u + 1]
            total = add_rounded(source[block, h * height : (h + 1) * height, :], got[place])
            if u < 2:
                sent[u] = total
            else:
                kept[h, u - 2] = total


def second_sum_kernel(table, kept, r0, r1, s0, s1, next_kept):
    for h, (got, sent) in enumerate(((r0, s0), (r1, s1))):
        go, stay = table[2 * h], table[2 * h + 1]
        sent[...] = add_rounded(kept[h, go], got[go])
        next_kept[h] = add_rounded(kept[h, stay], got[stay])


def third_sum_kernel(kept, r0, r1, s0, s1):
    s0[...] = add_rounded(kept[0], r0[...])
    s1[...] = add_rounded(kept[1], r1[...])


def gram_kernel(a, b, r0, r1, out, left, right):
    half = a.shape[0]
    out[:half, :] = add_rounded(a[...], r0[...])
    out[half:, :] = add_rounded(b[...], r1[...])
    g = out[...]
    for gram, side in ((left, 1), (right, 0)):
        gram[...] = lax.dot_general(
            g, g, (((side,), (side,)), ((), ())), preferred_element_type=jnp.float32
        )


def pick_kernel(table, source, out):
    for i in range(out.shape[0]):
        out[i] = source[table[i]]


def pick(table, source):
    return pl.pallas_call(
        pick_kernel,
        out_shape=jax.ShapeDtypeStruct(table.shape + source.shape[1:], source.dtype),
        in_specs=[SMEM, VMEM],
        out_specs=VMEM,
        compiler_params=params(4),
        cost_estimate=pl.CostEstimate(
            flops=0, bytes_accessed=4 * table.shape[0] * 65536, transcendentals=0
        ),
    )(table, source)


def square_iotas(n):
    return (
        lax.broadcasted_iota(jnp.int32, (n, n), 0),
        lax.broadcasted_iota(jnp.int32, (n, n), 1),
    )


def pack_kernel(stats, out):
    half = stats.shape[1] // 2
    i, j = square_iotas(half)
    row = lax.broadcasted_iota(jnp.int32, (8, 128), 0)
    for q in range(stats.shape[0]):
        low = stats[q, half:, half:]
        mixed = jnp.where(i <= j, stats[q, :half, :half], low).astype(jnp.bfloat16)
        side = stats[q, :half, half:].astype(jnp.bfloat16)
        diagonal = jnp.sum(jnp.where(i == j, low, 0.0), axis=0, keepdims=True)
        tail = jnp.where(
            row == 0, diagonal[:, :128], jnp.where(row == 1, diagonal[:, 128:], 0.0)
        ).astype(jnp.bfloat16)
        strips = (mixed[:, :128], mixed[:, 128:], side[:, :128], side[:, 128:])
        for c in range(16):
            out[c, q, :64, :] = strips[c // 4][64 * (c % 4) : 64 * (c % 4) + 64, :]
            out[c, q, 64:, :] = tail


def split(a):
    high = a.astype(jnp.bfloat16)
    return high, (a - high.astype(jnp.float32)).astype(jnp.bfloat16)


def product(a, b):
    dot = functools.partial(jnp.dot, preferred_element_type=jnp.float32)
    return dot(a[0], b[0]) + (dot(a[0], b[1]) + dot(a[1], b[0]))


def unpack(chunks, s, mixed, stat):
    half = mixed.shape[0]
    for c in range(16):
        strip = chunks[c, s, :64, :].astype(jnp.float32)
        rows = slice(64 * (c % 4), 64 * (c % 4) + 64)
        at = c // 4
        if at < 2:
            mixed[rows, 128 * at : 128 * at + 128] = strip
        else:
            stat[rows, half + 128 * (at - 2) : half + 128 * (at - 2) + 128] = strip
    tail = chunks[0, s, 64:, :].astype(jnp.float32)
    diagonal = jnp.concatenate([tail[0:1, :], tail[1:2, :]], axis=1)
    m = mixed[...]
    flipped = m.T
    i, j = square_iotas(half)
    stat[:half, :half] = jnp.where(i <= j, m, flipped)
    stat[half:, half:] = jnp.where(i > j, m, jnp.where(i == j, diagonal, flipped))
    stat[half:, :half] = stat[:half, half:].T


def update_kernel(chunks, gradient, left, right, out, mixed, stat):
    order_n = out.shape[0]
    sides = (0, 1)
    for s in sides:
        unpack(chunks, s, mixed.at[s], stat.at[s])
    i, j = square_iotas(order_n)
    identity = jnp.where(i == j, 1.25, 0.0)
    scale, first = [], []
    for s, gram in zip(sides, (left, right)):
        new_stat = decay_rate * stat[s] + (1.0 - decay_rate) * gram[...]
        squares = jnp.sum(new_stat * new_stat, axis=0, keepdims=True)
        frob_norm = jnp.sqrt(jnp.sum(squares, axis=1, keepdims=True) + 1e-06)
        scale.append(root_gain * math.sqrt(order_n) / frob_norm)
        first.append(identity - (0.25 * scale[s]) * new_stat)
    parts = [split(f) for f in first]
    squared = [product(f, f) for f in parts]
    parts = [split(f) for f in squared]
    fourth = [split(product(f, f)) for f in parts]
    rest = [split(squared[s] - 1.25 * first[s]) for s in sides]
    roots = []
    for s in sides:
        root = 1.25 * first[s] + product(fourth[s], rest[s])
        roots.append((jnp.sqrt(jnp.sqrt(scale[s])) * root).astype(jnp.bfloat16))
    applied = jnp.dot(gradient[...], roots[1], preferred_element_type=jnp.float32)
    update = jnp.dot(
        roots[0], applied.astype(jnp.bfloat16), preferred_element_type=jnp.float32
    )
    out[...] = (update_gain * update).astype(jnp.bfloat16)


def shape(*dims):
    return jax.ShapeDtypeStruct(dims, jnp.bfloat16)


def cost(flops, moved):
    return pl.CostEstimate(flops=flops, bytes_accessed=moved, transcendentals=0)


def exchange(arrays, step):
    return [
        lax.ppermute(a, ("dp", "core"), pairs(portion, step)) for portion, a in enumerate(arrays)
    ]


def first_sent(grad, tables):
    n, order_n = grad.shape[1], grad.shape[2]
    return pl.pallas_call(
        choose_kernel,
        out_shape=[shape(3, n // 2, order_n)] * 2,
        in_specs=[SMEM, VMEM],
        out_specs=[VMEM] * 2,
        compiler_params=params(12),
        cost_estimate=cost(0, 6 * n * order_n),
    )(tables[0], grad)


def gradient_sum(grad, sent, tables):
    n, order_n = grad.shape[1], grad.shape[2]
    half = n // 2
    unit = 2 * half * order_n
    *sent, kept = pl.pallas_call(
        first_sum_kernel,
        out_shape=[shape(2, half, order_n)] * 2 + [shape(2, 2, half, order_n)],
        in_specs=[SMEM] + [VMEM] * 3,
        out_specs=[VMEM] * 3,
        compiler_params=params(16),
        cost_estimate=cost(0, 24 * unit),
    )(tables[1], grad, *exchange(sent, 0))
    *sent, kept = pl.pallas_call(
        second_sum_kernel,
        out_shape=[shape(half, order_n)] * 2 + [shape(2, half, order_n)],
        in_specs=[SMEM] + [VMEM] * 3,
        out_specs=[VMEM] * 3,
        compiler_params=params(12),
        cost_estimate=cost(0, 12 * unit),
    )(tables[2], kept, *exchange(sent, 1))
    sent = pl.pallas_call(
        third_sum_kernel,
        out_shape=[shape(half, order_n)] * 2,
        in_specs=[VMEM] * 3,
        out_specs=[VMEM] * 2,
        compiler_params=params(8),
        cost_estimate=cost(0, 6 * unit),
    )(kept, *exchange(sent, 2))
    square = jax.ShapeDtypeStruct((n, order_n), jnp.float32)
    return pl.pallas_call(
        gram_kernel,
        out_shape=[shape(n, order_n), square, square],
        in_specs=[VMEM] * 4,
        out_specs=[VMEM] * 3,
        compiler_params=params(16),
        cost_estimate=cost(4 * n**3, 12 * unit),
    )(*sent, *exchange(sent, 3))


def body(grad_partial, statistics, owner_table):
    n_dp = lax.axis_size("dp")
    n_owner = lax.axis_size("z") * 2
    order_b = grad_partial.shape[3]
    slab = order_b // n_dp
    slots = statistics.shape[2]
    row = lax.axis_index("dp")
    core = lax.axis_index("core")
    col = 2 * lax.axis_index("z") + core
    lane_item, out_rows = home_tables()
    tables = [jnp.asarray(t)[2 * row + core] for t in tree_tables()]

    device = owner_table.reshape(-1)
    numbers = jnp.arange(device.shape[0], dtype=jnp.int32)
    earlier = numbers[None, :] < numbers[:, None]
    slot_of = jnp.sum(
        ((device[None, :] == device[:, None]) & earlier).astype(jnp.int32), axis=1
    )
    by_column = (device % n_owner).reshape(n_owner, 2 * blocks_col)
    place = ((device // n_owner) * slots + slot_of).reshape(n_owner, 2 * blocks_col)
    lane_from = jnp.sum(jnp.where(by_column == col, place, 0), axis=1)
    home = lax.dynamic_slice_in_dim(by_column, col, 1, axis=0)
    wanted = jnp.asarray(lane_item)[core]
    item_hot = wanted[:, None] == jnp.arange(2 * blocks_col)[None, :]
    item_from = jnp.sum(jnp.where(item_hot, home, 0), axis=1)

    packed = pl.pallas_call(
        pack_kernel,
        out_shape=shape(n_dp, slots, packed_rows, 128),
        in_specs=[VMEM],
        out_specs=VMEM,
        compiler_params=params(12),
        cost_estimate=cost(0, 3 * 1024 * 1024),
    )(statistics[0, 0])
    spread = lax.all_to_all(packed, "dp", split_axis=0, concat_axis=0, tiled=True)
    sent = first_sent(grad_partial[0], tables)
    spread, sent = lax.optimization_barrier((spread, sent))
    lanes = pick(lane_from, spread.reshape(slots * n_dp, packed_rows, 128))
    lanes = lax.all_to_all(lanes, ("z", "core"), split_axis=0, concat_axis=0, tiled=True)
    gradient, left, right = gradient_sum(grad_partial[0], sent, tables)
    lanes = pick(item_from, lanes).reshape(n_dp, 2, packed_rows, 128)
    chunks = lax.all_to_all(lanes, "dp", split_axis=0, concat_axis=0, tiled=True)

    full = (order_b, order_b)
    update = pl.pallas_call(
        update_kernel,
        out_shape=shape(*full),
        in_specs=[VMEM] * 4,
        out_specs=VMEM,
        scratch_shapes=[
            pltpu.VMEM((2, order_b // 2, order_b // 2), jnp.float32),
            pltpu.VMEM((2,) + full, jnp.float32),
        ],
        compiler_params=params(40),
        cost_estimate=cost(40 * order_b**3, 6 * 1024 * 1024),
    )(chunks, gradient, left, right)
    rows = update.reshape(n_dp, slab, order_b)
    rows = lax.all_to_all(rows, "dp", split_axis=0, concat_axis=0, tiled=True)
    return pick(jnp.asarray(out_rows)[core], rows)


def solution(mesh):
    n_dp, n_owner = mesh.devices.shape
    fine = Mesh(mesh.devices.reshape(n_dp, n_owner // 2, 2), ("dp", "z", "core"))
    column = ("z", "core")
    in_specs = (P("dp", column, None, None), P("dp", column, None, None, None), P())
    out_specs = P(column, "dp", None)
    return jax.shard_map(body, mesh=fine, in_specs=in_specs, out_specs=out_specs, check_vma=False)
```

time: 428 us -> 124 us (0.29)
  the two profiles are of different devices: /device:TPU:1 before, /device:TPU:32 now
where the time goes in v1:
time: 124 us; the launch traced here: 123 us
  starting transfers between devices  57.4 us (46%)
  waiting for transfers between devices  42.1 us (34%)
  Pallas kernels  14.8 us (12%)
  local copies, waits for them, and re-layouts  8.02 us (6%)
    ppermute x8, starting transfers between devices, exchange(): lax.ppermute(a, ('dp', 'core'), pairs(portion, step))  25.3 us
    ppermute x8, waiting for transfers between devices, exchange(): lax.ppermute(a, ('dp', 'core'), pairs(portion, step))  24.5 us
    all_to_all x1, starting transfers between devices, body(): lax.all_to_all(lanes, ('z', 'core'), split_axis=0, concat_axis=0, tiled=T...  15.4 us
    all_to_all x1, waiting for transfers between devices, body(): rows = lax.all_to_all(rows, 'dp', split_axis=0, concat_axis=0, tiled=True)  10.1 us
    all_to_all x1, waiting for transfers between devices, body(): lax.all_to_all(packed, 'dp', split_axis=0, concat_axis=0, tiled=True)  7.51 us
    pallas_call x1, Pallas kernels, body(): pl.pallas_call(update_kernel, out_shape=shape(*full), in_specs=[VMEM] * 4...  7.3 us
    all_to_all x1, starting transfers between devices, body(): lax.all_to_all(packed, 'dp', split_axis=0, concat_axis=0, tiled=True)  7.03 us
    all_to_all x1, starting transfers between devices, body(): lax.all_to_all(lanes, 'dp', split_axis=0, concat_axis=0, tiled=True)  5.35 us
  transfers between devices with their start and end apart: 12, of which 8 were waited for; matrix products, arithmetic and copies ran while one was open for 3% of the time, Pallas kernels for 5%

profile of v1, /device:TPU:32, one launch (start us, length us, event | category | flops | bytes accessed | tf_op | source)
XLA Modules:
  0.0 123.4 jit_solution(16141239761467635993)
XLA Ops:
  0.0 0.0 copy-start.3
  0.0 1.7 %copy-done.3 = f32[1,1,2,512,512]{4,3,2,1,0:T(8,128)S(1)} copy-done((f32[1,1,2,512,512]{4,3,2,1,0:T(8,128)S(1)}, f32[1,1,2,512,512]{4,3,2,1,0:T(8,128)}, u32[]{:S(2)}) %copy-start.3) | copy-done | bytes 2097176
  1.7 0.0 copy-start.6
  1.7 0.1 shard_map.82
  1.9 0.0 copy-start.2
  1.9 0.8 copy-done.2
  2.7 7.0 %all-to-all-start = ((bf16[16,2,72,128]{3,2,1,0:T(8,128)(2,1)}), bf16[16,2,72,128]{3,2,1,0:T(8,128)(2,1)S(1)}, u32[]{:S(2)}, u32[]{:S(2)}) async-start(bf16[16,2,72,128]{3,2,1,0:T(8,128)(2,1)} %copy-done.2), calls=%async_computation | async-start | bytes 1179648 | tf_op jit(solution)/shard_map/all_to_all | solution.py:354
  9.8 0.0 copy-done.6
  9.8 0.1 copy.18
  9.9 0.1 copy.23
  10.0 0.1 eq.45
  10.2 0.2 convert_reduce_fusion
  10.4 0.1 reduce_sum.38
  10.6 0.0 copy-start.8
  10.6 0.2 fusion.5
  10.8 0.1 reduce_sum.40
  10.9 0.1 reduce_sum.41.table
  11.0 0.7 fusion.10.table
  11.7 0.0 copy-done
  11.7 0.6 shard_map.83
  12.3 0.0 copy-start.4
  12.3 0.9 copy-done.4
  13.2 0.0 copy-start.5
  13.2 0.9 copy-done.5
  14.1 7.5 %all-to-all-done = bf16[16,2,72,128]{3,2,1,0:T(8,128)(2,1)S(1)} async-done(((bf16[16,2,72,128]{3,2,1,0:T(8,128)(2,1)}), bf16[16,2,72,128]{3,2,1,0:T(8,128)(2,1)S(1)}, u32[]{:S(2)}, u32[]{:S(2)}) %all-to-all-start) | async-done | bytes 589856 | tf_op jit(solution)/shard_map/all_to_all | solution.py:354
  21.6 0.6 shard_map.84
  22.2 0.0 copy-start.1
  22.2 0.8 copy-done.1
  23.1 15.4 %all-to-all-start.1 = ((bf16[32,72,128]{2,1,0:T(8,128)(2,1)}), bf16[32,72,128]{2,1,0:T(8,128)(2,1)S(1)}, u32[]{:S(2)}, u32[]{:S(2)}) async-start(bf16[32,72,128]{2,1,0:T(8,128)(2,1)} %copy-done.1), calls=%async_computation.1 | async-start | bytes 1179648 | tf_op jit(solution)/shard_map/all_to_all | solution.py:358
  38.4 2.0 %collective-permute-start = (bf16[3,256,512]{2,1,0:T(8,128)(2,1)}, bf16[3,256,512]{2,1,0:T(8,128)(2,1)}, u32[]{:S(2)}, u32[]{:S(2)}) collective-permute-start(bf16[3,256,512]{2,1,0:T(8,128)(2,1)} %copy-done.5), channel_id=1, source_target_pairs={{0,128},{1,385},{32,160},{33,417},{64,192},{65,449},{96,224},{97,4... | collective-permute-start | bytes 2359304 | tf_op jit(solution)/shard_map/ppermute | solution.py:265
  40.4 2.3 %collective-permute-start.1 = (bf16[3,256,512]{2,1,0:T(8,128)(2,1)}, bf16[3,256,512]{2,1,0:T(8,128)(2,1)}, u32[]{:S(2)}, u32[]{:S(2)}) collective-permute-start(bf16[3,256,512]{2,1,0:T(8,128)(2,1)} %copy-done.4), channel_id=1, source_target_pairs={{0,32},{1,97},{32,0},{33,65},{64,96},{65,33},{96,64},{97,1},{128,1... | collective-permute-start | bytes 2359304 | tf_op jit(solution)/shard_map/ppermute | solution.py:265
  42.7 0.1 reshape.22
  42.8 0.7 fusion.12.table
  43.5 0.7 fusion.11.table
  44.2 0.0 copy-done.8
  44.2 8.4 %collective-permute-done.r0 = bf16[3,256,512]{2,1,0:T(8,128)(2,1)} collective-permute-done((bf16[3,256,512]{2,1,0:T(8,128)(2,1)}, bf16[3,256,512]{2,1,0:T(8,128)(2,1)}, u32[]{:S(2)}, u32[]{:S(2)}) %collective-permute-start) | collective-permute-done | bytes 786464 | tf_op jit(solution)/shard_map/ppermute | solution.py:265
  52.6 2.0 %collective-permute-done.1.r1 = bf16[3,256,512]{2,1,0:T(8,128)(2,1)} collective-permute-done((bf16[3,256,512]{2,1,0:T(8,128)(2,1)}, bf16[3,256,512]{2,1,0:T(8,128)(2,1)}, u32[]{:S(2)}, u32[]{:S(2)}) %collective-permute-start.1) | collective-permute-done | bytes 786464 | tf_op jit(solution)/shard_map/ppermute | solution.py:265
  54.6 1.9 %shard_map.86 = (bf16[2,256,512]{2,1,0:T(8,128)(2,1)S(1)}, bf16[2,256,512]{2,1,0:T(8,128)(2,1)S(1)}, bf16[2,2,256,512]{3,2,1,0:T(8,128)(2,1)S(1)}) custom-call(s32[16]{0:T(128)S(1)} %fusion.12.table, bf16[5,512,512]{2,1,0:T(8,128)(2,1)S(1)} %bitcast.18, bf16[3,256,512]{2,1,0:T(8,128)(2,1)} %collective-permute-done.r0, ...), custom_call_target="tpu_custom_call" | custom-call | bytes 6291456 | tf_op jit(solution)/shard_map/pallas_call | solution.py:285
  56.5 3.8 %collective-permute-start.2 = (bf16[2,256,512]{2,1,0:T(8,128)(2,1)S(1)}, bf16[2,256,512]{2,1,0:T(8,128)(2,1)S(1)}, u32[]{:S(2)}, u32[]{:S(2)}) collective-permute-start(bf16[2,256,512]{2,1,0:T(8,128)(2,1)S(1)} %get-tuple-element.27), channel_id=1, source_target_pairs={{0,384},{1,129},{32,416},{33,161},{64,448},{65,193},{96,480},{97,2... | collective-permute-start | bytes 1572872 | tf_op jit(solution)/shard_map/ppermute | solution.py:265
  60.2 2.9 %collective-permute-start.3 = (bf16[2,256,512]{2,1,0:T(8,128)(2,1)S(1)}, bf16[2,256,512]{2,1,0:T(8,128)(2,1)S(1)}, u32[]{:S(2)}, u32[]{:S(2)}) collective-permute-start(bf16[2,256,512]{2,1,0:T(8,128)(2,1)S(1)} %get-tuple-element.28), channel_id=1, source_target_pairs={{0,96},{1,33},{32,64},{33,1},{64,32},{65,97},{96,0},{97,65},{128,2... | collective-permute-start | bytes 1572872 | tf_op jit(solution)/shard_map/ppermute | solution.py:265
  63.2 5.5 %collective-permute-done.2.r0 = bf16[2,256,512]{2,1,0:T(8,128)(2,1)S(1)} collective-permute-done((bf16[2,256,512]{2,1,0:T(8,128)(2,1)S(1)}, bf16[2,256,512]{2,1,0:T(8,128)(2,1)S(1)}, u32[]{:S(2)}, u32[]{:S(2)}) %collective-permute-start.2) | collective-permute-done | bytes 524320 | tf_op jit(solution)/shard_map/ppermute | solution.py:265
  68.7 3.8 %collective-permute-done.3.r1 = bf16[2,256,512]{2,1,0:T(8,128)(2,1)S(1)} collective-permute-done((bf16[2,256,512]{2,1,0:T(8,128)(2,1)S(1)}, bf16[2,256,512]{2,1,0:T(8,128)(2,1)S(1)}, u32[]{:S(2)}, u32[]{:S(2)}) %collective-permute-start.3) | collective-permute-done | bytes 524320 | tf_op jit(solution)/shard_map/ppermute | solution.py:265
  72.5 0.8 shard_map.87
  73.3 1.9 %collective-permute-start.4 = (bf16[256,512]{1,0:T(8,128)(2,1)S(1)}, bf16[256,512]{1,0:T(8,128)(2,1)S(1)}, u32[]{:S(2)}, u32[]{:S(2)}) collective-permute-start(bf16[256,512]{1,0:T(8,128)(2,1)S(1)} %get-tuple-element.30), channel_id=1, source_target_pairs={{0,32},{1,97},{32,0},{33,65},{64,96},{65,33},{96,64},{97,1},{128,1... | collective-permute-start | bytes 786440 | tf_op jit(solution)/shard_map/ppermute | solution.py:265
  75.3 2.8 %collective-permute-start.5 = (bf16[256,512]{1,0:T(8,128)(2,1)S(1)}, bf16[256,512]{1,0:T(8,128)(2,1)S(1)}, u32[]{:S(2)}, u32[]{:S(2)}) collective-permute-start(bf16[256,512]{1,0:T(8,128)(2,1)S(1)} %get-tuple-element.31), channel_id=1, source_target_pairs={{0,128},{1,385},{32,160},{33,417},{64,192},{65,449},{96,224},{97,4... | collective-permute-start | bytes 786440 | tf_op jit(solution)/shard_map/ppermute | solution.py:265
  78.0 0.2 select_reduce_fusion.table
  78.2 0.0 all-to-all-done.1.source
  78.2 1.4 %shard_map.85 = bf16[32,72,128]{2,1,0:T(8,128)(2,1)} custom-call(s32[32]{0:T(128)S(1)} %select_reduce_fusion.table, bf16[32,72,128]{2,1,0:T(8,128)(2,1)S(1)} %all-to-all-done.1.source), custom_call_target="tpu_custom_call" | custom-call | bytes 8388608 | tf_op jit(solution)/shard_map/pallas_call | solution.py:158
  79.6 5.3 %all-to-all-start.2 = ((bf16[16,2,72,128]{3,2,1,0:T(8,128)(2,1)}), bf16[16,2,72,128]{3,2,1,0:T(8,128)(2,1)S(1)}, u32[]{:S(2)}, u32[]{:S(2)}) async-start(bf16[16,2,72,128]{3,2,1,0:T(8,128)(2,1)} %bitcast.7), calls=%async_computation.2 | async-start | bytes 1179648 | tf_op jit(solution)/shard_map/all_to_all | solution.py:361
  85.0 0.0 collective-permute-done.4.r0
  85.0 0.0 collective-permute-done.5.r1
  85.0 0.1 shard_map.88
  85.1 5.0 %collective-permute-start.6 = (bf16[256,512]{1,0:T(8,128)(2,1)S(1)}, bf16[256,512]{1,0:T(8,128)(2,1)S(1)}, u32[]{:S(2)}, u32[]{:S(2)}) collective-permute-start(bf16[256,512]{1,0:T(8,128)(2,1)S(1)} %get-tuple-element.32.a), channel_id=1, source_target_pairs={{0,96},{1,33},{32,64},{33,1},{64,32},{65,97},{96,0},{97,65},{128,2... | collective-permute-start | bytes 786440 | tf_op jit(solution)/shard_map/ppermute | solution.py:265
  90.2 4.6 %collective-permute-start.7 = (bf16[256,512]{1,0:T(8,128)(2,1)S(1)}, bf16[256,512]{1,0:T(8,128)(2,1)S(1)}, u32[]{:S(2)}, u32[]{:S(2)}) collective-permute-start(bf16[256,512]{1,0:T(8,128)(2,1)S(1)} %get-tuple-element.33.b), channel_id=1, source_target_pairs={{0,384},{1,129},{32,416},{33,161},{64,448},{65,193},{96,480},{97,2... | collective-permute-start | bytes 786440 | tf_op jit(solution)/shard_map/ppermute | solution.py:265
  94.8 2.9 %collective-permute-done.6.r0 = bf16[256,512]{1,0:T(8,128)(2,1)S(1)} collective-permute-done((bf16[256,512]{1,0:T(8,128)(2,1)S(1)}, bf16[256,512]{1,0:T(8,128)(2,1)S(1)}, u32[]{:S(2)}, u32[]{:S(2)}) %collective-permute-start.6) | collective-permute-done | bytes 262176 | tf_op jit(solution)/shard_map/ppermute | solution.py:265
  97.6 2.0 %collective-permute-done.7.r1 = bf16[256,512]{1,0:T(8,128)(2,1)S(1)} collective-permute-done((bf16[256,512]{1,0:T(8,128)(2,1)S(1)}, bf16[256,512]{1,0:T(8,128)(2,1)S(1)}, u32[]{:S(2)}, u32[]{:S(2)}) %collective-permute-start.7) | collective-permute-done | bytes 262176 | tf_op jit(solution)/shard_map/ppermute | solution.py:265
  99.7 0.8 shard_map.89
  100.4 0.0 all-to-all-done.2.chunks
  100.4 0.0 copy-start.7
  100.4 7.3 %shard_map.90 = bf16[512,512]{1,0:T(8,128)(2,1)} custom-call(bf16[16,2,72,128]{3,2,1,0:T(8,128)(2,1)S(1)} %all-to-all-done.2.chunks, bf16[512,512]{1,0:T(8,128)(2,1)S(1)} %get-tuple-element.34.gradient, f32[512,512]{1,0:T(8,128)S(1)} %get-tuple-element.35.left, f32[512,512]{1,0:T(8,128)S(1)} %get-tuple-element.36.right), custom_call_target="tpu_custom_call" | custom-call | flops 5368709120 | bytes 6291456 | tf_op jit(solution)/shard_map/pallas_call | solution.py:364
  107.7 4.3 %all-to-all-start.3 = ((bf16[16,32,512]{2,1,0:T(8,128)(2,1)}), bf16[16,32,512]{2,1,0:T(8,128)(2,1)S(1)}, u32[]{:S(2)}, u32[]{:S(2)}) async-start(bf16[16,32,512]{2,1,0:T(8,128)(2,1)} %bitcast.10), calls=%async_computation.3 | async-start | bytes 1048576 | tf_op jit(solution)/shard_map/all_to_all | solution.py:377
  112.1 0.0 copy-done.7
  112.1 10.1 %all-to-all-done.3.source = bf16[16,32,512]{2,1,0:T(8,128)(2,1)S(1)} async-done(((bf16[16,32,512]{2,1,0:T(8,128)(2,1)}), bf16[16,32,512]{2,1,0:T(8,128)(2,1)S(1)}, u32[]{:S(2)}, u32[]{:S(2)}) %all-to-all-start.3) | async-done | bytes 524320 | tf_op jit(solution)/shard_map/all_to_all | solution.py:377
  122.2 1.2 shard_map.91
  (7 shorter events, 0.1 us)
Async XLA Ops:
  0.0 11.7 %copy-start = (bf16[1,5,512,512]{3,2,1,0:T(8,128)(2,1)S(1)}, bf16[1,5,512,512]{3,2,1,0:T(8,128)(2,1)}, u32[]{:S(2)}) copy-start(bf16[1,5,512,512]{3,2,1,0:T(8,128)(2,1)} %param.8) | copy-start | bytes 7864324
  0.0 1.7 %copy-start.3 = (f32[1,1,2,512,512]{4,3,2,1,0:T(8,128)S(1)}, f32[1,1,2,512,512]{4,3,2,1,0:T(8,128)}, u32[]{:S(2)}) copy-start(f32[1,1,2,512,512]{4,3,2,1,0:T(8,128)} %param.9) | copy-start | bytes 6291460
  1.7 8.0 %copy-start.6 = (s32[160,2]{0,1:T(2,128)S(1)}, s32[160,2]{0,1:T(2,128)}, u32[]{:S(2)}) copy-start(s32[160,2]{0,1:T(2,128)} %param.10) | copy-start | bytes 3844
  1.9 0.8 copy-start.2
  2.7 18.9 %all-to-all-start = ((bf16[16,2,72,128]{3,2,1,0:T(8,128)(2,1)}), bf16[16,2,72,128]{3,2,1,0:T(8,128)(2,1)S(1)}, u32[]{:S(2)}, u32[]{:S(2)}) async-start(bf16[16,2,72,128]{3,2,1,0:T(8,128)(2,1)} %copy-done.2), calls=%async_computation | async-start | bytes 1179648 | tf_op jit(solution)/shard_map/all_to_all | solution.py:354
  10.6 33.6 %copy-start.8 = (s32[2,32]{1,0:T(2,128)S(1)}, s32[2,32]{1,0:T(2,128)}, u32[]{:S(2)}) copy-start(s32[2,32]{1,0:T(2,128)} %constant.59.clone) | copy-start | bytes 772
  12.3 0.9 copy-start.4
  13.2 0.9 copy-start.5
  22.2 0.8 copy-start.1
  23.1 55.1 %all-to-all-start.1 = ((bf16[32,72,128]{2,1,0:T(8,128)(2,1)}), bf16[32,72,128]{2,1,0:T(8,128)(2,1)S(1)}, u32[]{:S(2)}, u32[]{:S(2)}) async-start(bf16[32,72,128]{2,1,0:T(8,128)(2,1)} %copy-done.1), calls=%async_computation.1 | async-start | bytes 1179648 | tf_op jit(solution)/shard_map/all_to_all | solution.py:358
  38.4 14.2 %collective-permute-start = (bf16[3,256,512]{2,1,0:T(8,128)(2,1)}, bf16[3,256,512]{2,1,0:T(8,128)(2,1)}, u32[]{:S(2)}, u32[]{:S(2)}) collective-permute-start(bf16[3,256,512]{2,1,0:T(8,128)(2,1)} %copy-done.5), channel_id=1, source_target_pairs={{0,128},{1,385},{32,160},{33,417},{64,192},{65,449},{96,224},{97,4... | collective-permute-start | bytes 2359304 | tf_op jit(solution)/shard_map/ppermute | solution.py:265
  40.4 14.2 %collective-permute-start.1 = (bf16[3,256,512]{2,1,0:T(8,128)(2,1)}, bf16[3,256,512]{2,1,0:T(8,128)(2,1)}, u32[]{:S(2)}, u32[]{:S(2)}) collective-permute-start(bf16[3,256,512]{2,1,0:T(8,128)(2,1)} %copy-done.4), channel_id=1, source_target_pairs={{0,32},{1,97},{32,0},{33,65},{64,96},{65,33},{96,64},{97,1},{128,1... | collective-permute-start | bytes 2359304 | tf_op jit(solution)/shard_map/ppermute | solution.py:265
  56.5 12.3 %collective-permute-start.2 = (bf16[2,256,512]{2,1,0:T(8,128)(2,1)S(1)}, bf16[2,256,512]{2,1,0:T(8,128)(2,1)S(1)}, u32[]{:S(2)}, u32[]{:S(2)}) collective-permute-start(bf16[2,256,512]{2,1,0:T(8,128)(2,1)S(1)} %get-tuple-element.27), channel_id=1, source_target_pairs={{0,384},{1,129},{32,416},{33,161},{64,448},{65,193},{96,480},{97,2... | collective-permute-start | bytes 1572872 | tf_op jit(solution)/shard_map/ppermute | solution.py:265
  60.2 12.3 %collective-permute-start.3 = (bf16[2,256,512]{2,1,0:T(8,128)(2,1)S(1)}, bf16[2,256,512]{2,1,0:T(8,128)(2,1)S(1)}, u32[]{:S(2)}, u32[]{:S(2)}) collective-permute-start(bf16[2,256,512]{2,1,0:T(8,128)(2,1)S(1)} %get-tuple-element.28), channel_id=1, source_target_pairs={{0,96},{1,33},{32,64},{33,1},{64,32},{65,97},{96,0},{97,65},{128,2... | collective-permute-start | bytes 1572872 | tf_op jit(solution)/shard_map/ppermute | solution.py:265
  73.3 11.7 %collective-permute-start.4 = (bf16[256,512]{1,0:T(8,128)(2,1)S(1)}, bf16[256,512]{1,0:T(8,128)(2,1)S(1)}, u32[]{:S(2)}, u32[]{:S(2)}) collective-permute-start(bf16[256,512]{1,0:T(8,128)(2,1)S(1)} %get-tuple-element.30), channel_id=1, source_target_pairs={{0,32},{1,97},{32,0},{33,65},{64,96},{65,33},{96,64},{97,1},{128,1... | collective-permute-start | bytes 786440 | tf_op jit(solution)/shard_map/ppermute | solution.py:265
  75.3 9.7 %collective-permute-start.5 = (bf16[256,512]{1,0:T(8,128)(2,1)S(1)}, bf16[256,512]{1,0:T(8,128)(2,1)S(1)}, u32[]{:S(2)}, u32[]{:S(2)}) collective-permute-start(bf16[256,512]{1,0:T(8,128)(2,1)S(1)} %get-tuple-element.31), channel_id=1, source_target_pairs={{0,128},{1,385},{32,160},{33,417},{64,192},{65,449},{96,224},{97,4... | collective-permute-start | bytes 786440 | tf_op jit(solution)/shard_map/ppermute | solution.py:265
  79.6 20.8 %all-to-all-start.2 = ((bf16[16,2,72,128]{3,2,1,0:T(8,128)(2,1)}), bf16[16,2,72,128]{3,2,1,0:T(8,128)(2,1)S(1)}, u32[]{:S(2)}, u32[]{:S(2)}) async-start(bf16[16,2,72,128]{3,2,1,0:T(8,128)(2,1)} %bitcast.7), calls=%async_computation.2 | async-start | bytes 1179648 | tf_op jit(solution)/shard_map/all_to_all | solution.py:361
  85.1 12.5 %collective-permute-start.6 = (bf16[256,512]{1,0:T(8,128)(2,1)S(1)}, bf16[256,512]{1,0:T(8,128)(2,1)S(1)}, u32[]{:S(2)}, u32[]{:S(2)}) collective-permute-start(bf16[256,512]{1,0:T(8,128)(2,1)S(1)} %get-tuple-element.32.a), channel_id=1, source_target_pairs={{0,96},{1,33},{32,64},{33,1},{64,32},{65,97},{96,0},{97,65},{128,2... | collective-permute-start | bytes 786440 | tf_op jit(solution)/shard_map/ppermute | solution.py:265
  90.2 9.5 %collective-permute-start.7 = (bf16[256,512]{1,0:T(8,128)(2,1)S(1)}, bf16[256,512]{1,0:T(8,128)(2,1)S(1)}, u32[]{:S(2)}, u32[]{:S(2)}) collective-permute-start(bf16[256,512]{1,0:T(8,128)(2,1)S(1)} %get-tuple-element.33.b), channel_id=1, source_target_pairs={{0,384},{1,129},{32,416},{33,161},{64,448},{65,193},{96,480},{97,2... | collective-permute-start | bytes 786440 | tf_op jit(solution)/shard_map/ppermute | solution.py:265
  100.4 11.7 %copy-start.7 = (s32[2,5]{1,0:T(2,128)S(1)}, s32[2,5]{1,0:T(2,128)}, u32[]{:S(2)}) copy-start(s32[2,5]{1,0:T(2,128)} %constant.60.clone) | copy-start | bytes 124
  107.7 14.4 %all-to-all-start.3 = ((bf16[16,32,512]{2,1,0:T(8,128)(2,1)}), bf16[16,32,512]{2,1,0:T(8,128)(2,1)S(1)}, u32[]{:S(2)}, u32[]{:S(2)}) async-start(bf16[16,32,512]{2,1,0:T(8,128)(2,1)} %bitcast.10), calls=%async_computation.3 | async-start | bytes 1048576 | tf_op jit(solution)/shard_map/all_to_all | solution.py:377

commit v2 on v1

--- a/solution.py
+++ b/solution.py
@@ -107,7 +107,14 @@
     return (a.astype(jnp.float32) + b.astype(jnp.float32)).astype(jnp.bfloat16)
 
 
+def my_row(table):
+    width = table.shape[0] // (2 * side_x * side_x)
+    base = (2 * lax.axis_index("dp") + lax.axis_index("core")) * width
+    return [table[base + k] for k in range(width)]
+
+
 def choose_kernel(table, source, s0, s1):
+    table = my_row(table)
     height = s0.shape[1]
     for h, sent in enumerate((s0, s1)):
         for u in range(3):
@@ -115,6 +122,7 @@
 
 
 def first_sum_kernel(table, source, r0, r1, s0, s1, kept):
+    table = my_row(table)
     height = r0.shape[1]
     for h, (got, sent) in enumerate(((r0, s0), (r1, s1))):
         for u in range(4):
@@ -127,6 +135,7 @@
 
 
 def second_sum_kernel(table, kept, r0, r1, s0, s1, next_kept):
+    table = my_row(table)
     for h, (got, sent) in enumerate(((r0, s0), (r1, s1))):
         go, stay = table[2 * h], table[2 * h + 1]
         sent[...] = add_rounded(kept[h, go], got[go])
@@ -192,14 +201,10 @@
             out[c, q, 64:, :] = tail
 
 
-def split(a):
-    high = a.astype(jnp.bfloat16)
-    return high, (a - high.astype(jnp.float32)).astype(jnp.bfloat16)
-
-
 def product(a, b):
-    dot = functools.partial(jnp.dot, preferred_element_type=jnp.float32)
-    return dot(a[0], b[0]) + (dot(a[0], b[1]) + dot(a[1], b[0]))
+    return jnp.dot(
+        a.astype(jnp.bfloat16), b.astype(jnp.bfloat16), preferred_element_type=jnp.float32
+    )
 
 
 def unpack(chunks, s, mixed, stat):
@@ -228,22 +233,23 @@
     for s in sides:
         unpack(chunks, s, mixed.at[s], stat.at[s])
     i, j = square_iotas(order_n)
-    identity = jnp.where(i == j, 1.25, 0.0)
-    scale, first = [], []
+    scale, quarter, square = [], [], []
     for s, gram in zip(sides, (left, right)):
         new_stat = decay_rate * stat[s] + (1.0 - decay_rate) * gram[...]
+        rounded = new_stat.astype(jnp.bfloat16)
+        new_stat = rounded.astype(jnp.float32)
         squares = jnp.sum(new_stat * new_stat, axis=0, keepdims=True)
         frob_norm = jnp.sqrt(jnp.sum(squares, axis=1, keepdims=True) + 1e-06)
         scale.append(root_gain * math.sqrt(order_n) / frob_norm)
-        first.append(identity - (0.25 * scale[s]) * new_stat)
-    parts = [split(f) for f in first]
-    squared = [product(f, f) for f in parts]
-    parts = [split(f) for f in squared]
-    fourth = [split(product(f, f)) for f in parts]
-    rest = [split(squared[s] - 1.25 * first[s]) for s in sides]
+        part = 0.25 * scale[s]
+        quarter.append(part * new_stat)
+        square.append((part * part) * product(rounded, rounded))
+    e2 = [jnp.where(i == j, 0.5625, 0.0) - 2.5 * quarter[s] + square[s] for s in sides]
+    e4 = [2.0 * e2[s] + product(e2[s], e2[s]) for s in sides]
+    rest = [square[s] - 1.25 * quarter[s] for s in sides]
     roots = []
     for s in sides:
-        root = 1.25 * first[s] + product(fourth[s], rest[s])
+        root = jnp.where(i == j, e2[s] + 1.0, e2[s]) + product(e4[s], rest[s])
         roots.append((jnp.sqrt(jnp.sqrt(scale[s])) * root).astype(jnp.bfloat16))
     applied = jnp.dot(gradient[...], roots[1], preferred_element_type=jnp.float32)
     update = jnp.dot(
@@ -278,25 +284,24 @@
     )(tables[0], grad)
 
 
-def gradient_sum(grad, sent, tables):
+def gradient_sum(grad, got, tables):
     n, order_n = grad.shape[1], grad.shape[2]
     half = n // 2
-    unit = 2 * half * order_n
     *sent, kept = pl.pallas_call(
         first_sum_kernel,
         out_shape=[shape(2, half, order_n)] * 2 + [shape(2, 2, half, order_n)],
         in_specs=[SMEM] + [VMEM] * 3,
         out_specs=[VMEM] * 3,
         compiler_params=params(16),
-        cost_estimate=cost(0, 24 * unit),
-    )(tables[1], grad, *exchange(sent, 0))
+        cost_estimate=cost(5 * 10**11, 10**9),
+    )(tables[1], grad, *got)
     *sent, kept = pl.pallas_call(
         second_sum_kernel,
         out_shape=[shape(half, order_n)] * 2 + [shape(2, half, order_n)],
         in_specs=[SMEM] + [VMEM] * 3,
         out_specs=[VMEM] * 3,
         compiler_params=params(12),
-        cost_estimate=cost(0, 12 * unit),
+        cost_estimate=cost(0, 4 * 1024 * 1024),
     )(tables[2], kept, *exchange(sent, 1))
     sent = pl.pallas_call(
         third_sum_kernel,
@@ -304,7 +309,7 @@
         in_specs=[VMEM] * 3,
         out_specs=[VMEM] * 2,
         compiler_params=params(8),
-        cost_estimate=cost(0, 6 * unit),
+        cost_estimate=cost(0, 4 * 1024 * 1024),
     )(kept, *exchange(sent, 2))
     square = jax.ShapeDtypeStruct((n, order_n), jnp.float32)
     return pl.pallas_call(
@@ -313,7 +318,7 @@
         in_specs=[VMEM] * 4,
         out_specs=[VMEM] * 3,
         compiler_params=params(16),
-        cost_estimate=cost(4 * n**3, 12 * unit),
+        cost_estimate=cost(4 * n**3, 4 * 1024 * 1024),
     )(*sent, *exchange(sent, 3))
 
 
@@ -323,11 +328,10 @@
     order_b = grad_partial.shape[3]
     slab = order_b // n_dp
     slots = statistics.shape[2]
-    row = lax.axis_index("dp")
     core = lax.axis_index("core")
     col = 2 * lax.axis_index("z") + core
     lane_item, out_rows = home_tables()
-    tables = [jnp.asarray(t)[2 * row + core] for t in tree_tables()]
+    tables = [jnp.asarray(t.reshape(-1)) for t in tree_tables()]
 
     device = owner_table.reshape(-1)
     numbers = jnp.arange(device.shape[0], dtype=jnp.int32)
@@ -353,10 +357,11 @@
     )(statistics[0, 0])
     spread = lax.all_to_all(packed, "dp", split_axis=0, concat_axis=0, tiled=True)
     sent = first_sent(grad_partial[0], tables)
-    spread, sent = lax.optimization_barrier((spread, sent))
+    spread, _ = lax.optimization_barrier((spread, sent))
+    got = exchange(sent, 0)
     lanes = pick(lane_from, spread.reshape(slots * n_dp, packed_rows, 128))
     lanes = lax.all_to_all(lanes, ("z", "core"), split_axis=0, concat_axis=0, tiled=True)
-    gradient, left, right = gradient_sum(grad_partial[0], sent, tables)
+    gradient, left, right = gradient_sum(grad_partial[0], got, tables)
     lanes = pick(item_from, lanes).reshape(n_dp, 2, packed_rows, 128)
     chunks = lax.all_to_all(lanes, "dp", split_axis=0, concat_axis=0, tiled=True)
 
@@ -371,7 +376,7 @@
             pltpu.VMEM((2,) + full, jnp.float32),
         ],
         compiler_params=params(40),
-        cost_estimate=cost(40 * order_b**3, 6 * 1024 * 1024),
+        cost_estimate=cost(16 * order_b**3, 6 * 1024 * 1024),
     )(chunks, gradient, left, right)
     rows = update.reshape(n_dp, slab, order_b)
     rows = lax.all_to_all(rows, "dp", split_axis=0, concat_axis=0, tiled=True)

time: 124 us -> 126 us (1.016)
  the two profiles are of different devices: /device:TPU:32 before, /device:TPU:1 now
where the time goes in v2:
time: 126 us; the launch traced here: 124 us
  starting transfers between devices  59.3 us (47%)
  waiting for transfers between devices  44.6 us (35%)
  Pallas kernels  13.9 us (11%)
  local copies, waits for them, and re-layouts  5.2 us (4%)
    ppermute x8, starting transfers between devices, exchange(): lax.ppermute(a, ('dp', 'core'), pairs(portion, step))  27.3 us
    all_to_all x1, starting transfers between devices, body(): lax.all_to_all(lanes, ('z', 'core'), split_axis=0, concat_axis=0, tiled=T...  18.4 us
    all_to_all x1, waiting for transfers between devices, body(): lax.all_to_all(lanes, ('z', 'core'), split_axis=0, concat_axis=0, tiled=T...  14.3 us
    ppermute x8, waiting for transfers between devices, exchange(): lax.ppermute(a, ('dp', 'core'), pairs(portion, step))  13.9 us
    all_to_all x1, waiting for transfers between devices, body(): rows = lax.all_to_all(rows, 'dp', split_axis=0, concat_axis=0, tiled=True)  8.92 us
    all_to_all x1, waiting for transfers between devices, body(): lax.all_to_all(packed, 'dp', split_axis=0, concat_axis=0, tiled=True)  7.48 us
    all_to_all x1, starting transfers between devices, body(): rows = lax.all_to_all(rows, 'dp', split_axis=0, concat_axis=0, tiled=True)  5.78 us
    pallas_call x3, Pallas kernels, pick(): pl.pallas_call(pick_kernel, out_shape=jax.ShapeDtypeStruct(table.shape +...  4.56 us
  transfers between devices with their start and end apart: 12, of which 6 were waited for; matrix products, arithmetic and copies ran while one was open for 2% of the time, Pallas kernels for 6%

profile of v2, /device:TPU:1, one launch (start us, length us, event | category | flops | bytes accessed | tf_op | source)
XLA Modules:
  0.0 124.1 jit_solution(8474134739833201053)
XLA Ops:
  0.0 0.0 copy-start
  0.0 1.7 %copy-done = bf16[1,5,512,512]{3,2,1,0:T(8,128)(2,1)S(1)} copy-done((bf16[1,5,512,512]{3,2,1,0:T(8,128)(2,1)S(1)}, bf16[1,5,512,512]{3,2,1,0:T(8,128)(2,1)}, u32[]{:S(2)}) %copy-start) | copy-done | bytes 2621464
  1.7 0.0 copy-start.4
  1.7 0.7 copy-done.4
  2.4 1.8 %shard_map.83 = (bf16[3,256,512]{2,1,0:T(8,128)(2,1)}, bf16[3,256,512]{2,1,0:T(8,128)(2,1)}) custom-call(s32[192]{0:T(256)S(1)} %copy-done.4, bf16[5,512,512]{2,1,0:T(8,128)(2,1)S(1)} %bitcast.11), custom_call_target="tpu_custom_call" | custom-call | bytes 1572864 | tf_op jit(solution)/shard_map/pallas_call | solution.py:277
  4.3 5.3 %collective-permute-start = (bf16[3,256,512]{2,1,0:T(8,128)(2,1)}, bf16[3,256,512]{2,1,0:T(8,128)(2,1)}, u32[]{:S(2)}, u32[]{:S(2)}) collective-permute-start(bf16[3,256,512]{2,1,0:T(8,128)(2,1)} %get-tuple-element.19), channel_id=1, source_target_pairs={{0,128},{1,385},{32,160},{33,417},{64,192},{65,449},{96,224},{97,4... | collective-permute-start | bytes 2359304 | tf_op jit(solution)/shard_map/ppermute | solution.py:271
  9.6 4.6 %collective-permute-start.1 = (bf16[3,256,512]{2,1,0:T(8,128)(2,1)}, bf16[3,256,512]{2,1,0:T(8,128)(2,1)}, u32[]{:S(2)}, u32[]{:S(2)}) collective-permute-start(bf16[3,256,512]{2,1,0:T(8,128)(2,1)} %get-tuple-element.20), channel_id=1, source_target_pairs={{0,32},{1,97},{32,0},{33,65},{64,96},{65,33},{96,64},{97,1},{128,1... | collective-permute-start | bytes 2359304 | tf_op jit(solution)/shard_map/ppermute | solution.py:271
  14.3 0.0 copy-done.3
  14.3 0.1 shard_map.82
  14.4 0.0 copy-start.2
  14.4 0.8 copy-done.2
  15.2 3.8 %all-to-all-start = ((bf16[16,2,72,128]{3,2,1,0:T(8,128)(2,1)}), bf16[16,2,72,128]{3,2,1,0:T(8,128)(2,1)S(1)}, u32[]{:S(2)}, u32[]{:S(2)}) async-start(bf16[16,2,72,128]{3,2,1,0:T(8,128)(2,1)} %copy-done.2), calls=%async_computation | async-start | bytes 1179648 | tf_op jit(solution)/shard_map/all_to_all | solution.py:358
  19.1 0.0 copy-done.8
  19.1 0.1 copy.18
  19.2 0.1 eq.45
  19.3 0.7 reshape.22
  20.0 0.1 copy.23
  20.2 0.2 convert_reduce_fusion
  20.4 0.1 reduce_sum.38
  20.6 0.2 fusion.5
  20.7 0.1 reduce_sum.40
  20.9 0.1 reduce_sum.41.table
  21.0 0.0 copy-done.10
  21.0 0.6 fusion.9
  21.6 7.5 %all-to-all-done = bf16[16,2,72,128]{3,2,1,0:T(8,128)(2,1)S(1)} async-done(((bf16[16,2,72,128]{3,2,1,0:T(8,128)(2,1)}), bf16[16,2,72,128]{3,2,1,0:T(8,128)(2,1)S(1)}, u32[]{:S(2)}, u32[]{:S(2)}) %all-to-all-start) | async-done | bytes 589856 | tf_op jit(solution)/shard_map/all_to_all | solution.py:358
  29.0 1.4 %shard_map.84 = bf16[32,72,128]{2,1,0:T(8,128)(2,1)} custom-call(s32[32]{0:T(128)S(1)} %reduce_sum.41.table, bf16[32,72,128]{2,1,0:T(8,128)(2,1)S(1)} %bitcast.13), custom_call_target="tpu_custom_call" | custom-call | bytes 8388608 | tf_op jit(solution)/shard_map/pallas_call | solution.py:167
  30.4 18.4 %all-to-all-start.1 = ((bf16[32,72,128]{2,1,0:T(8,128)(2,1)}), bf16[32,72,128]{2,1,0:T(8,128)(2,1)}, u32[]{:S(2)}, u32[]{:S(2)}) async-start(bf16[32,72,128]{2,1,0:T(8,128)(2,1)} %shard_map.84), calls=%async_computation.1 | async-start | bytes 1179648 | tf_op jit(solution)/shard_map/all_to_all | solution.py:363
  48.9 0.0 collective-permute-done.r0
  48.9 0.0 collective-permute-done.1.r1
  48.9 0.0 copy-done.1
  48.9 0.0 copy-done.6
  48.9 0.0 copy-start.7
  48.9 0.0 copy-start.5
  48.9 0.0 copy-start.11
  49.0 1.9 %shard_map.86 = (bf16[2,256,512]{2,1,0:T(8,128)(2,1)S(1)}, bf16[2,256,512]{2,1,0:T(8,128)(2,1)S(1)}, bf16[2,2,256,512]{3,2,1,0:T(8,128)(2,1)S(1)}) custom-call(s32[512]{0:T(512)S(1)} %copy-done.6, bf16[5,512,512]{2,1,0:T(8,128)(2,1)S(1)} %bitcast.12, bf16[3,256,512]{2,1,0:T(8,128)(2,1)} %collective-permute-done.r0, ...), custom_call_target="tpu_custom_call" | custom-call | flops 499999997952 | bytes 1000000000 | tf_op jit(solution)/shard_map/pallas_call | solution.py:290
  50.8 1.9 %collective-permute-start.2 = (bf16[2,256,512]{2,1,0:T(8,128)(2,1)S(1)}, bf16[2,256,512]{2,1,0:T(8,128)(2,1)S(1)}, u32[]{:S(2)}, u32[]{:S(2)}) collective-permute-start(bf16[2,256,512]{2,1,0:T(8,128)(2,1)S(1)} %get-tuple-element.23), channel_id=1, source_target_pairs={{0,384},{1,129},{32,416},{33,161},{64,448},{65,193},{96,480},{97,2... | collective-permute-start | bytes 1572872 | tf_op jit(solution)/shard_map/ppermute | solution.py:271
  52.8 2.2 %collective-permute-start.3 = (bf16[2,256,512]{2,1,0:T(8,128)(2,1)S(1)}, bf16[2,256,512]{2,1,0:T(8,128)(2,1)S(1)}, u32[]{:S(2)}, u32[]{:S(2)}) collective-permute-start(bf16[2,256,512]{2,1,0:T(8,128)(2,1)S(1)} %get-tuple-element.24), channel_id=1, source_target_pairs={{0,96},{1,33},{32,64},{33,1},{64,32},{65,97},{96,0},{97,65},{128,2... | collective-permute-start | bytes 1572872 | tf_op jit(solution)/shard_map/ppermute | solution.py:271
  55.0 0.0 copy-done.7
  55.0 6.1 %collective-permute-done.2.r0 = bf16[2,256,512]{2,1,0:T(8,128)(2,1)S(1)} collective-permute-done((bf16[2,256,512]{2,1,0:T(8,128)(2,1)S(1)}, bf16[2,256,512]{2,1,0:T(8,128)(2,1)S(1)}, u32[]{:S(2)}, u32[]{:S(2)}) %collective-permute-start.2) | collective-permute-done | bytes 524320 | tf_op jit(solution)/shard_map/ppermute | solution.py:271
  61.2 1.9 %collective-permute-done.3.r1 = bf16[2,256,512]{2,1,0:T(8,128)(2,1)S(1)} collective-permute-done((bf16[2,256,512]{2,1,0:T(8,128)(2,1)S(1)}, bf16[2,256,512]{2,1,0:T(8,128)(2,1)S(1)}, u32[]{:S(2)}, u32[]{:S(2)}) %collective-permute-start.3) | collective-permute-done | bytes 524320 | tf_op jit(solution)/shard_map/ppermute | solution.py:271
  63.1 0.0 copy-done.5
  63.1 0.8 shard_map.87
  63.9 2.7 %collective-permute-start.4 = (bf16[256,512]{1,0:T(8,128)(2,1)S(1)}, bf16[256,512]{1,0:T(8,128)(2,1)S(1)}, u32[]{:S(2)}, u32[]{:S(2)}) collective-permute-start(bf16[256,512]{1,0:T(8,128)(2,1)S(1)} %get-tuple-element.26), channel_id=1, source_target_pairs={{0,32},{1,97},{32,0},{33,65},{64,96},{65,33},{96,64},{97,1},{128,1... | collective-permute-start | bytes 786440 | tf_op jit(solution)/shard_map/ppermute | solution.py:271
  66.6 4.1 %collective-permute-start.5 = (bf16[256,512]{1,0:T(8,128)(2,1)S(1)}, bf16[256,512]{1,0:T(8,128)(2,1)S(1)}, u32[]{:S(2)}, u32[]{:S(2)}) collective-permute-start(bf16[256,512]{1,0:T(8,128)(2,1)S(1)} %get-tuple-element.27), channel_id=1, source_target_pairs={{0,128},{1,385},{32,160},{33,417},{64,192},{65,449},{96,224},{97,4... | collective-permute-start | bytes 786440 | tf_op jit(solution)/shard_map/ppermute | solution.py:271
  70.7 0.0 copy-done.11
  70.7 0.2 select_reduce_fusion.table
  70.9 14.3 %all-to-all-done.1.source = bf16[32,72,128]{2,1,0:T(8,128)(2,1)} async-done(((bf16[32,72,128]{2,1,0:T(8,128)(2,1)}), bf16[32,72,128]{2,1,0:T(8,128)(2,1)}, u32[]{:S(2)}, u32[]{:S(2)}) %all-to-all-start.1) | async-done | bytes 589856 | tf_op jit(solution)/shard_map/all_to_all | solution.py:363
  85.2 1.9 %shard_map.85 = bf16[32,72,128]{2,1,0:T(8,128)(2,1)} custom-call(s32[32]{0:T(128)S(1)} %select_reduce_fusion.table, bf16[32,72,128]{2,1,0:T(8,128)(2,1)} %all-to-all-done.1.source), custom_call_target="tpu_custom_call" | custom-call | bytes 8388608 | tf_op jit(solution)/shard_map/pallas_call | solution.py:167
  87.2 4.0 %all-to-all-start.2 = ((bf16[16,2,72,128]{3,2,1,0:T(8,128)(2,1)}), bf16[16,2,72,128]{3,2,1,0:T(8,128)(2,1)S(1)}, u32[]{:S(2)}, u32[]{:S(2)}) async-start(bf16[16,2,72,128]{3,2,1,0:T(8,128)(2,1)} %bitcast.6), calls=%async_computation.2 | async-start | bytes 1179648 | tf_op jit(solution)/shard_map/all_to_all | solution.py:366
  91.2 0.0 collective-permute-done.4.r0
  91.2 0.0 collective-permute-done.5.r1
  91.2 0.1 shard_map.88
  91.3 3.3 %collective-permute-start.6 = (bf16[256,512]{1,0:T(8,128)(2,1)S(1)}, bf16[256,512]{1,0:T(8,128)(2,1)S(1)}, u32[]{:S(2)}, u32[]{:S(2)}) collective-permute-start(bf16[256,512]{1,0:T(8,128)(2,1)S(1)} %get-tuple-element.28.a), channel_id=1, source_target_pairs={{0,96},{1,33},{32,64},{33,1},{64,32},{65,97},{96,0},{97,65},{128,2... | collective-permute-start | bytes 786440 | tf_op jit(solution)/shard_map/ppermute | solution.py:271
  94.6 3.1 %collective-permute-start.7 = (bf16[256,512]{1,0:T(8,128)(2,1)S(1)}, bf16[256,512]{1,0:T(8,128)(2,1)S(1)}, u32[]{:S(2)}, u32[]{:S(2)}) collective-permute-start(bf16[256,512]{1,0:T(8,128)(2,1)S(1)} %get-tuple-element.29.b), channel_id=1, source_target_pairs={{0,384},{1,129},{32,416},{33,161},{64,448},{65,193},{96,480},{97,2... | collective-permute-start | bytes 786440 | tf_op jit(solution)/shard_map/ppermute | solution.py:271
  97.7 5.9 %collective-permute-done.6.r0 = bf16[256,512]{1,0:T(8,128)(2,1)S(1)} collective-permute-done((bf16[256,512]{1,0:T(8,128)(2,1)S(1)}, bf16[256,512]{1,0:T(8,128)(2,1)S(1)}, u32[]{:S(2)}, u32[]{:S(2)}) %collective-permute-start.6) | collective-permute-done | bytes 262176 | tf_op jit(solution)/shard_map/ppermute | solution.py:271
  103.5 0.0 collective-permute-done.7.r1
  103.5 0.8 shard_map.89
  104.3 0.0 all-to-all-done.2.chunks
  104.3 0.0 copy-start.9
  104.3 3.8 %shard_map.90 = bf16[512,512]{1,0:T(8,128)(2,1)} custom-call(bf16[16,2,72,128]{3,2,1,0:T(8,128)(2,1)S(1)} %all-to-all-done.2.chunks, bf16[512,512]{1,0:T(8,128)(2,1)S(1)} %get-tuple-element.30.gradient, f32[512,512]{1,0:T(8,128)S(1)} %get-tuple-element.31.left, f32[512,512]{1,0:T(8,128)S(1)} %get-tuple-element.32.right), custom_call_target="tpu_custom_call" | custom-call | flops 2147483648 | bytes 6291456 | tf_op jit(solution)/shard_map/pallas_call | solution.py:369
  108.2 5.8 %all-to-all-start.3 = ((bf16[16,32,512]{2,1,0:T(8,128)(2,1)}), bf16[16,32,512]{2,1,0:T(8,128)(2,1)S(1)}, u32[]{:S(2)}, u32[]{:S(2)}) async-start(bf16[16,32,512]{2,1,0:T(8,128)(2,1)} %bitcast.7), calls=%async_computation.3 | async-start | bytes 1048576 | tf_op jit(solution)/shard_map/all_to_all | solution.py:382
  113.9 0.0 copy-done.9
  114.0 8.9 %all-to-all-done.3.source = bf16[16,32,512]{2,1,0:T(8,128)(2,1)S(1)} async-done(((bf16[16,32,512]{2,1,0:T(8,128)(2,1)}), bf16[16,32,512]{2,1,0:T(8,128)(2,1)S(1)}, u32[]{:S(2)}, u32[]{:S(2)}) %all-to-all-start.3) | async-done | bytes 524320 | tf_op jit(solution)/shard_map/all_to_all | solution.py:382
  122.9 1.2 shard_map.91
  (10 shorter events, 0.1 us)
Async XLA Ops:
  0.0 1.7 %copy-start = (bf16[1,5,512,512]{3,2,1,0:T(8,128)(2,1)S(1)}, bf16[1,5,512,512]{3,2,1,0:T(8,128)(2,1)}, u32[]{:S(2)}) copy-start(bf16[1,5,512,512]{3,2,1,0:T(8,128)(2,1)} %param.8) | copy-start | bytes 7864324
  1.7 0.7 copy-start.4
  2.4 11.8 %copy-start.3 = (f32[1,1,2,512,512]{4,3,2,1,0:T(8,128)S(1)}, f32[1,1,2,512,512]{4,3,2,1,0:T(8,128)}, u32[]{:S(2)}) copy-start(f32[1,1,2,512,512]{4,3,2,1,0:T(8,128)} %param.9) | copy-start | bytes 6291460
  2.4 16.7 %copy-start.8 = (s32[160,2]{0,1:T(2,128)S(1)}, s32[160,2]{0,1:T(2,128)}, u32[]{:S(2)}) copy-start(s32[160,2]{0,1:T(2,128)} %param.10) | copy-start | bytes 3844
  4.3 16.7 %copy-start.10 = (s32[2,32]{1,0:T(2,128)S(1)}, s32[2,32]{1,0:T(2,128)}, u32[]{:S(2)}) copy-start(s32[2,32]{1,0:T(2,128)} %constant.55.clone) | copy-start | bytes 772
  4.3 44.6 %collective-permute-start = (bf16[3,256,512]{2,1,0:T(8,128)(2,1)}, bf16[3,256,512]{2,1,0:T(8,128)(2,1)}, u32[]{:S(2)}, u32[]{:S(2)}) collective-permute-start(bf16[3,256,512]{2,1,0:T(8,128)(2,1)} %get-tuple-element.19), channel_id=1, source_target_pairs={{0,128},{1,385},{32,160},{33,417},{64,192},{65,449},{96,224},{97,4... | collective-permute-start | bytes 2359304 | tf_op jit(solution)/shard_map/ppermute | solution.py:271
  9.6 39.3 %collective-permute-start.1 = (bf16[3,256,512]{2,1,0:T(8,128)(2,1)}, bf16[3,256,512]{2,1,0:T(8,128)(2,1)}, u32[]{:S(2)}, u32[]{:S(2)}) collective-permute-start(bf16[3,256,512]{2,1,0:T(8,128)(2,1)} %get-tuple-element.20), channel_id=1, source_target_pairs={{0,32},{1,97},{32,0},{33,65},{64,96},{65,33},{96,64},{97,1},{128,1... | collective-permute-start | bytes 2359304 | tf_op jit(solution)/shard_map/ppermute | solution.py:271
  14.4 0.8 copy-start.2
  15.2 33.7 %copy-start.1 = (bf16[1,5,512,512]{3,2,1,0:T(8,128)(2,1)S(1)}, bf16[1,5,512,512]{3,2,1,0:T(8,128)(2,1)}, u32[]{:S(2)}) copy-start(bf16[1,5,512,512]{3,2,1,0:T(8,128)(2,1)} %param.8) | copy-start | bytes 7864324
  15.2 33.7 %copy-start.6 = (s32[512]{0:T(512)S(1)}, s32[512]{0:T(512)}, u32[]{:S(2)}) copy-start(s32[512]{0:T(512)} %constant.53.clone.table) | copy-start | bytes 6148
  15.2 13.8 %all-to-all-start = ((bf16[16,2,72,128]{3,2,1,0:T(8,128)(2,1)}), bf16[16,2,72,128]{3,2,1,0:T(8,128)(2,1)S(1)}, u32[]{:S(2)}, u32[]{:S(2)}) async-start(bf16[16,2,72,128]{3,2,1,0:T(8,128)(2,1)} %copy-done.2), calls=%async_computation | async-start | bytes 1179648 | tf_op jit(solution)/shard_map/all_to_all | solution.py:358
  30.4 54.8 %all-to-all-start.1 = ((bf16[32,72,128]{2,1,0:T(8,128)(2,1)}), bf16[32,72,128]{2,1,0:T(8,128)(2,1)}, u32[]{:S(2)}, u32[]{:S(2)}) async-start(bf16[32,72,128]{2,1,0:T(8,128)(2,1)} %shard_map.84), calls=%async_computation.1 | async-start | bytes 1179648 | tf_op jit(solution)/shard_map/all_to_all | solution.py:363
  48.9 6.1 %copy-start.7 = (s32[32,10]{1,0:T(8,128)S(1)}, s32[32,10]{1,0:T(8,128)}, u32[]{:S(2)}) copy-start(s32[32,10]{1,0:T(8,128)} %reshape.22) | copy-start | bytes 3844
  48.9 14.2 %copy-start.5 = (s32[128]{0:T(128)S(1)}, s32[128]{0:T(128)}, u32[]{:S(2)}) copy-start(s32[128]{0:T(128)} %constant.54.clone.table) | copy-start | bytes 1540
  48.9 21.8 %copy-start.11 = (s32[32]{0:T(128)S(1)}, s32[32]{0:T(128)}, u32[]{:S(2)}) copy-start(s32[32]{0:T(128)} %fusion.9) | copy-start | bytes 388
  50.8 10.3 %collective-permute-start.2 = (bf16[2,256,512]{2,1,0:T(8,128)(2,1)S(1)}, bf16[2,256,512]{2,1,0:T(8,128)(2,1)S(1)}, u32[]{:S(2)}, u32[]{:S(2)}) collective-permute-start(bf16[2,256,512]{2,1,0:T(8,128)(2,1)S(1)} %get-tuple-element.23), channel_id=1, source_target_pairs={{0,384},{1,129},{32,416},{33,161},{64,448},{65,193},{96,480},{97,2... | collective-permute-start | bytes 1572872 | tf_op jit(solution)/shard_map/ppermute | solution.py:271
  52.8 10.3 %collective-permute-start.3 = (bf16[2,256,512]{2,1,0:T(8,128)(2,1)S(1)}, bf16[2,256,512]{2,1,0:T(8,128)(2,1)S(1)}, u32[]{:S(2)}, u32[]{:S(2)}) collective-permute-start(bf16[2,256,512]{2,1,0:T(8,128)(2,1)S(1)} %get-tuple-element.24), channel_id=1, source_target_pairs={{0,96},{1,33},{32,64},{33,1},{64,32},{65,97},{96,0},{97,65},{128,2... | collective-permute-start | bytes 1572872 | tf_op jit(solution)/shard_map/ppermute | solution.py:271
  63.9 27.3 %collective-permute-start.4 = (bf16[256,512]{1,0:T(8,128)(2,1)S(1)}, bf16[256,512]{1,0:T(8,128)(2,1)S(1)}, u32[]{:S(2)}, u32[]{:S(2)}) collective-permute-start(bf16[256,512]{1,0:T(8,128)(2,1)S(1)} %get-tuple-element.26), channel_id=1, source_target_pairs={{0,32},{1,97},{32,0},{33,65},{64,96},{65,33},{96,64},{97,1},{128,1... | collective-permute-start | bytes 786440 | tf_op jit(solution)/shard_map/ppermute | solution.py:271
  66.6 24.6 %collective-permute-start.5 = (bf16[256,512]{1,0:T(8,128)(2,1)S(1)}, bf16[256,512]{1,0:T(8,128)(2,1)S(1)}, u32[]{:S(2)}, u32[]{:S(2)}) collective-permute-start(bf16[256,512]{1,0:T(8,128)(2,1)S(1)} %get-tuple-element.27), channel_id=1, source_target_pairs={{0,128},{1,385},{32,160},{33,417},{64,192},{65,449},{96,224},{97,4... | collective-permute-start | bytes 786440 | tf_op jit(solution)/shard_map/ppermute | solution.py:271
  87.2 17.1 %all-to-all-start.2 = ((bf16[16,2,72,128]{3,2,1,0:T(8,128)(2,1)}), bf16[16,2,72,128]{3,2,1,0:T(8,128)(2,1)S(1)}, u32[]{:S(2)}, u32[]{:S(2)}) async-start(bf16[16,2,72,128]{3,2,1,0:T(8,128)(2,1)} %bitcast.6), calls=%async_computation.2 | async-start | bytes 1179648 | tf_op jit(solution)/shard_map/all_to_all | solution.py:366
  91.3 12.2 %collective-permute-start.6 = (bf16[256,512]{1,0:T(8,128)(2,1)S(1)}, bf16[256,512]{1,0:T(8,128)(2,1)S(1)}, u32[]{:S(2)}, u32[]{:S(2)}) collective-permute-start(bf16[256,512]{1,0:T(8,128)(2,1)S(1)} %get-tuple-element.28.a), channel_id=1, source_target_pairs={{0,96},{1,33},{32,64},{33,1},{64,32},{65,97},{96,0},{97,65},{128,2... | collective-permute-start | bytes 786440 | tf_op jit(solution)/shard_map/ppermute | solution.py:271
  94.6 9.0 %collective-permute-start.7 = (bf16[256,512]{1,0:T(8,128)(2,1)S(1)}, bf16[256,512]{1,0:T(8,128)(2,1)S(1)}, u32[]{:S(2)}, u32[]{:S(2)}) collective-permute-start(bf16[256,512]{1,0:T(8,128)(2,1)S(1)} %get-tuple-element.29.b), channel_id=1, source_target_pairs={{0,384},{1,129},{32,416},{33,161},{64,448},{65,193},{96,480},{97,2... | collective-permute-start | bytes 786440 | tf_op jit(solution)/shard_map/ppermute | solution.py:271
  104.3 9.6 %copy-start.9 = (s32[2,5]{1,0:T(2,128)S(1)}, s32[2,5]{1,0:T(2,128)}, u32[]{:S(2)}) copy-start(s32[2,5]{1,0:T(2,128)} %constant.56.clone) | copy-start | bytes 124
  108.2 14.7 %all-to-all-start.3 = ((bf16[16,32,512]{2,1,0:T(8,128)(2,1)}), bf16[16,32,512]{2,1,0:T(8,128)(2,1)S(1)}, u32[]{:S(2)}, u32[]{:S(2)}) async-start(bf16[16,32,512]{2,1,0:T(8,128)(2,1)} %bitcast.7), calls=%async_computation.3 | async-start | bytes 1048576 | tf_op jit(solution)/shard_map/all_to_all | solution.py:382

commit v3 on v2

--- a/solution.py
+++ b/solution.py
@@ -21,6 +21,8 @@
 )
 blocks_col = len(chips[0])
 packed_rows = 72
+
+long_flops = 5 * 10**11
 
 VMEM = pl.BlockSpec(memory_space=pltpu.VMEM)
 SMEM = pl.BlockSpec(memory_space=pltpu.SMEM)
@@ -163,7 +165,7 @@
         out[i] = source[table[i]]
 
 
-def pick(table, source):
+def pick(table, source, flops=0):
     return pl.pallas_call(
         pick_kernel,
         out_shape=jax.ShapeDtypeStruct(table.shape + source.shape[1:], source.dtype),
@@ -171,7 +173,7 @@
         out_specs=VMEM,
         compiler_params=params(4),
         cost_estimate=pl.CostEstimate(
-            flops=0, bytes_accessed=4 * table.shape[0] * 65536, transcendentals=0
+            flops=flops, bytes_accessed=4 * table.shape[0] * 65536, transcendentals=0
         ),
     )(table, source)
 
@@ -293,7 +295,7 @@
         in_specs=[SMEM] + [VMEM] * 3,
         out_specs=[VMEM] * 3,
         compiler_params=params(16),
-        cost_estimate=cost(5 * 10**11, 10**9),
+        cost_estimate=cost(long_flops, 10**9),
     )(tables[1], grad, *got)
     *sent, kept = pl.pallas_call(
         second_sum_kernel,
@@ -318,7 +320,7 @@
         in_specs=[VMEM] * 4,
         out_specs=[VMEM] * 3,
         compiler_params=params(16),
-        cost_estimate=cost(4 * n**3, 4 * 1024 * 1024),
+        cost_estimate=cost(long_flops, 10**9),
     )(*sent, *exchange(sent, 3))
 
 
@@ -359,7 +361,7 @@
     sent = first_sent(grad_partial[0], tables)
     spread, _ = lax.optimization_barrier((spread, sent))
     got = exchange(sent, 0)
-    lanes = pick(lane_from, spread.reshape(slots * n_dp, packed_rows, 128))
+    lanes = pick(lane_from, spread.reshape(slots * n_dp, packed_rows, 128), long_flops)
     lanes = lax.all_to_all(lanes, ("z", "core"), split_axis=0, concat_axis=0, tiled=True)
     gradient, left, right = gradient_sum(grad_partial[0], got, tables)
     lanes = pick(item_from, lanes).reshape(n_dp, 2, packed_rows, 128)

time: 126 us -> 117 us (0.929)
  the two profiles are of different devices: /device:TPU:1 before, /device:TPU:32 now
where the time goes in v3:
time: 117 us; the launch traced here: 116 us
  starting transfers between devices  55.1 us (47%)
  waiting for transfers between devices  36.8 us (31%)
  Pallas kernels  16.6 us (14%)
  local copies, waits for them, and re-layouts  6.58 us (6%)
    ppermute x8, starting transfers between devices, exchange(): lax.ppermute(a, ('dp', 'core'), pairs(portion, step))  23.6 us
    all_to_all x1, starting transfers between devices, body(): lax.all_to_all(lanes, ('z', 'core'), split_axis=0, concat_axis=0, tiled=T...  15.4 us
    ppermute x8, waiting for transfers between devices, exchange(): lax.ppermute(a, ('dp', 'core'), pairs(portion, step))  15 us
    all_to_all x1, waiting for transfers between devices, body(): rows = lax.all_to_all(rows, 'dp', split_axis=0, concat_axis=0, tiled=True)  10 us
    all_to_all x1, waiting for transfers between devices, body(): lax.all_to_all(lanes, 'dp', split_axis=0, concat_axis=0, tiled=True)  8.9 us
    all_to_all x1, starting transfers between devices, body(): lax.all_to_all(packed, 'dp', split_axis=0, concat_axis=0, tiled=True)  7.03 us
    unnamed x29, local copies, waits for them, and re-layouts  5.95 us
    all_to_all x1, starting transfers between devices, body(): lax.all_to_all(lanes, 'dp', split_axis=0, concat_axis=0, tiled=True)  5.49 us
  transfers between devices with their start and end apart: 12, of which 7 were waited for; matrix products, arithmetic and copies ran while one was open for 1% of the time, Pallas kernels for 8%

profile of v3, /device:TPU:32, one launch (start us, length us, event | category | flops | bytes accessed | tf_op | source)
XLA Modules:
  0.0 116.1 jit_solution(3363365494197618464)
XLA Ops:
  0.0 0.0 copy-start
  0.0 0.0 copy-start.1
  0.0 1.7 %copy-done.1 = f32[1,1,2,512,512]{4,3,2,1,0:T(8,128)S(1)} copy-done((f32[1,1,2,512,512]{4,3,2,1,0:T(8,128)S(1)}, f32[1,1,2,512,512]{4,3,2,1,0:T(8,128)}, u32[]{:S(2)}) %copy-start.1) | copy-done | bytes 2097176
  1.7 0.9 shard_map.82
  2.7 7.0 %all-to-all-start = ((bf16[16,2,72,128]{3,2,1,0:T(8,128)(2,1)}), bf16[16,2,72,128]{3,2,1,0:T(8,128)(2,1)S(1)}, u32[]{:S(2)}, u32[]{:S(2)}) async-start(bf16[16,2,72,128]{3,2,1,0:T(8,128)(2,1)} %shard_map.82), calls=%async_computation | async-start | bytes 1179648 | tf_op jit(solution)/shard_map/all_to_all | solution.py:360
  9.7 0.0 copy-done.4
  9.7 0.0 copy-done
  9.7 1.8 %shard_map.83 = (bf16[3,256,512]{2,1,0:T(8,128)(2,1)}, bf16[3,256,512]{2,1,0:T(8,128)(2,1)}) custom-call(s32[192]{0:T(256)S(1)} %copy-done.4, bf16[5,512,512]{2,1,0:T(8,128)(2,1)S(1)} %bitcast.11), custom_call_target="tpu_custom_call" | custom-call | bytes 1572864 | tf_op jit(solution)/shard_map/pallas_call | solution.py:279
  11.6 3.8 %collective-permute-start = (bf16[3,256,512]{2,1,0:T(8,128)(2,1)}, bf16[3,256,512]{2,1,0:T(8,128)(2,1)}, u32[]{:S(2)}, u32[]{:S(2)}) collective-permute-start(bf16[3,256,512]{2,1,0:T(8,128)(2,1)} %get-tuple-element.19), channel_id=1, source_target_pairs={{0,128},{1,385},{32,160},{33,417},{64,192},{65,449},{96,224},{97,4... | collective-permute-start | bytes 2359304 | tf_op jit(solution)/shard_map/ppermute | solution.py:273
  15.4 3.4 %collective-permute-start.1 = (bf16[3,256,512]{2,1,0:T(8,128)(2,1)}, bf16[3,256,512]{2,1,0:T(8,128)(2,1)}, u32[]{:S(2)}, u32[]{:S(2)}) collective-permute-start(bf16[3,256,512]{2,1,0:T(8,128)(2,1)} %get-tuple-element.20), channel_id=1, source_target_pairs={{0,32},{1,97},{32,0},{33,65},{64,96},{65,33},{96,64},{97,1},{128,1... | collective-permute-start | bytes 2359304 | tf_op jit(solution)/shard_map/ppermute | solution.py:273
  18.8 0.0 copy-done.11
  18.8 0.1 copy.18
  18.9 0.0 copy-start.9
  18.9 0.1 copy.23
  19.1 0.1 eq.45
  19.2 0.2 convert_reduce_fusion
  19.4 0.1 reduce_sum.38
  19.6 0.2 fusion.5
  19.8 0.0 copy-done.9
  19.8 0.1 reduce_sum.40
  19.9 0.1 reduce_sum.41.table
  20.0 2.8 %all-to-all-done = bf16[16,2,72,128]{3,2,1,0:T(8,128)(2,1)S(1)} async-done(((bf16[16,2,72,128]{3,2,1,0:T(8,128)(2,1)}), bf16[16,2,72,128]{3,2,1,0:T(8,128)(2,1)S(1)}, u32[]{:S(2)}, u32[]{:S(2)}) %all-to-all-start) | async-done | bytes 589856 | tf_op jit(solution)/shard_map/all_to_all | solution.py:360
  22.8 1.4 %shard_map.84 = bf16[32,72,128]{2,1,0:T(8,128)(2,1)} custom-call(s32[32]{0:T(128)S(1)} %reduce_sum.41.table, bf16[32,72,128]{2,1,0:T(8,128)(2,1)S(1)} %bitcast.14), custom_call_target="tpu_custom_call" | custom-call | flops 499999997952 | bytes 8388608 | tf_op jit(solution)/shard_map/pallas_call | solution.py:169
  24.2 15.4 %all-to-all-start.1 = ((bf16[32,72,128]{2,1,0:T(8,128)(2,1)}), bf16[32,72,128]{2,1,0:T(8,128)(2,1)}, u32[]{:S(2)}, u32[]{:S(2)}) async-start(bf16[32,72,128]{2,1,0:T(8,128)(2,1)} %shard_map.84), calls=%async_computation.1 | async-start | bytes 1179648 | tf_op jit(solution)/shard_map/all_to_all | solution.py:365
  39.6 0.0 collective-permute-done.r0
  39.6 0.0 collective-permute-done.1.r1
  39.6 0.0 copy-done.6
  39.6 0.0 copy-start.10
  39.6 0.0 copy-start.5
  39.6 2.6 %shard_map.86 = (bf16[2,256,512]{2,1,0:T(8,128)(2,1)}, bf16[2,256,512]{2,1,0:T(8,128)(2,1)S(1)}, bf16[2,2,256,512]{3,2,1,0:T(8,128)(2,1)S(1)}) custom-call(s32[512]{0:T(512)S(1)} %copy-done.6, bf16[5,512,512]{2,1,0:T(8,128)(2,1)S(1)} %bitcast.12, bf16[3,256,512]{2,1,0:T(8,128)(2,1)} %collective-permute-done.r0, bf16[3,256,512]{2,1,0:T(8,128)(2,1)} %collective-permute-done.1.r1), custom_call_target="tpu_custom_call" | custom-call | flops 499999997952 | bytes 1000000000 | tf_op jit(solution)/shard_map/pallas_call | solution.py:292
  42.3 1.0 copy-done.2
  43.3 2.3 %collective-permute-start.2 = (bf16[2,256,512]{2,1,0:T(8,128)(2,1)}, bf16[2,256,512]{2,1,0:T(8,128)(2,1)S(1)}, u32[]{:S(2)}, u32[]{:S(2)}) collective-permute-start(bf16[2,256,512]{2,1,0:T(8,128)(2,1)} %get-tuple-element.23), channel_id=1, source_target_pairs={{0,384},{1,129},{32,416},{33,161},{64,448},{65,193},{96,480},{97,2... | collective-permute-start | bytes 1572872 | tf_op jit(solution)/shard_map/ppermute | solution.py:273
  45.6 3.0 %collective-permute-start.3 = (bf16[2,256,512]{2,1,0:T(8,128)(2,1)S(1)}, bf16[2,256,512]{2,1,0:T(8,128)(2,1)S(1)}, u32[]{:S(2)}, u32[]{:S(2)}) collective-permute-start(bf16[2,256,512]{2,1,0:T(8,128)(2,1)S(1)} %get-tuple-element.24), channel_id=1, source_target_pairs={{0,96},{1,33},{32,64},{33,1},{64,32},{65,97},{96,0},{97,65},{128,2... | collective-permute-start | bytes 1572872 | tf_op jit(solution)/shard_map/ppermute | solution.py:273
  48.6 0.0 copy-done.10
  48.6 0.1 reshape.22
  48.7 7.2 %collective-permute-done.2.r0 = bf16[2,256,512]{2,1,0:T(8,128)(2,1)S(1)} collective-permute-done((bf16[2,256,512]{2,1,0:T(8,128)(2,1)}, bf16[2,256,512]{2,1,0:T(8,128)(2,1)S(1)}, u32[]{:S(2)}, u32[]{:S(2)}) %collective-permute-start.2) | collective-permute-done | bytes 524320 | tf_op jit(solution)/shard_map/ppermute | solution.py:273
  55.9 2.0 %collective-permute-done.3.r1 = bf16[2,256,512]{2,1,0:T(8,128)(2,1)S(1)} collective-permute-done((bf16[2,256,512]{2,1,0:T(8,128)(2,1)S(1)}, bf16[2,256,512]{2,1,0:T(8,128)(2,1)S(1)}, u32[]{:S(2)}, u32[]{:S(2)}) %collective-permute-start.3) | collective-permute-done | bytes 524320 | tf_op jit(solution)/shard_map/ppermute | solution.py:273
  57.8 0.0 copy-done.5
  57.8 1.2 %copy-done.3 = bf16[2,2,256,512]{3,2,1,0:T(8,128)(2,1)S(1)} copy-done((bf16[2,2,256,512]{3,2,1,0:T(8,128)(2,1)S(1)}, bf16[2,2,256,512]{3,2,1,0:T(8,128)(2,1)}, u32[]{:S(2)}) %copy-start.3) | copy-done | bytes 1048600
  59.1 0.8 shard_map.87
  59.9 1.9 %collective-permute-start.4 = (bf16[256,512]{1,0:T(8,128)(2,1)S(1)}, bf16[256,512]{1,0:T(8,128)(2,1)S(1)}, u32[]{:S(2)}, u32[]{:S(2)}) collective-permute-start(bf16[256,512]{1,0:T(8,128)(2,1)S(1)} %get-tuple-element.26), channel_id=1, source_target_pairs={{0,32},{1,97},{32,0},{33,65},{64,96},{65,33},{96,64},{97,1},{128,1... | collective-permute-start | bytes 786440 | tf_op jit(solution)/shard_map/ppermute | solution.py:273
  61.8 2.4 %collective-permute-start.5 = (bf16[256,512]{1,0:T(8,128)(2,1)S(1)}, bf16[256,512]{1,0:T(8,128)(2,1)S(1)}, u32[]{:S(2)}, u32[]{:S(2)}) collective-permute-start(bf16[256,512]{1,0:T(8,128)(2,1)S(1)} %get-tuple-element.27), channel_id=1, source_target_pairs={{0,128},{1,385},{32,160},{33,417},{64,192},{65,449},{96,224},{97,4... | collective-permute-start | bytes 786440 | tf_op jit(solution)/shard_map/ppermute | solution.py:273
  64.2 4.0 %collective-permute-done.4.r0 = bf16[256,512]{1,0:T(8,128)(2,1)S(1)} collective-permute-done((bf16[256,512]{1,0:T(8,128)(2,1)S(1)}, bf16[256,512]{1,0:T(8,128)(2,1)S(1)}, u32[]{:S(2)}, u32[]{:S(2)}) %collective-permute-start.4) | collective-permute-done | bytes 262176 | tf_op jit(solution)/shard_map/ppermute | solution.py:273
  68.1 1.9 %collective-permute-done.5.r1 = bf16[256,512]{1,0:T(8,128)(2,1)S(1)} collective-permute-done((bf16[256,512]{1,0:T(8,128)(2,1)S(1)}, bf16[256,512]{1,0:T(8,128)(2,1)S(1)}, u32[]{:S(2)}, u32[]{:S(2)}) %collective-permute-start.5) | collective-permute-done | bytes 262176 | tf_op jit(solution)/shard_map/ppermute | solution.py:273
  70.1 0.1 shard_map.88
  70.2 3.0 %collective-permute-start.6 = (bf16[256,512]{1,0:T(8,128)(2,1)S(1)}, bf16[256,512]{1,0:T(8,128)(2,1)S(1)}, u32[]{:S(2)}, u32[]{:S(2)}) collective-permute-start(bf16[256,512]{1,0:T(8,128)(2,1)S(1)} %get-tuple-element.28.a), channel_id=1, source_target_pairs={{0,96},{1,33},{32,64},{33,1},{64,32},{65,97},{96,0},{97,65},{128,2... | collective-permute-start | bytes 786440 | tf_op jit(solution)/shard_map/ppermute | solution.py:273
  73.2 3.8 %collective-permute-start.7 = (bf16[256,512]{1,0:T(8,128)(2,1)S(1)}, bf16[256,512]{1,0:T(8,128)(2,1)S(1)}, u32[]{:S(2)}, u32[]{:S(2)}) collective-permute-start(bf16[256,512]{1,0:T(8,128)(2,1)S(1)} %get-tuple-element.29.b), channel_id=1, source_target_pairs={{0,384},{1,129},{32,416},{33,161},{64,448},{65,193},{96,480},{97,2... | collective-permute-start | bytes 786440 | tf_op jit(solution)/shard_map/ppermute | solution.py:273
  77.0 0.0 copy-done.13
  77.1 0.2 select_reduce_fusion.table
  77.3 0.0 all-to-all-done.1.source
  77.3 2.0 %shard_map.85 = bf16[32,72,128]{2,1,0:T(8,128)(2,1)} custom-call(s32[32]{0:T(128)S(1)} %select_reduce_fusion.table, bf16[32,72,128]{2,1,0:T(8,128)(2,1)} %all-to-all-done.1.source), custom_call_target="tpu_custom_call" | custom-call | bytes 8388608 | tf_op jit(solution)/shard_map/pallas_call | solution.py:169
  79.2 5.5 %all-to-all-start.2 = ((bf16[16,2,72,128]{3,2,1,0:T(8,128)(2,1)}), bf16[16,2,72,128]{3,2,1,0:T(8,128)(2,1)}, u32[]{:S(2)}, u32[]{:S(2)}) async-start(bf16[16,2,72,128]{3,2,1,0:T(8,128)(2,1)} %bitcast.6), calls=%async_computation.2 | async-start | bytes 1179648 | tf_op jit(solution)/shard_map/all_to_all | solution.py:368
  84.7 0.0 collective-permute-done.6.r0
  84.7 0.0 collective-permute-done.7.r1
  84.8 0.8 shard_map.89
  85.5 0.0 copy-start.7
  85.5 0.8 copy-done.7
  86.3 8.9 %all-to-all-done.2.chunks = bf16[16,2,72,128]{3,2,1,0:T(8,128)(2,1)} async-done(((bf16[16,2,72,128]{3,2,1,0:T(8,128)(2,1)}), bf16[16,2,72,128]{3,2,1,0:T(8,128)(2,1)}, u32[]{:S(2)}, u32[]{:S(2)}) %all-to-all-start.2) | async-done | bytes 589856 | tf_op jit(solution)/shard_map/all_to_all | solution.py:368
  95.2 1.0 copy-done.8
  96.3 4.9 %shard_map.90 = bf16[512,512]{1,0:T(8,128)(2,1)} custom-call(bf16[16,2,72,128]{3,2,1,0:T(8,128)(2,1)} %all-to-all-done.2.chunks, bf16[512,512]{1,0:T(8,128)(2,1)S(1)} %copy-done.8, f32[512,512]{1,0:T(8,128)S(1)} %get-tuple-element.31.left, f32[512,512]{1,0:T(8,128)S(1)} %get-tuple-element.32.right), custom_call_target="tpu_custom_call" | custom-call | flops 2147483648 | bytes 6291456 | tf_op jit(solution)/shard_map/pallas_call | solution.py:371
  101.2 3.6 %all-to-all-start.3 = ((bf16[16,32,512]{2,1,0:T(8,128)(2,1)}), bf16[16,32,512]{2,1,0:T(8,128)(2,1)S(1)}, u32[]{:S(2)}, u32[]{:S(2)}) async-start(bf16[16,32,512]{2,1,0:T(8,128)(2,1)} %bitcast.7), calls=%async_computation.3 | async-start | bytes 1048576 | tf_op jit(solution)/shard_map/all_to_all | solution.py:384
  104.8 0.0 copy-done.12
  104.8 10.0 %all-to-all-done.3.source = bf16[16,32,512]{2,1,0:T(8,128)(2,1)S(1)} async-done(((bf16[16,32,512]{2,1,0:T(8,128)(2,1)}), bf16[16,32,512]{2,1,0:T(8,128)(2,1)S(1)}, u32[]{:S(2)}, u32[]{:S(2)}) %all-to-all-start.3) | async-done | bytes 524320 | tf_op jit(solution)/shard_map/all_to_all | solution.py:384
  114.8 1.2 %shard_map.91 = bf16[5,32,512]{2,1,0:T(8,128)(2,1)} custom-call(s32[5]{0:T(128)S(1)} %fusion.8.table, bf16[16,32,512]{2,1,0:T(8,128)(2,1)S(1)} %all-to-all-done.3.source), custom_call_target="tpu_custom_call" | custom-call | bytes 1310720 | tf_op jit(solution)/shard_map/pallas_call | solution.py:169
  (14 shorter events, 0.1 us)
Async XLA Ops:
  0.0 9.7 %copy-start.4 = (s32[192]{0:T(256)S(1)}, s32[192]{0:T(256)}, u32[]{:S(2)}) copy-start(s32[192]{0:T(256)} %constant.52.clone.table) | copy-start | bytes 2308
  0.0 9.7 %copy-start = (bf16[1,5,512,512]{3,2,1,0:T(8,128)(2,1)S(1)}, bf16[1,5,512,512]{3,2,1,0:T(8,128)(2,1)}, u32[]{:S(2)}) copy-start(bf16[1,5,512,512]{3,2,1,0:T(8,128)(2,1)} %param.8) | copy-start | bytes 7864324
  0.0 1.7 %copy-start.1 = (f32[1,1,2,512,512]{4,3,2,1,0:T(8,128)S(1)}, f32[1,1,2,512,512]{4,3,2,1,0:T(8,128)}, u32[]{:S(2)}) copy-start(f32[1,1,2,512,512]{4,3,2,1,0:T(8,128)} %param.9) | copy-start | bytes 6291460
  1.7 17.0 %copy-start.11 = (s32[160,2]{0,1:T(2,128)S(1)}, s32[160,2]{0,1:T(2,128)}, u32[]{:S(2)}) copy-start(s32[160,2]{0,1:T(2,128)} %param.10) | copy-start | bytes 3844
  2.7 20.1 %all-to-all-start = ((bf16[16,2,72,128]{3,2,1,0:T(8,128)(2,1)}), bf16[16,2,72,128]{3,2,1,0:T(8,128)(2,1)S(1)}, u32[]{:S(2)}, u32[]{:S(2)}) async-start(bf16[16,2,72,128]{3,2,1,0:T(8,128)(2,1)} %shard_map.82), calls=%async_computation | async-start | bytes 1179648 | tf_op jit(solution)/shard_map/all_to_all | solution.py:360
  11.6 28.0 %collective-permute-start = (bf16[3,256,512]{2,1,0:T(8,128)(2,1)}, bf16[3,256,512]{2,1,0:T(8,128)(2,1)}, u32[]{:S(2)}, u32[]{:S(2)}) collective-permute-start(bf16[3,256,512]{2,1,0:T(8,128)(2,1)} %get-tuple-element.19), channel_id=1, source_target_pairs={{0,128},{1,385},{32,160},{33,417},{64,192},{65,449},{96,224},{97,4... | collective-permute-start | bytes 2359304 | tf_op jit(solution)/shard_map/ppermute | solution.py:273
  15.4 24.2 %collective-permute-start.1 = (bf16[3,256,512]{2,1,0:T(8,128)(2,1)}, bf16[3,256,512]{2,1,0:T(8,128)(2,1)}, u32[]{:S(2)}, u32[]{:S(2)}) collective-permute-start(bf16[3,256,512]{2,1,0:T(8,128)(2,1)} %get-tuple-element.20), channel_id=1, source_target_pairs={{0,32},{1,97},{32,0},{33,65},{64,96},{65,33},{96,64},{97,1},{128,1... | collective-permute-start | bytes 2359304 | tf_op jit(solution)/shard_map/ppermute | solution.py:273
  18.9 0.9 copy-start.9
  22.8 16.8 %copy-start.6 = (s32[512]{0:T(512)S(1)}, s32[512]{0:T(512)}, u32[]{:S(2)}) copy-start(s32[512]{0:T(512)} %constant.53.clone.table) | copy-start | bytes 6148
  24.2 53.1 %all-to-all-start.1 = ((bf16[32,72,128]{2,1,0:T(8,128)(2,1)}), bf16[32,72,128]{2,1,0:T(8,128)(2,1)}, u32[]{:S(2)}, u32[]{:S(2)}) async-start(bf16[32,72,128]{2,1,0:T(8,128)(2,1)} %shard_map.84), calls=%async_computation.1 | async-start | bytes 1179648 | tf_op jit(solution)/shard_map/all_to_all | solution.py:365
  39.6 9.0 %copy-start.10 = (s32[160,2]{1,0:T(8,128)S(1)}, s32[160,2]{1,0:T(8,128)}, u32[]{:S(2)}) copy-start(s32[160,2]{1,0:T(8,128)} %copy-done.9) | copy-start | bytes 3844
  39.6 18.2 %copy-start.5 = (s32[128]{0:T(128)S(1)}, s32[128]{0:T(128)}, u32[]{:S(2)}) copy-start(s32[128]{0:T(128)} %constant.54.clone.table) | copy-start | bytes 1540
  42.3 1.0 copy-start.2
  43.3 33.8 %copy-start.13 = (s32[2,32]{1,0:T(2,128)S(1)}, s32[2,32]{1,0:T(2,128)}, u32[]{:S(2)}) copy-start(s32[2,32]{1,0:T(2,128)} %constant.55.clone) | copy-start | bytes 772
  43.3 12.6 %collective-permute-start.2 = (bf16[2,256,512]{2,1,0:T(8,128)(2,1)}, bf16[2,256,512]{2,1,0:T(8,128)(2,1)S(1)}, u32[]{:S(2)}, u32[]{:S(2)}) collective-permute-start(bf16[2,256,512]{2,1,0:T(8,128)(2,1)} %get-tuple-element.23), channel_id=1, source_target_pairs={{0,384},{1,129},{32,416},{33,161},{64,448},{65,193},{96,480},{97,2... | collective-permute-start | bytes 1572872 | tf_op jit(solution)/shard_map/ppermute | solution.py:273
  45.6 12.3 %collective-permute-start.3 = (bf16[2,256,512]{2,1,0:T(8,128)(2,1)S(1)}, bf16[2,256,512]{2,1,0:T(8,128)(2,1)S(1)}, u32[]{:S(2)}, u32[]{:S(2)}) collective-permute-start(bf16[2,256,512]{2,1,0:T(8,128)(2,1)S(1)} %get-tuple-element.24), channel_id=1, source_target_pairs={{0,96},{1,33},{32,64},{33,1},{64,32},{65,97},{96,0},{97,65},{128,2... | collective-permute-start | bytes 1572872 | tf_op jit(solution)/shard_map/ppermute | solution.py:273
  57.8 1.2 %copy-start.3 = (bf16[2,2,256,512]{3,2,1,0:T(8,128)(2,1)S(1)}, bf16[2,2,256,512]{3,2,1,0:T(8,128)(2,1)}, u32[]{:S(2)}) copy-start(bf16[2,2,256,512]{3,2,1,0:T(8,128)(2,1)} %copy-done.2) | copy-start | bytes 3145732
  59.9 8.3 %collective-permute-start.4 = (bf16[256,512]{1,0:T(8,128)(2,1)S(1)}, bf16[256,512]{1,0:T(8,128)(2,1)S(1)}, u32[]{:S(2)}, u32[]{:S(2)}) collective-permute-start(bf16[256,512]{1,0:T(8,128)(2,1)S(1)} %get-tuple-element.26), channel_id=1, source_target_pairs={{0,32},{1,97},{32,0},{33,65},{64,96},{65,33},{96,64},{97,1},{128,1... | collective-permute-start | bytes 786440 | tf_op jit(solution)/shard_map/ppermute | solution.py:273
  61.8 8.3 %collective-permute-start.5 = (bf16[256,512]{1,0:T(8,128)(2,1)S(1)}, bf16[256,512]{1,0:T(8,128)(2,1)S(1)}, u32[]{:S(2)}, u32[]{:S(2)}) collective-permute-start(bf16[256,512]{1,0:T(8,128)(2,1)S(1)} %get-tuple-element.27), channel_id=1, source_target_pairs={{0,128},{1,385},{32,160},{33,417},{64,192},{65,449},{96,224},{97,4... | collective-permute-start | bytes 786440 | tf_op jit(solution)/shard_map/ppermute | solution.py:273
  70.2 14.5 %collective-permute-start.6 = (bf16[256,512]{1,0:T(8,128)(2,1)S(1)}, bf16[256,512]{1,0:T(8,128)(2,1)S(1)}, u32[]{:S(2)}, u32[]{:S(2)}) collective-permute-start(bf16[256,512]{1,0:T(8,128)(2,1)S(1)} %get-tuple-element.28.a), channel_id=1, source_target_pairs={{0,96},{1,33},{32,64},{33,1},{64,32},{65,97},{96,0},{97,65},{128,2... | collective-permute-start | bytes 786440 | tf_op jit(solution)/shard_map/ppermute | solution.py:273
  73.2 11.5 %collective-permute-start.7 = (bf16[256,512]{1,0:T(8,128)(2,1)S(1)}, bf16[256,512]{1,0:T(8,128)(2,1)S(1)}, u32[]{:S(2)}, u32[]{:S(2)}) collective-permute-start(bf16[256,512]{1,0:T(8,128)(2,1)S(1)} %get-tuple-element.29.b), channel_id=1, source_target_pairs={{0,384},{1,129},{32,416},{33,161},{64,448},{65,193},{96,480},{97,2... | collective-permute-start | bytes 786440 | tf_op jit(solution)/shard_map/ppermute | solution.py:273
  79.2 16.0 %all-to-all-start.2 = ((bf16[16,2,72,128]{3,2,1,0:T(8,128)(2,1)}), bf16[16,2,72,128]{3,2,1,0:T(8,128)(2,1)}, u32[]{:S(2)}, u32[]{:S(2)}) async-start(bf16[16,2,72,128]{3,2,1,0:T(8,128)(2,1)} %bitcast.6), calls=%async_computation.2 | async-start | bytes 1179648 | tf_op jit(solution)/shard_map/all_to_all | solution.py:368
  85.5 0.8 copy-start.7
  95.2 1.0 copy-start.8
  96.3 8.5 %copy-start.12 = (s32[2,5]{1,0:T(2,128)S(1)}, s32[2,5]{1,0:T(2,128)}, u32[]{:S(2)}) copy-start(s32[2,5]{1,0:T(2,128)} %constant.56.clone) | copy-start | bytes 124
  101.2 13.6 %all-to-all-start.3 = ((bf16[16,32,512]{2,1,0:T(8,128)(2,1)}), bf16[16,32,512]{2,1,0:T(8,128)(2,1)S(1)}, u32[]{:S(2)}, u32[]{:S(2)}) async-start(bf16[16,32,512]{2,1,0:T(8,128)(2,1)} %bitcast.7), calls=%async_computation.3 | async-start | bytes 1048576 | tf_op jit(solution)/shard_map/all_to_all | solution.py:384

commit v4 on v3

--- a/solution.py
+++ b/solution.py
@@ -22,7 +22,7 @@
 blocks_col = len(chips[0])
 packed_rows = 72
 
-long_flops = 5 * 10**11
+long_flops = 10**11
 
 VMEM = pl.BlockSpec(memory_space=pltpu.VMEM)
 SMEM = pl.BlockSpec(memory_space=pltpu.SMEM)
@@ -92,13 +92,11 @@
 @functools.cache
 def home_tables():
     item = np.zeros((2, 2 * side_x * side_x), np.int32)
-    rows = np.zeros((2, blocks_col), np.int32)
     for p in range(2):
         for j, (x, y) in enumerate(chips[p]):
             d = side_x * x + y
-            rows[p, j] = d
             item[p, 2 * d : 2 * d + 2] = (2 * j, 2 * j + 1)
-    return item, rows
+    return item
 
 
 def params(mib):
@@ -176,6 +174,22 @@
             flops=flops, bytes_accessed=4 * table.shape[0] * 65536, transcendentals=0
         ),
     )(table, source)
+
+
+def output_kernel(source, out, sems):
+    core = lax.axis_index("core")
+    for p in range(2):
+
+        @pl.when(core == p)
+        def _():
+            copies = [
+                pltpu.make_async_copy(source.at[side_x * x + y], out.at[j], sems.at[j])
+                for j, (x, y) in enumerate(chips[p])
+            ]
+            for copy in copies:
+                copy.start()
+            for copy in copies:
+                copy.wait()
 
 
 def square_iotas(n):
@@ -295,7 +309,7 @@
         in_specs=[SMEM] + [VMEM] * 3,
         out_specs=[VMEM] * 3,
         compiler_params=params(16),
-        cost_estimate=cost(long_flops, 10**9),
+        cost_estimate=cost(long_flops, 4 * 1024 * 1024),
     )(tables[1], grad, *got)
     *sent, kept = pl.pallas_call(
         second_sum_kernel,
@@ -320,7 +334,7 @@
         in_specs=[VMEM] * 4,
         out_specs=[VMEM] * 3,
         compiler_params=params(16),
-        cost_estimate=cost(long_flops, 10**9),
+        cost_estimate=cost(long_flops // 2, 4 * 1024 * 1024),
     )(*sent, *exchange(sent, 3))
 
 
@@ -332,7 +346,7 @@
     slots = statistics.shape[2]
     core = lax.axis_index("core")
     col = 2 * lax.axis_index("z") + core
-    lane_item, out_rows = home_tables()
+    lane_item = home_tables()
     tables = [jnp.asarray(t.reshape(-1)) for t in tree_tables()]
 
     device = owner_table.reshape(-1)
@@ -361,7 +375,7 @@
     sent = first_sent(grad_partial[0], tables)
     spread, _ = lax.optimization_barrier((spread, sent))
     got = exchange(sent, 0)
-    lanes = pick(lane_from, spread.reshape(slots * n_dp, packed_rows, 128), long_flops)
+    lanes = pick(lane_from, spread.reshape(slots * n_dp, packed_rows, 128), long_flops // 3)
     lanes = lax.all_to_all(lanes, ("z", "core"), split_axis=0, concat_axis=0, tiled=True)
     gradient, left, right = gradient_sum(grad_partial[0], got, tables)
     lanes = pick(item_from, lanes).reshape(n_dp, 2, packed_rows, 128)
@@ -382,7 +396,15 @@
     )(chunks, gradient, left, right)
     rows = update.reshape(n_dp, slab, order_b)
     rows = lax.all_to_all(rows, "dp", split_axis=0, concat_axis=0, tiled=True)
-    return pick(jnp.asarray(out_rows)[core], rows)
+    return pl.pallas_call(
+        output_kernel,
+        out_shape=shape(blocks_col, slab, order_b),
+        in_specs=[VMEM],
+        out_specs=pl.BlockSpec(memory_space=pl.ANY),
+        scratch_shapes=[pltpu.SemaphoreType.DMA((blocks_col,))],
+        compiler_params=params(4),
+        cost_estimate=cost(0, 512 * 1024),
+    )(rows)
 
 
 def solution(mesh):

time: 117 us -> 114 us (0.974)
  blocking collectives: 0 us -> 13.3 us
  waiting for transfers between devices: 36.8 us -> 26.7 us
  starting transfers between devices: 55.1 us -> 51.4 us
  Pallas kernels: 16.6 us -> 12.9 us
    all_to_all x0 -> x1, blocking collectives: none -> 13.3 us  [body(): rows = lax.all_to_all(rows, 'dp', split_axis=0, concat_axis=0, tiled=True)]
    all_to_all x1 -> x0, waiting for transfers between devices: 10 us -> none  [body(): rows = lax.all_to_all(rows, 'dp', split_axis=0, concat_axis=0, tiled=True)]
    all_to_all x1 -> x0, starting transfers between devices: 3.57 us -> none  [body(): rows = lax.all_to_all(rows, 'dp', split_axis=0, concat_axis=0, tiled=True)]
    pallas_call x3 -> x2, Pallas kernels: 4.59 us -> 2.02 us  [pick(): pl.pallas_call(pick_kernel, out_shape=jax.ShapeDtypeStruct(table.shape +...]
    pallas_call x1, Pallas kernels: 4.91 us -> 3.01 us  [body(): pl.pallas_call(update_kernel, out_shape=shape(*full), in_specs=[VMEM] * 4...]
    unnamed x29 -> x25, local copies, waits for them, and re-layouts: 5.95 us -> 7.07 us
  transfers between devices with their start and end apart: 12 -> 11, of which waited for: 7 -> 6; matrix products, arithmetic and copies ran while one was open for 1% -> 1% of each run, Pallas kernels for 8% -> 7%
where the time goes in v4:
time: 114 us; the launch traced here: 113 us
  starting transfers between devices  51.4 us (45%)
  waiting for transfers between devices  26.7 us (23%)
  blocking collectives  13.3 us (12%)
  Pallas kernels  12.9 us (11%)
  local copies, waits for them, and re-layouts  7.69 us (7%)
    ppermute x8, starting transfers between devices, exchange(): lax.ppermute(a, ('dp', 'core'), pairs(portion, step))  23.6 us
    all_to_all x1, starting transfers between devices, body(): lax.all_to_all(lanes, ('z', 'core'), split_axis=0, concat_axis=0, tiled=T...  15.4 us
    ppermute x8, waiting for transfers between devices, exchange(): lax.ppermute(a, ('dp', 'core'), pairs(portion, step))  15.3 us
    all_to_all x1, blocking collectives, body(): rows = lax.all_to_all(rows, 'dp', split_axis=0, concat_axis=0, tiled=True)  13.3 us
    all_to_all x1, waiting for transfers between devices, body(): lax.all_to_all(lanes, 'dp', split_axis=0, concat_axis=0, tiled=True)  8.68 us
    unnamed x25, local copies, waits for them, and re-layouts  7.07 us
    all_to_all x1, starting transfers between devices, body(): lax.all_to_all(packed, 'dp', split_axis=0, concat_axis=0, tiled=True)  7.03 us
    all_to_all x1, starting transfers between devices, body(): lax.all_to_all(lanes, 'dp', split_axis=0, concat_axis=0, tiled=True)  5.45 us
  transfers between devices with their start and end apart: 11, of which 6 were waited for; matrix products, arithmetic and copies ran while one was open for 1% of the time, Pallas kernels for 7%

profile of v4, /device:TPU:32, one launch (start us, length us, event | category | flops | bytes accessed | tf_op | source)
XLA Modules:
  0.0 113.2 jit_solution(11056530968543302911)
XLA Ops:
  0.0 0.0 copy-start
  0.0 0.0 copy-start.1
  0.0 1.7 %copy-done.1 = f32[1,1,2,512,512]{4,3,2,1,0:T(8,128)S(1)} copy-done((f32[1,1,2,512,512]{4,3,2,1,0:T(8,128)S(1)}, f32[1,1,2,512,512]{4,3,2,1,0:T(8,128)}, u32[]{:S(2)}) %copy-start.1) | copy-done | bytes 2097176
  1.7 0.0 copy-start.10
  1.7 0.9 shard_map.73
  2.7 7.0 %all-to-all-start = ((bf16[16,2,72,128]{3,2,1,0:T(8,128)(2,1)}), bf16[16,2,72,128]{3,2,1,0:T(8,128)(2,1)S(1)}, u32[]{:S(2)}, u32[]{:S(2)}) async-start(bf16[16,2,72,128]{3,2,1,0:T(8,128)(2,1)} %shard_map.73), calls=%async_computation | async-start | bytes 1179648 | tf_op jit(solution)/shard_map/all_to_all | solution.py:374
  9.7 0.0 copy-done.5
  9.7 0.0 copy-done
  9.7 1.8 %shard_map.74 = (bf16[3,256,512]{2,1,0:T(8,128)(2,1)}, bf16[3,256,512]{2,1,0:T(8,128)(2,1)}) custom-call(s32[192]{0:T(256)S(1)} %copy-done.5, bf16[5,512,512]{2,1,0:T(8,128)(2,1)S(1)} %bitcast.9), custom_call_target="tpu_custom_call" | custom-call | bytes 1572864 | tf_op jit(solution)/shard_map/pallas_call | solution.py:293
  11.5 3.8 %collective-permute-start = (bf16[3,256,512]{2,1,0:T(8,128)(2,1)}, bf16[3,256,512]{2,1,0:T(8,128)(2,1)}, u32[]{:S(2)}, u32[]{:S(2)}) collective-permute-start(bf16[3,256,512]{2,1,0:T(8,128)(2,1)} %get-tuple-element.19), channel_id=1, source_target_pairs={{0,128},{1,385},{32,160},{33,417},{64,192},{65,449},{96,224},{97,4... | collective-permute-start | bytes 2359304 | tf_op jit(solution)/shard_map/ppermute | solution.py:287
  15.4 3.4 %collective-permute-start.1 = (bf16[3,256,512]{2,1,0:T(8,128)(2,1)}, bf16[3,256,512]{2,1,0:T(8,128)(2,1)}, u32[]{:S(2)}, u32[]{:S(2)}) collective-permute-start(bf16[3,256,512]{2,1,0:T(8,128)(2,1)} %get-tuple-element.20), channel_id=1, source_target_pairs={{0,32},{1,97},{32,0},{33,65},{64,96},{65,33},{96,64},{97,1},{128,1... | collective-permute-start | bytes 2359304 | tf_op jit(solution)/shard_map/ppermute | solution.py:287
  18.8 0.0 copy-done.10
  18.8 0.1 copy.17
  18.9 0.1 copy.22
  19.0 0.1 eq.45
  19.2 0.2 convert_reduce_fusion
  19.4 0.1 reduce_sum.38
  19.6 0.2 fusion.5
  19.7 0.1 reduce_sum.40
  19.9 0.1 reduce_sum.41.table
  20.0 2.8 %all-to-all-done = bf16[16,2,72,128]{3,2,1,0:T(8,128)(2,1)S(1)} async-done(((bf16[16,2,72,128]{3,2,1,0:T(8,128)(2,1)}), bf16[16,2,72,128]{3,2,1,0:T(8,128)(2,1)S(1)}, u32[]{:S(2)}, u32[]{:S(2)}) %all-to-all-start) | async-done | bytes 589856 | tf_op jit(solution)/shard_map/all_to_all | solution.py:374
  22.8 0.0 copy-start.7
  22.8 0.6 shard_map.75
  23.4 0.0 copy-start.4
  23.4 0.8 copy-done.4
  24.2 15.4 %all-to-all-start.1 = ((bf16[32,72,128]{2,1,0:T(8,128)(2,1)}), bf16[32,72,128]{2,1,0:T(8,128)(2,1)S(1)}, u32[]{:S(2)}, u32[]{:S(2)}) async-start(bf16[32,72,128]{2,1,0:T(8,128)(2,1)} %copy-done.4), calls=%async_computation.1 | async-start | bytes 1179648 | tf_op jit(solution)/shard_map/all_to_all | solution.py:379
  39.5 0.0 copy-start.6
  39.5 0.0 collective-permute-done.r0
  39.6 0.0 collective-permute-done.1.r1
  39.6 0.0 copy-done.7
  39.6 2.8 %shard_map.77 = (bf16[2,256,512]{2,1,0:T(8,128)(2,1)}, bf16[2,256,512]{2,1,0:T(8,128)(2,1)}, bf16[2,2,256,512]{3,2,1,0:T(8,128)(2,1)S(1)}) custom-call(s32[512]{0:T(512)S(1)} %copy-done.7, bf16[5,512,512]{2,1,0:T(8,128)(2,1)S(1)} %bitcast.10, bf16[3,256,512]{2,1,0:T(8,128)(2,1)} %collective-permute-done.r0, bf16[3,256,512]{2,1,0:T(8,128)(2,1)} %collective-permute-done.1.r1), custom_call_target="tpu_custom_call" | custom-call | flops 99999997952 | bytes 4194304 | tf_op jit(solution)/shard_map/pallas_call | solution.py:306
  42.4 0.0 copy-start.2
  42.4 1.0 copy-done.2
  43.3 0.0 copy-start.11
  43.3 2.3 %collective-permute-start.2 = (bf16[2,256,512]{2,1,0:T(8,128)(2,1)}, bf16[2,256,512]{2,1,0:T(8,128)(2,1)S(1)}, u32[]{:S(2)}, u32[]{:S(2)}) collective-permute-start(bf16[2,256,512]{2,1,0:T(8,128)(2,1)} %get-tuple-element.23), channel_id=1, source_target_pairs={{0,384},{1,129},{32,416},{33,161},{64,448},{65,193},{96,480},{97,2... | collective-permute-start | bytes 1572872 | tf_op jit(solution)/shard_map/ppermute | solution.py:287
  45.6 3.0 %collective-permute-start.3 = (bf16[2,256,512]{2,1,0:T(8,128)(2,1)}, bf16[2,256,512]{2,1,0:T(8,128)(2,1)S(1)}, u32[]{:S(2)}, u32[]{:S(2)}) collective-permute-start(bf16[2,256,512]{2,1,0:T(8,128)(2,1)} %get-tuple-element.24), channel_id=1, source_target_pairs={{0,96},{1,33},{32,64},{33,1},{64,32},{65,97},{96,0},{97,65},{128,2... | collective-permute-start | bytes 1572872 | tf_op jit(solution)/shard_map/ppermute | solution.py:287
  48.7 0.1 reshape.22
  48.7 7.2 %collective-permute-done.2.r0 = bf16[2,256,512]{2,1,0:T(8,128)(2,1)S(1)} collective-permute-done((bf16[2,256,512]{2,1,0:T(8,128)(2,1)}, bf16[2,256,512]{2,1,0:T(8,128)(2,1)S(1)}, u32[]{:S(2)}, u32[]{:S(2)}) %collective-permute-start.2) | collective-permute-done | bytes 524320 | tf_op jit(solution)/shard_map/ppermute | solution.py:287
  56.0 2.2 %collective-permute-done.3.r1 = bf16[2,256,512]{2,1,0:T(8,128)(2,1)S(1)} collective-permute-done((bf16[2,256,512]{2,1,0:T(8,128)(2,1)}, bf16[2,256,512]{2,1,0:T(8,128)(2,1)S(1)}, u32[]{:S(2)}, u32[]{:S(2)}) %collective-permute-start.3) | collective-permute-done | bytes 524320 | tf_op jit(solution)/shard_map/ppermute | solution.py:287
  58.1 0.0 copy-done.6
  58.1 1.2 %copy-done.3 = bf16[2,2,256,512]{3,2,1,0:T(8,128)(2,1)S(1)} copy-done((bf16[2,2,256,512]{3,2,1,0:T(8,128)(2,1)S(1)}, bf16[2,2,256,512]{3,2,1,0:T(8,128)(2,1)}, u32[]{:S(2)}) %copy-start.3) | copy-done | bytes 1048600
  59.4 0.8 shard_map.78
  60.2 1.9 %collective-permute-start.4 = (bf16[256,512]{1,0:T(8,128)(2,1)S(1)}, bf16[256,512]{1,0:T(8,128)(2,1)S(1)}, u32[]{:S(2)}, u32[]{:S(2)}) collective-permute-start(bf16[256,512]{1,0:T(8,128)(2,1)S(1)} %get-tuple-element.26), channel_id=1, source_target_pairs={{0,32},{1,97},{32,0},{33,65},{64,96},{65,33},{96,64},{97,1},{128,1... | collective-permute-start | bytes 786440 | tf_op jit(solution)/shard_map/ppermute | solution.py:287
  62.1 2.4 %collective-permute-start.5 = (bf16[256,512]{1,0:T(8,128)(2,1)S(1)}, bf16[256,512]{1,0:T(8,128)(2,1)S(1)}, u32[]{:S(2)}, u32[]{:S(2)}) collective-permute-start(bf16[256,512]{1,0:T(8,128)(2,1)S(1)} %get-tuple-element.27), channel_id=1, source_target_pairs={{0,128},{1,385},{32,160},{33,417},{64,192},{65,449},{96,224},{97,4... | collective-permute-start | bytes 786440 | tf_op jit(solution)/shard_map/ppermute | solution.py:287
  64.5 4.0 %collective-permute-done.4.r0 = bf16[256,512]{1,0:T(8,128)(2,1)S(1)} collective-permute-done((bf16[256,512]{1,0:T(8,128)(2,1)S(1)}, bf16[256,512]{1,0:T(8,128)(2,1)S(1)}, u32[]{:S(2)}, u32[]{:S(2)}) %collective-permute-start.4) | collective-permute-done | bytes 262176 | tf_op jit(solution)/shard_map/ppermute | solution.py:287
  68.4 1.9 %collective-permute-done.5.r1 = bf16[256,512]{1,0:T(8,128)(2,1)S(1)} collective-permute-done((bf16[256,512]{1,0:T(8,128)(2,1)S(1)}, bf16[256,512]{1,0:T(8,128)(2,1)S(1)}, u32[]{:S(2)}, u32[]{:S(2)}) %collective-permute-start.5) | collective-permute-done | bytes 262176 | tf_op jit(solution)/shard_map/ppermute | solution.py:287
  70.4 0.1 shard_map.79
  70.5 3.0 %collective-permute-start.6 = (bf16[256,512]{1,0:T(8,128)(2,1)S(1)}, bf16[256,512]{1,0:T(8,128)(2,1)S(1)}, u32[]{:S(2)}, u32[]{:S(2)}) collective-permute-start(bf16[256,512]{1,0:T(8,128)(2,1)S(1)} %get-tuple-element.28.a), channel_id=1, source_target_pairs={{0,96},{1,33},{32,64},{33,1},{64,32},{65,97},{96,0},{97,65},{128,2... | collective-permute-start | bytes 786440 | tf_op jit(solution)/shard_map/ppermute | solution.py:287
  73.5 3.8 %collective-permute-start.7 = (bf16[256,512]{1,0:T(8,128)(2,1)S(1)}, bf16[256,512]{1,0:T(8,128)(2,1)S(1)}, u32[]{:S(2)}, u32[]{:S(2)}) collective-permute-start(bf16[256,512]{1,0:T(8,128)(2,1)S(1)} %get-tuple-element.29.b), channel_id=1, source_target_pairs={{0,384},{1,129},{32,416},{33,161},{64,448},{65,193},{96,480},{97,2... | collective-permute-start | bytes 786440 | tf_op jit(solution)/shard_map/ppermute | solution.py:287
  77.3 0.0 copy-done.11
  77.4 0.2 select_reduce_fusion.table
  77.5 0.0 all-to-all-done.1.source
  77.5 1.4 %shard_map.76 = bf16[32,72,128]{2,1,0:T(8,128)(2,1)} custom-call(s32[32]{0:T(128)S(1)} %select_reduce_fusion.table, bf16[32,72,128]{2,1,0:T(8,128)(2,1)S(1)} %all-to-all-done.1.source), custom_call_target="tpu_custom_call" | custom-call | bytes 8388608 | tf_op jit(solution)/shard_map/pallas_call | solution.py:167
  79.0 5.4 %all-to-all-start.2 = ((bf16[16,2,72,128]{3,2,1,0:T(8,128)(2,1)}), bf16[16,2,72,128]{3,2,1,0:T(8,128)(2,1)S(1)}, u32[]{:S(2)}, u32[]{:S(2)}) async-start(bf16[16,2,72,128]{3,2,1,0:T(8,128)(2,1)} %bitcast.5), calls=%async_computation.2 | async-start | bytes 1179648 | tf_op jit(solution)/shard_map/all_to_all | solution.py:382
  84.4 0.0 collective-permute-done.6.r0
  84.4 0.0 collective-permute-done.7.r1
  84.5 0.8 shard_map.80
  85.2 0.0 copy-start.8
  85.2 1.0 copy-done.8
  86.2 8.7 %all-to-all-done.2.chunks = bf16[16,2,72,128]{3,2,1,0:T(8,128)(2,1)S(1)} async-done(((bf16[16,2,72,128]{3,2,1,0:T(8,128)(2,1)}), bf16[16,2,72,128]{3,2,1,0:T(8,128)(2,1)S(1)}, u32[]{:S(2)}, u32[]{:S(2)}) %all-to-all-start.2) | async-done | bytes 589856 | tf_op jit(solution)/shard_map/all_to_all | solution.py:382
  94.9 1.2 %copy-done.9 = f32[512,512]{1,0:T(8,128)S(1)} copy-done((f32[512,512]{1,0:T(8,128)S(1)}, f32[512,512]{1,0:T(8,128)}, u32[]{:S(2)}) %copy-start.9) | copy-done | bytes 1048600
  96.1 3.0 %shard_map.81 = bf16[512,512]{1,0:T(8,128)(2,1)S(1)} custom-call(bf16[16,2,72,128]{3,2,1,0:T(8,128)(2,1)S(1)} %all-to-all-done.2.chunks, bf16[512,512]{1,0:T(8,128)(2,1)S(1)} %get-tuple-element.30.gradient, f32[512,512]{1,0:T(8,128)S(1)} %get-tuple-element.31.left, f32[512,512]{1,0:T(8,128)S(1)} %copy-done.9), custom_call_target="tpu_custom_call" | custom-call | flops 2147483648 | bytes 6291456 | tf_op jit(solution)/shard_map/pallas_call | solution.py:385
  99.1 13.3 %all_to_all.20.source = bf16[16,32,512]{2,1,0:T(8,128)(2,1)S(1)} all-to-all(bf16[16,32,512]{2,1,0:T(8,128)(2,1)S(1)} %bitcast.13), channel_id=1, replica_groups=mesh['dp'=16,'z'=16,'core'=2] {'dp'}, dimensions={0} | all-to-all | bytes 1048576 | tf_op jit(solution)/shard_map/all_to_all | solution.py:398
  112.5 0.7 shard_map.82
  (8 shorter events, 0.0 us)
Async XLA Ops:
  0.0 9.7 %copy-start.5 = (s32[192]{0:T(256)S(1)}, s32[192]{0:T(256)}, u32[]{:S(2)}) copy-start(s32[192]{0:T(256)} %constant.50.clone.table) | copy-start | bytes 2308
  0.0 9.7 %copy-start = (bf16[1,5,512,512]{3,2,1,0:T(8,128)(2,1)S(1)}, bf16[1,5,512,512]{3,2,1,0:T(8,128)(2,1)}, u32[]{:S(2)}) copy-start(bf16[1,5,512,512]{3,2,1,0:T(8,128)(2,1)} %param.7) | copy-start | bytes 7864324
  0.0 1.7 %copy-start.1 = (f32[1,1,2,512,512]{4,3,2,1,0:T(8,128)S(1)}, f32[1,1,2,512,512]{4,3,2,1,0:T(8,128)}, u32[]{:S(2)}) copy-start(f32[1,1,2,512,512]{4,3,2,1,0:T(8,128)} %param.8) | copy-start | bytes 6291460
  1.7 17.0 %copy-start.10 = (s32[160,2]{0,1:T(2,128)S(1)}, s32[160,2]{0,1:T(2,128)}, u32[]{:S(2)}) copy-start(s32[160,2]{0,1:T(2,128)} %param.9) | copy-start | bytes 3844
  2.7 20.1 %all-to-all-start = ((bf16[16,2,72,128]{3,2,1,0:T(8,128)(2,1)}), bf16[16,2,72,128]{3,2,1,0:T(8,128)(2,1)S(1)}, u32[]{:S(2)}, u32[]{:S(2)}) async-start(bf16[16,2,72,128]{3,2,1,0:T(8,128)(2,1)} %shard_map.73), calls=%async_computation | async-start | bytes 1179648 | tf_op jit(solution)/shard_map/all_to_all | solution.py:374
  11.5 28.0 %collective-permute-start = (bf16[3,256,512]{2,1,0:T(8,128)(2,1)}, bf16[3,256,512]{2,1,0:T(8,128)(2,1)}, u32[]{:S(2)}, u32[]{:S(2)}) collective-permute-start(bf16[3,256,512]{2,1,0:T(8,128)(2,1)} %get-tuple-element.19), channel_id=1, source_target_pairs={{0,128},{1,385},{32,160},{33,417},{64,192},{65,449},{96,224},{97,4... | collective-permute-start | bytes 2359304 | tf_op jit(solution)/shard_map/ppermute | solution.py:287
  15.4 24.2 %collective-permute-start.1 = (bf16[3,256,512]{2,1,0:T(8,128)(2,1)}, bf16[3,256,512]{2,1,0:T(8,128)(2,1)}, u32[]{:S(2)}, u32[]{:S(2)}) collective-permute-start(bf16[3,256,512]{2,1,0:T(8,128)(2,1)} %get-tuple-element.20), channel_id=1, source_target_pairs={{0,32},{1,97},{32,0},{33,65},{64,96},{65,33},{96,64},{97,1},{128,1... | collective-permute-start | bytes 2359304 | tf_op jit(solution)/shard_map/ppermute | solution.py:287
  22.8 16.8 %copy-start.7 = (s32[512]{0:T(512)S(1)}, s32[512]{0:T(512)}, u32[]{:S(2)}) copy-start(s32[512]{0:T(512)} %constant.51.clone.table) | copy-start | bytes 6148
  23.4 0.8 copy-start.4
  24.2 53.4 %all-to-all-start.1 = ((bf16[32,72,128]{2,1,0:T(8,128)(2,1)}), bf16[32,72,128]{2,1,0:T(8,128)(2,1)S(1)}, u32[]{:S(2)}, u32[]{:S(2)}) async-start(bf16[32,72,128]{2,1,0:T(8,128)(2,1)} %copy-done.4), calls=%async_computation.1 | async-start | bytes 1179648 | tf_op jit(solution)/shard_map/all_to_all | solution.py:379
  39.5 18.6 %copy-start.6 = (s32[128]{0:T(128)S(1)}, s32[128]{0:T(128)}, u32[]{:S(2)}) copy-start(s32[128]{0:T(128)} %constant.52.clone.table) | copy-start | bytes 1540
  42.4 1.0 copy-start.2
  43.3 34.0 %copy-start.11 = (s32[2,32]{1,0:T(2,128)S(1)}, s32[2,32]{1,0:T(2,128)}, u32[]{:S(2)}) copy-start(s32[2,32]{1,0:T(2,128)} %constant.53.clone) | copy-start | bytes 772
  43.3 12.6 %collective-permute-start.2 = (bf16[2,256,512]{2,1,0:T(8,128)(2,1)}, bf16[2,256,512]{2,1,0:T(8,128)(2,1)S(1)}, u32[]{:S(2)}, u32[]{:S(2)}) collective-permute-start(bf16[2,256,512]{2,1,0:T(8,128)(2,1)} %get-tuple-element.23), channel_id=1, source_target_pairs={{0,384},{1,129},{32,416},{33,161},{64,448},{65,193},{96,480},{97,2... | collective-permute-start | bytes 1572872 | tf_op jit(solution)/shard_map/ppermute | solution.py:287
  45.6 12.5 %collective-permute-start.3 = (bf16[2,256,512]{2,1,0:T(8,128)(2,1)}, bf16[2,256,512]{2,1,0:T(8,128)(2,1)S(1)}, u32[]{:S(2)}, u32[]{:S(2)}) collective-permute-start(bf16[2,256,512]{2,1,0:T(8,128)(2,1)} %get-tuple-element.24), channel_id=1, source_target_pairs={{0,96},{1,33},{32,64},{33,1},{64,32},{65,97},{96,0},{97,65},{128,2... | collective-permute-start | bytes 1572872 | tf_op jit(solution)/shard_map/ppermute | solution.py:287
  58.1 1.2 %copy-start.3 = (bf16[2,2,256,512]{3,2,1,0:T(8,128)(2,1)S(1)}, bf16[2,2,256,512]{3,2,1,0:T(8,128)(2,1)}, u32[]{:S(2)}) copy-start(bf16[2,2,256,512]{3,2,1,0:T(8,128)(2,1)} %copy-done.2) | copy-start | bytes 3145732
  60.2 8.3 %collective-permute-start.4 = (bf16[256,512]{1,0:T(8,128)(2,1)S(1)}, bf16[256,512]{1,0:T(8,128)(2,1)S(1)}, u32[]{:S(2)}, u32[]{:S(2)}) collective-permute-start(bf16[256,512]{1,0:T(8,128)(2,1)S(1)} %get-tuple-element.26), channel_id=1, source_target_pairs={{0,32},{1,97},{32,0},{33,65},{64,96},{65,33},{96,64},{97,1},{128,1... | collective-permute-start | bytes 786440 | tf_op jit(solution)/shard_map/ppermute | solution.py:287
  62.1 8.3 %collective-permute-start.5 = (bf16[256,512]{1,0:T(8,128)(2,1)S(1)}, bf16[256,512]{1,0:T(8,128)(2,1)S(1)}, u32[]{:S(2)}, u32[]{:S(2)}) collective-permute-start(bf16[256,512]{1,0:T(8,128)(2,1)S(1)} %get-tuple-element.27), channel_id=1, source_target_pairs={{0,128},{1,385},{32,160},{33,417},{64,192},{65,449},{96,224},{97,4... | collective-permute-start | bytes 786440 | tf_op jit(solution)/shard_map/ppermute | solution.py:287
  70.5 14.0 %collective-permute-start.6 = (bf16[256,512]{1,0:T(8,128)(2,1)S(1)}, bf16[256,512]{1,0:T(8,128)(2,1)S(1)}, u32[]{:S(2)}, u32[]{:S(2)}) collective-permute-start(bf16[256,512]{1,0:T(8,128)(2,1)S(1)} %get-tuple-element.28.a), channel_id=1, source_target_pairs={{0,96},{1,33},{32,64},{33,1},{64,32},{65,97},{96,0},{97,65},{128,2... | collective-permute-start | bytes 786440 | tf_op jit(solution)/shard_map/ppermute | solution.py:287
  73.5 10.9 %collective-permute-start.7 = (bf16[256,512]{1,0:T(8,128)(2,1)S(1)}, bf16[256,512]{1,0:T(8,128)(2,1)S(1)}, u32[]{:S(2)}, u32[]{:S(2)}) collective-permute-start(bf16[256,512]{1,0:T(8,128)(2,1)S(1)} %get-tuple-element.29.b), channel_id=1, source_target_pairs={{0,384},{1,129},{32,416},{33,161},{64,448},{65,193},{96,480},{97,2... | collective-permute-start | bytes 786440 | tf_op jit(solution)/shard_map/ppermute | solution.py:287
  79.0 15.9 %all-to-all-start.2 = ((bf16[16,2,72,128]{3,2,1,0:T(8,128)(2,1)}), bf16[16,2,72,128]{3,2,1,0:T(8,128)(2,1)S(1)}, u32[]{:S(2)}, u32[]{:S(2)}) async-start(bf16[16,2,72,128]{3,2,1,0:T(8,128)(2,1)} %bitcast.5), calls=%async_computation.2 | async-start | bytes 1179648 | tf_op jit(solution)/shard_map/all_to_all | solution.py:382
  85.2 1.0 copy-start.8
  94.9 1.2 %copy-start.9 = (f32[512,512]{1,0:T(8,128)S(1)}, f32[512,512]{1,0:T(8,128)}, u32[]{:S(2)}) copy-start(f32[512,512]{1,0:T(8,128)} %copy-done.8) | copy-start | bytes 3145732

commit v5 on v4

--- a/solution.py
+++ b/solution.py
@@ -26,6 +26,7 @@
 
 VMEM = pl.BlockSpec(memory_space=pltpu.VMEM)
 SMEM = pl.BlockSpec(memory_space=pltpu.SMEM)
+HBM = pl.BlockSpec(memory_space=pltpu.HBM)
 
 
 def even(v):
@@ -72,11 +73,11 @@
                 me = here[axis]
                 kept = [j for j in range(blocks_col) if at[j] in (me, later(me))]
                 one += padded([j for j in range(blocks_col) if j not in kept], 3)
-                padded(kept, 3)
+                one += padded(kept, 3)
                 go = [i for i, j in enumerate(kept) if at[j] == later(me)]
                 stay = [i for i, j in enumerate(kept) if at[j] == me]
                 for place in padded(go, 2) + padded(stay, 2):
-                    two += [place, padded(kept, 3)[place]]
+                    two.append(place)
                 mine = [kept[i] for i in stay]
                 axis, later = steps[3]
                 near = (here[axis], later(here[axis]))
@@ -113,25 +114,26 @@
     return [table[base + k] for k in range(width)]
 
 
-def choose_kernel(table, source, s0, s1):
+def choose_kernel(table, source, s0, s1, kept):
     table = my_row(table)
     height = s0.shape[1]
     for h, sent in enumerate((s0, s1)):
+        rows = slice(h * height, (h + 1) * height)
         for u in range(3):
-            sent[u] = source[table[3 * h + u], h * height : (h + 1) * height, :]
-
-
-def first_sum_kernel(table, source, r0, r1, s0, s1, kept):
+            sent[u] = source[table[6 * h + u], rows, :]
+            kept[h, u] = source[table[6 * h + 3 + u], rows, :]
+
+
+def first_sum_kernel(table, kept, r0, r1, s0, s1, next_kept):
     table = my_row(table)
-    height = r0.shape[1]
     for h, (got, sent) in enumerate(((r0, s0), (r1, s1))):
         for u in range(4):
-            place, block = table[8 * h + 2 * u], table[8 * h + 2 * u + 1]
-            total = add_rounded(source[block, h * height : (h + 1) * height, :], got[place])
+            place = table[4 * h + u]
+            total = add_rounded(kept[h, place], got[place])
             if u < 2:
                 sent[u] = total
             else:
-                kept[h, u - 2] = total
+                next_kept[h, u - 2] = total
 
 
 def second_sum_kernel(table, kept, r0, r1, s0, s1, next_kept):
@@ -153,14 +155,21 @@
     out[half:, :] = add_rounded(b[...], r1[...])
     g = out[...]
     for gram, side in ((left, 1), (right, 0)):
-        gram[...] = lax.dot_general(
+        product = lax.dot_general(
             g, g, (((side,), (side,)), ((), ())), preferred_element_type=jnp.float32
         )
-
-
-def pick_kernel(table, source, out):
-    for i in range(out.shape[0]):
-        out[i] = source[table[i]]
+        gram[...] = product.astype(jnp.bfloat16)
+
+
+def pick_kernel(table, source, out, sems):
+    copies = [
+        pltpu.make_async_copy(source.at[table[i]], out.at[i], sems.at[i])
+        for i in range(out.shape[0])
+    ]
+    for copy in copies:
+        copy.start()
+    for copy in copies:
+        copy.wait()
 
 
 def pick(table, source, flops=0):
@@ -168,11 +177,10 @@
         pick_kernel,
         out_shape=jax.ShapeDtypeStruct(table.shape + source.shape[1:], source.dtype),
         in_specs=[SMEM, VMEM],
-        out_specs=VMEM,
+        out_specs=HBM,
+        scratch_shapes=[pltpu.SemaphoreType.DMA(table.shape)],
         compiler_params=params(4),
-        cost_estimate=pl.CostEstimate(
-            flops=flops, bytes_accessed=4 * table.shape[0] * 65536, transcendentals=0
-        ),
+        cost_estimate=cost(flops, 1024 * 1024),
     )(table, source)
 
 
@@ -199,22 +207,46 @@
     )
 
 
-def pack_kernel(stats, out):
+def pack_kernel(stats, out, quarters, packed, in_sems, out_sems):
     half = stats.shape[1] // 2
     i, j = square_iotas(half)
     row = lax.broadcasted_iota(jnp.int32, (8, 128), 0)
-    for q in range(stats.shape[0]):
-        low = stats[q, half:, half:]
-        mixed = jnp.where(i <= j, stats[q, :half, :half], low).astype(jnp.bfloat16)
-        side = stats[q, :half, half:].astype(jnp.bfloat16)
+    corners = ((0, 0), (0, half), (half, half))
+    slots = range(stats.shape[0])
+    loads = [
+        [
+            pltpu.make_async_copy(
+                stats.at[q, pl.ds(at, half), pl.ds(left, half)],
+                quarters.at[q, k],
+                in_sems.at[3 * q + k],
+            )
+            for k, (at, left) in enumerate(corners)
+        ]
+        for q in slots
+    ]
+    stores = [
+        pltpu.make_async_copy(packed.at[q], out.at[:, q], out_sems.at[q]) for q in slots
+    ]
+    for q in slots:
+        for load in loads[q]:
+            load.start()
+    for q in slots:
+        for load in loads[q]:
+            load.wait()
+        low = quarters[q, 2]
+        mixed = jnp.where(i <= j, quarters[q, 0], low).astype(jnp.bfloat16)
+        side = quarters[q, 1].astype(jnp.bfloat16)
         diagonal = jnp.sum(jnp.where(i == j, low, 0.0), axis=0, keepdims=True)
         tail = jnp.where(
             row == 0, diagonal[:, :128], jnp.where(row == 1, diagonal[:, 128:], 0.0)
         ).astype(jnp.bfloat16)
         strips = (mixed[:, :128], mixed[:, 128:], side[:, :128], side[:, 128:])
         for c in range(16):
-            out[c, q, :64, :] = strips[c // 4][64 * (c % 4) : 64 * (c % 4) + 64, :]
-            out[c, q, 64:, :] = tail
+            packed[q, c, :64, :] = strips[c // 4][64 * (c % 4) : 64 * (c % 4) + 64, :]
+            packed[q, c, 64:, :] = tail
+        stores[q].start()
+    for q in slots:
+        stores[q].wait()
 
 
 def product(a, b):
@@ -251,7 +283,7 @@
     i, j = square_iotas(order_n)
     scale, quarter, square = [], [], []
     for s, gram in zip(sides, (left, right)):
-        new_stat = decay_rate * stat[s] + (1.0 - decay_rate) * gram[...]
+        new_stat = decay_rate * stat[s] + (1.0 - decay_rate) * gram[...].astype(jnp.float32)
         rounded = new_stat.astype(jnp.bfloat16)
         new_stat = rounded.astype(jnp.float32)
         squares = jnp.sum(new_stat * new_stat, axis=0, keepdims=True)
@@ -292,17 +324,17 @@
     n, order_n = grad.shape[1], grad.shape[2]
     return pl.pallas_call(
         choose_kernel,
-        out_shape=[shape(3, n // 2, order_n)] * 2,
+        out_shape=[shape(3, n // 2, order_n)] * 2 + [shape(2, 3, n // 2, order_n)],
         in_specs=[SMEM, VMEM],
-        out_specs=[VMEM] * 2,
-        compiler_params=params(12),
-        cost_estimate=cost(0, 6 * n * order_n),
+        out_specs=[VMEM] * 3,
+        compiler_params=params(16),
+        cost_estimate=cost(0, 12 * n * order_n),
     )(tables[0], grad)
 
 
-def gradient_sum(grad, got, tables):
-    n, order_n = grad.shape[1], grad.shape[2]
-    half = n // 2
+def gradient_sum(kept, got, tables):
+    half, order_n = kept.shape[2], kept.shape[3]
+    n = 2 * half
     *sent, kept = pl.pallas_call(
         first_sum_kernel,
         out_shape=[shape(2, half, order_n)] * 2 + [shape(2, 2, half, order_n)],
@@ -310,7 +342,7 @@
         out_specs=[VMEM] * 3,
         compiler_params=params(16),
         cost_estimate=cost(long_flops, 4 * 1024 * 1024),
-    )(tables[1], grad, *got)
+    )(tables[1], kept, *got)
     *sent, kept = pl.pallas_call(
         second_sum_kernel,
         out_shape=[shape(half, order_n)] * 2 + [shape(2, half, order_n)],
@@ -327,10 +359,9 @@
         compiler_params=params(8),
         cost_estimate=cost(0, 4 * 1024 * 1024),
     )(kept, *exchange(sent, 2))
-    square = jax.ShapeDtypeStruct((n, order_n), jnp.float32)
     return pl.pallas_call(
         gram_kernel,
-        out_shape=[shape(n, order_n), square, square],
+        out_shape=[shape(n, order_n)] * 3,
         in_specs=[VMEM] * 4,
         out_specs=[VMEM] * 3,
         compiler_params=params(16),
@@ -366,18 +397,24 @@
     packed = pl.pallas_call(
         pack_kernel,
         out_shape=shape(n_dp, slots, packed_rows, 128),
-        in_specs=[VMEM],
-        out_specs=VMEM,
+        in_specs=[HBM],
+        out_specs=HBM,
+        scratch_shapes=[
+            pltpu.VMEM((slots, 3, order_b // 2, order_b // 2), jnp.float32),
+            pltpu.VMEM((slots, n_dp, packed_rows, 128), jnp.bfloat16),
+            pltpu.SemaphoreType.DMA((3 * slots,)),
+            pltpu.SemaphoreType.DMA((slots,)),
+        ],
         compiler_params=params(12),
         cost_estimate=cost(0, 3 * 1024 * 1024),
     )(statistics[0, 0])
     spread = lax.all_to_all(packed, "dp", split_axis=0, concat_axis=0, tiled=True)
-    sent = first_sent(grad_partial[0], tables)
+    *sent, kept = first_sent(grad_partial[0], tables)
     spread, _ = lax.optimization_barrier((spread, sent))
     got = exchange(sent, 0)
     lanes = pick(lane_from, spread.reshape(slots * n_dp, packed_rows, 128), long_flops // 3)
     lanes = lax.all_to_all(lanes, ("z", "core"), split_axis=0, concat_axis=0, tiled=True)
-    gradient, left, right = gradient_sum(grad_partial[0], got, tables)
+    gradient, left, right = gradient_sum(kept, got, tables)
     lanes = pick(item_from, lanes).reshape(n_dp, 2, packed_rows, 128)
     chunks = lax.all_to_all(lanes, "dp", split_axis=0, concat_axis=0, tiled=True)
 
@@ -400,7 +437,7 @@
         output_kernel,
         out_shape=shape(blocks_col, slab, order_b),
         in_specs=[VMEM],
-        out_specs=pl.BlockSpec(memory_space=pl.ANY),
+        out_specs=HBM,
         scratch_shapes=[pltpu.SemaphoreType.DMA((blocks_col,))],
         compiler_params=params(4),
         cost_estimate=cost(0, 512 * 1024),

time: 114 us -> 114 us (level)
  waiting for transfers between devices: 26.7 us -> 24.7 us
  starting transfers between devices: 51.4 us -> 53.2 us
  Pallas kernels: 12.9 us -> 14.3 us
    ppermute x8, starting transfers between devices: 23.6 us -> 25.9 us  [exchange(): lax.ppermute(a, ('dp', 'core'), pairs(portion, step))]
    all_to_all x1, waiting for transfers between devices: 2.79 us -> 0.86 us  [body(): lax.all_to_all(packed, 'dp', split_axis=0, concat_axis=0, tiled=True)]
    pallas_call x2, Pallas kernels: 2.02 us -> 3.32 us  [pick(): pl.pallas_call(pick_kernel, out_shape=jax.ShapeDtypeStruct(table.shape +...]
    unnamed x25 -> x23, local copies, waits for them, and re-layouts: 7.07 us -> 6.46 us
  transfers between devices with their start and end apart: 11 -> 11, of which waited for: 6 -> 6; matrix products, arithmetic and copies ran while one was open for 1% -> 1% of each run, Pallas kernels for 7% -> 8%
where the time goes in v5:
time: 114 us
  starting transfers between devices  53.2 us (47%)
  waiting for transfers between devices  24.7 us (22%)
  Pallas kernels  14.3 us (13%)
  blocking collectives  13.3 us (12%)
  local copies, waits for them, and re-layouts  7.08 us (6%)
    ppermute x8, starting transfers between devices, exchange(): lax.ppermute(a, ('dp', 'core'), pairs(portion, step))  25.9 us
    all_to_all x1, starting transfers between devices, body(): lax.all_to_all(lanes, ('z', 'core'), split_axis=0, concat_axis=0, tiled=T...  15.4 us
    ppermute x8, waiting for transfers between devices, exchange(): lax.ppermute(a, ('dp', 'core'), pairs(portion, step))  14.2 us
    all_to_all x1, blocking collectives, body(): rows = lax.all_to_all(rows, 'dp', split_axis=0, concat_axis=0, tiled=True)  13.3 us
    all_to_all x1, waiting for transfers between devices, body(): lax.all_to_all(lanes, 'dp', split_axis=0, concat_axis=0, tiled=True)  9.65 us
    all_to_all x1, starting transfers between devices, body(): lax.all_to_all(packed, 'dp', split_axis=0, concat_axis=0, tiled=True)  7.05 us
    unnamed x23, local copies, waits for them, and re-layouts  6.46 us
    all_to_all x1, starting transfers between devices, body(): lax.all_to_all(lanes, 'dp', split_axis=0, concat_axis=0, tiled=True)  4.91 us
  transfers between devices with their start and end apart: 11, of which 6 were waited for; matrix products, arithmetic and copies ran while one was open for 1% of the time, Pallas kernels for 8%

profile of v5, /device:TPU:32, one launch (start us, length us, event | category | flops | bytes accessed | tf_op | source)
XLA Modules:
  0.0 113.7 jit_solution(14636062933026050740)
XLA Ops:
  0.0 0.0 copy-start
  0.0 0.0 copy-start.1
  0.0 1.7 %copy-done.1 = f32[1,1,2,512,512]{4,3,2,1,0:T(8,128)S(1)} copy-done((f32[1,1,2,512,512]{4,3,2,1,0:T(8,128)S(1)}, f32[1,1,2,512,512]{4,3,2,1,0:T(8,128)}, u32[]{:S(2)}) %copy-start.1) | copy-done | bytes 2097176
  1.7 1.1 shard_map.73
  2.8 0.0 copy-start.9
  2.8 7.0 %all-to-all-start = ((bf16[16,2,72,128]{3,2,1,0:T(8,128)(2,1)}), bf16[16,2,72,128]{3,2,1,0:T(8,128)(2,1)S(1)}, u32[]{:S(2)}, u32[]{:S(2)}) async-start(bf16[16,2,72,128]{3,2,1,0:T(8,128)(2,1)} %shard_map.73), calls=%async_computation | async-start | bytes 1179648 | tf_op jit(solution)/shard_map/all_to_all | solution.py:411
  9.9 0.0 copy-done.2
  9.9 0.0 copy-done
  9.9 1.9 %shard_map.74 = (bf16[3,256,512]{2,1,0:T(8,128)(2,1)}, bf16[3,256,512]{2,1,0:T(8,128)(2,1)}, bf16[2,3,256,512]{3,2,1,0:T(8,128)(2,1)S(1)}) custom-call(s32[384]{0:T(512)S(1)} %copy-done.2, bf16[5,512,512]{2,1,0:T(8,128)(2,1)S(1)} %bitcast.9), custom_call_target="tpu_custom_call" | custom-call | bytes 3145728 | tf_op jit(solution)/shard_map/pallas_call | solution.py:325
  11.8 0.0 copy-start.4
  11.8 1.2 %copy-done.4 = bf16[2,3,256,512]{3,2,1,0:T(8,128)(2,1)} copy-done((bf16[2,3,256,512]{3,2,1,0:T(8,128)(2,1)}, bf16[2,3,256,512]{3,2,1,0:T(8,128)(2,1)S(1)}, u32[]{:S(2)}) %copy-start.4) | copy-done | bytes 1572888
  13.0 3.8 %collective-permute-start = (bf16[3,256,512]{2,1,0:T(8,128)(2,1)}, bf16[3,256,512]{2,1,0:T(8,128)(2,1)S(1)}, u32[]{:S(2)}, u32[]{:S(2)}) collective-permute-start(bf16[3,256,512]{2,1,0:T(8,128)(2,1)} %get-tuple-element.20), channel_id=1, source_target_pairs={{0,128},{1,385},{32,160},{33,417},{64,192},{65,449},{96,224},{97,4... | collective-permute-start | bytes 2359304 | tf_op jit(solution)/shard_map/ppermute | solution.py:319
  16.8 3.4 %collective-permute-start.1 = (bf16[3,256,512]{2,1,0:T(8,128)(2,1)}, bf16[3,256,512]{2,1,0:T(8,128)(2,1)S(1)}, u32[]{:S(2)}, u32[]{:S(2)}) collective-permute-start(bf16[3,256,512]{2,1,0:T(8,128)(2,1)} %get-tuple-element.21), channel_id=1, source_target_pairs={{0,32},{1,97},{32,0},{33,65},{64,96},{65,33},{96,64},{97,1},{128,1... | collective-permute-start | bytes 2359304 | tf_op jit(solution)/shard_map/ppermute | solution.py:319
  20.2 0.0 copy-done.9
  20.2 0.1 copy.17
  20.3 0.1 copy.22
  20.5 0.1 eq.45
  20.6 0.2 convert_reduce_fusion
  20.9 0.1 reduce_sum.38
  21.0 0.2 fusion.5
  21.2 0.1 reduce_sum.40
  21.3 0.1 reduce_sum.41.table
  21.4 0.9 all-to-all-done
  22.3 0.0 copy-start.8
  22.3 1.6 %shard_map.75 = bf16[32,72,128]{2,1,0:T(8,128)(2,1)} custom-call(s32[32]{0:T(128)S(1)} %reduce_sum.41.table, bf16[32,72,128]{2,1,0:T(8,128)(2,1)S(1)} %bitcast.11), custom_call_target="tpu_custom_call" | custom-call | flops 33333334016 | bytes 1048576 | tf_op jit(solution)/shard_map/pallas_call | solution.py:176
  23.9 15.4 %all-to-all-start.1 = ((bf16[32,72,128]{2,1,0:T(8,128)(2,1)}), bf16[32,72,128]{2,1,0:T(8,128)(2,1)S(1)}, u32[]{:S(2)}, u32[]{:S(2)}) async-start(bf16[32,72,128]{2,1,0:T(8,128)(2,1)} %shard_map.75), calls=%async_computation.1 | async-start | bytes 1179648 | tf_op jit(solution)/shard_map/all_to_all | solution.py:416
  39.3 0.0 collective-permute-done.r0
  39.3 0.0 collective-permute-done.1.r1
  39.3 0.0 copy-start.6
  39.3 0.9 copy-done.6
  40.2 0.0 copy-done.8
  40.2 0.0 copy-start.5
  40.2 1.4 %copy-done.5 = bf16[2,3,256,512]{3,2,1,0:T(8,128)(2,1)S(1)} copy-done((bf16[2,3,256,512]{3,2,1,0:T(8,128)(2,1)S(1)}, bf16[2,3,256,512]{3,2,1,0:T(8,128)(2,1)}, u32[]{:S(2)}) %copy-start.5) | copy-done | bytes 1572888
  41.6 0.0 copy-start.7
  41.6 1.1 copy-done.7
  42.8 0.0 copy-start.3
  42.8 1.9 %shard_map.77 = (bf16[2,256,512]{2,1,0:T(8,128)(2,1)}, bf16[2,256,512]{2,1,0:T(8,128)(2,1)}, bf16[2,2,256,512]{3,2,1,0:T(8,128)(2,1)S(1)}) custom-call(s32[256]{0:T(256)S(1)} %copy-done.8, bf16[2,3,256,512]{3,2,1,0:T(8,128)(2,1)S(1)} %copy-done.5, bf16[3,256,512]{2,1,0:T(8,128)(2,1)S(1)} %collective-permute-done.r0, bf16[3,256,512]{2,1,0:T(8,128)(2,1)S(1)} %copy-done.7), custom_call_target="tpu_custom_call" | custom-call | flops 99999997952 | bytes 4194304 | tf_op jit(solution)/shard_map/pallas_call | solution.py:338
  44.7 0.0 copy-start.10
  44.7 3.3 %collective-permute-start.2 = (bf16[2,256,512]{2,1,0:T(8,128)(2,1)}, bf16[2,256,512]{2,1,0:T(8,128)(2,1)S(1)}, u32[]{:S(2)}, u32[]{:S(2)}) collective-permute-start(bf16[2,256,512]{2,1,0:T(8,128)(2,1)} %get-tuple-element.25), channel_id=1, source_target_pairs={{0,384},{1,129},{32,416},{33,161},{64,448},{65,193},{96,480},{97,2... | collective-permute-start | bytes 1572872 | tf_op jit(solution)/shard_map/ppermute | solution.py:319
  48.0 4.0 %collective-permute-start.3 = (bf16[2,256,512]{2,1,0:T(8,128)(2,1)}, bf16[2,256,512]{2,1,0:T(8,128)(2,1)S(1)}, u32[]{:S(2)}, u32[]{:S(2)}) collective-permute-start(bf16[2,256,512]{2,1,0:T(8,128)(2,1)} %get-tuple-element.26), channel_id=1, source_target_pairs={{0,96},{1,33},{32,64},{33,1},{64,32},{65,97},{96,0},{97,65},{128,2... | collective-permute-start | bytes 1572872 | tf_op jit(solution)/shard_map/ppermute | solution.py:319
  52.0 0.1 reshape.22
  52.1 5.3 %collective-permute-done.2.r0 = bf16[2,256,512]{2,1,0:T(8,128)(2,1)S(1)} collective-permute-done((bf16[2,256,512]{2,1,0:T(8,128)(2,1)}, bf16[2,256,512]{2,1,0:T(8,128)(2,1)S(1)}, u32[]{:S(2)}, u32[]{:S(2)}) %collective-permute-start.2) | collective-permute-done | bytes 524320 | tf_op jit(solution)/shard_map/ppermute | solution.py:319
  57.3 3.1 %collective-permute-done.3.r1 = bf16[2,256,512]{2,1,0:T(8,128)(2,1)S(1)} collective-permute-done((bf16[2,256,512]{2,1,0:T(8,128)(2,1)}, bf16[2,256,512]{2,1,0:T(8,128)(2,1)S(1)}, u32[]{:S(2)}, u32[]{:S(2)}) %collective-permute-start.3) | collective-permute-done | bytes 524320 | tf_op jit(solution)/shard_map/ppermute | solution.py:319
  60.5 0.0 copy-done.3
  60.5 1.4 %shard_map.78 = (bf16[256,512]{1,0:T(8,128)(2,1)}, bf16[256,512]{1,0:T(8,128)(2,1)S(1)}, bf16[2,256,512]{2,1,0:T(8,128)(2,1)S(1)}) custom-call(s32[128]{0:T(128)S(1)} %copy-done.3, bf16[2,2,256,512]{3,2,1,0:T(8,128)(2,1)S(1)} %get-tuple-element.24.kept, bf16[2,256,512]{2,1,0:T(8,128)(2,1)S(1)} %collective-permute-done.2.r0, ...), custom_call_target="tpu_custom_call" | custom-call | bytes 4194304 | tf_op jit(solution)/shard_map/pallas_call | solution.py:346
  61.9 1.9 %collective-permute-start.4 = (bf16[256,512]{1,0:T(8,128)(2,1)}, bf16[256,512]{1,0:T(8,128)(2,1)S(1)}, u32[]{:S(2)}, u32[]{:S(2)}) collective-permute-start(bf16[256,512]{1,0:T(8,128)(2,1)} %get-tuple-element.28), channel_id=1, source_target_pairs={{0,32},{1,97},{32,0},{33,65},{64,96},{65,33},{96,64},{97,1},{128,1... | collective-permute-start | bytes 786440 | tf_op jit(solution)/shard_map/ppermute | solution.py:319
  63.8 2.5 %collective-permute-start.5 = (bf16[256,512]{1,0:T(8,128)(2,1)S(1)}, bf16[256,512]{1,0:T(8,128)(2,1)S(1)}, u32[]{:S(2)}, u32[]{:S(2)}) collective-permute-start(bf16[256,512]{1,0:T(8,128)(2,1)S(1)} %get-tuple-element.29), channel_id=1, source_target_pairs={{0,128},{1,385},{32,160},{33,417},{64,192},{65,449},{96,224},{97,4... | collective-permute-start | bytes 786440 | tf_op jit(solution)/shard_map/ppermute | solution.py:319
  66.3 4.0 %collective-permute-done.4.r0 = bf16[256,512]{1,0:T(8,128)(2,1)S(1)} collective-permute-done((bf16[256,512]{1,0:T(8,128)(2,1)}, bf16[256,512]{1,0:T(8,128)(2,1)S(1)}, u32[]{:S(2)}, u32[]{:S(2)}) %collective-permute-start.4) | collective-permute-done | bytes 262176 | tf_op jit(solution)/shard_map/ppermute | solution.py:319
  70.4 1.7 %collective-permute-done.5.r1 = bf16[256,512]{1,0:T(8,128)(2,1)S(1)} collective-permute-done((bf16[256,512]{1,0:T(8,128)(2,1)S(1)}, bf16[256,512]{1,0:T(8,128)(2,1)S(1)}, u32[]{:S(2)}, u32[]{:S(2)}) %collective-permute-start.5) | collective-permute-done | bytes 262176 | tf_op jit(solution)/shard_map/ppermute | solution.py:319
  72.1 0.1 shard_map.79
  72.2 4.0 %collective-permute-start.6 = (bf16[256,512]{1,0:T(8,128)(2,1)S(1)}, bf16[256,512]{1,0:T(8,128)(2,1)S(1)}, u32[]{:S(2)}, u32[]{:S(2)}) collective-permute-start(bf16[256,512]{1,0:T(8,128)(2,1)S(1)} %get-tuple-element.30.a), channel_id=1, source_target_pairs={{0,96},{1,33},{32,64},{33,1},{64,32},{65,97},{96,0},{97,65},{128,2... | collective-permute-start | bytes 786440 | tf_op jit(solution)/shard_map/ppermute | solution.py:319
  76.2 3.1 %collective-permute-start.7 = (bf16[256,512]{1,0:T(8,128)(2,1)S(1)}, bf16[256,512]{1,0:T(8,128)(2,1)S(1)}, u32[]{:S(2)}, u32[]{:S(2)}) collective-permute-start(bf16[256,512]{1,0:T(8,128)(2,1)S(1)} %get-tuple-element.31.b), channel_id=1, source_target_pairs={{0,384},{1,129},{32,416},{33,161},{64,448},{65,193},{96,480},{97,2... | collective-permute-start | bytes 786440 | tf_op jit(solution)/shard_map/ppermute | solution.py:319
  79.3 0.0 copy-done.10
  79.3 0.2 select_reduce_fusion.table
  79.5 0.0 all-to-all-done.1.source
  79.5 1.7 %shard_map.76 = bf16[32,72,128]{2,1,0:T(8,128)(2,1)} custom-call(s32[32]{0:T(128)S(1)} %select_reduce_fusion.table, bf16[32,72,128]{2,1,0:T(8,128)(2,1)S(1)} %all-to-all-done.1.source), custom_call_target="tpu_custom_call" | custom-call | bytes 1048576 | tf_op jit(solution)/shard_map/pallas_call | solution.py:176
  81.2 4.9 %all-to-all-start.2 = ((bf16[16,2,72,128]{3,2,1,0:T(8,128)(2,1)}), bf16[16,2,72,128]{3,2,1,0:T(8,128)(2,1)S(1)}, u32[]{:S(2)}, u32[]{:S(2)}) async-start(bf16[16,2,72,128]{3,2,1,0:T(8,128)(2,1)} %bitcast.5), calls=%async_computation.2 | async-start | bytes 1179648 | tf_op jit(solution)/shard_map/all_to_all | solution.py:419
  86.1 0.0 collective-permute-done.6.r0
  86.1 0.0 collective-permute-done.7.r1
  86.1 0.8 shard_map.80
  86.9 9.7 %all-to-all-done.2.chunks = bf16[16,2,72,128]{3,2,1,0:T(8,128)(2,1)S(1)} async-done(((bf16[16,2,72,128]{3,2,1,0:T(8,128)(2,1)}), bf16[16,2,72,128]{3,2,1,0:T(8,128)(2,1)S(1)}, u32[]{:S(2)}, u32[]{:S(2)}) %all-to-all-start.2) | async-done | bytes 589856 | tf_op jit(solution)/shard_map/all_to_all | solution.py:419
  96.6 3.1 %shard_map.81 = bf16[512,512]{1,0:T(8,128)(2,1)S(1)} custom-call(bf16[16,2,72,128]{3,2,1,0:T(8,128)(2,1)S(1)} %all-to-all-done.2.chunks, bf16[512,512]{1,0:T(8,128)(2,1)S(1)} %get-tuple-element.32.gradient, bf16[512,512]{1,0:T(8,128)(2,1)S(1)} %get-tuple-element.33.left, bf16[512,512]{1,0:T(8,128)(2,1)S(1)} %get-tuple-element.34.right), custom_call_target="tpu_custom_call" | custom-call | flops 2147483648 | bytes 6291456 | tf_op jit(solution)/shard_map/pallas_call | solution.py:422
  99.6 13.3 %all_to_all.20.source = bf16[16,32,512]{2,1,0:T(8,128)(2,1)S(1)} all-to-all(bf16[16,32,512]{2,1,0:T(8,128)(2,1)S(1)} %bitcast.12), channel_id=1, replica_groups=mesh['dp'=16,'z'=16,'core'=2] {'dp'}, dimensions={0} | all-to-all | bytes 1048576 | tf_op jit(solution)/shard_map/all_to_all | solution.py:435
  113.0 0.7 shard_map.82
  (6 shorter events, 0.0 us)
Async XLA Ops:
  0.0 9.9 %copy-start.2 = (s32[384]{0:T(512)S(1)}, s32[384]{0:T(512)}, u32[]{:S(2)}) copy-start(s32[384]{0:T(512)} %constant.50.clone.table) | copy-start | bytes 4612
  0.0 9.9 %copy-start = (bf16[1,5,512,512]{3,2,1,0:T(8,128)(2,1)S(1)}, bf16[1,5,512,512]{3,2,1,0:T(8,128)(2,1)}, u32[]{:S(2)}) copy-start(bf16[1,5,512,512]{3,2,1,0:T(8,128)(2,1)} %param.7) | copy-start | bytes 7864324
  0.0 1.7 %copy-start.1 = (f32[1,1,2,512,512]{4,3,2,1,0:T(8,128)S(1)}, f32[1,1,2,512,512]{4,3,2,1,0:T(8,128)}, u32[]{:S(2)}) copy-start(f32[1,1,2,512,512]{4,3,2,1,0:T(8,128)} %param.8) | copy-start | bytes 6291460
  2.8 17.4 %copy-start.9 = (s32[160,2]{0,1:T(2,128)S(1)}, s32[160,2]{0,1:T(2,128)}, u32[]{:S(2)}) copy-start(s32[160,2]{0,1:T(2,128)} %param.9) | copy-start | bytes 3844
  2.8 19.4 %all-to-all-start = ((bf16[16,2,72,128]{3,2,1,0:T(8,128)(2,1)}), bf16[16,2,72,128]{3,2,1,0:T(8,128)(2,1)S(1)}, u32[]{:S(2)}, u32[]{:S(2)}) async-start(bf16[16,2,72,128]{3,2,1,0:T(8,128)(2,1)} %shard_map.73), calls=%async_computation | async-start | bytes 1179648 | tf_op jit(solution)/shard_map/all_to_all | solution.py:411
  11.8 1.2 %copy-start.4 = (bf16[2,3,256,512]{3,2,1,0:T(8,128)(2,1)}, bf16[2,3,256,512]{3,2,1,0:T(8,128)(2,1)S(1)}, u32[]{:S(2)}) copy-start(bf16[2,3,256,512]{3,2,1,0:T(8,128)(2,1)S(1)} %get-tuple-element.23.kept) | copy-start | bytes 4718596
  13.0 26.3 %collective-permute-start = (bf16[3,256,512]{2,1,0:T(8,128)(2,1)}, bf16[3,256,512]{2,1,0:T(8,128)(2,1)S(1)}, u32[]{:S(2)}, u32[]{:S(2)}) collective-permute-start(bf16[3,256,512]{2,1,0:T(8,128)(2,1)} %get-tuple-element.20), channel_id=1, source_target_pairs={{0,128},{1,385},{32,160},{33,417},{64,192},{65,449},{96,224},{97,4... | collective-permute-start | bytes 2359304 | tf_op jit(solution)/shard_map/ppermute | solution.py:319
  16.8 22.5 %collective-permute-start.1 = (bf16[3,256,512]{2,1,0:T(8,128)(2,1)}, bf16[3,256,512]{2,1,0:T(8,128)(2,1)S(1)}, u32[]{:S(2)}, u32[]{:S(2)}) collective-permute-start(bf16[3,256,512]{2,1,0:T(8,128)(2,1)} %get-tuple-element.21), channel_id=1, source_target_pairs={{0,32},{1,97},{32,0},{33,65},{64,96},{65,33},{96,64},{97,1},{128,1... | collective-permute-start | bytes 2359304 | tf_op jit(solution)/shard_map/ppermute | solution.py:319
  22.3 17.9 %copy-start.8 = (s32[256]{0:T(256)S(1)}, s32[256]{0:T(256)}, u32[]{:S(2)}) copy-start(s32[256]{0:T(256)} %constant.51.clone.table) | copy-start | bytes 3076
  23.9 55.6 %all-to-all-start.1 = ((bf16[32,72,128]{2,1,0:T(8,128)(2,1)}), bf16[32,72,128]{2,1,0:T(8,128)(2,1)S(1)}, u32[]{:S(2)}, u32[]{:S(2)}) async-start(bf16[32,72,128]{2,1,0:T(8,128)(2,1)} %shard_map.75), calls=%async_computation.1 | async-start | bytes 1179648 | tf_op jit(solution)/shard_map/all_to_all | solution.py:416
  39.3 0.9 copy-start.6
  40.2 1.4 %copy-start.5 = (bf16[2,3,256,512]{3,2,1,0:T(8,128)(2,1)S(1)}, bf16[2,3,256,512]{3,2,1,0:T(8,128)(2,1)}, u32[]{:S(2)}) copy-start(bf16[2,3,256,512]{3,2,1,0:T(8,128)(2,1)} %copy-done.4) | copy-start | bytes 4718596
  41.6 1.1 copy-start.7
  42.8 17.7 %copy-start.3 = (s32[128]{0:T(128)S(1)}, s32[128]{0:T(128)}, u32[]{:S(2)}) copy-start(s32[128]{0:T(128)} %constant.52.clone.table) | copy-start | bytes 1540
  44.7 34.6 %copy-start.10 = (s32[2,32]{1,0:T(2,128)S(1)}, s32[2,32]{1,0:T(2,128)}, u32[]{:S(2)}) copy-start(s32[2,32]{1,0:T(2,128)} %constant.53.clone) | copy-start | bytes 772
  44.7 12.6 %collective-permute-start.2 = (bf16[2,256,512]{2,1,0:T(8,128)(2,1)}, bf16[2,256,512]{2,1,0:T(8,128)(2,1)S(1)}, u32[]{:S(2)}, u32[]{:S(2)}) collective-permute-start(bf16[2,256,512]{2,1,0:T(8,128)(2,1)} %get-tuple-element.25), channel_id=1, source_target_pairs={{0,384},{1,129},{32,416},{33,161},{64,448},{65,193},{96,480},{97,2... | collective-permute-start | bytes 1572872 | tf_op jit(solution)/shard_map/ppermute | solution.py:319
  48.0 12.5 %collective-permute-start.3 = (bf16[2,256,512]{2,1,0:T(8,128)(2,1)}, bf16[2,256,512]{2,1,0:T(8,128)(2,1)S(1)}, u32[]{:S(2)}, u32[]{:S(2)}) collective-permute-start(bf16[2,256,512]{2,1,0:T(8,128)(2,1)} %get-tuple-element.26), channel_id=1, source_target_pairs={{0,96},{1,33},{32,64},{33,1},{64,32},{65,97},{96,0},{97,65},{128,2... | collective-permute-start | bytes 1572872 | tf_op jit(solution)/shard_map/ppermute | solution.py:319
  61.9 8.5 %collective-permute-start.4 = (bf16[256,512]{1,0:T(8,128)(2,1)}, bf16[256,512]{1,0:T(8,128)(2,1)S(1)}, u32[]{:S(2)}, u32[]{:S(2)}) collective-permute-start(bf16[256,512]{1,0:T(8,128)(2,1)} %get-tuple-element.28), channel_id=1, source_target_pairs={{0,32},{1,97},{32,0},{33,65},{64,96},{65,33},{96,64},{97,1},{128,1... | collective-permute-start | bytes 786440 | tf_op jit(solution)/shard_map/ppermute | solution.py:319
  63.8 8.3 %collective-permute-start.5 = (bf16[256,512]{1,0:T(8,128)(2,1)S(1)}, bf16[256,512]{1,0:T(8,128)(2,1)S(1)}, u32[]{:S(2)}, u32[]{:S(2)}) collective-permute-start(bf16[256,512]{1,0:T(8,128)(2,1)S(1)} %get-tuple-element.29), channel_id=1, source_target_pairs={{0,128},{1,385},{32,160},{33,417},{64,192},{65,449},{96,224},{97,4... | collective-permute-start | bytes 786440 | tf_op jit(solution)/shard_map/ppermute | solution.py:319
  72.2 13.9 %collective-permute-start.6 = (bf16[256,512]{1,0:T(8,128)(2,1)S(1)}, bf16[256,512]{1,0:T(8,128)(2,1)S(1)}, u32[]{:S(2)}, u32[]{:S(2)}) collective-permute-start(bf16[256,512]{1,0:T(8,128)(2,1)S(1)} %get-tuple-element.30.a), channel_id=1, source_target_pairs={{0,96},{1,33},{32,64},{33,1},{64,32},{65,97},{96,0},{97,65},{128,2... | collective-permute-start | bytes 786440 | tf_op jit(solution)/shard_map/ppermute | solution.py:319
  76.2 9.9 %collective-permute-start.7 = (bf16[256,512]{1,0:T(8,128)(2,1)S(1)}, bf16[256,512]{1,0:T(8,128)(2,1)S(1)}, u32[]{:S(2)}, u32[]{:S(2)}) collective-permute-start(bf16[256,512]{1,0:T(8,128)(2,1)S(1)} %get-tuple-element.31.b), channel_id=1, source_target_pairs={{0,384},{1,129},{32,416},{33,161},{64,448},{65,193},{96,480},{97,2... | collective-permute-start | bytes 786440 | tf_op jit(solution)/shard_map/ppermute | solution.py:319
  81.2 15.4 %all-to-all-start.2 = ((bf16[16,2,72,128]{3,2,1,0:T(8,128)(2,1)}), bf16[16,2,72,128]{3,2,1,0:T(8,128)(2,1)S(1)}, u32[]{:S(2)}, u32[]{:S(2)}) async-start(bf16[16,2,72,128]{3,2,1,0:T(8,128)(2,1)} %bitcast.5), calls=%async_computation.2 | async-start | bytes 1179648 | tf_op jit(solution)/shard_map/all_to_all | solution.py:419

commit v6 on v5

--- a/solution.py
+++ b/solution.py
@@ -23,6 +23,8 @@
 packed_rows = 72
 
 long_flops = 10**11
+
+most_mib = 60
 
 VMEM = pl.BlockSpec(memory_space=pltpu.VMEM)
 SMEM = pl.BlockSpec(memory_space=pltpu.SMEM)
@@ -114,19 +116,31 @@
     return [table[base + k] for k in range(width)]
 
 
-def choose_kernel(table, source, s0, s1, kept):
+def choose_kernel(table, source, s0, s1):
     table = my_row(table)
     height = s0.shape[1]
     for h, sent in enumerate((s0, s1)):
-        rows = slice(h * height, (h + 1) * height)
         for u in range(3):
-            sent[u] = source[table[6 * h + u], rows, :]
-            kept[h, u] = source[table[6 * h + 3 + u], rows, :]
-
-
-def first_sum_kernel(table, kept, r0, r1, s0, s1, next_kept):
-    table = my_row(table)
+            sent[u] = source[table[6 * h + u], h * height : (h + 1) * height, :]
+
+
+def first_sum_kernel(sent_table, table, source, r0, r1, s0, s1, next_kept, kept, sems):
+    sent_table, table = my_row(sent_table), my_row(table)
+    height = r0.shape[1]
+    loads = [
+        pltpu.make_async_copy(
+            source.at[sent_table[6 * h + 3 + u], pl.ds(h * height, height), :],
+            kept.at[h, u],
+            sems.at[3 * h + u],
+        )
+        for h in range(2)
+        for u in range(3)
+    ]
+    for load in loads:
+        load.start()
     for h, (got, sent) in enumerate(((r0, s0), (r1, s1))):
+        for load in loads[3 * h : 3 * h + 3]:
+            load.wait()
         for u in range(4):
             place = table[4 * h + u]
             total = add_rounded(kept[h, place], got[place])
@@ -161,15 +175,9 @@
         gram[...] = product.astype(jnp.bfloat16)
 
 
-def pick_kernel(table, source, out, sems):
-    copies = [
-        pltpu.make_async_copy(source.at[table[i]], out.at[i], sems.at[i])
-        for i in range(out.shape[0])
-    ]
-    for copy in copies:
-        copy.start()
-    for copy in copies:
-        copy.wait()
+def pick_kernel(table, source, out):
+    for i in range(out.shape[0]):
+        out[i] = source[table[i]]
 
 
 def pick(table, source, flops=0):
@@ -177,10 +185,9 @@
         pick_kernel,
         out_shape=jax.ShapeDtypeStruct(table.shape + source.shape[1:], source.dtype),
         in_specs=[SMEM, VMEM],
-        out_specs=HBM,
-        scratch_shapes=[pltpu.SemaphoreType.DMA(table.shape)],
+        out_specs=VMEM,
         compiler_params=params(4),
-        cost_estimate=cost(flops, 1024 * 1024),
+        cost_estimate=cost(flops, 4 * 1024 * 1024),
     )(table, source)
 
 
@@ -324,25 +331,29 @@
     n, order_n = grad.shape[1], grad.shape[2]
     return pl.pallas_call(
         choose_kernel,
-        out_shape=[shape(3, n // 2, order_n)] * 2 + [shape(2, 3, n // 2, order_n)],
+        out_shape=[shape(3, n // 2, order_n)] * 2,
         in_specs=[SMEM, VMEM],
-        out_specs=[VMEM] * 3,
-        compiler_params=params(16),
+        out_specs=[VMEM] * 2,
+        compiler_params=params(most_mib),
         cost_estimate=cost(0, 12 * n * order_n),
     )(tables[0], grad)
 
 
-def gradient_sum(kept, got, tables):
-    half, order_n = kept.shape[2], kept.shape[3]
-    n = 2 * half
+def gradient_sum(grad, got, tables):
+    n, order_n = grad.shape[1], grad.shape[2]
+    half = n // 2
     *sent, kept = pl.pallas_call(
         first_sum_kernel,
         out_shape=[shape(2, half, order_n)] * 2 + [shape(2, 2, half, order_n)],
-        in_specs=[SMEM] + [VMEM] * 3,
+        in_specs=[SMEM, SMEM, HBM, VMEM, VMEM],
         out_specs=[VMEM] * 3,
+        scratch_shapes=[
+            pltpu.VMEM((2, 3, half, order_n), jnp.bfloat16),
+            pltpu.SemaphoreType.DMA((6,)),
+        ],
         compiler_params=params(16),
         cost_estimate=cost(long_flops, 4 * 1024 * 1024),
-    )(tables[1], kept, *got)
+    )(tables[0], tables[1], grad, *got)
     *sent, kept = pl.pallas_call(
         second_sum_kernel,
         out_shape=[shape(half, order_n)] * 2 + [shape(2, half, order_n)],
@@ -405,16 +416,16 @@
             pltpu.SemaphoreType.DMA((3 * slots,)),
             pltpu.SemaphoreType.DMA((slots,)),
         ],
-        compiler_params=params(12),
+        compiler_params=params(most_mib),
         cost_estimate=cost(0, 3 * 1024 * 1024),
     )(statistics[0, 0])
     spread = lax.all_to_all(packed, "dp", split_axis=0, concat_axis=0, tiled=True)
-    *sent, kept = first_sent(grad_partial[0], tables)
+    sent = first_sent(grad_partial[0], tables)
     spread, _ = lax.optimization_barrier((spread, sent))
     got = exchange(sent, 0)
     lanes = pick(lane_from, spread.reshape(slots * n_dp, packed_rows, 128), long_flops // 3)
     lanes = lax.all_to_all(lanes, ("z", "core"), split_axis=0, concat_axis=0, tiled=True)
-    gradient, left, right = gradient_sum(kept, got, tables)
+    gradient, left, right = gradient_sum(grad_partial[0], got, tables)
     lanes = pick(item_from, lanes).reshape(n_dp, 2, packed_rows, 128)
     chunks = lax.all_to_all(lanes, "dp", split_axis=0, concat_axis=0, tiled=True)
 

time: 114 us -> 112 us (0.982)
  local copies, waits for them, and re-layouts: 7.08 us -> 3.75 us
  Pallas kernels: 14.3 us -> 15.6 us
    unnamed x23 -> x19, local copies, waits for them, and re-layouts: 6.46 us -> 3.13 us
    pallas_call x2, Pallas kernels: 3.32 us -> 1.99 us  [pick(): pl.pallas_call(pick_kernel, out_shape=jax.ShapeDtypeStruct(table.shape +...]
  transfers between devices with their start and end apart: 11 -> 11, of which waited for: 6 -> 6; matrix products, arithmetic and copies ran while one was open for 1% -> 1% of each run, Pallas kernels for 8% -> 9%
where the time goes in v6:
time: 112 us
  starting transfers between devices  53 us (47%)
  waiting for transfers between devices  24.9 us (22%)
  Pallas kernels  15.6 us (14%)
  blocking collectives  13.3 us (12%)
  local copies, waits for them, and re-layouts  3.75 us (3%)
    ppermute x8, starting transfers between devices, exchange(): lax.ppermute(a, ('dp', 'core'), pairs(portion, step))  25.7 us
    all_to_all x1, starting transfers between devices, body(): lax.all_to_all(lanes, ('z', 'core'), split_axis=0, concat_axis=0, tiled=T...  15.4 us
    ppermute x8, waiting for transfers between devices, exchange(): lax.ppermute(a, ('dp', 'core'), pairs(portion, step))  14.2 us
    all_to_all x1, blocking collectives, body(): rows = lax.all_to_all(rows, 'dp', split_axis=0, concat_axis=0, tiled=True)  13.3 us
    all_to_all x1, waiting for transfers between devices, body(): lax.all_to_all(lanes, 'dp', split_axis=0, concat_axis=0, tiled=True)  9.65 us
    all_to_all x1, starting transfers between devices, body(): lax.all_to_all(packed, 'dp', split_axis=0, concat_axis=0, tiled=True)  7.05 us
    all_to_all x1, starting transfers between devices, body(): lax.all_to_all(lanes, 'dp', split_axis=0, concat_axis=0, tiled=True)  4.9 us
    unnamed x19, local copies, waits for them, and re-layouts  3.13 us
  transfers between devices with their start and end apart: 11, of which 6 were waited for; matrix products, arithmetic and copies ran while one was open for 1% of the time, Pallas kernels for 9%

profile of v6, /device:TPU:32, one launch (start us, length us, event | category | flops | bytes accessed | tf_op | source)
XLA Modules:
  0.0 111.7 jit_solution(9049674418463228470)
XLA Ops:
  0.0 0.0 copy-start.7
  0.0 2.2 %shard_map.73 = bf16[16,2,72,128]{3,2,1,0:T(8,128)(2,1)} custom-call(f32[2,512,512]{2,1,0:T(8,128)} %bitcast.13), custom_call_target="tpu_custom_call" | custom-call | bytes 3145728 | tf_op jit(solution)/shard_map/pallas_call | solution.py:408
  2.2 7.0 %all-to-all-start = ((bf16[16,2,72,128]{3,2,1,0:T(8,128)(2,1)}), bf16[16,2,72,128]{3,2,1,0:T(8,128)(2,1)S(1)}, u32[]{:S(2)}, u32[]{:S(2)}) async-start(bf16[16,2,72,128]{3,2,1,0:T(8,128)(2,1)} %shard_map.73), calls=%async_computation | async-start | bytes 1179648 | tf_op jit(solution)/shard_map/all_to_all | solution.py:422
  9.2 3.0 %shard_map.74 = (bf16[3,256,512]{2,1,0:T(8,128)(2,1)}, bf16[3,256,512]{2,1,0:T(8,128)(2,1)}) custom-call(s32[384]{0:T(512)} %constant.50.clone.table.sent_table, bf16[5,512,512]{2,1,0:T(8,128)(2,1)} %bitcast.9), custom_call_target="tpu_custom_call" | custom-call | bytes 3145728 | tf_op jit(solution)/shard_map/pallas_call | solution.py:332
  12.3 3.8 %collective-permute-start = (bf16[3,256,512]{2,1,0:T(8,128)(2,1)}, bf16[3,256,512]{2,1,0:T(8,128)(2,1)}, u32[]{:S(2)}, u32[]{:S(2)}) collective-permute-start(bf16[3,256,512]{2,1,0:T(8,128)(2,1)} %get-tuple-element.19), channel_id=1, source_target_pairs={{0,128},{1,385},{32,160},{33,417},{64,192},{65,449},{96,224},{97,4... | collective-permute-start | bytes 2359304 | tf_op jit(solution)/shard_map/ppermute | solution.py:326
  16.1 3.4 %collective-permute-start.1 = (bf16[3,256,512]{2,1,0:T(8,128)(2,1)}, bf16[3,256,512]{2,1,0:T(8,128)(2,1)}, u32[]{:S(2)}, u32[]{:S(2)}) collective-permute-start(bf16[3,256,512]{2,1,0:T(8,128)(2,1)} %get-tuple-element.20), channel_id=1, source_target_pairs={{0,32},{1,97},{32,0},{33,65},{64,96},{65,33},{96,64},{97,1},{128,1... | collective-permute-start | bytes 2359304 | tf_op jit(solution)/shard_map/ppermute | solution.py:326
  19.5 0.0 copy-done.7
  19.5 0.1 copy.17
  19.6 0.1 copy.22
  19.8 0.1 eq.45
  19.9 0.2 convert_reduce_fusion
  20.1 0.1 reduce_sum.38
  20.3 0.2 fusion.5
  20.5 0.1 reduce_sum.40
  20.6 0.1 reduce_sum.41.table
  20.7 1.0 all-to-all-done
  21.7 0.0 copy-start
  21.7 0.0 copy-start.4
  21.7 0.0 copy-start.6
  21.7 0.6 shard_map.75
  22.3 0.0 copy-start.3
  22.3 0.8 copy-done.3
  23.1 15.4 %all-to-all-start.1 = ((bf16[32,72,128]{2,1,0:T(8,128)(2,1)}), bf16[32,72,128]{2,1,0:T(8,128)(2,1)S(1)}, u32[]{:S(2)}, u32[]{:S(2)}) async-start(bf16[32,72,128]{2,1,0:T(8,128)(2,1)} %copy-done.3), calls=%async_computation.1 | async-start | bytes 1179648 | tf_op jit(solution)/shard_map/all_to_all | solution.py:427
  38.5 0.0 copy-start.5
  38.5 0.0 collective-permute-done.r0
  38.5 0.0 collective-permute-done.1.r1
  38.5 0.0 copy-done
  38.5 0.0 copy-done.4
  38.6 0.0 copy-done.6
  38.6 3.0 %shard_map.77 = (bf16[2,256,512]{2,1,0:T(8,128)(2,1)}, bf16[2,256,512]{2,1,0:T(8,128)(2,1)}, bf16[2,2,256,512]{3,2,1,0:T(8,128)(2,1)S(1)}) custom-call(s32[384]{0:T(512)S(1)} %copy-done.4, s32[256]{0:T(256)S(1)} %copy-done.6, bf16[5,512,512]{2,1,0:T(8,128)(2,1)S(1)} %bitcast.10, bf16[3,256,512]{2,1,0:T(8,128)(2,1)} %collective-permute-done.r0, ...), custom_call_target="tpu_custom_call" | custom-call | flops 99999997952 | bytes 4194304 | tf_op jit(solution)/shard_map/pallas_call | solution.py:345
  41.6 0.0 copy-start.1
  41.6 1.0 copy-done.1
  42.5 0.0 copy-start.8
  42.5 3.1 %collective-permute-start.2 = (bf16[2,256,512]{2,1,0:T(8,128)(2,1)}, bf16[2,256,512]{2,1,0:T(8,128)(2,1)S(1)}, u32[]{:S(2)}, u32[]{:S(2)}) collective-permute-start(bf16[2,256,512]{2,1,0:T(8,128)(2,1)} %get-tuple-element.23), channel_id=1, source_target_pairs={{0,384},{1,129},{32,416},{33,161},{64,448},{65,193},{96,480},{97,2... | collective-permute-start | bytes 1572872 | tf_op jit(solution)/shard_map/ppermute | solution.py:326
  45.7 4.0 %collective-permute-start.3 = (bf16[2,256,512]{2,1,0:T(8,128)(2,1)}, bf16[2,256,512]{2,1,0:T(8,128)(2,1)S(1)}, u32[]{:S(2)}, u32[]{:S(2)}) collective-permute-start(bf16[2,256,512]{2,1,0:T(8,128)(2,1)} %get-tuple-element.24), channel_id=1, source_target_pairs={{0,96},{1,33},{32,64},{33,1},{64,32},{65,97},{96,0},{97,65},{128,2... | collective-permute-start | bytes 1572872 | tf_op jit(solution)/shard_map/ppermute | solution.py:326
  49.6 0.1 reshape.22
  49.7 5.4 %collective-permute-done.2.r0 = bf16[2,256,512]{2,1,0:T(8,128)(2,1)S(1)} collective-permute-done((bf16[2,256,512]{2,1,0:T(8,128)(2,1)}, bf16[2,256,512]{2,1,0:T(8,128)(2,1)S(1)}, u32[]{:S(2)}, u32[]{:S(2)}) %collective-permute-start.2) | collective-permute-done | bytes 524320 | tf_op jit(solution)/shard_map/ppermute | solution.py:326
  55.2 3.0 %collective-permute-done.3.r1 = bf16[2,256,512]{2,1,0:T(8,128)(2,1)S(1)} collective-permute-done((bf16[2,256,512]{2,1,0:T(8,128)(2,1)}, bf16[2,256,512]{2,1,0:T(8,128)(2,1)S(1)}, u32[]{:S(2)}, u32[]{:S(2)}) %collective-permute-start.3) | collective-permute-done | bytes 524320 | tf_op jit(solution)/shard_map/ppermute | solution.py:326
  58.2 0.0 copy-done.5
  58.2 0.0 copy-start.2
  58.2 1.2 %copy-done.2 = bf16[2,2,256,512]{3,2,1,0:T(8,128)(2,1)S(1)} copy-done((bf16[2,2,256,512]{3,2,1,0:T(8,128)(2,1)S(1)}, bf16[2,2,256,512]{3,2,1,0:T(8,128)(2,1)}, u32[]{:S(2)}) %copy-start.2) | copy-done | bytes 1048600
  59.4 0.8 shard_map.78
  60.2 1.9 %collective-permute-start.4 = (bf16[256,512]{1,0:T(8,128)(2,1)S(1)}, bf16[256,512]{1,0:T(8,128)(2,1)S(1)}, u32[]{:S(2)}, u32[]{:S(2)}) collective-permute-start(bf16[256,512]{1,0:T(8,128)(2,1)S(1)} %get-tuple-element.26), channel_id=1, source_target_pairs={{0,32},{1,97},{32,0},{33,65},{64,96},{65,33},{96,64},{97,1},{128,1... | collective-permute-start | bytes 786440 | tf_op jit(solution)/shard_map/ppermute | solution.py:326
  62.1 2.5 %collective-permute-start.5 = (bf16[256,512]{1,0:T(8,128)(2,1)S(1)}, bf16[256,512]{1,0:T(8,128)(2,1)S(1)}, u32[]{:S(2)}, u32[]{:S(2)}) collective-permute-start(bf16[256,512]{1,0:T(8,128)(2,1)S(1)} %get-tuple-element.27), channel_id=1, source_target_pairs={{0,128},{1,385},{32,160},{33,417},{64,192},{65,449},{96,224},{97,4... | collective-permute-start | bytes 786440 | tf_op jit(solution)/shard_map/ppermute | solution.py:326
  64.6 3.8 %collective-permute-done.4.r0 = bf16[256,512]{1,0:T(8,128)(2,1)S(1)} collective-permute-done((bf16[256,512]{1,0:T(8,128)(2,1)S(1)}, bf16[256,512]{1,0:T(8,128)(2,1)S(1)}, u32[]{:S(2)}, u32[]{:S(2)}) %collective-permute-start.4) | collective-permute-done | bytes 262176 | tf_op jit(solution)/shard_map/ppermute | solution.py:326
  68.5 1.9 %collective-permute-done.5.r1 = bf16[256,512]{1,0:T(8,128)(2,1)S(1)} collective-permute-done((bf16[256,512]{1,0:T(8,128)(2,1)S(1)}, bf16[256,512]{1,0:T(8,128)(2,1)S(1)}, u32[]{:S(2)}, u32[]{:S(2)}) %collective-permute-start.5) | collective-permute-done | bytes 262176 | tf_op jit(solution)/shard_map/ppermute | solution.py:326
  70.4 0.1 shard_map.79
  70.5 4.0 %collective-permute-start.6 = (bf16[256,512]{1,0:T(8,128)(2,1)S(1)}, bf16[256,512]{1,0:T(8,128)(2,1)S(1)}, u32[]{:S(2)}, u32[]{:S(2)}) collective-permute-start(bf16[256,512]{1,0:T(8,128)(2,1)S(1)} %get-tuple-element.28.a), channel_id=1, source_target_pairs={{0,96},{1,33},{32,64},{33,1},{64,32},{65,97},{96,0},{97,65},{128,2... | collective-permute-start | bytes 786440 | tf_op jit(solution)/shard_map/ppermute | solution.py:326
  74.5 3.1 %collective-permute-start.7 = (bf16[256,512]{1,0:T(8,128)(2,1)S(1)}, bf16[256,512]{1,0:T(8,128)(2,1)S(1)}, u32[]{:S(2)}, u32[]{:S(2)}) collective-permute-start(bf16[256,512]{1,0:T(8,128)(2,1)S(1)} %get-tuple-element.29.b), channel_id=1, source_target_pairs={{0,384},{1,129},{32,416},{33,161},{64,448},{65,193},{96,480},{97,2... | collective-permute-start | bytes 786440 | tf_op jit(solution)/shard_map/ppermute | solution.py:326
  77.6 0.0 copy-done.8
  77.6 0.2 select_reduce_fusion.table
  77.8 0.0 all-to-all-done.1.source
  77.8 1.4 %shard_map.76 = bf16[32,72,128]{2,1,0:T(8,128)(2,1)} custom-call(s32[32]{0:T(128)S(1)} %select_reduce_fusion.table, bf16[32,72,128]{2,1,0:T(8,128)(2,1)S(1)} %all-to-all-done.1.source), custom_call_target="tpu_custom_call" | custom-call | bytes 4194304 | tf_op jit(solution)/shard_map/pallas_call | solution.py:184
  79.2 4.9 %all-to-all-start.2 = ((bf16[16,2,72,128]{3,2,1,0:T(8,128)(2,1)}), bf16[16,2,72,128]{3,2,1,0:T(8,128)(2,1)S(1)}, u32[]{:S(2)}, u32[]{:S(2)}) async-start(bf16[16,2,72,128]{3,2,1,0:T(8,128)(2,1)} %bitcast.5), calls=%async_computation.2 | async-start | bytes 1179648 | tf_op jit(solution)/shard_map/all_to_all | solution.py:430
  84.1 0.0 collective-permute-done.6.r0
  84.1 0.0 collective-permute-done.7.r1
  84.1 0.8 shard_map.80
  84.9 9.7 %all-to-all-done.2.chunks = bf16[16,2,72,128]{3,2,1,0:T(8,128)(2,1)S(1)} async-done(((bf16[16,2,72,128]{3,2,1,0:T(8,128)(2,1)}), bf16[16,2,72,128]{3,2,1,0:T(8,128)(2,1)S(1)}, u32[]{:S(2)}, u32[]{:S(2)}) %all-to-all-start.2) | async-done | bytes 589856 | tf_op jit(solution)/shard_map/all_to_all | solution.py:430
  94.6 3.1 %shard_map.81 = bf16[512,512]{1,0:T(8,128)(2,1)S(1)} custom-call(bf16[16,2,72,128]{3,2,1,0:T(8,128)(2,1)S(1)} %all-to-all-done.2.chunks, bf16[512,512]{1,0:T(8,128)(2,1)S(1)} %get-tuple-element.30.gradient, bf16[512,512]{1,0:T(8,128)(2,1)S(1)} %get-tuple-element.31.left, bf16[512,512]{1,0:T(8,128)(2,1)S(1)} %get-tuple-element.32.right), custom_call_target="tpu_custom_call" | custom-call | flops 2147483648 | bytes 6291456 | tf_op jit(solution)/shard_map/pallas_call | solution.py:433
  97.6 13.3 %all_to_all.20.source = bf16[16,32,512]{2,1,0:T(8,128)(2,1)S(1)} all-to-all(bf16[16,32,512]{2,1,0:T(8,128)(2,1)S(1)} %bitcast.12), channel_id=1, replica_groups=mesh['dp'=16,'z'=16,'core'=2] {'dp'}, dimensions={0} | all-to-all | bytes 1048576 | tf_op jit(solution)/shard_map/all_to_all | solution.py:446
  111.0 0.7 shard_map.82
  (5 shorter events, 0.0 us)
Async XLA Ops:
  0.0 19.5 %copy-start.7 = (s32[160,2]{0,1:T(2,128)S(1)}, s32[160,2]{0,1:T(2,128)}, u32[]{:S(2)}) copy-start(s32[160,2]{0,1:T(2,128)} %param.9) | copy-start | bytes 3844
  2.2 19.5 %all-to-all-start = ((bf16[16,2,72,128]{3,2,1,0:T(8,128)(2,1)}), bf16[16,2,72,128]{3,2,1,0:T(8,128)(2,1)S(1)}, u32[]{:S(2)}, u32[]{:S(2)}) async-start(bf16[16,2,72,128]{3,2,1,0:T(8,128)(2,1)} %shard_map.73), calls=%async_computation | async-start | bytes 1179648 | tf_op jit(solution)/shard_map/all_to_all | solution.py:422
  12.3 26.2 %collective-permute-start = (bf16[3,256,512]{2,1,0:T(8,128)(2,1)}, bf16[3,256,512]{2,1,0:T(8,128)(2,1)}, u32[]{:S(2)}, u32[]{:S(2)}) collective-permute-start(bf16[3,256,512]{2,1,0:T(8,128)(2,1)} %get-tuple-element.19), channel_id=1, source_target_pairs={{0,128},{1,385},{32,160},{33,417},{64,192},{65,449},{96,224},{97,4... | collective-permute-start | bytes 2359304 | tf_op jit(solution)/shard_map/ppermute | solution.py:326
  16.1 22.4 %collective-permute-start.1 = (bf16[3,256,512]{2,1,0:T(8,128)(2,1)}, bf16[3,256,512]{2,1,0:T(8,128)(2,1)}, u32[]{:S(2)}, u32[]{:S(2)}) collective-permute-start(bf16[3,256,512]{2,1,0:T(8,128)(2,1)} %get-tuple-element.20), channel_id=1, source_target_pairs={{0,32},{1,97},{32,0},{33,65},{64,96},{65,33},{96,64},{97,1},{128,1... | collective-permute-start | bytes 2359304 | tf_op jit(solution)/shard_map/ppermute | solution.py:326
  21.7 16.8 %copy-start = (bf16[1,5,512,512]{3,2,1,0:T(8,128)(2,1)S(1)}, bf16[1,5,512,512]{3,2,1,0:T(8,128)(2,1)}, u32[]{:S(2)}) copy-start(bf16[1,5,512,512]{3,2,1,0:T(8,128)(2,1)} %param.7) | copy-start | bytes 7864324
  21.7 16.8 %copy-start.4 = (s32[384]{0:T(512)S(1)}, s32[384]{0:T(512)}, u32[]{:S(2)}) copy-start(s32[384]{0:T(512)} %constant.50.clone.table.sent_table) | copy-start | bytes 4612
  21.7 16.8 %copy-start.6 = (s32[256]{0:T(256)S(1)}, s32[256]{0:T(256)}, u32[]{:S(2)}) copy-start(s32[256]{0:T(256)} %constant.51.clone.table) | copy-start | bytes 3076
  22.3 0.8 copy-start.3
  23.1 54.7 %all-to-all-start.1 = ((bf16[32,72,128]{2,1,0:T(8,128)(2,1)}), bf16[32,72,128]{2,1,0:T(8,128)(2,1)S(1)}, u32[]{:S(2)}, u32[]{:S(2)}) async-start(bf16[32,72,128]{2,1,0:T(8,128)(2,1)} %copy-done.3), calls=%async_computation.1 | async-start | bytes 1179648 | tf_op jit(solution)/shard_map/all_to_all | solution.py:427
  38.5 19.7 %copy-start.5 = (s32[128]{0:T(128)S(1)}, s32[128]{0:T(128)}, u32[]{:S(2)}) copy-start(s32[128]{0:T(128)} %constant.52.clone.table) | copy-start | bytes 1540
  41.6 1.0 copy-start.1
  42.5 35.0 %copy-start.8 = (s32[2,32]{1,0:T(2,128)S(1)}, s32[2,32]{1,0:T(2,128)}, u32[]{:S(2)}) copy-start(s32[2,32]{1,0:T(2,128)} %constant.53.clone) | copy-start | bytes 772
  42.5 12.6 %collective-permute-start.2 = (bf16[2,256,512]{2,1,0:T(8,128)(2,1)}, bf16[2,256,512]{2,1,0:T(8,128)(2,1)S(1)}, u32[]{:S(2)}, u32[]{:S(2)}) collective-permute-start(bf16[2,256,512]{2,1,0:T(8,128)(2,1)} %get-tuple-element.23), channel_id=1, source_target_pairs={{0,384},{1,129},{32,416},{33,161},{64,448},{65,193},{96,480},{97,2... | collective-permute-start | bytes 1572872 | tf_op jit(solution)/shard_map/ppermute | solution.py:326
  45.7 12.5 %collective-permute-start.3 = (bf16[2,256,512]{2,1,0:T(8,128)(2,1)}, bf16[2,256,512]{2,1,0:T(8,128)(2,1)S(1)}, u32[]{:S(2)}, u32[]{:S(2)}) collective-permute-start(bf16[2,256,512]{2,1,0:T(8,128)(2,1)} %get-tuple-element.24), channel_id=1, source_target_pairs={{0,96},{1,33},{32,64},{33,1},{64,32},{65,97},{96,0},{97,65},{128,2... | collective-permute-start | bytes 1572872 | tf_op jit(solution)/shard_map/ppermute | solution.py:326
  58.2 1.2 %copy-start.2 = (bf16[2,2,256,512]{3,2,1,0:T(8,128)(2,1)S(1)}, bf16[2,2,256,512]{3,2,1,0:T(8,128)(2,1)}, u32[]{:S(2)}) copy-start(bf16[2,2,256,512]{3,2,1,0:T(8,128)(2,1)} %copy-done.1) | copy-start | bytes 3145732
  60.2 8.3 %collective-permute-start.4 = (bf16[256,512]{1,0:T(8,128)(2,1)S(1)}, bf16[256,512]{1,0:T(8,128)(2,1)S(1)}, u32[]{:S(2)}, u32[]{:S(2)}) collective-permute-start(bf16[256,512]{1,0:T(8,128)(2,1)S(1)} %get-tuple-element.26), channel_id=1, source_target_pairs={{0,32},{1,97},{32,0},{33,65},{64,96},{65,33},{96,64},{97,1},{128,1... | collective-permute-start | bytes 786440 | tf_op jit(solution)/shard_map/ppermute | solution.py:326
  62.1 8.3 %collective-permute-start.5 = (bf16[256,512]{1,0:T(8,128)(2,1)S(1)}, bf16[256,512]{1,0:T(8,128)(2,1)S(1)}, u32[]{:S(2)}, u32[]{:S(2)}) collective-permute-start(bf16[256,512]{1,0:T(8,128)(2,1)S(1)} %get-tuple-element.27), channel_id=1, source_target_pairs={{0,128},{1,385},{32,160},{33,417},{64,192},{65,449},{96,224},{97,4... | collective-permute-start | bytes 786440 | tf_op jit(solution)/shard_map/ppermute | solution.py:326
  70.5 13.6 %collective-permute-start.6 = (bf16[256,512]{1,0:T(8,128)(2,1)S(1)}, bf16[256,512]{1,0:T(8,128)(2,1)S(1)}, u32[]{:S(2)}, u32[]{:S(2)}) collective-permute-start(bf16[256,512]{1,0:T(8,128)(2,1)S(1)} %get-tuple-element.28.a), channel_id=1, source_target_pairs={{0,96},{1,33},{32,64},{33,1},{64,32},{65,97},{96,0},{97,65},{128,2... | collective-permute-start | bytes 786440 | tf_op jit(solution)/shard_map/ppermute | solution.py:326
  74.5 9.6 %collective-permute-start.7 = (bf16[256,512]{1,0:T(8,128)(2,1)S(1)}, bf16[256,512]{1,0:T(8,128)(2,1)S(1)}, u32[]{:S(2)}, u32[]{:S(2)}) collective-permute-start(bf16[256,512]{1,0:T(8,128)(2,1)S(1)} %get-tuple-element.29.b), channel_id=1, source_target_pairs={{0,384},{1,129},{32,416},{33,161},{64,448},{65,193},{96,480},{97,2... | collective-permute-start | bytes 786440 | tf_op jit(solution)/shard_map/ppermute | solution.py:326
  79.2 15.4 %all-to-all-start.2 = ((bf16[16,2,72,128]{3,2,1,0:T(8,128)(2,1)}), bf16[16,2,72,128]{3,2,1,0:T(8,128)(2,1)S(1)}, u32[]{:S(2)}, u32[]{:S(2)}) async-start(bf16[16,2,72,128]{3,2,1,0:T(8,128)(2,1)} %bitcast.5), calls=%async_computation.2 | async-start | bytes 1179648 | tf_op jit(solution)/shard_map/all_to_all | solution.py:430

commit v7 on v5

--- a/solution.py
+++ b/solution.py
@@ -24,6 +24,8 @@
 
 long_flops = 10**11
 
+most_mib = 60
+
 VMEM = pl.BlockSpec(memory_space=pltpu.VMEM)
 SMEM = pl.BlockSpec(memory_space=pltpu.SMEM)
 HBM = pl.BlockSpec(memory_space=pltpu.HBM)
@@ -38,7 +40,7 @@
 
 
 def order(portion, core):
-    first, later = (even, odd) if core == 0 else (odd, even)
+    first, later = (even, odd) if core == portion else (odd, even)
     one, two = portion, 1 - portion
     return ((one, first), (one, later), (two, first), (two, later))
 
@@ -114,39 +116,36 @@
     return [table[base + k] for k in range(width)]
 
 
-def choose_kernel(table, source, s0, s1, kept):
+def choose_kernel(table, source, s0, s1, k0, k1):
     table = my_row(table)
     height = s0.shape[1]
-    for h, sent in enumerate((s0, s1)):
+    for h, (sent, kept) in enumerate(((s0, k0), (s1, k1))):
         rows = slice(h * height, (h + 1) * height)
         for u in range(3):
             sent[u] = source[table[6 * h + u], rows, :]
-            kept[h, u] = source[table[6 * h + 3 + u], rows, :]
-
-
-def first_sum_kernel(table, kept, r0, r1, s0, s1, next_kept):
+            kept[u] = source[table[6 * h + 3 + u], rows, :]
+
+
+def first_sum_kernel(portion, table, kept, got, sent, next_kept):
     table = my_row(table)
-    for h, (got, sent) in enumerate(((r0, s0), (r1, s1))):
-        for u in range(4):
-            place = table[4 * h + u]
-            total = add_rounded(kept[h, place], got[place])
-            if u < 2:
-                sent[u] = total
-            else:
-                next_kept[h, u - 2] = total
-
-
-def second_sum_kernel(table, kept, r0, r1, s0, s1, next_kept):
+    for u in range(4):
+        place = table[4 * portion + u]
+        total = add_rounded(kept[place], got[place])
+        if u < 2:
+            sent[u] = total
+        else:
+            next_kept[u - 2] = total
+
+
+def second_sum_kernel(portion, table, kept, got, sent, next_kept):
     table = my_row(table)
-    for h, (got, sent) in enumerate(((r0, s0), (r1, s1))):
-        go, stay = table[2 * h], table[2 * h + 1]
-        sent[...] = add_rounded(kept[h, go], got[go])
-        next_kept[h] = add_rounded(kept[h, stay], got[stay])
-
-
-def third_sum_kernel(kept, r0, r1, s0, s1):
-    s0[...] = add_rounded(kept[0], r0[...])
-    s1[...] = add_rounded(kept[1], r1[...])
+    go, stay = table[2 * portion], table[2 * portion + 1]
+    sent[...] = add_rounded(kept[go], got[go])
+    next_kept[...] = add_rounded(kept[stay], got[stay])
+
+
+def third_sum_kernel(kept, got, sent):
+    sent[...] = add_rounded(kept[...], got[...])
 
 
 def gram_kernel(a, b, r0, r1, out, left, right):
@@ -161,15 +160,9 @@
         gram[...] = product.astype(jnp.bfloat16)
 
 
-def pick_kernel(table, source, out, sems):
-    copies = [
-        pltpu.make_async_copy(source.at[table[i]], out.at[i], sems.at[i])
-        for i in range(out.shape[0])
-    ]
-    for copy in copies:
-        copy.start()
-    for copy in copies:
-        copy.wait()
+def pick_kernel(table, source, out):
+    for i in range(out.shape[0]):
+        out[i] = source[table[i]]
 
 
 def pick(table, source, flops=0):
@@ -177,10 +170,9 @@
         pick_kernel,
         out_shape=jax.ShapeDtypeStruct(table.shape + source.shape[1:], source.dtype),
         in_specs=[SMEM, VMEM],
-        out_specs=HBM,
-        scratch_shapes=[pltpu.SemaphoreType.DMA(table.shape)],
+        out_specs=VMEM,
         compiler_params=params(4),
-        cost_estimate=cost(flops, 1024 * 1024),
+        cost_estimate=cost(flops, 4 * 1024 * 1024),
     )(table, source)
 
 
@@ -314,59 +306,65 @@
     return pl.CostEstimate(flops=flops, bytes_accessed=moved, transcendentals=0)
 
 
-def exchange(arrays, step):
-    return [
-        lax.ppermute(a, ("dp", "core"), pairs(portion, step)) for portion, a in enumerate(arrays)
-    ]
+def exchange(array, portion, step):
+    return lax.ppermute(array, ("dp", "core"), pairs(portion, step))
 
 
 def first_sent(grad, tables):
     n, order_n = grad.shape[1], grad.shape[2]
     return pl.pallas_call(
         choose_kernel,
-        out_shape=[shape(3, n // 2, order_n)] * 2 + [shape(2, 3, n // 2, order_n)],
+        out_shape=[shape(3, n // 2, order_n)] * 4,
         in_specs=[SMEM, VMEM],
-        out_specs=[VMEM] * 3,
-        compiler_params=params(16),
+        out_specs=[VMEM] * 4,
+        compiler_params=params(most_mib),
         cost_estimate=cost(0, 12 * n * order_n),
     )(tables[0], grad)
 
 
 def gradient_sum(kept, got, tables):
-    half, order_n = kept.shape[2], kept.shape[3]
+    half, order_n = kept[0].shape[1], kept[0].shape[2]
     n = 2 * half
-    *sent, kept = pl.pallas_call(
-        first_sum_kernel,
-        out_shape=[shape(2, half, order_n)] * 2 + [shape(2, 2, half, order_n)],
-        in_specs=[SMEM] + [VMEM] * 3,
-        out_specs=[VMEM] * 3,
-        compiler_params=params(16),
-        cost_estimate=cost(long_flops, 4 * 1024 * 1024),
-    )(tables[1], kept, *got)
-    *sent, kept = pl.pallas_call(
-        second_sum_kernel,
-        out_shape=[shape(half, order_n)] * 2 + [shape(2, half, order_n)],
-        in_specs=[SMEM] + [VMEM] * 3,
-        out_specs=[VMEM] * 3,
-        compiler_params=params(12),
-        cost_estimate=cost(0, 4 * 1024 * 1024),
-    )(tables[2], kept, *exchange(sent, 1))
-    sent = pl.pallas_call(
-        third_sum_kernel,
-        out_shape=[shape(half, order_n)] * 2,
-        in_specs=[VMEM] * 3,
-        out_specs=[VMEM] * 2,
-        compiler_params=params(8),
-        cost_estimate=cost(0, 4 * 1024 * 1024),
-    )(kept, *exchange(sent, 2))
+    small = 1024 * 1024
+    sent, kept, got = [None, None], list(kept), list(got)
+    for h in range(2):
+        if h == 1:
+            got[1], _ = lax.optimization_barrier((got[1], sent[0]))
+        sent[h], kept[h] = pl.pallas_call(
+            functools.partial(first_sum_kernel, h),
+            out_shape=[shape(2, half, order_n)] * 2,
+            in_specs=[SMEM, VMEM, VMEM],
+            out_specs=[VMEM] * 2,
+            compiler_params=params(8),
+            cost_estimate=cost(long_flops if h == 0 else 0, 2 * small),
+        )(tables[1], kept[h], got[h])
+    for h in range(2):
+        sent[h], kept[h] = pl.pallas_call(
+            functools.partial(second_sum_kernel, h),
+            out_shape=[shape(half, order_n)] * 2,
+            in_specs=[SMEM, VMEM, VMEM],
+            out_specs=[VMEM] * 2,
+            compiler_params=params(8),
+            cost_estimate=cost(0, small),
+        )(tables[2], kept[h], exchange(sent[h], h, 1))
+    for h in range(2):
+        sent[h] = pl.pallas_call(
+            third_sum_kernel,
+            out_shape=shape(half, order_n),
+            in_specs=[VMEM] * 2,
+            out_specs=VMEM,
+            compiler_params=params(8),
+            cost_estimate=cost(0, small),
+        )(kept[h], exchange(sent[h], h, 2))
+    got = [exchange(sent[h], h, 3) for h in range(2)]
     return pl.pallas_call(
         gram_kernel,
         out_shape=[shape(n, order_n)] * 3,
         in_specs=[VMEM] * 4,
         out_specs=[VMEM] * 3,
         compiler_params=params(16),
-        cost_estimate=cost(long_flops // 2, 4 * 1024 * 1024),
-    )(*sent, *exchange(sent, 3))
+        cost_estimate=cost(long_flops // 2, 4 * small),
+    )(*sent, *got)
 
 
 def body(grad_partial, statistics, owner_table):
@@ -405,16 +403,16 @@
             pltpu.SemaphoreType.DMA((3 * slots,)),
             pltpu.SemaphoreType.DMA((slots,)),
         ],
-        compiler_params=params(12),
+        compiler_params=params(most_mib),
         cost_estimate=cost(0, 3 * 1024 * 1024),
     )(statistics[0, 0])
     spread = lax.all_to_all(packed, "dp", split_axis=0, concat_axis=0, tiled=True)
-    *sent, kept = first_sent(grad_partial[0], tables)
+    *sent, k0, k1 = first_sent(grad_partial[0], tables)
     spread, _ = lax.optimization_barrier((spread, sent))
-    got = exchange(sent, 0)
+    got = [exchange(a, portion, 0) for portion, a in enumerate(sent)]
     lanes = pick(lane_from, spread.reshape(slots * n_dp, packed_rows, 128), long_flops // 3)
     lanes = lax.all_to_all(lanes, ("z", "core"), split_axis=0, concat_axis=0, tiled=True)
-    gradient, left, right = gradient_sum(kept, got, tables)
+    gradient, left, right = gradient_sum((k0, k1), got, tables)
     lanes = pick(item_from, lanes).reshape(n_dp, 2, packed_rows, 128)
     chunks = lax.all_to_all(lanes, "dp", split_axis=0, concat_axis=0, tiled=True)
 

time: 114 us -> 111 us (0.974)
  the two profiles are of different devices: /device:TPU:32 before, /device:TPU:1 now
where the time goes in v7:
time: 111 us; the launch traced here: 110 us
  starting transfers between devices  51.9 us (47%)
  waiting for transfers between devices  22.5 us (20%)
  Pallas kernels  17 us (15%)
  blocking collectives  12.8 us (12%)
  local copies, waits for them, and re-layouts  4.78 us (4%)
    ppermute x8, starting transfers between devices, exchange(): return lax.ppermute(array, ('dp', 'core'), pairs(portion, step))  23.2 us
    all_to_all x1, starting transfers between devices, body(): lax.all_to_all(lanes, ('z', 'core'), split_axis=0, concat_axis=0, tiled=T...  17 us
    all_to_all x1, blocking collectives, body(): rows = lax.all_to_all(rows, 'dp', split_axis=0, concat_axis=0, tiled=True)  12.8 us
    all_to_all x1, waiting for transfers between devices, body(): lax.all_to_all(lanes, 'dp', split_axis=0, concat_axis=0, tiled=True)  10.1 us
    ppermute x8, waiting for transfers between devices, exchange(): return lax.ppermute(array, ('dp', 'core'), pairs(portion, step))  8.16 us
    all_to_all x1, starting transfers between devices, body(): lax.all_to_all(packed, 'dp', split_axis=0, concat_axis=0, tiled=True)  7.6 us
    all_to_all x1, waiting for transfers between devices, body(): lax.all_to_all(lanes, ('z', 'core'), split_axis=0, concat_axis=0, tiled=T...  4.21 us
    all_to_all x1, starting transfers between devices, body(): lax.all_to_all(lanes, 'dp', split_axis=0, concat_axis=0, tiled=True)  4.07 us
  transfers between devices with their start and end apart: 11, of which 6 were waited for; matrix products, arithmetic and copies ran while one was open for 2% of the time, Pallas kernels for 10%

profile of v7, /device:TPU:1, one launch (start us, length us, event | category | flops | bytes accessed | tf_op | source)
XLA Modules:
  0.0 109.9 jit_solution(4296811189005547907)
XLA Ops:
  0.0 0.0 copy-start.7
  0.0 2.2 %shard_map.73 = bf16[16,2,72,128]{3,2,1,0:T(8,128)(2,1)} custom-call(f32[2,512,512]{2,1,0:T(8,128)} %bitcast.12), custom_call_target="tpu_custom_call" | custom-call | bytes 3145728 | tf_op jit(solution)/shard_map/pallas_call | solution.py:395
  2.2 7.6 %all-to-all-start = ((bf16[16,2,72,128]{3,2,1,0:T(8,128)(2,1)}), bf16[16,2,72,128]{3,2,1,0:T(8,128)(2,1)S(1)}, u32[]{:S(2)}, u32[]{:S(2)}) async-start(bf16[16,2,72,128]{3,2,1,0:T(8,128)(2,1)} %shard_map.73), calls=%async_computation | async-start | bytes 1179648 | tf_op jit(solution)/shard_map/all_to_all | solution.py:409
  9.8 3.6 %shard_map.74 = (bf16[3,256,512]{2,1,0:T(8,128)(2,1)}, bf16[3,256,512]{2,1,0:T(8,128)(2,1)}, bf16[3,256,512]{2,1,0:T(8,128)(2,1)}, bf16[3,256,512]{2,1,0:T(8,128)(2,1)}) custom-call(s32[384]{0:T(512)} %constant.50.clone.table, bf16[5,512,512]{2,1,0:T(8,128)(2,1)} %bitcast.11), custom_call_target="tpu_custom_call" | custom-call | bytes 3145728 | tf_op jit(solution)/shard_map/pallas_call | solution.py:315
  13.4 4.5 %collective-permute-start = (bf16[3,256,512]{2,1,0:T(8,128)(2,1)}, bf16[3,256,512]{2,1,0:T(8,128)(2,1)S(1)}, u32[]{:S(2)}, u32[]{:S(2)}) collective-permute-start(bf16[3,256,512]{2,1,0:T(8,128)(2,1)} %get-tuple-element.22), channel_id=1, source_target_pairs={{0,128},{1,385},{32,160},{33,417},{64,192},{65,449},{96,224},{97,4... | collective-permute-start | bytes 2359304 | tf_op jit(solution)/shard_map/ppermute | solution.py:310
  17.9 3.1 %collective-permute-start.3 = (bf16[3,256,512]{2,1,0:T(8,128)(2,1)}, bf16[3,256,512]{2,1,0:T(8,128)(2,1)S(1)}, u32[]{:S(2)}, u32[]{:S(2)}) collective-permute-start(bf16[3,256,512]{2,1,0:T(8,128)(2,1)} %get-tuple-element.23), channel_id=1, source_target_pairs={{0,96},{1,33},{32,64},{33,1},{64,32},{65,97},{96,0},{97,65},{128,2... | collective-permute-start | bytes 2359304 | tf_op jit(solution)/shard_map/ppermute | solution.py:310
  21.0 0.0 copy-done.7
  21.0 0.1 copy.17
  21.1 0.0 copy-start.6
  21.2 0.1 copy.22
  21.3 0.1 eq.45
  21.5 0.2 convert_reduce_fusion
  21.7 0.1 reduce_sum.38
  21.8 0.2 fusion.5
  22.0 0.1 reduce_sum.40
  22.1 0.1 reduce_sum.41.table
  22.2 0.0 all-to-all-done
  22.3 0.0 copy-start.2
  22.3 1.4 %shard_map.75 = bf16[32,72,128]{2,1,0:T(8,128)(2,1)} custom-call(s32[32]{0:T(128)S(1)} %reduce_sum.41.table, bf16[32,72,128]{2,1,0:T(8,128)(2,1)S(1)} %bitcast.9), custom_call_target="tpu_custom_call" | custom-call | flops 33333334016 | bytes 4194304 | tf_op jit(solution)/shard_map/pallas_call | solution.py:169
  23.7 0.0 copy-done.6
  23.7 17.0 %all-to-all-start.1 = ((bf16[32,72,128]{2,1,0:T(8,128)(2,1)}), bf16[32,72,128]{2,1,0:T(8,128)(2,1)S(1)}, u32[]{:S(2)}, u32[]{:S(2)}) async-start(bf16[32,72,128]{2,1,0:T(8,128)(2,1)} %shard_map.75), calls=%async_computation.1 | async-start | bytes 1179648 | tf_op jit(solution)/shard_map/all_to_all | solution.py:414
  40.7 0.0 collective-permute-done.got
  40.7 0.0 copy-start.4
  40.7 0.9 copy-done.4
  41.6 0.0 copy-done.2
  41.6 0.0 copy-start.3
  41.6 1.1 %copy-done.3 = bf16[3,256,512]{2,1,0:T(8,128)(2,1)S(1)} copy-done((bf16[3,256,512]{2,1,0:T(8,128)(2,1)S(1)}, bf16[3,256,512]{2,1,0:T(8,128)(2,1)}, u32[]{:S(2)}) %copy-start.3) | copy-done | bytes 786456
  42.7 0.0 copy-start.5
  42.7 1.1 %copy-done.5 = bf16[3,256,512]{2,1,0:T(8,128)(2,1)S(1)} copy-done((bf16[3,256,512]{2,1,0:T(8,128)(2,1)S(1)}, bf16[3,256,512]{2,1,0:T(8,128)(2,1)}, u32[]{:S(2)}) %copy-start.5) | copy-done | bytes 786456
  43.9 0.0 copy-start
  43.9 0.0 copy-start.1
  43.9 0.8 shard_map.77
  44.7 2.2 %collective-permute-start.1 = (bf16[2,256,512]{2,1,0:T(8,128)(2,1)S(1)}, bf16[2,256,512]{2,1,0:T(8,128)(2,1)S(1)}, u32[]{:S(2)}, u32[]{:S(2)}) collective-permute-start(bf16[2,256,512]{2,1,0:T(8,128)(2,1)S(1)} %get-tuple-element.27), channel_id=1, source_target_pairs={{0,384},{1,129},{32,416},{33,161},{64,448},{65,193},{96,480},{97,2... | collective-permute-start | bytes 1572872 | tf_op jit(solution)/shard_map/ppermute | solution.py:310
  46.9 0.0 collective-permute-done.3.got
  46.9 0.0 copy-done
  46.9 0.0 copy-start.8
  46.9 1.5 %shard_map.80 = (bf16[2,256,512]{2,1,0:T(8,128)(2,1)}, bf16[2,256,512]{2,1,0:T(8,128)(2,1)S(1)}) custom-call(s32[256]{0:T(256)S(1)} %copy-done.2, bf16[3,256,512]{2,1,0:T(8,128)(2,1)S(1)} %copy-done, bf16[3,256,512]{2,1,0:T(8,128)(2,1)S(1)} %collective-permute-done.3.got), custom_call_target="tpu_custom_call" | custom-call | bytes 2097152 | tf_op jit(solution)/shard_map/pallas_call | solution.py:333
  48.4 1.9 %collective-permute-start.4 = (bf16[2,256,512]{2,1,0:T(8,128)(2,1)}, bf16[2,256,512]{2,1,0:T(8,128)(2,1)S(1)}, u32[]{:S(2)}, u32[]{:S(2)}) collective-permute-start(bf16[2,256,512]{2,1,0:T(8,128)(2,1)} %get-tuple-element.33), channel_id=1, source_target_pairs={{0,32},{1,97},{32,0},{33,65},{64,96},{65,33},{96,64},{97,1},{128,1... | collective-permute-start | bytes 1572872 | tf_op jit(solution)/shard_map/ppermute | solution.py:310
  50.4 1.0 reshape.22
  51.3 3.6 %collective-permute-done.1.got = bf16[2,256,512]{2,1,0:T(8,128)(2,1)S(1)} collective-permute-done((bf16[2,256,512]{2,1,0:T(8,128)(2,1)S(1)}, bf16[2,256,512]{2,1,0:T(8,128)(2,1)S(1)}, u32[]{:S(2)}, u32[]{:S(2)}) %collective-permute-start.1) | collective-permute-done | bytes 524320 | tf_op jit(solution)/shard_map/ppermute | solution.py:310
  54.9 0.0 copy-done.1
  54.9 0.7 shard_map.78
  55.6 2.2 %collective-permute-start.2 = (bf16[256,512]{1,0:T(8,128)(2,1)S(1)}, bf16[256,512]{1,0:T(8,128)(2,1)S(1)}, u32[]{:S(2)}, u32[]{:S(2)}) collective-permute-start(bf16[256,512]{1,0:T(8,128)(2,1)S(1)} %get-tuple-element.29), channel_id=1, source_target_pairs={{0,32},{1,97},{32,0},{33,65},{64,96},{65,33},{96,64},{97,1},{128,1... | collective-permute-start | bytes 786440 | tf_op jit(solution)/shard_map/ppermute | solution.py:310
  57.8 2.3 %collective-permute-done.4.got = bf16[2,256,512]{2,1,0:T(8,128)(2,1)S(1)} collective-permute-done((bf16[2,256,512]{2,1,0:T(8,128)(2,1)}, bf16[2,256,512]{2,1,0:T(8,128)(2,1)S(1)}, u32[]{:S(2)}, u32[]{:S(2)}) %collective-permute-start.4) | collective-permute-done | bytes 524320 | tf_op jit(solution)/shard_map/ppermute | solution.py:310
  60.1 0.7 shard_map.81
  60.8 3.1 %collective-permute-start.5 = (bf16[256,512]{1,0:T(8,128)(2,1)S(1)}, bf16[256,512]{1,0:T(8,128)(2,1)S(1)}, u32[]{:S(2)}, u32[]{:S(2)}) collective-permute-start(bf16[256,512]{1,0:T(8,128)(2,1)S(1)} %get-tuple-element.35), channel_id=1, source_target_pairs={{0,384},{1,129},{32,416},{33,161},{64,448},{65,193},{96,480},{97,2... | collective-permute-start | bytes 786440 | tf_op jit(solution)/shard_map/ppermute | solution.py:310
  63.9 0.3 collective-permute-done.2.got
  64.2 0.1 shard_map.79.a
  64.3 1.9 %collective-permute-start.6 = (bf16[256,512]{1,0:T(8,128)(2,1)S(1)}, bf16[256,512]{1,0:T(8,128)(2,1)S(1)}, u32[]{:S(2)}, u32[]{:S(2)}) collective-permute-start(bf16[256,512]{1,0:T(8,128)(2,1)S(1)} %shard_map.79.a), channel_id=1, source_target_pairs={{0,96},{1,33},{32,64},{33,1},{64,32},{65,97},{96,0},{97,65},{128,2... | collective-permute-start | bytes 786440 | tf_op jit(solution)/shard_map/ppermute | solution.py:310
  66.2 2.0 %collective-permute-done.5.got = bf16[256,512]{1,0:T(8,128)(2,1)S(1)} collective-permute-done((bf16[256,512]{1,0:T(8,128)(2,1)S(1)}, bf16[256,512]{1,0:T(8,128)(2,1)S(1)}, u32[]{:S(2)}, u32[]{:S(2)}) %collective-permute-start.5) | collective-permute-done | bytes 262176 | tf_op jit(solution)/shard_map/ppermute | solution.py:310
  68.2 0.1 shard_map.82.b
  68.2 4.3 %collective-permute-start.7 = (bf16[256,512]{1,0:T(8,128)(2,1)S(1)}, bf16[256,512]{1,0:T(8,128)(2,1)S(1)}, u32[]{:S(2)}, u32[]{:S(2)}) collective-permute-start(bf16[256,512]{1,0:T(8,128)(2,1)S(1)} %shard_map.82.b), channel_id=1, source_target_pairs={{0,128},{1,385},{32,160},{33,417},{64,192},{65,449},{96,224},{97,4... | collective-permute-start | bytes 786440 | tf_op jit(solution)/shard_map/ppermute | solution.py:310
  72.6 0.0 copy-done.8
  72.6 0.2 select_reduce_fusion.table
  72.8 4.2 %all-to-all-done.1.source = bf16[32,72,128]{2,1,0:T(8,128)(2,1)S(1)} async-done(((bf16[32,72,128]{2,1,0:T(8,128)(2,1)}), bf16[32,72,128]{2,1,0:T(8,128)(2,1)S(1)}, u32[]{:S(2)}, u32[]{:S(2)}) %all-to-all-start.1) | async-done | bytes 589856 | tf_op jit(solution)/shard_map/all_to_all | solution.py:414
  77.0 1.4 %shard_map.76 = bf16[32,72,128]{2,1,0:T(8,128)(2,1)} custom-call(s32[32]{0:T(128)S(1)} %select_reduce_fusion.table, bf16[32,72,128]{2,1,0:T(8,128)(2,1)S(1)} %all-to-all-done.1.source), custom_call_target="tpu_custom_call" | custom-call | bytes 4194304 | tf_op jit(solution)/shard_map/pallas_call | solution.py:169
  78.4 4.1 %all-to-all-start.2 = ((bf16[16,2,72,128]{3,2,1,0:T(8,128)(2,1)}), bf16[16,2,72,128]{3,2,1,0:T(8,128)(2,1)S(1)}, u32[]{:S(2)}, u32[]{:S(2)}) async-start(bf16[16,2,72,128]{3,2,1,0:T(8,128)(2,1)} %bitcast.5), calls=%async_computation.2 | async-start | bytes 1179648 | tf_op jit(solution)/shard_map/all_to_all | solution.py:417
  82.5 0.0 collective-permute-done.6.r0
  82.5 0.0 collective-permute-done.7.r1
  82.5 0.8 shard_map.83
  83.3 10.1 %all-to-all-done.2.chunks = bf16[16,2,72,128]{3,2,1,0:T(8,128)(2,1)S(1)} async-done(((bf16[16,2,72,128]{3,2,1,0:T(8,128)(2,1)}), bf16[16,2,72,128]{3,2,1,0:T(8,128)(2,1)S(1)}, u32[]{:S(2)}, u32[]{:S(2)}) %all-to-all-start.2) | async-done | bytes 589856 | tf_op jit(solution)/shard_map/all_to_all | solution.py:417
  93.4 3.1 %shard_map.84 = bf16[512,512]{1,0:T(8,128)(2,1)S(1)} custom-call(bf16[16,2,72,128]{3,2,1,0:T(8,128)(2,1)S(1)} %all-to-all-done.2.chunks, bf16[512,512]{1,0:T(8,128)(2,1)S(1)} %get-tuple-element.36.gradient, bf16[512,512]{1,0:T(8,128)(2,1)S(1)} %get-tuple-element.37.left, bf16[512,512]{1,0:T(8,128)(2,1)S(1)} %get-tuple-element.38.right), custom_call_target="tpu_custom_call" | custom-call | flops 2147483648 | bytes 6291456 | tf_op jit(solution)/shard_map/pallas_call | solution.py:420
  96.5 12.8 %all_to_all.20.source = bf16[16,32,512]{2,1,0:T(8,128)(2,1)S(1)} all-to-all(bf16[16,32,512]{2,1,0:T(8,128)(2,1)S(1)} %bitcast.10), channel_id=1, replica_groups=mesh['dp'=16,'z'=16,'core'=2] {'dp'}, dimensions={0} | all-to-all | bytes 1048576 | tf_op jit(solution)/shard_map/all_to_all | solution.py:433
  109.2 0.7 shard_map.85
  (5 shorter events, 0.0 us)
Async XLA Ops:
  0.0 21.0 %copy-start.7 = (s32[160,2]{0,1:T(2,128)S(1)}, s32[160,2]{0,1:T(2,128)}, u32[]{:S(2)}) copy-start(s32[160,2]{0,1:T(2,128)} %param.9) | copy-start | bytes 3844
  2.2 20.1 %all-to-all-start = ((bf16[16,2,72,128]{3,2,1,0:T(8,128)(2,1)}), bf16[16,2,72,128]{3,2,1,0:T(8,128)(2,1)S(1)}, u32[]{:S(2)}, u32[]{:S(2)}) async-start(bf16[16,2,72,128]{3,2,1,0:T(8,128)(2,1)} %shard_map.73), calls=%async_computation | async-start | bytes 1179648 | tf_op jit(solution)/shard_map/all_to_all | solution.py:409
  13.4 27.3 %collective-permute-start = (bf16[3,256,512]{2,1,0:T(8,128)(2,1)}, bf16[3,256,512]{2,1,0:T(8,128)(2,1)S(1)}, u32[]{:S(2)}, u32[]{:S(2)}) collective-permute-start(bf16[3,256,512]{2,1,0:T(8,128)(2,1)} %get-tuple-element.22), channel_id=1, source_target_pairs={{0,128},{1,385},{32,160},{33,417},{64,192},{65,449},{96,224},{97,4... | collective-permute-start | bytes 2359304 | tf_op jit(solution)/shard_map/ppermute | solution.py:310
  17.9 29.0 %collective-permute-start.3 = (bf16[3,256,512]{2,1,0:T(8,128)(2,1)}, bf16[3,256,512]{2,1,0:T(8,128)(2,1)S(1)}, u32[]{:S(2)}, u32[]{:S(2)}) collective-permute-start(bf16[3,256,512]{2,1,0:T(8,128)(2,1)} %get-tuple-element.23), channel_id=1, source_target_pairs={{0,96},{1,33},{32,64},{33,1},{64,32},{65,97},{96,0},{97,65},{128,2... | collective-permute-start | bytes 2359304 | tf_op jit(solution)/shard_map/ppermute | solution.py:310
  21.1 2.5 %copy-start.6 = (s32[160,2]{1,0:T(8,128)}, s32[160,2]{1,0:T(8,128)S(1)}, u32[]{:S(2)}) copy-start(s32[160,2]{1,0:T(8,128)S(1)} %copy.17) | copy-start | bytes 3844
  22.3 19.4 %copy-start.2 = (s32[256]{0:T(256)S(1)}, s32[256]{0:T(256)}, u32[]{:S(2)}) copy-start(s32[256]{0:T(256)} %constant.51.clone.table) | copy-start | bytes 3076
  23.7 53.3 %all-to-all-start.1 = ((bf16[32,72,128]{2,1,0:T(8,128)(2,1)}), bf16[32,72,128]{2,1,0:T(8,128)(2,1)S(1)}, u32[]{:S(2)}, u32[]{:S(2)}) async-start(bf16[32,72,128]{2,1,0:T(8,128)(2,1)} %shard_map.75), calls=%async_computation.1 | async-start | bytes 1179648 | tf_op jit(solution)/shard_map/all_to_all | solution.py:414
  40.7 0.9 copy-start.4
  41.6 1.1 %copy-start.3 = (bf16[3,256,512]{2,1,0:T(8,128)(2,1)S(1)}, bf16[3,256,512]{2,1,0:T(8,128)(2,1)}, u32[]{:S(2)}) copy-start(bf16[3,256,512]{2,1,0:T(8,128)(2,1)} %get-tuple-element.25.kept) | copy-start | bytes 2359300
  42.7 1.1 %copy-start.5 = (bf16[3,256,512]{2,1,0:T(8,128)(2,1)S(1)}, bf16[3,256,512]{2,1,0:T(8,128)(2,1)}, u32[]{:S(2)}) copy-start(bf16[3,256,512]{2,1,0:T(8,128)(2,1)} %copy-done.4) | copy-start | bytes 2359300
  43.9 3.0 %copy-start = (bf16[3,256,512]{2,1,0:T(8,128)(2,1)S(1)}, bf16[3,256,512]{2,1,0:T(8,128)(2,1)}, u32[]{:S(2)}) copy-start(bf16[3,256,512]{2,1,0:T(8,128)(2,1)} %get-tuple-element.30.kept) | copy-start | bytes 2359300
  43.9 11.0 %copy-start.1 = (s32[128]{0:T(128)S(1)}, s32[128]{0:T(128)}, u32[]{:S(2)}) copy-start(s32[128]{0:T(128)} %constant.52.clone.table) | copy-start | bytes 1540
  44.7 10.2 %collective-permute-start.1 = (bf16[2,256,512]{2,1,0:T(8,128)(2,1)S(1)}, bf16[2,256,512]{2,1,0:T(8,128)(2,1)S(1)}, u32[]{:S(2)}, u32[]{:S(2)}) collective-permute-start(bf16[2,256,512]{2,1,0:T(8,128)(2,1)S(1)} %get-tuple-element.27), channel_id=1, source_target_pairs={{0,384},{1,129},{32,416},{33,161},{64,448},{65,193},{96,480},{97,2... | collective-permute-start | bytes 1572872 | tf_op jit(solution)/shard_map/ppermute | solution.py:310
  46.9 25.6 %copy-start.8 = (s32[2,32]{1,0:T(2,128)S(1)}, s32[2,32]{1,0:T(2,128)}, u32[]{:S(2)}) copy-start(s32[2,32]{1,0:T(2,128)} %constant.53.clone) | copy-start | bytes 772
  48.4 11.6 %collective-permute-start.4 = (bf16[2,256,512]{2,1,0:T(8,128)(2,1)}, bf16[2,256,512]{2,1,0:T(8,128)(2,1)S(1)}, u32[]{:S(2)}, u32[]{:S(2)}) collective-permute-start(bf16[2,256,512]{2,1,0:T(8,128)(2,1)} %get-tuple-element.33), channel_id=1, source_target_pairs={{0,32},{1,97},{32,0},{33,65},{64,96},{65,33},{96,64},{97,1},{128,1... | collective-permute-start | bytes 1572872 | tf_op jit(solution)/shard_map/ppermute | solution.py:310
  55.6 8.6 %collective-permute-start.2 = (bf16[256,512]{1,0:T(8,128)(2,1)S(1)}, bf16[256,512]{1,0:T(8,128)(2,1)S(1)}, u32[]{:S(2)}, u32[]{:S(2)}) collective-permute-start(bf16[256,512]{1,0:T(8,128)(2,1)S(1)} %get-tuple-element.29), channel_id=1, source_target_pairs={{0,32},{1,97},{32,0},{33,65},{64,96},{65,33},{96,64},{97,1},{128,1... | collective-permute-start | bytes 786440 | tf_op jit(solution)/shard_map/ppermute | solution.py:310
  60.8 7.4 %collective-permute-start.5 = (bf16[256,512]{1,0:T(8,128)(2,1)S(1)}, bf16[256,512]{1,0:T(8,128)(2,1)S(1)}, u32[]{:S(2)}, u32[]{:S(2)}) collective-permute-start(bf16[256,512]{1,0:T(8,128)(2,1)S(1)} %get-tuple-element.35), channel_id=1, source_target_pairs={{0,384},{1,129},{32,416},{33,161},{64,448},{65,193},{96,480},{97,2... | collective-permute-start | bytes 786440 | tf_op jit(solution)/shard_map/ppermute | solution.py:310
  64.3 18.2 %collective-permute-start.6 = (bf16[256,512]{1,0:T(8,128)(2,1)S(1)}, bf16[256,512]{1,0:T(8,128)(2,1)S(1)}, u32[]{:S(2)}, u32[]{:S(2)}) collective-permute-start(bf16[256,512]{1,0:T(8,128)(2,1)S(1)} %shard_map.79.a), channel_id=1, source_target_pairs={{0,96},{1,33},{32,64},{33,1},{64,32},{65,97},{96,0},{97,65},{128,2... | collective-permute-start | bytes 786440 | tf_op jit(solution)/shard_map/ppermute | solution.py:310
  68.2 14.3 %collective-permute-start.7 = (bf16[256,512]{1,0:T(8,128)(2,1)S(1)}, bf16[256,512]{1,0:T(8,128)(2,1)S(1)}, u32[]{:S(2)}, u32[]{:S(2)}) collective-permute-start(bf16[256,512]{1,0:T(8,128)(2,1)S(1)} %shard_map.82.b), channel_id=1, source_target_pairs={{0,128},{1,385},{32,160},{33,417},{64,192},{65,449},{96,224},{97,4... | collective-permute-start | bytes 786440 | tf_op jit(solution)/shard_map/ppermute | solution.py:310
  78.4 15.0 %all-to-all-start.2 = ((bf16[16,2,72,128]{3,2,1,0:T(8,128)(2,1)}), bf16[16,2,72,128]{3,2,1,0:T(8,128)(2,1)S(1)}, u32[]{:S(2)}, u32[]{:S(2)}) async-start(bf16[16,2,72,128]{3,2,1,0:T(8,128)(2,1)} %bitcast.5), calls=%async_computation.2 | async-start | bytes 1179648 | tf_op jit(solution)/shard_map/all_to_all | solution.py:417

commit v8 on v7

--- a/solution.py
+++ b/solution.py
@@ -25,6 +25,7 @@
 long_flops = 10**11
 
 most_mib = 60
+sum_mib = 61.5
 
 VMEM = pl.BlockSpec(memory_space=pltpu.VMEM)
 SMEM = pl.BlockSpec(memory_space=pltpu.SMEM)
@@ -103,7 +104,7 @@
 
 
 def params(mib):
-    return pltpu.CompilerParams(vmem_limit_bytes=mib * 1024 * 1024)
+    return pltpu.CompilerParams(vmem_limit_bytes=int(mib * 1024 * 1024))
 
 
 def add_rounded(a, b):
@@ -116,18 +117,29 @@
     return [table[base + k] for k in range(width)]
 
 
-def choose_kernel(table, source, s0, s1, k0, k1):
+def choose_kernel(table, source, s0, s1):
     table = my_row(table)
     height = s0.shape[1]
-    for h, (sent, kept) in enumerate(((s0, k0), (s1, k1))):
-        rows = slice(h * height, (h + 1) * height)
+    for h, sent in enumerate((s0, s1)):
         for u in range(3):
-            sent[u] = source[table[6 * h + u], rows, :]
-            kept[u] = source[table[6 * h + 3 + u], rows, :]
-
-
-def first_sum_kernel(portion, table, kept, got, sent, next_kept):
-    table = my_row(table)
+            sent[u] = source[table[6 * h + u], h * height : (h + 1) * height, :]
+
+
+def first_sum_kernel(portion, units, table, source, got, sent, next_kept, kept, sems):
+    units, table = my_row(units), my_row(table)
+    height = got.shape[1]
+    loads = [
+        pltpu.make_async_copy(
+            source.at[units[6 * portion + 3 + u], pl.ds(portion * height, height), :],
+            kept.at[u],
+            sems.at[u],
+        )
+        for u in range(3)
+    ]
+    for load in loads:
+        load.start()
+    for load in loads:
+        load.wait()
     for u in range(4):
         place = table[4 * portion + u]
         total = add_rounded(kept[place], got[place])
@@ -314,30 +326,34 @@
     n, order_n = grad.shape[1], grad.shape[2]
     return pl.pallas_call(
         choose_kernel,
-        out_shape=[shape(3, n // 2, order_n)] * 4,
+        out_shape=[shape(3, n // 2, order_n)] * 2,
         in_specs=[SMEM, VMEM],
-        out_specs=[VMEM] * 4,
+        out_specs=[VMEM] * 2,
         compiler_params=params(most_mib),
         cost_estimate=cost(0, 12 * n * order_n),
     )(tables[0], grad)
 
 
-def gradient_sum(kept, got, tables):
-    half, order_n = kept[0].shape[1], kept[0].shape[2]
-    n = 2 * half
+def gradient_sum(grad, got, tables):
+    n, order_n = grad.shape[1], grad.shape[2]
+    half = n // 2
     small = 1024 * 1024
-    sent, kept, got = [None, None], list(kept), list(got)
+    sent, kept, got = [None, None], [None, None], list(got)
     for h in range(2):
         if h == 1:
             got[1], _ = lax.optimization_barrier((got[1], sent[0]))
         sent[h], kept[h] = pl.pallas_call(
             functools.partial(first_sum_kernel, h),
             out_shape=[shape(2, half, order_n)] * 2,
-            in_specs=[SMEM, VMEM, VMEM],
+            in_specs=[SMEM, SMEM, HBM, VMEM],
             out_specs=[VMEM] * 2,
-            compiler_params=params(8),
+            scratch_shapes=[
+                pltpu.VMEM((3, half, order_n), jnp.bfloat16),
+                pltpu.SemaphoreType.DMA((3,)),
+            ],
+            compiler_params=params(sum_mib),
             cost_estimate=cost(long_flops if h == 0 else 0, 2 * small),
-        )(tables[1], kept[h], got[h])
+        )(tables[0], tables[1], grad, got[h])
     for h in range(2):
         sent[h], kept[h] = pl.pallas_call(
             functools.partial(second_sum_kernel, h),
@@ -407,12 +423,12 @@
         cost_estimate=cost(0, 3 * 1024 * 1024),
     )(statistics[0, 0])
     spread = lax.all_to_all(packed, "dp", split_axis=0, concat_axis=0, tiled=True)
-    *sent, k0, k1 = first_sent(grad_partial[0], tables)
+    sent = first_sent(grad_partial[0], tables)
     spread, _ = lax.optimization_barrier((spread, sent))
     got = [exchange(a, portion, 0) for portion, a in enumerate(sent)]
     lanes = pick(lane_from, spread.reshape(slots * n_dp, packed_rows, 128), long_flops // 3)
     lanes = lax.all_to_all(lanes, ("z", "core"), split_axis=0, concat_axis=0, tiled=True)
-    gradient, left, right = gradient_sum((k0, k1), got, tables)
+    gradient, left, right = gradient_sum(grad_partial[0], got, tables)
     lanes = pick(item_from, lanes).reshape(n_dp, 2, packed_rows, 128)
     chunks = lax.all_to_all(lanes, "dp", split_axis=0, concat_axis=0, tiled=True)
 

time: 111 us -> 112 us (level)
  Pallas kernels: 17 us -> 21 us
  waiting for transfers between devices: 22.5 us -> 18.7 us
    pallas_call x2, Pallas kernels: 2.32 us -> 6.93 us  [gradient_sum(): pl.pallas_call(functools.partial(first_sum_kernel, h), out_shape=[shape(2...]
    all_to_all x1, waiting for transfers between devices: 4.21 us -> 0.64 us  [body(): lax.all_to_all(lanes, ('z', 'core'), split_axis=0, concat_axis=0, tiled=T...]
    unnamed x19 -> x17, local copies, waits for them, and re-layouts: 3.28 us -> 3.89 us
  transfers between devices with their start and end apart: 11 -> 11, of which waited for: 6 -> 5; matrix products, arithmetic and copies ran while one was open for 2% -> 1% of each run, Pallas kernels for 10% -> 14%
where the time goes in v8:
time: 112 us; the launch traced here: 110 us
  starting transfers between devices  52.3 us (47%)
  Pallas kernels  21 us (19%)
  waiting for transfers between devices  18.7 us (17%)
  blocking collectives  12.4 us (11%)
  local copies, waits for them, and re-layouts  4.51 us (4%)
    ppermute x8, starting transfers between devices, exchange(): return lax.ppermute(array, ('dp', 'core'), pairs(portion, step))  23.6 us
    all_to_all x1, starting transfers between devices, body(): lax.all_to_all(lanes, ('z', 'core'), split_axis=0, concat_axis=0, tiled=T...  17 us
    all_to_all x1, blocking collectives, body(): rows = lax.all_to_all(rows, 'dp', split_axis=0, concat_axis=0, tiled=True)  12.4 us
    all_to_all x1, waiting for transfers between devices, body(): lax.all_to_all(lanes, 'dp', split_axis=0, concat_axis=0, tiled=True)  9.36 us
    ppermute x8, waiting for transfers between devices, exchange(): return lax.ppermute(array, ('dp', 'core'), pairs(portion, step))  8.74 us
    all_to_all x1, starting transfers between devices, body(): lax.all_to_all(packed, 'dp', split_axis=0, concat_axis=0, tiled=True)  7.6 us
    pallas_call x2, Pallas kernels, gradient_sum(): pl.pallas_call(functools.partial(first_sum_kernel, h), out_shape=[shape(2...  6.93 us
    all_to_all x1, starting transfers between devices, body(): lax.all_to_all(lanes, 'dp', split_axis=0, concat_axis=0, tiled=True)  4.07 us
  transfers between devices with their start and end apart: 11, of which 5 were waited for; matrix products, arithmetic and copies ran while one was open for 1% of the time, Pallas kernels for 14%

profile of v8, /device:TPU:1, one launch (start us, length us, event | category | flops | bytes accessed | tf_op | source)
XLA Modules:
  0.0 110.1 jit_solution(17048940270058860983)
XLA Ops:
  0.0 0.0 copy-start.5
  0.0 2.2 %shard_map.73 = bf16[16,2,72,128]{3,2,1,0:T(8,128)(2,1)} custom-call(f32[2,512,512]{2,1,0:T(8,128)} %bitcast.14), custom_call_target="tpu_custom_call" | custom-call | bytes 3145728 | tf_op jit(solution)/shard_map/pallas_call | solution.py:411
  2.2 7.6 %all-to-all-start = ((bf16[16,2,72,128]{3,2,1,0:T(8,128)(2,1)}), bf16[16,2,72,128]{3,2,1,0:T(8,128)(2,1)S(1)}, u32[]{:S(2)}, u32[]{:S(2)}) async-start(bf16[16,2,72,128]{3,2,1,0:T(8,128)(2,1)} %shard_map.73), calls=%async_computation | async-start | bytes 1179648 | tf_op jit(solution)/shard_map/all_to_all | solution.py:425
  9.8 3.1 %shard_map.74 = (bf16[3,256,512]{2,1,0:T(8,128)(2,1)}, bf16[3,256,512]{2,1,0:T(8,128)(2,1)}) custom-call(s32[384]{0:T(512)} %constant.50.clone.table.units, bf16[5,512,512]{2,1,0:T(8,128)(2,1)} %bitcast.11), custom_call_target="tpu_custom_call" | custom-call | bytes 3145728 | tf_op jit(solution)/shard_map/pallas_call | solution.py:327
  12.9 4.5 %collective-permute-start = (bf16[3,256,512]{2,1,0:T(8,128)(2,1)}, bf16[3,256,512]{2,1,0:T(8,128)(2,1)S(1)}, u32[]{:S(2)}, u32[]{:S(2)}) collective-permute-start(bf16[3,256,512]{2,1,0:T(8,128)(2,1)} %get-tuple-element.20), channel_id=1, source_target_pairs={{0,128},{1,385},{32,160},{33,417},{64,192},{65,449},{96,224},{97,4... | collective-permute-start | bytes 2359304 | tf_op jit(solution)/shard_map/ppermute | solution.py:322
  17.3 3.1 %collective-permute-start.3 = (bf16[3,256,512]{2,1,0:T(8,128)(2,1)}, bf16[3,256,512]{2,1,0:T(8,128)(2,1)}, u32[]{:S(2)}, u32[]{:S(2)}) collective-permute-start(bf16[3,256,512]{2,1,0:T(8,128)(2,1)} %get-tuple-element.21), channel_id=1, source_target_pairs={{0,96},{1,33},{32,64},{33,1},{64,32},{65,97},{96,0},{97,65},{128,2... | collective-permute-start | bytes 2359304 | tf_op jit(solution)/shard_map/ppermute | solution.py:322
  20.5 0.0 copy-done.5
  20.5 0.1 copy.17
  20.6 0.1 copy.22
  20.7 0.1 eq.45
  20.9 0.2 convert_reduce_fusion
  21.1 0.1 reduce_sum.38
  21.3 0.2 fusion.5
  21.4 0.1 reduce_sum.40
  21.6 0.1 reduce_sum.41.table
  21.7 0.0 all-to-all-done
  21.7 1.4 %shard_map.75 = bf16[32,72,128]{2,1,0:T(8,128)(2,1)} custom-call(s32[32]{0:T(128)S(1)} %reduce_sum.41.table, bf16[32,72,128]{2,1,0:T(8,128)(2,1)S(1)} %bitcast.9), custom_call_target="tpu_custom_call" | custom-call | flops 33333334016 | bytes 4194304 | tf_op jit(solution)/shard_map/pallas_call | solution.py:181
  23.1 17.0 %all-to-all-start.1 = ((bf16[32,72,128]{2,1,0:T(8,128)(2,1)}), bf16[32,72,128]{2,1,0:T(8,128)(2,1)S(1)}, u32[]{:S(2)}, u32[]{:S(2)}) async-start(bf16[32,72,128]{2,1,0:T(8,128)(2,1)} %shard_map.75), calls=%async_computation.1 | async-start | bytes 1179648 | tf_op jit(solution)/shard_map/all_to_all | solution.py:430
  40.1 0.0 collective-permute-done.got
  40.2 0.0 copy-start.6
  40.2 0.9 copy-done.6
  41.1 3.4 %shard_map.77 = (bf16[2,256,512]{2,1,0:T(8,128)(2,1)}, bf16[2,256,512]{2,1,0:T(8,128)(2,1)}) custom-call(s32[384]{0:T(512)} %constant.50.clone.table.units, s32[256]{0:T(256)} %constant.51.clone.table, bf16[5,512,512]{2,1,0:T(8,128)(2,1)} %bitcast.12, bf16[3,256,512]{2,1,0:T(8,128)(2,1)} %copy-done.6), custom_call_target="tpu_custom_call" | custom-call | flops 99999997952 | bytes 2097152 | tf_op jit(solution)/shard_map/pallas_call | solution.py:345
  44.5 0.0 copy-start.1
  44.5 0.0 copy-start.2
  44.5 2.3 %collective-permute-start.1 = (bf16[2,256,512]{2,1,0:T(8,128)(2,1)}, bf16[2,256,512]{2,1,0:T(8,128)(2,1)S(1)}, u32[]{:S(2)}, u32[]{:S(2)}) collective-permute-start(bf16[2,256,512]{2,1,0:T(8,128)(2,1)} %get-tuple-element.24), channel_id=1, source_target_pairs={{0,384},{1,129},{32,416},{33,161},{64,448},{65,193},{96,480},{97,2... | collective-permute-start | bytes 1572872 | tf_op jit(solution)/shard_map/ppermute | solution.py:322
  46.9 0.0 collective-permute-done.3.got
  46.9 3.5 %shard_map.80 = (bf16[2,256,512]{2,1,0:T(8,128)(2,1)}, bf16[2,256,512]{2,1,0:T(8,128)(2,1)}) custom-call(s32[384]{0:T(512)} %constant.50.clone.table.units, s32[256]{0:T(256)} %constant.51.clone.table, bf16[5,512,512]{2,1,0:T(8,128)(2,1)} %bitcast.13, bf16[3,256,512]{2,1,0:T(8,128)(2,1)} %collective-permute-done.3.got), custom_call_target="tpu_custom_call" | custom-call | bytes 2097152 | tf_op jit(solution)/shard_map/pallas_call | solution.py:345
  50.4 0.0 copy-start.7
  50.4 1.9 %collective-permute-start.4 = (bf16[2,256,512]{2,1,0:T(8,128)(2,1)}, bf16[2,256,512]{2,1,0:T(8,128)(2,1)S(1)}, u32[]{:S(2)}, u32[]{:S(2)}) collective-permute-start(bf16[2,256,512]{2,1,0:T(8,128)(2,1)} %get-tuple-element.29), channel_id=1, source_target_pairs={{0,32},{1,97},{32,0},{33,65},{64,96},{65,33},{96,64},{97,1},{128,1... | collective-permute-start | bytes 1572872 | tf_op jit(solution)/shard_map/ppermute | solution.py:322
  52.3 0.1 reshape.22
  52.4 2.7 %collective-permute-done.1.got = bf16[2,256,512]{2,1,0:T(8,128)(2,1)S(1)} collective-permute-done((bf16[2,256,512]{2,1,0:T(8,128)(2,1)}, bf16[2,256,512]{2,1,0:T(8,128)(2,1)S(1)}, u32[]{:S(2)}, u32[]{:S(2)}) %collective-permute-start.1) | collective-permute-done | bytes 524320 | tf_op jit(solution)/shard_map/ppermute | solution.py:322
  55.1 0.0 copy-done.1
  55.1 0.0 copy-done.2
  55.1 0.7 shard_map.78
  55.8 2.2 %collective-permute-start.2 = (bf16[256,512]{1,0:T(8,128)(2,1)S(1)}, bf16[256,512]{1,0:T(8,128)(2,1)S(1)}, u32[]{:S(2)}, u32[]{:S(2)}) collective-permute-start(bf16[256,512]{1,0:T(8,128)(2,1)S(1)} %get-tuple-element.26), channel_id=1, source_target_pairs={{0,32},{1,97},{32,0},{33,65},{64,96},{65,33},{96,64},{97,1},{128,1... | collective-permute-start | bytes 786440 | tf_op jit(solution)/shard_map/ppermute | solution.py:322
  58.0 4.0 %collective-permute-done.4.got = bf16[2,256,512]{2,1,0:T(8,128)(2,1)S(1)} collective-permute-done((bf16[2,256,512]{2,1,0:T(8,128)(2,1)}, bf16[2,256,512]{2,1,0:T(8,128)(2,1)S(1)}, u32[]{:S(2)}, u32[]{:S(2)}) %collective-permute-start.4) | collective-permute-done | bytes 524320 | tf_op jit(solution)/shard_map/ppermute | solution.py:322
  62.0 0.0 copy-start
  62.0 1.0 copy-done
  63.1 0.7 shard_map.81
  63.8 3.1 %collective-permute-start.5 = (bf16[256,512]{1,0:T(8,128)(2,1)S(1)}, bf16[256,512]{1,0:T(8,128)(2,1)S(1)}, u32[]{:S(2)}, u32[]{:S(2)}) collective-permute-start(bf16[256,512]{1,0:T(8,128)(2,1)S(1)} %get-tuple-element.31), channel_id=1, source_target_pairs={{0,384},{1,129},{32,416},{33,161},{64,448},{65,193},{96,480},{97,2... | collective-permute-start | bytes 786440 | tf_op jit(solution)/shard_map/ppermute | solution.py:322
  66.9 0.0 collective-permute-done.2.got
  66.9 0.1 shard_map.79.a
  67.0 1.9 %collective-permute-start.6 = (bf16[256,512]{1,0:T(8,128)(2,1)S(1)}, bf16[256,512]{1,0:T(8,128)(2,1)S(1)}, u32[]{:S(2)}, u32[]{:S(2)}) collective-permute-start(bf16[256,512]{1,0:T(8,128)(2,1)S(1)} %shard_map.79.a), channel_id=1, source_target_pairs={{0,96},{1,33},{32,64},{33,1},{64,32},{65,97},{96,0},{97,65},{128,2... | collective-permute-start | bytes 786440 | tf_op jit(solution)/shard_map/ppermute | solution.py:322
  68.9 2.0 %collective-permute-done.5.got = bf16[256,512]{1,0:T(8,128)(2,1)S(1)} collective-permute-done((bf16[256,512]{1,0:T(8,128)(2,1)S(1)}, bf16[256,512]{1,0:T(8,128)(2,1)S(1)}, u32[]{:S(2)}, u32[]{:S(2)}) %collective-permute-start.5) | collective-permute-done | bytes 262176 | tf_op jit(solution)/shard_map/ppermute | solution.py:322
  70.9 0.1 shard_map.82.b
  70.9 4.6 %collective-permute-start.7 = (bf16[256,512]{1,0:T(8,128)(2,1)S(1)}, bf16[256,512]{1,0:T(8,128)(2,1)S(1)}, u32[]{:S(2)}, u32[]{:S(2)}) collective-permute-start(bf16[256,512]{1,0:T(8,128)(2,1)S(1)} %shard_map.82.b), channel_id=1, source_target_pairs={{0,128},{1,385},{32,160},{33,417},{64,192},{65,449},{96,224},{97,4... | collective-permute-start | bytes 786440 | tf_op jit(solution)/shard_map/ppermute | solution.py:322
  75.5 0.0 copy-done.7
  75.6 0.2 select_reduce_fusion.table
  75.8 0.6 all-to-all-done.1.source
  76.4 1.4 %shard_map.76 = bf16[32,72,128]{2,1,0:T(8,128)(2,1)} custom-call(s32[32]{0:T(128)S(1)} %select_reduce_fusion.table, bf16[32,72,128]{2,1,0:T(8,128)(2,1)S(1)} %all-to-all-done.1.source), custom_call_target="tpu_custom_call" | custom-call | bytes 4194304 | tf_op jit(solution)/shard_map/pallas_call | solution.py:181
  77.8 4.1 %all-to-all-start.2 = ((bf16[16,2,72,128]{3,2,1,0:T(8,128)(2,1)}), bf16[16,2,72,128]{3,2,1,0:T(8,128)(2,1)S(1)}, u32[]{:S(2)}, u32[]{:S(2)}) async-start(bf16[16,2,72,128]{3,2,1,0:T(8,128)(2,1)} %bitcast.5), calls=%async_computation.2 | async-start | bytes 1179648 | tf_op jit(solution)/shard_map/all_to_all | solution.py:433
  81.9 0.0 collective-permute-done.6.r0
  81.9 0.0 collective-permute-done.7.r1
  81.9 0.8 shard_map.83
  82.7 0.0 copy-start.3
  82.7 0.8 copy-done.3
  83.5 9.4 %all-to-all-done.2.chunks = bf16[16,2,72,128]{3,2,1,0:T(8,128)(2,1)S(1)} async-done(((bf16[16,2,72,128]{3,2,1,0:T(8,128)(2,1)}), bf16[16,2,72,128]{3,2,1,0:T(8,128)(2,1)S(1)}, u32[]{:S(2)}, u32[]{:S(2)}) %all-to-all-start.2) | async-done | bytes 589856 | tf_op jit(solution)/shard_map/all_to_all | solution.py:433
  92.9 0.0 copy-start.4
  92.9 1.0 copy-done.4
  93.9 3.1 %shard_map.84 = bf16[512,512]{1,0:T(8,128)(2,1)S(1)} custom-call(bf16[16,2,72,128]{3,2,1,0:T(8,128)(2,1)S(1)} %all-to-all-done.2.chunks, bf16[512,512]{1,0:T(8,128)(2,1)S(1)} %get-tuple-element.32.gradient, bf16[512,512]{1,0:T(8,128)(2,1)S(1)} %get-tuple-element.33.left, bf16[512,512]{1,0:T(8,128)(2,1)S(1)} %copy-done.4), custom_call_target="tpu_custom_call" | custom-call | flops 2147483648 | bytes 6291456 | tf_op jit(solution)/shard_map/pallas_call | solution.py:436
  97.0 12.4 %all_to_all.20.source = bf16[16,32,512]{2,1,0:T(8,128)(2,1)S(1)} all-to-all(bf16[16,32,512]{2,1,0:T(8,128)(2,1)S(1)} %bitcast.10), channel_id=1, replica_groups=mesh['dp'=16,'z'=16,'core'=2] {'dp'}, dimensions={0} | all-to-all | bytes 1048576 | tf_op jit(solution)/shard_map/all_to_all | solution.py:449
  109.4 0.7 shard_map.85
  (5 shorter events, 0.0 us)
Async XLA Ops:
  0.0 20.5 %copy-start.5 = (s32[160,2]{0,1:T(2,128)S(1)}, s32[160,2]{0,1:T(2,128)}, u32[]{:S(2)}) copy-start(s32[160,2]{0,1:T(2,128)} %param.9) | copy-start | bytes 3844
  2.2 19.5 %all-to-all-start = ((bf16[16,2,72,128]{3,2,1,0:T(8,128)(2,1)}), bf16[16,2,72,128]{3,2,1,0:T(8,128)(2,1)S(1)}, u32[]{:S(2)}, u32[]{:S(2)}) async-start(bf16[16,2,72,128]{3,2,1,0:T(8,128)(2,1)} %shard_map.73), calls=%async_computation | async-start | bytes 1179648 | tf_op jit(solution)/shard_map/all_to_all | solution.py:425
  12.9 27.3 %collective-permute-start = (bf16[3,256,512]{2,1,0:T(8,128)(2,1)}, bf16[3,256,512]{2,1,0:T(8,128)(2,1)S(1)}, u32[]{:S(2)}, u32[]{:S(2)}) collective-permute-start(bf16[3,256,512]{2,1,0:T(8,128)(2,1)} %get-tuple-element.20), channel_id=1, source_target_pairs={{0,128},{1,385},{32,160},{33,417},{64,192},{65,449},{96,224},{97,4... | collective-permute-start | bytes 2359304 | tf_op jit(solution)/shard_map/ppermute | solution.py:322
  17.3 29.5 %collective-permute-start.3 = (bf16[3,256,512]{2,1,0:T(8,128)(2,1)}, bf16[3,256,512]{2,1,0:T(8,128)(2,1)}, u32[]{:S(2)}, u32[]{:S(2)}) collective-permute-start(bf16[3,256,512]{2,1,0:T(8,128)(2,1)} %get-tuple-element.21), channel_id=1, source_target_pairs={{0,96},{1,33},{32,64},{33,1},{64,32},{65,97},{96,0},{97,65},{128,2... | collective-permute-start | bytes 2359304 | tf_op jit(solution)/shard_map/ppermute | solution.py:322
  23.1 53.3 %all-to-all-start.1 = ((bf16[32,72,128]{2,1,0:T(8,128)(2,1)}), bf16[32,72,128]{2,1,0:T(8,128)(2,1)S(1)}, u32[]{:S(2)}, u32[]{:S(2)}) async-start(bf16[32,72,128]{2,1,0:T(8,128)(2,1)} %shard_map.75), calls=%async_computation.1 | async-start | bytes 1179648 | tf_op jit(solution)/shard_map/all_to_all | solution.py:430
  40.2 0.9 copy-start.6
  44.5 10.6 %copy-start.1 = (bf16[2,256,512]{2,1,0:T(8,128)(2,1)S(1)}, bf16[2,256,512]{2,1,0:T(8,128)(2,1)}, u32[]{:S(2)}) copy-start(bf16[2,256,512]{2,1,0:T(8,128)(2,1)} %get-tuple-element.23.kept) | copy-start | bytes 1572868
  44.5 10.6 %copy-start.2 = (s32[128]{0:T(128)S(1)}, s32[128]{0:T(128)}, u32[]{:S(2)}) copy-start(s32[128]{0:T(128)} %constant.52.clone.table) | copy-start | bytes 1540
  44.5 10.6 %collective-permute-start.1 = (bf16[2,256,512]{2,1,0:T(8,128)(2,1)}, bf16[2,256,512]{2,1,0:T(8,128)(2,1)S(1)}, u32[]{:S(2)}, u32[]{:S(2)}) collective-permute-start(bf16[2,256,512]{2,1,0:T(8,128)(2,1)} %get-tuple-element.24), channel_id=1, source_target_pairs={{0,384},{1,129},{32,416},{33,161},{64,448},{65,193},{96,480},{97,2... | collective-permute-start | bytes 1572872 | tf_op jit(solution)/shard_map/ppermute | solution.py:322
  50.4 25.2 %copy-start.7 = (s32[2,32]{1,0:T(2,128)S(1)}, s32[2,32]{1,0:T(2,128)}, u32[]{:S(2)}) copy-start(s32[2,32]{1,0:T(2,128)} %constant.53.clone) | copy-start | bytes 772
  50.4 11.6 %collective-permute-start.4 = (bf16[2,256,512]{2,1,0:T(8,128)(2,1)}, bf16[2,256,512]{2,1,0:T(8,128)(2,1)S(1)}, u32[]{:S(2)}, u32[]{:S(2)}) collective-permute-start(bf16[2,256,512]{2,1,0:T(8,128)(2,1)} %get-tuple-element.29), channel_id=1, source_target_pairs={{0,32},{1,97},{32,0},{33,65},{64,96},{65,33},{96,64},{97,1},{128,1... | collective-permute-start | bytes 1572872 | tf_op jit(solution)/shard_map/ppermute | solution.py:322
  55.8 11.1 %collective-permute-start.2 = (bf16[256,512]{1,0:T(8,128)(2,1)S(1)}, bf16[256,512]{1,0:T(8,128)(2,1)S(1)}, u32[]{:S(2)}, u32[]{:S(2)}) collective-permute-start(bf16[256,512]{1,0:T(8,128)(2,1)S(1)} %get-tuple-element.26), channel_id=1, source_target_pairs={{0,32},{1,97},{32,0},{33,65},{64,96},{65,33},{96,64},{97,1},{128,1... | collective-permute-start | bytes 786440 | tf_op jit(solution)/shard_map/ppermute | solution.py:322
  62.0 1.0 copy-start
  63.8 7.1 %collective-permute-start.5 = (bf16[256,512]{1,0:T(8,128)(2,1)S(1)}, bf16[256,512]{1,0:T(8,128)(2,1)S(1)}, u32[]{:S(2)}, u32[]{:S(2)}) collective-permute-start(bf16[256,512]{1,0:T(8,128)(2,1)S(1)} %get-tuple-element.31), channel_id=1, source_target_pairs={{0,384},{1,129},{32,416},{33,161},{64,448},{65,193},{96,480},{97,2... | collective-permute-start | bytes 786440 | tf_op jit(solution)/shard_map/ppermute | solution.py:322
  67.0 14.9 %collective-permute-start.6 = (bf16[256,512]{1,0:T(8,128)(2,1)S(1)}, bf16[256,512]{1,0:T(8,128)(2,1)S(1)}, u32[]{:S(2)}, u32[]{:S(2)}) collective-permute-start(bf16[256,512]{1,0:T(8,128)(2,1)S(1)} %shard_map.79.a), channel_id=1, source_target_pairs={{0,96},{1,33},{32,64},{33,1},{64,32},{65,97},{96,0},{97,65},{128,2... | collective-permute-start | bytes 786440 | tf_op jit(solution)/shard_map/ppermute | solution.py:322
  70.9 11.0 %collective-permute-start.7 = (bf16[256,512]{1,0:T(8,128)(2,1)S(1)}, bf16[256,512]{1,0:T(8,128)(2,1)S(1)}, u32[]{:S(2)}, u32[]{:S(2)}) collective-permute-start(bf16[256,512]{1,0:T(8,128)(2,1)S(1)} %shard_map.82.b), channel_id=1, source_target_pairs={{0,128},{1,385},{32,160},{33,417},{64,192},{65,449},{96,224},{97,4... | collective-permute-start | bytes 786440 | tf_op jit(solution)/shard_map/ppermute | solution.py:322
  77.8 15.0 %all-to-all-start.2 = ((bf16[16,2,72,128]{3,2,1,0:T(8,128)(2,1)}), bf16[16,2,72,128]{3,2,1,0:T(8,128)(2,1)S(1)}, u32[]{:S(2)}, u32[]{:S(2)}) async-start(bf16[16,2,72,128]{3,2,1,0:T(8,128)(2,1)} %bitcast.5), calls=%async_computation.2 | async-start | bytes 1179648 | tf_op jit(solution)/shard_map/all_to_all | solution.py:433
  82.7 0.8 copy-start.3
  92.9 1.0 copy-start.4

commit v9 on v7

--- a/solution.py
+++ b/solution.py
@@ -160,17 +160,27 @@
         gram[...] = product.astype(jnp.bfloat16)
 
 
-def pick_kernel(table, source, out):
-    for i in range(out.shape[0]):
-        out[i] = source[table[i]]
+def pick_kernel(table, source, out, staged, sems):
+    group = out.shape[0] // 4
+    stores = []
+    for g in range(4):
+        rows = pl.ds(g * group, group)
+        for i in range(g * group, (g + 1) * group):
+            staged[i] = source[table[i]]
+        stores.append(pltpu.make_async_copy(staged.at[rows], out.at[rows], sems.at[g]))
+        stores[g].start()
+    for store in stores:
+        store.wait()
 
 
 def pick(table, source, flops=0):
+    out = table.shape + source.shape[1:]
     return pl.pallas_call(
         pick_kernel,
-        out_shape=jax.ShapeDtypeStruct(table.shape + source.shape[1:], source.dtype),
+        out_shape=jax.ShapeDtypeStruct(out, source.dtype),
         in_specs=[SMEM, VMEM],
-        out_specs=VMEM,
+        out_specs=HBM,
+        scratch_shapes=[pltpu.VMEM(out, source.dtype), pltpu.SemaphoreType.DMA((4,))],
         compiler_params=params(4),
         cost_estimate=cost(flops, 4 * 1024 * 1024),
     )(table, source)
@@ -247,43 +257,53 @@
     )
 
 
-def unpack(chunks, s, mixed, stat):
+def add_statistic(chunks, s, gram, mixed, side, stat):
     half = mixed.shape[0]
     for c in range(16):
         strip = chunks[c, s, :64, :].astype(jnp.float32)
         rows = slice(64 * (c % 4), 64 * (c % 4) + 64)
-        at = c // 4
-        if at < 2:
-            mixed[rows, 128 * at : 128 * at + 128] = strip
+        cols = slice(128 * (c // 4 % 2), 128 * (c // 4 % 2) + 128)
+        if c < 8:
+            mixed[rows, cols] = strip
         else:
-            stat[rows, half + 128 * (at - 2) : half + 128 * (at - 2) + 128] = strip
+            side[rows, cols] = strip
     tail = chunks[0, s, 64:, :].astype(jnp.float32)
     diagonal = jnp.concatenate([tail[0:1, :], tail[1:2, :]], axis=1)
     m = mixed[...]
     flipped = m.T
     i, j = square_iotas(half)
-    stat[:half, :half] = jnp.where(i <= j, m, flipped)
-    stat[half:, half:] = jnp.where(i > j, m, jnp.where(i == j, diagonal, flipped))
-    stat[half:, :half] = stat[:half, half:].T
-
-
-def update_kernel(chunks, gradient, left, right, out, mixed, stat):
+    upper, lower = slice(0, half), slice(half, 2 * half)
+    low = jnp.where(i > j, m, jnp.where(i == j, diagonal, flipped))
+    total = 0.0
+    for old, rows, cols in (
+        (jnp.where(i <= j, m, flipped), upper, upper),
+        (low, lower, lower),
+        (side[...], upper, lower),
+    ):
+        added = decay_rate * old + (1.0 - decay_rate) * gram[rows, cols].astype(jnp.float32)
+        rounded = added.astype(jnp.bfloat16)
+        stat[rows, cols] = rounded
+        wide = rounded.astype(jnp.float32)
+        squares = jnp.sum(wide * wide, axis=0, keepdims=True)
+        if rows is not cols:
+            stat[cols, rows] = wide.T.astype(jnp.bfloat16)
+            squares = 2.0 * squares
+        total = total + squares
+    return total
+
+
+def update_kernel(chunks, gradient, left, right, out, mixed, side, stat):
     order_n = out.shape[0]
     sides = (0, 1)
-    for s in sides:
-        unpack(chunks, s, mixed.at[s], stat.at[s])
     i, j = square_iotas(order_n)
     scale, quarter, square = [], [], []
     for s, gram in zip(sides, (left, right)):
-        new_stat = decay_rate * stat[s] + (1.0 - decay_rate) * gram[...].astype(jnp.float32)
-        rounded = new_stat.astype(jnp.bfloat16)
-        new_stat = rounded.astype(jnp.float32)
-        squares = jnp.sum(new_stat * new_stat, axis=0, keepdims=True)
+        squares = add_statistic(chunks, s, gram, mixed.at[s], side.at[s], stat.at[s])
         frob_norm = jnp.sqrt(jnp.sum(squares, axis=1, keepdims=True) + 1e-06)
         scale.append(root_gain * math.sqrt(order_n) / frob_norm)
         part = 0.25 * scale[s]
-        quarter.append(part * new_stat)
-        square.append((part * part) * product(rounded, rounded))
+        quarter.append(part * stat[s].astype(jnp.float32))
+        square.append((part * part) * product(stat[s], stat[s]))
     e2 = [jnp.where(i == j, 0.5625, 0.0) - 2.5 * quarter[s] + square[s] for s in sides]
     e4 = [2.0 * e2[s] + product(e2[s], e2[s]) for s in sides]
     rest = [square[s] - 1.25 * quarter[s] for s in sides]
@@ -378,15 +398,13 @@
     lane_item = home_tables()
     tables = [jnp.asarray(t.reshape(-1)) for t in tree_tables()]
 
-    device = owner_table.reshape(-1)
-    numbers = jnp.arange(device.shape[0], dtype=jnp.int32)
-    earlier = numbers[None, :] < numbers[:, None]
-    slot_of = jnp.sum(
-        ((device[None, :] == device[:, None]) & earlier).astype(jnp.int32), axis=1
-    )
-    by_column = (device % n_owner).reshape(n_owner, 2 * blocks_col)
-    place = ((device // n_owner) * slots + slot_of).reshape(n_owner, 2 * blocks_col)
-    lane_from = jnp.sum(jnp.where(by_column == col, place, 0), axis=1)
+    device = owner_table.reshape(n_owner, 2 * blocks_col)
+    by_column = device % n_owner
+    lane_row = jnp.max(jnp.where(by_column == col, device // n_owner, -1), axis=1)
+    numbers = jnp.arange(n_owner, dtype=jnp.int32)
+    same = (lane_row[None, :] == lane_row[:, None]) & (numbers[None, :] < numbers[:, None])
+    lane_slot = jnp.sum(same.astype(jnp.int32), axis=1)
+    lane_from = jnp.where(lane_row < 0, 0, lane_row * slots + lane_slot)
     home = lax.dynamic_slice_in_dim(by_column, col, 1, axis=0)
     wanted = jnp.asarray(lane_item)[core]
     item_hot = wanted[:, None] == jnp.arange(2 * blocks_col)[None, :]
@@ -424,7 +442,8 @@
         out_specs=VMEM,
         scratch_shapes=[
             pltpu.VMEM((2, order_b // 2, order_b // 2), jnp.float32),
-            pltpu.VMEM((2,) + full, jnp.float32),
+            pltpu.VMEM((2, order_b // 2, order_b // 2), jnp.float32),
+            pltpu.VMEM((2,) + full, jnp.bfloat16),
         ],
         compiler_params=params(40),
         cost_estimate=cost(16 * order_b**3, 6 * 1024 * 1024),

time: 111 us -> 111 us (level)
  local copies, waits for them, and re-layouts: 4.78 us -> 3.46 us
    unnamed x19 -> x17, local copies, waits for them, and re-layouts: 3.28 us -> 3.28 us
  transfers between devices with their start and end apart: 11 -> 11, of which waited for: 6 -> 6; matrix products, arithmetic and copies ran while one was open for 2% -> 1% of each run, Pallas kernels for 10% -> 10%
where the time goes in v9:
time: 111 us; the launch traced here: 109 us
  starting transfers between devices  51.9 us (47%)
  waiting for transfers between devices  23.3 us (21%)
  Pallas kernels  16.9 us (15%)
  blocking collectives  12.8 us (12%)
  local copies, waits for them, and re-layouts  3.46 us (3%)
    ppermute x8, starting transfers between devices, exchange(): return lax.ppermute(array, ('dp', 'core'), pairs(portion, step))  23.2 us
    all_to_all x1, starting transfers between devices, body(): lax.all_to_all(lanes, ('z', 'core'), split_axis=0, concat_axis=0, tiled=T...  17 us
    all_to_all x1, blocking collectives, body(): rows = lax.all_to_all(rows, 'dp', split_axis=0, concat_axis=0, tiled=True)  12.8 us
    all_to_all x1, waiting for transfers between devices, body(): lax.all_to_all(lanes, 'dp', split_axis=0, concat_axis=0, tiled=True)  10.1 us
    ppermute x8, waiting for transfers between devices, exchange(): return lax.ppermute(array, ('dp', 'core'), pairs(portion, step))  8.93 us
    all_to_all x1, starting transfers between devices, body(): lax.all_to_all(packed, 'dp', split_axis=0, concat_axis=0, tiled=True)  7.6 us
    all_to_all x1, waiting for transfers between devices, body(): lax.all_to_all(lanes, ('z', 'core'), split_axis=0, concat_axis=0, tiled=T...  4.2 us
    all_to_all x1, starting transfers between devices, body(): lax.all_to_all(lanes, 'dp', split_axis=0, concat_axis=0, tiled=True)  4.08 us
  transfers between devices with their start and end apart: 11, of which 6 were waited for; matrix products, arithmetic and copies ran while one was open for 1% of the time, Pallas kernels for 10%

profile of v9, /device:TPU:1, one launch (start us, length us, event | category | flops | bytes accessed | tf_op | source)
XLA Modules:
  0.0 109.2 jit_solution(11529300744370041957)
XLA Ops:
  0.0 0.0 copy-start.6
  0.0 2.2 %shard_map.73 = bf16[16,2,72,128]{3,2,1,0:T(8,128)(2,1)} custom-call(f32[2,512,512]{2,1,0:T(8,128)} %bitcast.12), custom_call_target="tpu_custom_call" | custom-call | bytes 3145728 | tf_op jit(solution)/shard_map/pallas_call | solution.py:413
  2.2 7.6 %all-to-all-start = ((bf16[16,2,72,128]{3,2,1,0:T(8,128)(2,1)}), bf16[16,2,72,128]{3,2,1,0:T(8,128)(2,1)S(1)}, u32[]{:S(2)}, u32[]{:S(2)}) async-start(bf16[16,2,72,128]{3,2,1,0:T(8,128)(2,1)} %shard_map.73), calls=%async_computation | async-start | bytes 1179648 | tf_op jit(solution)/shard_map/all_to_all | solution.py:427
  9.8 3.6 %shard_map.74 = (bf16[3,256,512]{2,1,0:T(8,128)(2,1)}, bf16[3,256,512]{2,1,0:T(8,128)(2,1)}, bf16[3,256,512]{2,1,0:T(8,128)(2,1)}, bf16[3,256,512]{2,1,0:T(8,128)(2,1)}) custom-call(s32[384]{0:T(512)} %constant.54.clone.table, bf16[5,512,512]{2,1,0:T(8,128)(2,1)} %bitcast.11), custom_call_target="tpu_custom_call" | custom-call | bytes 3145728 | tf_op jit(solution)/shard_map/pallas_call | solution.py:335
  13.4 4.5 %collective-permute-start = (bf16[3,256,512]{2,1,0:T(8,128)(2,1)}, bf16[3,256,512]{2,1,0:T(8,128)(2,1)S(1)}, u32[]{:S(2)}, u32[]{:S(2)}) collective-permute-start(bf16[3,256,512]{2,1,0:T(8,128)(2,1)} %get-tuple-element.22), channel_id=1, source_target_pairs={{0,128},{1,385},{32,160},{33,417},{64,192},{65,449},{96,224},{97,4... | collective-permute-start | bytes 2359304 | tf_op jit(solution)/shard_map/ppermute | solution.py:330
  17.9 3.1 %collective-permute-start.3 = (bf16[3,256,512]{2,1,0:T(8,128)(2,1)}, bf16[3,256,512]{2,1,0:T(8,128)(2,1)S(1)}, u32[]{:S(2)}, u32[]{:S(2)}) collective-permute-start(bf16[3,256,512]{2,1,0:T(8,128)(2,1)} %get-tuple-element.23), channel_id=1, source_target_pairs={{0,96},{1,33},{32,64},{33,1},{64,32},{65,97},{96,0},{97,65},{128,2... | collective-permute-start | bytes 2359304 | tf_op jit(solution)/shard_map/ppermute | solution.py:330
  21.0 0.0 copy-done.6
  21.1 0.1 reduce_max.14
  21.2 0.1 reduce_max.18
  21.3 0.2 convert_reduce_fusion
  21.5 0.0 all-to-all-done
  21.5 0.0 copy-start.2
  21.5 1.4 %shard_map.75 = bf16[32,72,128]{2,1,0:T(8,128)(2,1)} custom-call(s32[32]{0:T(128)S(1)} %compare_select_fusion.1.table, bf16[32,72,128]{2,1,0:T(8,128)(2,1)S(1)} %bitcast.9), custom_call_target="tpu_custom_call" | custom-call | flops 33333334016 | bytes 4194304 | tf_op jit(solution)/shard_map/pallas_call | solution.py:178
  22.9 17.0 %all-to-all-start.1 = ((bf16[32,72,128]{2,1,0:T(8,128)(2,1)}), bf16[32,72,128]{2,1,0:T(8,128)(2,1)S(1)}, u32[]{:S(2)}, u32[]{:S(2)}) async-start(bf16[32,72,128]{2,1,0:T(8,128)(2,1)} %shard_map.75), calls=%async_computation.1 | async-start | bytes 1179648 | tf_op jit(solution)/shard_map/all_to_all | solution.py:432
  40.0 0.0 collective-permute-done.got
  40.0 0.0 copy-start.4
  40.0 0.9 copy-done.4
  40.9 0.0 copy-done.2
  40.9 0.0 copy-start.3
  40.9 1.1 %copy-done.3 = bf16[3,256,512]{2,1,0:T(8,128)(2,1)S(1)} copy-done((bf16[3,256,512]{2,1,0:T(8,128)(2,1)S(1)}, bf16[3,256,512]{2,1,0:T(8,128)(2,1)}, u32[]{:S(2)}) %copy-start.3) | copy-done | bytes 786456
  42.0 0.0 copy-start.5
  42.0 1.1 %copy-done.5 = bf16[3,256,512]{2,1,0:T(8,128)(2,1)S(1)} copy-done((bf16[3,256,512]{2,1,0:T(8,128)(2,1)S(1)}, bf16[3,256,512]{2,1,0:T(8,128)(2,1)}, u32[]{:S(2)}) %copy-start.5) | copy-done | bytes 786456
  43.2 0.0 copy-start
  43.2 0.0 copy-start.1
  43.2 0.8 shard_map.77
  44.0 2.2 %collective-permute-start.1 = (bf16[2,256,512]{2,1,0:T(8,128)(2,1)S(1)}, bf16[2,256,512]{2,1,0:T(8,128)(2,1)S(1)}, u32[]{:S(2)}, u32[]{:S(2)}) collective-permute-start(bf16[2,256,512]{2,1,0:T(8,128)(2,1)S(1)} %get-tuple-element.27), channel_id=1, source_target_pairs={{0,384},{1,129},{32,416},{33,161},{64,448},{65,193},{96,480},{97,2... | collective-permute-start | bytes 1572872 | tf_op jit(solution)/shard_map/ppermute | solution.py:330
  46.2 0.0 collective-permute-done.3.got
  46.2 0.0 copy-done
  46.2 0.0 copy-start.7
  46.2 1.5 %shard_map.80 = (bf16[2,256,512]{2,1,0:T(8,128)(2,1)}, bf16[2,256,512]{2,1,0:T(8,128)(2,1)S(1)}) custom-call(s32[256]{0:T(256)S(1)} %copy-done.2, bf16[3,256,512]{2,1,0:T(8,128)(2,1)S(1)} %copy-done, bf16[3,256,512]{2,1,0:T(8,128)(2,1)S(1)} %collective-permute-done.3.got), custom_call_target="tpu_custom_call" | custom-call | bytes 2097152 | tf_op jit(solution)/shard_map/pallas_call | solution.py:353
  47.7 1.9 %collective-permute-start.4 = (bf16[2,256,512]{2,1,0:T(8,128)(2,1)}, bf16[2,256,512]{2,1,0:T(8,128)(2,1)S(1)}, u32[]{:S(2)}, u32[]{:S(2)}) collective-permute-start(bf16[2,256,512]{2,1,0:T(8,128)(2,1)} %get-tuple-element.33), channel_id=1, source_target_pairs={{0,32},{1,97},{32,0},{33,65},{64,96},{65,33},{96,64},{97,1},{128,1... | collective-permute-start | bytes 1572872 | tf_op jit(solution)/shard_map/ppermute | solution.py:330
  49.6 0.1 copy.9
  49.8 0.1 reshape.16
  49.8 4.4 %collective-permute-done.1.got = bf16[2,256,512]{2,1,0:T(8,128)(2,1)S(1)} collective-permute-done((bf16[2,256,512]{2,1,0:T(8,128)(2,1)S(1)}, bf16[2,256,512]{2,1,0:T(8,128)(2,1)S(1)}, u32[]{:S(2)}, u32[]{:S(2)}) %collective-permute-start.1) | collective-permute-done | bytes 524320 | tf_op jit(solution)/shard_map/ppermute | solution.py:330
  54.2 0.0 copy-done.1
  54.2 0.7 shard_map.78
  54.9 2.2 %collective-permute-start.2 = (bf16[256,512]{1,0:T(8,128)(2,1)S(1)}, bf16[256,512]{1,0:T(8,128)(2,1)S(1)}, u32[]{:S(2)}, u32[]{:S(2)}) collective-permute-start(bf16[256,512]{1,0:T(8,128)(2,1)S(1)} %get-tuple-element.29), channel_id=1, source_target_pairs={{0,32},{1,97},{32,0},{33,65},{64,96},{65,33},{96,64},{97,1},{128,1... | collective-permute-start | bytes 786440 | tf_op jit(solution)/shard_map/ppermute | solution.py:330
  57.1 2.3 %collective-permute-done.4.got = bf16[2,256,512]{2,1,0:T(8,128)(2,1)S(1)} collective-permute-done((bf16[2,256,512]{2,1,0:T(8,128)(2,1)}, bf16[2,256,512]{2,1,0:T(8,128)(2,1)S(1)}, u32[]{:S(2)}, u32[]{:S(2)}) %collective-permute-start.4) | collective-permute-done | bytes 524320 | tf_op jit(solution)/shard_map/ppermute | solution.py:330
  59.4 0.7 shard_map.81
  60.0 3.1 %collective-permute-start.5 = (bf16[256,512]{1,0:T(8,128)(2,1)S(1)}, bf16[256,512]{1,0:T(8,128)(2,1)S(1)}, u32[]{:S(2)}, u32[]{:S(2)}) collective-permute-start(bf16[256,512]{1,0:T(8,128)(2,1)S(1)} %get-tuple-element.35), channel_id=1, source_target_pairs={{0,384},{1,129},{32,416},{33,161},{64,448},{65,193},{96,480},{97,2... | collective-permute-start | bytes 786440 | tf_op jit(solution)/shard_map/ppermute | solution.py:330
  63.2 0.3 collective-permute-done.2.got
  63.5 0.1 shard_map.79.a
  63.6 1.9 %collective-permute-start.6 = (bf16[256,512]{1,0:T(8,128)(2,1)S(1)}, bf16[256,512]{1,0:T(8,128)(2,1)S(1)}, u32[]{:S(2)}, u32[]{:S(2)}) collective-permute-start(bf16[256,512]{1,0:T(8,128)(2,1)S(1)} %shard_map.79.a), channel_id=1, source_target_pairs={{0,96},{1,33},{32,64},{33,1},{64,32},{65,97},{96,0},{97,65},{128,2... | collective-permute-start | bytes 786440 | tf_op jit(solution)/shard_map/ppermute | solution.py:330
  65.5 2.0 %collective-permute-done.5.got = bf16[256,512]{1,0:T(8,128)(2,1)S(1)} collective-permute-done((bf16[256,512]{1,0:T(8,128)(2,1)S(1)}, bf16[256,512]{1,0:T(8,128)(2,1)S(1)}, u32[]{:S(2)}, u32[]{:S(2)}) %collective-permute-start.5) | collective-permute-done | bytes 262176 | tf_op jit(solution)/shard_map/ppermute | solution.py:330
  67.5 0.1 shard_map.82.b
  67.5 4.3 %collective-permute-start.7 = (bf16[256,512]{1,0:T(8,128)(2,1)S(1)}, bf16[256,512]{1,0:T(8,128)(2,1)S(1)}, u32[]{:S(2)}, u32[]{:S(2)}) collective-permute-start(bf16[256,512]{1,0:T(8,128)(2,1)S(1)} %shard_map.82.b), channel_id=1, source_target_pairs={{0,128},{1,385},{32,160},{33,417},{64,192},{65,449},{96,224},{97,4... | collective-permute-start | bytes 786440 | tf_op jit(solution)/shard_map/ppermute | solution.py:330
  71.8 0.0 copy-done.7
  71.9 0.2 select_reduce_fusion.table
  72.1 4.2 %all-to-all-done.1.source = bf16[32,72,128]{2,1,0:T(8,128)(2,1)S(1)} async-done(((bf16[32,72,128]{2,1,0:T(8,128)(2,1)}), bf16[32,72,128]{2,1,0:T(8,128)(2,1)S(1)}, u32[]{:S(2)}, u32[]{:S(2)}) %all-to-all-start.1) | async-done | bytes 589856 | tf_op jit(solution)/shard_map/all_to_all | solution.py:432
  76.3 1.4 %shard_map.76 = bf16[32,72,128]{2,1,0:T(8,128)(2,1)} custom-call(s32[32]{0:T(128)S(1)} %select_reduce_fusion.table, bf16[32,72,128]{2,1,0:T(8,128)(2,1)S(1)} %all-to-all-done.1.source), custom_call_target="tpu_custom_call" | custom-call | bytes 4194304 | tf_op jit(solution)/shard_map/pallas_call | solution.py:178
  77.7 4.1 %all-to-all-start.2 = ((bf16[16,2,72,128]{3,2,1,0:T(8,128)(2,1)}), bf16[16,2,72,128]{3,2,1,0:T(8,128)(2,1)S(1)}, u32[]{:S(2)}, u32[]{:S(2)}) async-start(bf16[16,2,72,128]{3,2,1,0:T(8,128)(2,1)} %bitcast.5), calls=%async_computation.2 | async-start | bytes 1179648 | tf_op jit(solution)/shard_map/all_to_all | solution.py:435
  81.8 0.0 collective-permute-done.6.r0
  81.8 0.0 collective-permute-done.7.r1
  81.8 0.8 shard_map.83
  82.6 10.1 %all-to-all-done.2.chunks = bf16[16,2,72,128]{3,2,1,0:T(8,128)(2,1)S(1)} async-done(((bf16[16,2,72,128]{3,2,1,0:T(8,128)(2,1)}), bf16[16,2,72,128]{3,2,1,0:T(8,128)(2,1)S(1)}, u32[]{:S(2)}, u32[]{:S(2)}) %all-to-all-start.2) | async-done | bytes 589856 | tf_op jit(solution)/shard_map/all_to_all | solution.py:435
  92.7 3.0 %shard_map.84 = bf16[512,512]{1,0:T(8,128)(2,1)S(1)} custom-call(bf16[16,2,72,128]{3,2,1,0:T(8,128)(2,1)S(1)} %all-to-all-done.2.chunks, bf16[512,512]{1,0:T(8,128)(2,1)S(1)} %get-tuple-element.36.gradient, bf16[512,512]{1,0:T(8,128)(2,1)S(1)} %get-tuple-element.37.left, bf16[512,512]{1,0:T(8,128)(2,1)S(1)} %get-tuple-element.38.right), custom_call_target="tpu_custom_call" | custom-call | flops 2147483648 | bytes 6291456 | tf_op jit(solution)/shard_map/pallas_call | solution.py:438
  95.7 12.8 %all_to_all.20.source = bf16[16,32,512]{2,1,0:T(8,128)(2,1)S(1)} all-to-all(bf16[16,32,512]{2,1,0:T(8,128)(2,1)S(1)} %bitcast.10), channel_id=1, replica_groups=mesh['dp'=16,'z'=16,'core'=2] {'dp'}, dimensions={0} | all-to-all | bytes 1048576 | tf_op jit(solution)/shard_map/all_to_all | solution.py:452
  108.5 0.7 shard_map.85
  (6 shorter events, 0.1 us)
Async XLA Ops:
  0.0 21.0 %copy-start.6 = (s32[160,2]{0,1:T(2,128)S(1)}, s32[160,2]{0,1:T(2,128)}, u32[]{:S(2)}) copy-start(s32[160,2]{0,1:T(2,128)} %param.9) | copy-start | bytes 3844
  2.2 19.3 %all-to-all-start = ((bf16[16,2,72,128]{3,2,1,0:T(8,128)(2,1)}), bf16[16,2,72,128]{3,2,1,0:T(8,128)(2,1)S(1)}, u32[]{:S(2)}, u32[]{:S(2)}) async-start(bf16[16,2,72,128]{3,2,1,0:T(8,128)(2,1)} %shard_map.73), calls=%async_computation | async-start | bytes 1179648 | tf_op jit(solution)/shard_map/all_to_all | solution.py:427
  13.4 26.5 %collective-permute-start = (bf16[3,256,512]{2,1,0:T(8,128)(2,1)}, bf16[3,256,512]{2,1,0:T(8,128)(2,1)S(1)}, u32[]{:S(2)}, u32[]{:S(2)}) collective-permute-start(bf16[3,256,512]{2,1,0:T(8,128)(2,1)} %get-tuple-element.22), channel_id=1, source_target_pairs={{0,128},{1,385},{32,160},{33,417},{64,192},{65,449},{96,224},{97,4... | collective-permute-start | bytes 2359304 | tf_op jit(solution)/shard_map/ppermute | solution.py:330
  17.9 28.2 %collective-permute-start.3 = (bf16[3,256,512]{2,1,0:T(8,128)(2,1)}, bf16[3,256,512]{2,1,0:T(8,128)(2,1)S(1)}, u32[]{:S(2)}, u32[]{:S(2)}) collective-permute-start(bf16[3,256,512]{2,1,0:T(8,128)(2,1)} %get-tuple-element.23), channel_id=1, source_target_pairs={{0,96},{1,33},{32,64},{33,1},{64,32},{65,97},{96,0},{97,65},{128,2... | collective-permute-start | bytes 2359304 | tf_op jit(solution)/shard_map/ppermute | solution.py:330
  21.5 19.4 %copy-start.2 = (s32[256]{0:T(256)S(1)}, s32[256]{0:T(256)}, u32[]{:S(2)}) copy-start(s32[256]{0:T(256)} %constant.55.clone.table) | copy-start | bytes 3076
  22.9 53.3 %all-to-all-start.1 = ((bf16[32,72,128]{2,1,0:T(8,128)(2,1)}), bf16[32,72,128]{2,1,0:T(8,128)(2,1)S(1)}, u32[]{:S(2)}, u32[]{:S(2)}) async-start(bf16[32,72,128]{2,1,0:T(8,128)(2,1)} %shard_map.75), calls=%async_computation.1 | async-start | bytes 1179648 | tf_op jit(solution)/shard_map/all_to_all | solution.py:432
  40.0 0.9 copy-start.4
  40.9 1.1 %copy-start.3 = (bf16[3,256,512]{2,1,0:T(8,128)(2,1)S(1)}, bf16[3,256,512]{2,1,0:T(8,128)(2,1)}, u32[]{:S(2)}) copy-start(bf16[3,256,512]{2,1,0:T(8,128)(2,1)} %get-tuple-element.25.kept) | copy-start | bytes 2359300
  42.0 1.1 %copy-start.5 = (bf16[3,256,512]{2,1,0:T(8,128)(2,1)S(1)}, bf16[3,256,512]{2,1,0:T(8,128)(2,1)}, u32[]{:S(2)}) copy-start(bf16[3,256,512]{2,1,0:T(8,128)(2,1)} %copy-done.4) | copy-start | bytes 2359300
  43.2 3.0 %copy-start = (bf16[3,256,512]{2,1,0:T(8,128)(2,1)S(1)}, bf16[3,256,512]{2,1,0:T(8,128)(2,1)}, u32[]{:S(2)}) copy-start(bf16[3,256,512]{2,1,0:T(8,128)(2,1)} %get-tuple-element.30.kept) | copy-start | bytes 2359300
  43.2 11.0 %copy-start.1 = (s32[128]{0:T(128)S(1)}, s32[128]{0:T(128)}, u32[]{:S(2)}) copy-start(s32[128]{0:T(128)} %constant.56.clone.table) | copy-start | bytes 1540
  44.0 10.2 %collective-permute-start.1 = (bf16[2,256,512]{2,1,0:T(8,128)(2,1)S(1)}, bf16[2,256,512]{2,1,0:T(8,128)(2,1)S(1)}, u32[]{:S(2)}, u32[]{:S(2)}) collective-permute-start(bf16[2,256,512]{2,1,0:T(8,128)(2,1)S(1)} %get-tuple-element.27), channel_id=1, source_target_pairs={{0,384},{1,129},{32,416},{33,161},{64,448},{65,193},{96,480},{97,2... | collective-permute-start | bytes 1572872 | tf_op jit(solution)/shard_map/ppermute | solution.py:330
  46.2 25.6 %copy-start.7 = (s32[2,32]{1,0:T(2,128)S(1)}, s32[2,32]{1,0:T(2,128)}, u32[]{:S(2)}) copy-start(s32[2,32]{1,0:T(2,128)} %constant.57.clone) | copy-start | bytes 772
  47.7 11.6 %collective-permute-start.4 = (bf16[2,256,512]{2,1,0:T(8,128)(2,1)}, bf16[2,256,512]{2,1,0:T(8,128)(2,1)S(1)}, u32[]{:S(2)}, u32[]{:S(2)}) collective-permute-start(bf16[2,256,512]{2,1,0:T(8,128)(2,1)} %get-tuple-element.33), channel_id=1, source_target_pairs={{0,32},{1,97},{32,0},{33,65},{64,96},{65,33},{96,64},{97,1},{128,1... | collective-permute-start | bytes 1572872 | tf_op jit(solution)/shard_map/ppermute | solution.py:330
  54.9 8.6 %collective-permute-start.2 = (bf16[256,512]{1,0:T(8,128)(2,1)S(1)}, bf16[256,512]{1,0:T(8,128)(2,1)S(1)}, u32[]{:S(2)}, u32[]{:S(2)}) collective-permute-start(bf16[256,512]{1,0:T(8,128)(2,1)S(1)} %get-tuple-element.29), channel_id=1, source_target_pairs={{0,32},{1,97},{32,0},{33,65},{64,96},{65,33},{96,64},{97,1},{128,1... | collective-permute-start | bytes 786440 | tf_op jit(solution)/shard_map/ppermute | solution.py:330
  60.0 7.4 %collective-permute-start.5 = (bf16[256,512]{1,0:T(8,128)(2,1)S(1)}, bf16[256,512]{1,0:T(8,128)(2,1)S(1)}, u32[]{:S(2)}, u32[]{:S(2)}) collective-permute-start(bf16[256,512]{1,0:T(8,128)(2,1)S(1)} %get-tuple-element.35), channel_id=1, source_target_pairs={{0,384},{1,129},{32,416},{33,161},{64,448},{65,193},{96,480},{97,2... | collective-permute-start | bytes 786440 | tf_op jit(solution)/shard_map/ppermute | solution.py:330
  63.6 18.2 %collective-permute-start.6 = (bf16[256,512]{1,0:T(8,128)(2,1)S(1)}, bf16[256,512]{1,0:T(8,128)(2,1)S(1)}, u32[]{:S(2)}, u32[]{:S(2)}) collective-permute-start(bf16[256,512]{1,0:T(8,128)(2,1)S(1)} %shard_map.79.a), channel_id=1, source_target_pairs={{0,96},{1,33},{32,64},{33,1},{64,32},{65,97},{96,0},{97,65},{128,2... | collective-permute-start | bytes 786440 | tf_op jit(solution)/shard_map/ppermute | solution.py:330
  67.5 14.3 %collective-permute-start.7 = (bf16[256,512]{1,0:T(8,128)(2,1)S(1)}, bf16[256,512]{1,0:T(8,128)(2,1)S(1)}, u32[]{:S(2)}, u32[]{:S(2)}) collective-permute-start(bf16[256,512]{1,0:T(8,128)(2,1)S(1)} %shard_map.82.b), channel_id=1, source_target_pairs={{0,128},{1,385},{32,160},{33,417},{64,192},{65,449},{96,224},{97,4... | collective-permute-start | bytes 786440 | tf_op jit(solution)/shard_map/ppermute | solution.py:330
  77.7 15.0 %all-to-all-start.2 = ((bf16[16,2,72,128]{3,2,1,0:T(8,128)(2,1)}), bf16[16,2,72,128]{3,2,1,0:T(8,128)(2,1)S(1)}, u32[]{:S(2)}, u32[]{:S(2)}) async-start(bf16[16,2,72,128]{3,2,1,0:T(8,128)(2,1)} %bitcast.5), calls=%async_computation.2 | async-start | bytes 1179648 | tf_op jit(solution)/shard_map/all_to_all | solution.py:435

commit v10 on v9

--- a/solution.py
+++ b/solution.py
@@ -383,7 +383,7 @@
         in_specs=[VMEM] * 4,
         out_specs=[VMEM] * 3,
         compiler_params=params(16),
-        cost_estimate=cost(long_flops // 2, 4 * small),
+        cost_estimate=cost(7 * 10**9, 4 * small),
     )(*sent, *got)
 
 

time: 111 us -> 111 us (level)
  no operation moved by 1% of the time
where the time goes in v10:
time: 111 us; the launch traced here: 109 us
  starting transfers between devices  51.9 us (47%)
  waiting for transfers between devices  23.3 us (21%)
  Pallas kernels  16.9 us (15%)
  blocking collectives  12.8 us (12%)
  local copies, waits for them, and re-layouts  3.46 us (3%)
    ppermute x8, starting transfers between devices, exchange(): return lax.ppermute(array, ('dp', 'core'), pairs(portion, step))  23.2 us
    all_to_all x1, starting transfers between devices, body(): lax.all_to_all(lanes, ('z', 'core'), split_axis=0, concat_axis=0, tiled=T...  17 us
    all_to_all x1, blocking collectives, body(): rows = lax.all_to_all(rows, 'dp', split_axis=0, concat_axis=0, tiled=True)  12.8 us
    all_to_all x1, waiting for transfers between devices, body(): lax.all_to_all(lanes, 'dp', split_axis=0, concat_axis=0, tiled=True)  10.1 us
    ppermute x8, waiting for transfers between devices, exchange(): return lax.ppermute(array, ('dp', 'core'), pairs(portion, step))  8.93 us
    all_to_all x1, starting transfers between devices, body(): lax.all_to_all(packed, 'dp', split_axis=0, concat_axis=0, tiled=True)  7.6 us
    all_to_all x1, waiting for transfers between devices, body(): lax.all_to_all(lanes, ('z', 'core'), split_axis=0, concat_axis=0, tiled=T...  4.2 us
    all_to_all x1, starting transfers between devices, body(): lax.all_to_all(lanes, 'dp', split_axis=0, concat_axis=0, tiled=True)  4.08 us
  transfers between devices with their start and end apart: 11, of which 6 were waited for; matrix products, arithmetic and copies ran while one was open for 1% of the time, Pallas kernels for 10%

profile of v10, /device:TPU:1, one launch (start us, length us, event | category | flops | bytes accessed | tf_op | source)
XLA Modules:
  0.0 109.2 jit_solution(11529300744370041957)
XLA Ops:
  0.0 0.0 copy-start.6
  0.0 2.2 %shard_map.73 = bf16[16,2,72,128]{3,2,1,0:T(8,128)(2,1)} custom-call(f32[2,512,512]{2,1,0:T(8,128)} %bitcast.12), custom_call_target="tpu_custom_call" | custom-call | bytes 3145728 | tf_op jit(solution)/shard_map/pallas_call | solution.py:413
  2.2 7.6 %all-to-all-start = ((bf16[16,2,72,128]{3,2,1,0:T(8,128)(2,1)}), bf16[16,2,72,128]{3,2,1,0:T(8,128)(2,1)S(1)}, u32[]{:S(2)}, u32[]{:S(2)}) async-start(bf16[16,2,72,128]{3,2,1,0:T(8,128)(2,1)} %shard_map.73), calls=%async_computation | async-start | bytes 1179648 | tf_op jit(solution)/shard_map/all_to_all | solution.py:427
  9.8 3.6 %shard_map.74 = (bf16[3,256,512]{2,1,0:T(8,128)(2,1)}, bf16[3,256,512]{2,1,0:T(8,128)(2,1)}, bf16[3,256,512]{2,1,0:T(8,128)(2,1)}, bf16[3,256,512]{2,1,0:T(8,128)(2,1)}) custom-call(s32[384]{0:T(512)} %constant.54.clone.table, bf16[5,512,512]{2,1,0:T(8,128)(2,1)} %bitcast.11), custom_call_target="tpu_custom_call" | custom-call | bytes 3145728 | tf_op jit(solution)/shard_map/pallas_call | solution.py:335
  13.4 4.5 %collective-permute-start = (bf16[3,256,512]{2,1,0:T(8,128)(2,1)}, bf16[3,256,512]{2,1,0:T(8,128)(2,1)S(1)}, u32[]{:S(2)}, u32[]{:S(2)}) collective-permute-start(bf16[3,256,512]{2,1,0:T(8,128)(2,1)} %get-tuple-element.22), channel_id=1, source_target_pairs={{0,128},{1,385},{32,160},{33,417},{64,192},{65,449},{96,224},{97,4... | collective-permute-start | bytes 2359304 | tf_op jit(solution)/shard_map/ppermute | solution.py:330
  17.9 3.1 %collective-permute-start.3 = (bf16[3,256,512]{2,1,0:T(8,128)(2,1)}, bf16[3,256,512]{2,1,0:T(8,128)(2,1)S(1)}, u32[]{:S(2)}, u32[]{:S(2)}) collective-permute-start(bf16[3,256,512]{2,1,0:T(8,128)(2,1)} %get-tuple-element.23), channel_id=1, source_target_pairs={{0,96},{1,33},{32,64},{33,1},{64,32},{65,97},{96,0},{97,65},{128,2... | collective-permute-start | bytes 2359304 | tf_op jit(solution)/shard_map/ppermute | solution.py:330
  21.0 0.0 copy-done.6
  21.1 0.1 reduce_max.14
  21.2 0.1 reduce_max.18
  21.3 0.2 convert_reduce_fusion
  21.5 0.0 all-to-all-done
  21.5 0.0 copy-start.2
  21.5 1.4 %shard_map.75 = bf16[32,72,128]{2,1,0:T(8,128)(2,1)} custom-call(s32[32]{0:T(128)S(1)} %compare_select_fusion.1.table, bf16[32,72,128]{2,1,0:T(8,128)(2,1)S(1)} %bitcast.9), custom_call_target="tpu_custom_call" | custom-call | flops 33333334016 | bytes 4194304 | tf_op jit(solution)/shard_map/pallas_call | solution.py:178
  22.9 17.0 %all-to-all-start.1 = ((bf16[32,72,128]{2,1,0:T(8,128)(2,1)}), bf16[32,72,128]{2,1,0:T(8,128)(2,1)S(1)}, u32[]{:S(2)}, u32[]{:S(2)}) async-start(bf16[32,72,128]{2,1,0:T(8,128)(2,1)} %shard_map.75), calls=%async_computation.1 | async-start | bytes 1179648 | tf_op jit(solution)/shard_map/all_to_all | solution.py:432
  40.0 0.0 collective-permute-done.got
  40.0 0.0 copy-start.4
  40.0 0.9 copy-done.4
  40.9 0.0 copy-done.2
  40.9 0.0 copy-start.3
  40.9 1.1 %copy-done.3 = bf16[3,256,512]{2,1,0:T(8,128)(2,1)S(1)} copy-done((bf16[3,256,512]{2,1,0:T(8,128)(2,1)S(1)}, bf16[3,256,512]{2,1,0:T(8,128)(2,1)}, u32[]{:S(2)}) %copy-start.3) | copy-done | bytes 786456
  42.0 0.0 copy-start.5
  42.0 1.1 %copy-done.5 = bf16[3,256,512]{2,1,0:T(8,128)(2,1)S(1)} copy-done((bf16[3,256,512]{2,1,0:T(8,128)(2,1)S(1)}, bf16[3,256,512]{2,1,0:T(8,128)(2,1)}, u32[]{:S(2)}) %copy-start.5) | copy-done | bytes 786456
  43.2 0.0 copy-start
  43.2 0.0 copy-start.1
  43.2 0.8 shard_map.77
  44.0 2.2 %collective-permute-start.1 = (bf16[2,256,512]{2,1,0:T(8,128)(2,1)S(1)}, bf16[2,256,512]{2,1,0:T(8,128)(2,1)S(1)}, u32[]{:S(2)}, u32[]{:S(2)}) collective-permute-start(bf16[2,256,512]{2,1,0:T(8,128)(2,1)S(1)} %get-tuple-element.27), channel_id=1, source_target_pairs={{0,384},{1,129},{32,416},{33,161},{64,448},{65,193},{96,480},{97,2... | collective-permute-start | bytes 1572872 | tf_op jit(solution)/shard_map/ppermute | solution.py:330
  46.2 0.0 collective-permute-done.3.got
  46.2 0.0 copy-done
  46.2 0.0 copy-start.7
  46.2 1.5 %shard_map.80 = (bf16[2,256,512]{2,1,0:T(8,128)(2,1)}, bf16[2,256,512]{2,1,0:T(8,128)(2,1)S(1)}) custom-call(s32[256]{0:T(256)S(1)} %copy-done.2, bf16[3,256,512]{2,1,0:T(8,128)(2,1)S(1)} %copy-done, bf16[3,256,512]{2,1,0:T(8,128)(2,1)S(1)} %collective-permute-done.3.got), custom_call_target="tpu_custom_call" | custom-call | bytes 2097152 | tf_op jit(solution)/shard_map/pallas_call | solution.py:353
  47.7 1.9 %collective-permute-start.4 = (bf16[2,256,512]{2,1,0:T(8,128)(2,1)}, bf16[2,256,512]{2,1,0:T(8,128)(2,1)S(1)}, u32[]{:S(2)}, u32[]{:S(2)}) collective-permute-start(bf16[2,256,512]{2,1,0:T(8,128)(2,1)} %get-tuple-element.33), channel_id=1, source_target_pairs={{0,32},{1,97},{32,0},{33,65},{64,96},{65,33},{96,64},{97,1},{128,1... | collective-permute-start | bytes 1572872 | tf_op jit(solution)/shard_map/ppermute | solution.py:330
  49.6 0.1 copy.9
  49.8 0.1 reshape.16
  49.8 4.4 %collective-permute-done.1.got = bf16[2,256,512]{2,1,0:T(8,128)(2,1)S(1)} collective-permute-done((bf16[2,256,512]{2,1,0:T(8,128)(2,1)S(1)}, bf16[2,256,512]{2,1,0:T(8,128)(2,1)S(1)}, u32[]{:S(2)}, u32[]{:S(2)}) %collective-permute-start.1) | collective-permute-done | bytes 524320 | tf_op jit(solution)/shard_map/ppermute | solution.py:330
  54.2 0.0 copy-done.1
  54.2 0.7 shard_map.78
  54.9 2.2 %collective-permute-start.2 = (bf16[256,512]{1,0:T(8,128)(2,1)S(1)}, bf16[256,512]{1,0:T(8,128)(2,1)S(1)}, u32[]{:S(2)}, u32[]{:S(2)}) collective-permute-start(bf16[256,512]{1,0:T(8,128)(2,1)S(1)} %get-tuple-element.29), channel_id=1, source_target_pairs={{0,32},{1,97},{32,0},{33,65},{64,96},{65,33},{96,64},{97,1},{128,1... | collective-permute-start | bytes 786440 | tf_op jit(solution)/shard_map/ppermute | solution.py:330
  57.1 2.3 %collective-permute-done.4.got = bf16[2,256,512]{2,1,0:T(8,128)(2,1)S(1)} collective-permute-done((bf16[2,256,512]{2,1,0:T(8,128)(2,1)}, bf16[2,256,512]{2,1,0:T(8,128)(2,1)S(1)}, u32[]{:S(2)}, u32[]{:S(2)}) %collective-permute-start.4) | collective-permute-done | bytes 524320 | tf_op jit(solution)/shard_map/ppermute | solution.py:330
  59.4 0.7 shard_map.81
  60.0 3.1 %collective-permute-start.5 = (bf16[256,512]{1,0:T(8,128)(2,1)S(1)}, bf16[256,512]{1,0:T(8,128)(2,1)S(1)}, u32[]{:S(2)}, u32[]{:S(2)}) collective-permute-start(bf16[256,512]{1,0:T(8,128)(2,1)S(1)} %get-tuple-element.35), channel_id=1, source_target_pairs={{0,384},{1,129},{32,416},{33,161},{64,448},{65,193},{96,480},{97,2... | collective-permute-start | bytes 786440 | tf_op jit(solution)/shard_map/ppermute | solution.py:330
  63.2 0.3 collective-permute-done.2.got
  63.5 0.1 shard_map.79.a
  63.6 1.9 %collective-permute-start.6 = (bf16[256,512]{1,0:T(8,128)(2,1)S(1)}, bf16[256,512]{1,0:T(8,128)(2,1)S(1)}, u32[]{:S(2)}, u32[]{:S(2)}) collective-permute-start(bf16[256,512]{1,0:T(8,128)(2,1)S(1)} %shard_map.79.a), channel_id=1, source_target_pairs={{0,96},{1,33},{32,64},{33,1},{64,32},{65,97},{96,0},{97,65},{128,2... | collective-permute-start | bytes 786440 | tf_op jit(solution)/shard_map/ppermute | solution.py:330
  65.5 2.0 %collective-permute-done.5.got = bf16[256,512]{1,0:T(8,128)(2,1)S(1)} collective-permute-done((bf16[256,512]{1,0:T(8,128)(2,1)S(1)}, bf16[256,512]{1,0:T(8,128)(2,1)S(1)}, u32[]{:S(2)}, u32[]{:S(2)}) %collective-permute-start.5) | collective-permute-done | bytes 262176 | tf_op jit(solution)/shard_map/ppermute | solution.py:330
  67.5 0.1 shard_map.82.b
  67.5 4.3 %collective-permute-start.7 = (bf16[256,512]{1,0:T(8,128)(2,1)S(1)}, bf16[256,512]{1,0:T(8,128)(2,1)S(1)}, u32[]{:S(2)}, u32[]{:S(2)}) collective-permute-start(bf16[256,512]{1,0:T(8,128)(2,1)S(1)} %shard_map.82.b), channel_id=1, source_target_pairs={{0,128},{1,385},{32,160},{33,417},{64,192},{65,449},{96,224},{97,4... | collective-permute-start | bytes 786440 | tf_op jit(solution)/shard_map/ppermute | solution.py:330
  71.8 0.0 copy-done.7
  71.9 0.2 select_reduce_fusion.table
  72.1 4.2 %all-to-all-done.1.source = bf16[32,72,128]{2,1,0:T(8,128)(2,1)S(1)} async-done(((bf16[32,72,128]{2,1,0:T(8,128)(2,1)}), bf16[32,72,128]{2,1,0:T(8,128)(2,1)S(1)}, u32[]{:S(2)}, u32[]{:S(2)}) %all-to-all-start.1) | async-done | bytes 589856 | tf_op jit(solution)/shard_map/all_to_all | solution.py:432
  76.3 1.4 %shard_map.76 = bf16[32,72,128]{2,1,0:T(8,128)(2,1)} custom-call(s32[32]{0:T(128)S(1)} %select_reduce_fusion.table, bf16[32,72,128]{2,1,0:T(8,128)(2,1)S(1)} %all-to-all-done.1.source), custom_call_target="tpu_custom_call" | custom-call | bytes 4194304 | tf_op jit(solution)/shard_map/pallas_call | solution.py:178
  77.7 4.1 %all-to-all-start.2 = ((bf16[16,2,72,128]{3,2,1,0:T(8,128)(2,1)}), bf16[16,2,72,128]{3,2,1,0:T(8,128)(2,1)S(1)}, u32[]{:S(2)}, u32[]{:S(2)}) async-start(bf16[16,2,72,128]{3,2,1,0:T(8,128)(2,1)} %bitcast.5), calls=%async_computation.2 | async-start | bytes 1179648 | tf_op jit(solution)/shard_map/all_to_all | solution.py:435
  81.8 0.0 collective-permute-done.6.r0
  81.8 0.0 collective-permute-done.7.r1
  81.8 0.8 shard_map.83
  82.6 10.1 %all-to-all-done.2.chunks = bf16[16,2,72,128]{3,2,1,0:T(8,128)(2,1)S(1)} async-done(((bf16[16,2,72,128]{3,2,1,0:T(8,128)(2,1)}), bf16[16,2,72,128]{3,2,1,0:T(8,128)(2,1)S(1)}, u32[]{:S(2)}, u32[]{:S(2)}) %all-to-all-start.2) | async-done | bytes 589856 | tf_op jit(solution)/shard_map/all_to_all | solution.py:435
  92.7 3.0 %shard_map.84 = bf16[512,512]{1,0:T(8,128)(2,1)S(1)} custom-call(bf16[16,2,72,128]{3,2,1,0:T(8,128)(2,1)S(1)} %all-to-all-done.2.chunks, bf16[512,512]{1,0:T(8,128)(2,1)S(1)} %get-tuple-element.36.gradient, bf16[512,512]{1,0:T(8,128)(2,1)S(1)} %get-tuple-element.37.left, bf16[512,512]{1,0:T(8,128)(2,1)S(1)} %get-tuple-element.38.right), custom_call_target="tpu_custom_call" | custom-call | flops 2147483648 | bytes 6291456 | tf_op jit(solution)/shard_map/pallas_call | solution.py:438
  95.7 12.8 %all_to_all.20.source = bf16[16,32,512]{2,1,0:T(8,128)(2,1)S(1)} all-to-all(bf16[16,32,512]{2,1,0:T(8,128)(2,1)S(1)} %bitcast.10), channel_id=1, replica_groups=mesh['dp'=16,'z'=16,'core'=2] {'dp'}, dimensions={0} | all-to-all | bytes 1048576 | tf_op jit(solution)/shard_map/all_to_all | solution.py:452
  108.5 0.7 shard_map.85
  (6 shorter events, 0.1 us)
Async XLA Ops:
  0.0 21.0 %copy-start.6 = (s32[160,2]{0,1:T(2,128)S(1)}, s32[160,2]{0,1:T(2,128)}, u32[]{:S(2)}) copy-start(s32[160,2]{0,1:T(2,128)} %param.9) | copy-start | bytes 3844
  2.2 19.3 %all-to-all-start = ((bf16[16,2,72,128]{3,2,1,0:T(8,128)(2,1)}), bf16[16,2,72,128]{3,2,1,0:T(8,128)(2,1)S(1)}, u32[]{:S(2)}, u32[]{:S(2)}) async-start(bf16[16,2,72,128]{3,2,1,0:T(8,128)(2,1)} %shard_map.73), calls=%async_computation | async-start | bytes 1179648 | tf_op jit(solution)/shard_map/all_to_all | solution.py:427
  13.4 26.5 %collective-permute-start = (bf16[3,256,512]{2,1,0:T(8,128)(2,1)}, bf16[3,256,512]{2,1,0:T(8,128)(2,1)S(1)}, u32[]{:S(2)}, u32[]{:S(2)}) collective-permute-start(bf16[3,256,512]{2,1,0:T(8,128)(2,1)} %get-tuple-element.22), channel_id=1, source_target_pairs={{0,128},{1,385},{32,160},{33,417},{64,192},{65,449},{96,224},{97,4... | collective-permute-start | bytes 2359304 | tf_op jit(solution)/shard_map/ppermute | solution.py:330
  17.9 28.2 %collective-permute-start.3 = (bf16[3,256,512]{2,1,0:T(8,128)(2,1)}, bf16[3,256,512]{2,1,0:T(8,128)(2,1)S(1)}, u32[]{:S(2)}, u32[]{:S(2)}) collective-permute-start(bf16[3,256,512]{2,1,0:T(8,128)(2,1)} %get-tuple-element.23), channel_id=1, source_target_pairs={{0,96},{1,33},{32,64},{33,1},{64,32},{65,97},{96,0},{97,65},{128,2... | collective-permute-start | bytes 2359304 | tf_op jit(solution)/shard_map/ppermute | solution.py:330
  21.5 19.4 %copy-start.2 = (s32[256]{0:T(256)S(1)}, s32[256]{0:T(256)}, u32[]{:S(2)}) copy-start(s32[256]{0:T(256)} %constant.55.clone.table) | copy-start | bytes 3076
  22.9 53.3 %all-to-all-start.1 = ((bf16[32,72,128]{2,1,0:T(8,128)(2,1)}), bf16[32,72,128]{2,1,0:T(8,128)(2,1)S(1)}, u32[]{:S(2)}, u32[]{:S(2)}) async-start(bf16[32,72,128]{2,1,0:T(8,128)(2,1)} %shard_map.75), calls=%async_computation.1 | async-start | bytes 1179648 | tf_op jit(solution)/shard_map/all_to_all | solution.py:432
  40.0 0.9 copy-start.4
  40.9 1.1 %copy-start.3 = (bf16[3,256,512]{2,1,0:T(8,128)(2,1)S(1)}, bf16[3,256,512]{2,1,0:T(8,128)(2,1)}, u32[]{:S(2)}) copy-start(bf16[3,256,512]{2,1,0:T(8,128)(2,1)} %get-tuple-element.25.kept) | copy-start | bytes 2359300
  42.0 1.1 %copy-start.5 = (bf16[3,256,512]{2,1,0:T(8,128)(2,1)S(1)}, bf16[3,256,512]{2,1,0:T(8,128)(2,1)}, u32[]{:S(2)}) copy-start(bf16[3,256,512]{2,1,0:T(8,128)(2,1)} %copy-done.4) | copy-start | bytes 2359300
  43.2 3.0 %copy-start = (bf16[3,256,512]{2,1,0:T(8,128)(2,1)S(1)}, bf16[3,256,512]{2,1,0:T(8,128)(2,1)}, u32[]{:S(2)}) copy-start(bf16[3,256,512]{2,1,0:T(8,128)(2,1)} %get-tuple-element.30.kept) | copy-start | bytes 2359300
  43.2 11.0 %copy-start.1 = (s32[128]{0:T(128)S(1)}, s32[128]{0:T(128)}, u32[]{:S(2)}) copy-start(s32[128]{0:T(128)} %constant.56.clone.table) | copy-start | bytes 1540
  44.0 10.2 %collective-permute-start.1 = (bf16[2,256,512]{2,1,0:T(8,128)(2,1)S(1)}, bf16[2,256,512]{2,1,0:T(8,128)(2,1)S(1)}, u32[]{:S(2)}, u32[]{:S(2)}) collective-permute-start(bf16[2,256,512]{2,1,0:T(8,128)(2,1)S(1)} %get-tuple-element.27), channel_id=1, source_target_pairs={{0,384},{1,129},{32,416},{33,161},{64,448},{65,193},{96,480},{97,2... | collective-permute-start | bytes 1572872 | tf_op jit(solution)/shard_map/ppermute | solution.py:330
  46.2 25.6 %copy-start.7 = (s32[2,32]{1,0:T(2,128)S(1)}, s32[2,32]{1,0:T(2,128)}, u32[]{:S(2)}) copy-start(s32[2,32]{1,0:T(2,128)} %constant.57.clone) | copy-start | bytes 772
  47.7 11.6 %collective-permute-start.4 = (bf16[2,256,512]{2,1,0:T(8,128)(2,1)}, bf16[2,256,512]{2,1,0:T(8,128)(2,1)S(1)}, u32[]{:S(2)}, u32[]{:S(2)}) collective-permute-start(bf16[2,256,512]{2,1,0:T(8,128)(2,1)} %get-tuple-element.33), channel_id=1, source_target_pairs={{0,32},{1,97},{32,0},{33,65},{64,96},{65,33},{96,64},{97,1},{128,1... | collective-permute-start | bytes 1572872 | tf_op jit(solution)/shard_map/ppermute | solution.py:330
  54.9 8.6 %collective-permute-start.2 = (bf16[256,512]{1,0:T(8,128)(2,1)S(1)}, bf16[256,512]{1,0:T(8,128)(2,1)S(1)}, u32[]{:S(2)}, u32[]{:S(2)}) collective-permute-start(bf16[256,512]{1,0:T(8,128)(2,1)S(1)} %get-tuple-element.29), channel_id=1, source_target_pairs={{0,32},{1,97},{32,0},{33,65},{64,96},{65,33},{96,64},{97,1},{128,1... | collective-permute-start | bytes 786440 | tf_op jit(solution)/shard_map/ppermute | solution.py:330
  60.0 7.4 %collective-permute-start.5 = (bf16[256,512]{1,0:T(8,128)(2,1)S(1)}, bf16[256,512]{1,0:T(8,128)(2,1)S(1)}, u32[]{:S(2)}, u32[]{:S(2)}) collective-permute-start(bf16[256,512]{1,0:T(8,128)(2,1)S(1)} %get-tuple-element.35), channel_id=1, source_target_pairs={{0,384},{1,129},{32,416},{33,161},{64,448},{65,193},{96,480},{97,2... | collective-permute-start | bytes 786440 | tf_op jit(solution)/shard_map/ppermute | solution.py:330
  63.6 18.2 %collective-permute-start.6 = (bf16[256,512]{1,0:T(8,128)(2,1)S(1)}, bf16[256,512]{1,0:T(8,128)(2,1)S(1)}, u32[]{:S(2)}, u32[]{:S(2)}) collective-permute-start(bf16[256,512]{1,0:T(8,128)(2,1)S(1)} %shard_map.79.a), channel_id=1, source_target_pairs={{0,96},{1,33},{32,64},{33,1},{64,32},{65,97},{96,0},{97,65},{128,2... | collective-permute-start | bytes 786440 | tf_op jit(solution)/shard_map/ppermute | solution.py:330
  67.5 14.3 %collective-permute-start.7 = (bf16[256,512]{1,0:T(8,128)(2,1)S(1)}, bf16[256,512]{1,0:T(8,128)(2,1)S(1)}, u32[]{:S(2)}, u32[]{:S(2)}) collective-permute-start(bf16[256,512]{1,0:T(8,128)(2,1)S(1)} %shard_map.82.b), channel_id=1, source_target_pairs={{0,128},{1,385},{32,160},{33,417},{64,192},{65,449},{96,224},{97,4... | collective-permute-start | bytes 786440 | tf_op jit(solution)/shard_map/ppermute | solution.py:330
  77.7 15.0 %all-to-all-start.2 = ((bf16[16,2,72,128]{3,2,1,0:T(8,128)(2,1)}), bf16[16,2,72,128]{3,2,1,0:T(8,128)(2,1)S(1)}, u32[]{:S(2)}, u32[]{:S(2)}) async-start(bf16[16,2,72,128]{3,2,1,0:T(8,128)(2,1)} %bitcast.5), calls=%async_computation.2 | async-start | bytes 1179648 | tf_op jit(solution)/shard_map/all_to_all | solution.py:435

commit v11 on v10

--- a/solution.py
+++ b/solution.py
@@ -383,7 +383,7 @@
         in_specs=[VMEM] * 4,
         out_specs=[VMEM] * 3,
         compiler_params=params(16),
-        cost_estimate=cost(7 * 10**9, 4 * small),
+        cost_estimate=cost(35 * 10**8, 4 * small),
     )(*sent, *got)
 
 

time: 111 us -> 111 us (level)
  no operation moved by 1% of the time
where the time goes in v11:
time: 111 us; the launch traced here: 109 us
  starting transfers between devices  51.9 us (47%)
  waiting for transfers between devices  23.3 us (21%)
  Pallas kernels  16.9 us (15%)
  blocking collectives  12.8 us (12%)
  local copies, waits for them, and re-layouts  3.46 us (3%)
    ppermute x8, starting transfers between devices, exchange(): return lax.ppermute(array, ('dp', 'core'), pairs(portion, step))  23.2 us
    all_to_all x1, starting transfers between devices, body(): lax.all_to_all(lanes, ('z', 'core'), split_axis=0, concat_axis=0, tiled=T...  17 us
    all_to_all x1, blocking collectives, body(): rows = lax.all_to_all(rows, 'dp', split_axis=0, concat_axis=0, tiled=True)  12.8 us
    all_to_all x1, waiting for transfers between devices, body(): lax.all_to_all(lanes, 'dp', split_axis=0, concat_axis=0, tiled=True)  10.1 us
    ppermute x8, waiting for transfers between devices, exchange(): return lax.ppermute(array, ('dp', 'core'), pairs(portion, step))  8.87 us
    all_to_all x1, starting transfers between devices, body(): lax.all_to_all(packed, 'dp', split_axis=0, concat_axis=0, tiled=True)  7.6 us
    all_to_all x1, waiting for transfers between devices, body(): lax.all_to_all(lanes, ('z', 'core'), split_axis=0, concat_axis=0, tiled=T...  4.25 us
    all_to_all x1, starting transfers between devices, body(): lax.all_to_all(lanes, 'dp', split_axis=0, concat_axis=0, tiled=True)  4.08 us
  transfers between devices with their start and end apart: 11, of which 6 were waited for; matrix products, arithmetic and copies ran while one was open for 1% of the time, Pallas kernels for 10%

profile of v11, /device:TPU:1, one launch (start us, length us, event | category | flops | bytes accessed | tf_op | source)
XLA Modules:
  0.0 109.2 jit_solution(6767009216551019495)
XLA Ops:
  0.0 0.0 copy-start.6
  0.0 2.2 %shard_map.73 = bf16[16,2,72,128]{3,2,1,0:T(8,128)(2,1)} custom-call(f32[2,512,512]{2,1,0:T(8,128)} %bitcast.12), custom_call_target="tpu_custom_call" | custom-call | bytes 3145728 | tf_op jit(solution)/shard_map/pallas_call | solution.py:413
  2.2 7.6 %all-to-all-start = ((bf16[16,2,72,128]{3,2,1,0:T(8,128)(2,1)}), bf16[16,2,72,128]{3,2,1,0:T(8,128)(2,1)S(1)}, u32[]{:S(2)}, u32[]{:S(2)}) async-start(bf16[16,2,72,128]{3,2,1,0:T(8,128)(2,1)} %shard_map.73), calls=%async_computation | async-start | bytes 1179648 | tf_op jit(solution)/shard_map/all_to_all | solution.py:427
  9.8 3.6 %shard_map.74 = (bf16[3,256,512]{2,1,0:T(8,128)(2,1)}, bf16[3,256,512]{2,1,0:T(8,128)(2,1)}, bf16[3,256,512]{2,1,0:T(8,128)(2,1)}, bf16[3,256,512]{2,1,0:T(8,128)(2,1)}) custom-call(s32[384]{0:T(512)} %constant.54.clone.table, bf16[5,512,512]{2,1,0:T(8,128)(2,1)} %bitcast.11), custom_call_target="tpu_custom_call" | custom-call | bytes 3145728 | tf_op jit(solution)/shard_map/pallas_call | solution.py:335
  13.4 4.5 %collective-permute-start = (bf16[3,256,512]{2,1,0:T(8,128)(2,1)}, bf16[3,256,512]{2,1,0:T(8,128)(2,1)S(1)}, u32[]{:S(2)}, u32[]{:S(2)}) collective-permute-start(bf16[3,256,512]{2,1,0:T(8,128)(2,1)} %get-tuple-element.22), channel_id=1, source_target_pairs={{0,128},{1,385},{32,160},{33,417},{64,192},{65,449},{96,224},{97,4... | collective-permute-start | bytes 2359304 | tf_op jit(solution)/shard_map/ppermute | solution.py:330
  17.9 3.1 %collective-permute-start.3 = (bf16[3,256,512]{2,1,0:T(8,128)(2,1)}, bf16[3,256,512]{2,1,0:T(8,128)(2,1)S(1)}, u32[]{:S(2)}, u32[]{:S(2)}) collective-permute-start(bf16[3,256,512]{2,1,0:T(8,128)(2,1)} %get-tuple-element.23), channel_id=1, source_target_pairs={{0,96},{1,33},{32,64},{33,1},{64,32},{65,97},{96,0},{97,65},{128,2... | collective-permute-start | bytes 2359304 | tf_op jit(solution)/shard_map/ppermute | solution.py:330
  21.0 0.0 copy-done.6
  21.1 0.1 reduce_max.14
  21.2 0.1 reduce_max.18
  21.3 0.2 convert_reduce_fusion
  21.5 0.0 all-to-all-done
  21.5 0.0 copy-start.2
  21.5 1.4 %shard_map.75 = bf16[32,72,128]{2,1,0:T(8,128)(2,1)} custom-call(s32[32]{0:T(128)S(1)} %compare_select_fusion.1.table, bf16[32,72,128]{2,1,0:T(8,128)(2,1)S(1)} %bitcast.9), custom_call_target="tpu_custom_call" | custom-call | flops 33333334016 | bytes 4194304 | tf_op jit(solution)/shard_map/pallas_call | solution.py:178
  22.9 17.0 %all-to-all-start.1 = ((bf16[32,72,128]{2,1,0:T(8,128)(2,1)}), bf16[32,72,128]{2,1,0:T(8,128)(2,1)S(1)}, u32[]{:S(2)}, u32[]{:S(2)}) async-start(bf16[32,72,128]{2,1,0:T(8,128)(2,1)} %shard_map.75), calls=%async_computation.1 | async-start | bytes 1179648 | tf_op jit(solution)/shard_map/all_to_all | solution.py:432
  40.0 0.0 collective-permute-done.got
  40.0 0.0 copy-start.4
  40.0 0.9 copy-done.4
  40.9 0.0 copy-done.2
  40.9 0.0 copy-start.3
  40.9 1.1 %copy-done.3 = bf16[3,256,512]{2,1,0:T(8,128)(2,1)S(1)} copy-done((bf16[3,256,512]{2,1,0:T(8,128)(2,1)S(1)}, bf16[3,256,512]{2,1,0:T(8,128)(2,1)}, u32[]{:S(2)}) %copy-start.3) | copy-done | bytes 786456
  42.0 0.0 copy-start.5
  42.0 1.1 %copy-done.5 = bf16[3,256,512]{2,1,0:T(8,128)(2,1)S(1)} copy-done((bf16[3,256,512]{2,1,0:T(8,128)(2,1)S(1)}, bf16[3,256,512]{2,1,0:T(8,128)(2,1)}, u32[]{:S(2)}) %copy-start.5) | copy-done | bytes 786456
  43.2 0.0 copy-start
  43.2 0.0 copy-start.1
  43.2 0.8 shard_map.77
  44.0 0.0 copy-start.7
  44.0 2.2 %collective-permute-start.1 = (bf16[2,256,512]{2,1,0:T(8,128)(2,1)S(1)}, bf16[2,256,512]{2,1,0:T(8,128)(2,1)S(1)}, u32[]{:S(2)}, u32[]{:S(2)}) collective-permute-start(bf16[2,256,512]{2,1,0:T(8,128)(2,1)S(1)} %get-tuple-element.27), channel_id=1, source_target_pairs={{0,384},{1,129},{32,416},{33,161},{64,448},{65,193},{96,480},{97,2... | collective-permute-start | bytes 1572872 | tf_op jit(solution)/shard_map/ppermute | solution.py:330
  46.2 0.0 collective-permute-done.3.got
  46.2 0.0 copy-done
  46.2 1.5 %shard_map.80 = (bf16[2,256,512]{2,1,0:T(8,128)(2,1)}, bf16[2,256,512]{2,1,0:T(8,128)(2,1)S(1)}) custom-call(s32[256]{0:T(256)S(1)} %copy-done.2, bf16[3,256,512]{2,1,0:T(8,128)(2,1)S(1)} %copy-done, bf16[3,256,512]{2,1,0:T(8,128)(2,1)S(1)} %collective-permute-done.3.got), custom_call_target="tpu_custom_call" | custom-call | bytes 2097152 | tf_op jit(solution)/shard_map/pallas_call | solution.py:353
  47.7 1.9 %collective-permute-start.4 = (bf16[2,256,512]{2,1,0:T(8,128)(2,1)}, bf16[2,256,512]{2,1,0:T(8,128)(2,1)S(1)}, u32[]{:S(2)}, u32[]{:S(2)}) collective-permute-start(bf16[2,256,512]{2,1,0:T(8,128)(2,1)} %get-tuple-element.33), channel_id=1, source_target_pairs={{0,32},{1,97},{32,0},{33,65},{64,96},{65,33},{96,64},{97,1},{128,1... | collective-permute-start | bytes 1572872 | tf_op jit(solution)/shard_map/ppermute | solution.py:330
  49.6 0.1 copy.9
  49.8 0.1 reshape.16
  49.9 4.3 %collective-permute-done.1.got = bf16[2,256,512]{2,1,0:T(8,128)(2,1)S(1)} collective-permute-done((bf16[2,256,512]{2,1,0:T(8,128)(2,1)S(1)}, bf16[2,256,512]{2,1,0:T(8,128)(2,1)S(1)}, u32[]{:S(2)}, u32[]{:S(2)}) %collective-permute-start.1) | collective-permute-done | bytes 524320 | tf_op jit(solution)/shard_map/ppermute | solution.py:330
  54.2 0.0 copy-done.1
  54.2 0.7 shard_map.78
  54.9 2.2 %collective-permute-start.2 = (bf16[256,512]{1,0:T(8,128)(2,1)S(1)}, bf16[256,512]{1,0:T(8,128)(2,1)S(1)}, u32[]{:S(2)}, u32[]{:S(2)}) collective-permute-start(bf16[256,512]{1,0:T(8,128)(2,1)S(1)} %get-tuple-element.29), channel_id=1, source_target_pairs={{0,32},{1,97},{32,0},{33,65},{64,96},{65,33},{96,64},{97,1},{128,1... | collective-permute-start | bytes 786440 | tf_op jit(solution)/shard_map/ppermute | solution.py:330
  57.1 2.3 %collective-permute-done.4.got = bf16[2,256,512]{2,1,0:T(8,128)(2,1)S(1)} collective-permute-done((bf16[2,256,512]{2,1,0:T(8,128)(2,1)}, bf16[2,256,512]{2,1,0:T(8,128)(2,1)S(1)}, u32[]{:S(2)}, u32[]{:S(2)}) %collective-permute-start.4) | collective-permute-done | bytes 524320 | tf_op jit(solution)/shard_map/ppermute | solution.py:330
  59.4 0.7 shard_map.81
  60.0 3.1 %collective-permute-start.5 = (bf16[256,512]{1,0:T(8,128)(2,1)S(1)}, bf16[256,512]{1,0:T(8,128)(2,1)S(1)}, u32[]{:S(2)}, u32[]{:S(2)}) collective-permute-start(bf16[256,512]{1,0:T(8,128)(2,1)S(1)} %get-tuple-element.35), channel_id=1, source_target_pairs={{0,384},{1,129},{32,416},{33,161},{64,448},{65,193},{96,480},{97,2... | collective-permute-start | bytes 786440 | tf_op jit(solution)/shard_map/ppermute | solution.py:330
  63.2 0.0 copy-done.7
  63.2 0.3 collective-permute-done.2.got
  63.5 0.1 shard_map.79.a
  63.6 1.9 %collective-permute-start.6 = (bf16[256,512]{1,0:T(8,128)(2,1)S(1)}, bf16[256,512]{1,0:T(8,128)(2,1)S(1)}, u32[]{:S(2)}, u32[]{:S(2)}) collective-permute-start(bf16[256,512]{1,0:T(8,128)(2,1)S(1)} %shard_map.79.a), channel_id=1, source_target_pairs={{0,96},{1,33},{32,64},{33,1},{64,32},{65,97},{96,0},{97,65},{128,2... | collective-permute-start | bytes 786440 | tf_op jit(solution)/shard_map/ppermute | solution.py:330
  65.5 1.9 %collective-permute-done.5.got = bf16[256,512]{1,0:T(8,128)(2,1)S(1)} collective-permute-done((bf16[256,512]{1,0:T(8,128)(2,1)S(1)}, bf16[256,512]{1,0:T(8,128)(2,1)S(1)}, u32[]{:S(2)}, u32[]{:S(2)}) %collective-permute-start.5) | collective-permute-done | bytes 262176 | tf_op jit(solution)/shard_map/ppermute | solution.py:330
  67.5 0.1 shard_map.82.b
  67.5 4.3 %collective-permute-start.7 = (bf16[256,512]{1,0:T(8,128)(2,1)S(1)}, bf16[256,512]{1,0:T(8,128)(2,1)S(1)}, u32[]{:S(2)}, u32[]{:S(2)}) collective-permute-start(bf16[256,512]{1,0:T(8,128)(2,1)S(1)} %shard_map.82.b), channel_id=1, source_target_pairs={{0,128},{1,385},{32,160},{33,417},{64,192},{65,449},{96,224},{97,4... | collective-permute-start | bytes 786440 | tf_op jit(solution)/shard_map/ppermute | solution.py:330
  71.8 0.2 select_reduce_fusion.table
  72.0 4.2 %all-to-all-done.1.source = bf16[32,72,128]{2,1,0:T(8,128)(2,1)S(1)} async-done(((bf16[32,72,128]{2,1,0:T(8,128)(2,1)}), bf16[32,72,128]{2,1,0:T(8,128)(2,1)S(1)}, u32[]{:S(2)}, u32[]{:S(2)}) %all-to-all-start.1) | async-done | bytes 589856 | tf_op jit(solution)/shard_map/all_to_all | solution.py:432
  76.3 1.4 %shard_map.76 = bf16[32,72,128]{2,1,0:T(8,128)(2,1)} custom-call(s32[32]{0:T(128)S(1)} %select_reduce_fusion.table, bf16[32,72,128]{2,1,0:T(8,128)(2,1)S(1)} %all-to-all-done.1.source), custom_call_target="tpu_custom_call" | custom-call | bytes 4194304 | tf_op jit(solution)/shard_map/pallas_call | solution.py:178
  77.7 4.1 %all-to-all-start.2 = ((bf16[16,2,72,128]{3,2,1,0:T(8,128)(2,1)}), bf16[16,2,72,128]{3,2,1,0:T(8,128)(2,1)S(1)}, u32[]{:S(2)}, u32[]{:S(2)}) async-start(bf16[16,2,72,128]{3,2,1,0:T(8,128)(2,1)} %bitcast.5), calls=%async_computation.2 | async-start | bytes 1179648 | tf_op jit(solution)/shard_map/all_to_all | solution.py:435
  81.8 0.0 collective-permute-done.6.r0
  81.8 0.0 collective-permute-done.7.r1
  81.8 0.8 shard_map.83
  82.6 10.1 %all-to-all-done.2.chunks = bf16[16,2,72,128]{3,2,1,0:T(8,128)(2,1)S(1)} async-done(((bf16[16,2,72,128]{3,2,1,0:T(8,128)(2,1)}), bf16[16,2,72,128]{3,2,1,0:T(8,128)(2,1)S(1)}, u32[]{:S(2)}, u32[]{:S(2)}) %all-to-all-start.2) | async-done | bytes 589856 | tf_op jit(solution)/shard_map/all_to_all | solution.py:435
  92.7 3.0 %shard_map.84 = bf16[512,512]{1,0:T(8,128)(2,1)S(1)} custom-call(bf16[16,2,72,128]{3,2,1,0:T(8,128)(2,1)S(1)} %all-to-all-done.2.chunks, bf16[512,512]{1,0:T(8,128)(2,1)S(1)} %get-tuple-element.36.gradient, bf16[512,512]{1,0:T(8,128)(2,1)S(1)} %get-tuple-element.37.left, bf16[512,512]{1,0:T(8,128)(2,1)S(1)} %get-tuple-element.38.right), custom_call_target="tpu_custom_call" | custom-call | flops 2147483648 | bytes 6291456 | tf_op jit(solution)/shard_map/pallas_call | solution.py:438
  95.7 12.8 %all_to_all.20.source = bf16[16,32,512]{2,1,0:T(8,128)(2,1)S(1)} all-to-all(bf16[16,32,512]{2,1,0:T(8,128)(2,1)S(1)} %bitcast.10), channel_id=1, replica_groups=mesh['dp'=16,'z'=16,'core'=2] {'dp'}, dimensions={0} | all-to-all | bytes 1048576 | tf_op jit(solution)/shard_map/all_to_all | solution.py:452
  108.5 0.7 shard_map.85
  (6 shorter events, 0.1 us)
Async XLA Ops:
  0.0 21.0 %copy-start.6 = (s32[160,2]{0,1:T(2,128)S(1)}, s32[160,2]{0,1:T(2,128)}, u32[]{:S(2)}) copy-start(s32[160,2]{0,1:T(2,128)} %param.9) | copy-start | bytes 3844
  2.2 19.3 %all-to-all-start = ((bf16[16,2,72,128]{3,2,1,0:T(8,128)(2,1)}), bf16[16,2,72,128]{3,2,1,0:T(8,128)(2,1)S(1)}, u32[]{:S(2)}, u32[]{:S(2)}) async-start(bf16[16,2,72,128]{3,2,1,0:T(8,128)(2,1)} %shard_map.73), calls=%async_computation | async-start | bytes 1179648 | tf_op jit(solution)/shard_map/all_to_all | solution.py:427
  13.4 26.5 %collective-permute-start = (bf16[3,256,512]{2,1,0:T(8,128)(2,1)}, bf16[3,256,512]{2,1,0:T(8,128)(2,1)S(1)}, u32[]{:S(2)}, u32[]{:S(2)}) collective-permute-start(bf16[3,256,512]{2,1,0:T(8,128)(2,1)} %get-tuple-element.22), channel_id=1, source_target_pairs={{0,128},{1,385},{32,160},{33,417},{64,192},{65,449},{96,224},{97,4... | collective-permute-start | bytes 2359304 | tf_op jit(solution)/shard_map/ppermute | solution.py:330
  17.9 28.3 %collective-permute-start.3 = (bf16[3,256,512]{2,1,0:T(8,128)(2,1)}, bf16[3,256,512]{2,1,0:T(8,128)(2,1)S(1)}, u32[]{:S(2)}, u32[]{:S(2)}) collective-permute-start(bf16[3,256,512]{2,1,0:T(8,128)(2,1)} %get-tuple-element.23), channel_id=1, source_target_pairs={{0,96},{1,33},{32,64},{33,1},{64,32},{65,97},{96,0},{97,65},{128,2... | collective-permute-start | bytes 2359304 | tf_op jit(solution)/shard_map/ppermute | solution.py:330
  21.5 19.4 %copy-start.2 = (s32[256]{0:T(256)S(1)}, s32[256]{0:T(256)}, u32[]{:S(2)}) copy-start(s32[256]{0:T(256)} %constant.55.clone.table) | copy-start | bytes 3076
  22.9 53.3 %all-to-all-start.1 = ((bf16[32,72,128]{2,1,0:T(8,128)(2,1)}), bf16[32,72,128]{2,1,0:T(8,128)(2,1)S(1)}, u32[]{:S(2)}, u32[]{:S(2)}) async-start(bf16[32,72,128]{2,1,0:T(8,128)(2,1)} %shard_map.75), calls=%async_computation.1 | async-start | bytes 1179648 | tf_op jit(solution)/shard_map/all_to_all | solution.py:432
  40.0 0.9 copy-start.4
  40.9 1.1 %copy-start.3 = (bf16[3,256,512]{2,1,0:T(8,128)(2,1)S(1)}, bf16[3,256,512]{2,1,0:T(8,128)(2,1)}, u32[]{:S(2)}) copy-start(bf16[3,256,512]{2,1,0:T(8,128)(2,1)} %get-tuple-element.25.kept) | copy-start | bytes 2359300
  42.0 1.1 %copy-start.5 = (bf16[3,256,512]{2,1,0:T(8,128)(2,1)S(1)}, bf16[3,256,512]{2,1,0:T(8,128)(2,1)}, u32[]{:S(2)}) copy-start(bf16[3,256,512]{2,1,0:T(8,128)(2,1)} %copy-done.4) | copy-start | bytes 2359300
  43.2 3.0 %copy-start = (bf16[3,256,512]{2,1,0:T(8,128)(2,1)S(1)}, bf16[3,256,512]{2,1,0:T(8,128)(2,1)}, u32[]{:S(2)}) copy-start(bf16[3,256,512]{2,1,0:T(8,128)(2,1)} %get-tuple-element.30.kept) | copy-start | bytes 2359300
  43.2 11.0 %copy-start.1 = (s32[128]{0:T(128)S(1)}, s32[128]{0:T(128)}, u32[]{:S(2)}) copy-start(s32[128]{0:T(128)} %constant.56.clone.table) | copy-start | bytes 1540
  44.0 19.2 %copy-start.7 = (s32[2,32]{1,0:T(2,128)S(1)}, s32[2,32]{1,0:T(2,128)}, u32[]{:S(2)}) copy-start(s32[2,32]{1,0:T(2,128)} %constant.57.clone) | copy-start | bytes 772
  44.0 10.2 %collective-permute-start.1 = (bf16[2,256,512]{2,1,0:T(8,128)(2,1)S(1)}, bf16[2,256,512]{2,1,0:T(8,128)(2,1)S(1)}, u32[]{:S(2)}, u32[]{:S(2)}) collective-permute-start(bf16[2,256,512]{2,1,0:T(8,128)(2,1)S(1)} %get-tuple-element.27), channel_id=1, source_target_pairs={{0,384},{1,129},{32,416},{33,161},{64,448},{65,193},{96,480},{97,2... | collective-permute-start | bytes 1572872 | tf_op jit(solution)/shard_map/ppermute | solution.py:330
  47.7 11.6 %collective-permute-start.4 = (bf16[2,256,512]{2,1,0:T(8,128)(2,1)}, bf16[2,256,512]{2,1,0:T(8,128)(2,1)S(1)}, u32[]{:S(2)}, u32[]{:S(2)}) collective-permute-start(bf16[2,256,512]{2,1,0:T(8,128)(2,1)} %get-tuple-element.33), channel_id=1, source_target_pairs={{0,32},{1,97},{32,0},{33,65},{64,96},{65,33},{96,64},{97,1},{128,1... | collective-permute-start | bytes 1572872 | tf_op jit(solution)/shard_map/ppermute | solution.py:330
  54.9 8.6 %collective-permute-start.2 = (bf16[256,512]{1,0:T(8,128)(2,1)S(1)}, bf16[256,512]{1,0:T(8,128)(2,1)S(1)}, u32[]{:S(2)}, u32[]{:S(2)}) collective-permute-start(bf16[256,512]{1,0:T(8,128)(2,1)S(1)} %get-tuple-element.29), channel_id=1, source_target_pairs={{0,32},{1,97},{32,0},{33,65},{64,96},{65,33},{96,64},{97,1},{128,1... | collective-permute-start | bytes 786440 | tf_op jit(solution)/shard_map/ppermute | solution.py:330
  60.0 7.4 %collective-permute-start.5 = (bf16[256,512]{1,0:T(8,128)(2,1)S(1)}, bf16[256,512]{1,0:T(8,128)(2,1)S(1)}, u32[]{:S(2)}, u32[]{:S(2)}) collective-permute-start(bf16[256,512]{1,0:T(8,128)(2,1)S(1)} %get-tuple-element.35), channel_id=1, source_target_pairs={{0,384},{1,129},{32,416},{33,161},{64,448},{65,193},{96,480},{97,2... | collective-permute-start | bytes 786440 | tf_op jit(solution)/shard_map/ppermute | solution.py:330
  63.6 18.2 %collective-permute-start.6 = (bf16[256,512]{1,0:T(8,128)(2,1)S(1)}, bf16[256,512]{1,0:T(8,128)(2,1)S(1)}, u32[]{:S(2)}, u32[]{:S(2)}) collective-permute-start(bf16[256,512]{1,0:T(8,128)(2,1)S(1)} %shard_map.79.a), channel_id=1, source_target_pairs={{0,96},{1,33},{32,64},{33,1},{64,32},{65,97},{96,0},{97,65},{128,2... | collective-permute-start | bytes 786440 | tf_op jit(solution)/shard_map/ppermute | solution.py:330
  67.5 14.3 %collective-permute-start.7 = (bf16[256,512]{1,0:T(8,128)(2,1)S(1)}, bf16[256,512]{1,0:T(8,128)(2,1)S(1)}, u32[]{:S(2)}, u32[]{:S(2)}) collective-permute-start(bf16[256,512]{1,0:T(8,128)(2,1)S(1)} %shard_map.82.b), channel_id=1, source_target_pairs={{0,128},{1,385},{32,160},{33,417},{64,192},{65,449},{96,224},{97,4... | collective-permute-start | bytes 786440 | tf_op jit(solution)/shard_map/ppermute | solution.py:330
  77.7 15.0 %all-to-all-start.2 = ((bf16[16,2,72,128]{3,2,1,0:T(8,128)(2,1)}), bf16[16,2,72,128]{3,2,1,0:T(8,128)(2,1)S(1)}, u32[]{:S(2)}, u32[]{:S(2)}) async-start(bf16[16,2,72,128]{3,2,1,0:T(8,128)(2,1)} %bitcast.5), calls=%async_computation.2 | async-start | bytes 1179648 | tf_op jit(solution)/shard_map/all_to_all | solution.py:435

commit v12 on v11

--- a/solution.py
+++ b/solution.py
@@ -116,14 +116,19 @@
     return [table[base + k] for k in range(width)]
 
 
-def choose_kernel(table, source, s0, s1, k0, k1):
+def choose_kernel(table, source, s0, s1, k0, k1, sems):
     table = my_row(table)
     height = s0.shape[1]
-    for h, (sent, kept) in enumerate(((s0, k0), (s1, k1))):
-        rows = slice(h * height, (h + 1) * height)
-        for u in range(3):
-            sent[u] = source[table[6 * h + u], rows, :]
-            kept[u] = source[table[6 * h + 3 + u], rows, :]
+    copies = []
+    for half_outs, first in (((s0, s1), 0), ((k0, k1), 3)):
+        for h, out in enumerate(half_outs):
+            for u in range(3):
+                unit = source.at[table[6 * h + first + u], pl.ds(h * height, height), :]
+                copies.append(pltpu.make_async_copy(unit, out.at[u], sems.at[len(copies)]))
+    for copy in copies:
+        copy.start()
+    for copy in copies:
+        copy.wait()
 
 
 def first_sum_kernel(portion, table, kept, got, sent, next_kept):
@@ -336,7 +341,8 @@
         choose_kernel,
         out_shape=[shape(3, n // 2, order_n)] * 4,
         in_specs=[SMEM, VMEM],
-        out_specs=[VMEM] * 4,
+        out_specs=[HBM] * 4,
+        scratch_shapes=[pltpu.SemaphoreType.DMA((12,))],
         compiler_params=params(most_mib),
         cost_estimate=cost(0, 12 * n * order_n),
     )(tables[0], grad)

time: 111 us -> 111 us (level)
  no operation moved by 1% of the time
where the time goes in v12:
time: 111 us; the launch traced here: 109 us
  starting transfers between devices  51.9 us (47%)
  waiting for transfers between devices  23.3 us (21%)
  Pallas kernels  16.8 us (15%)
  blocking collectives  12.8 us (12%)
  local copies, waits for them, and re-layouts  3.46 us (3%)
    ppermute x8, starting transfers between devices, exchange(): return lax.ppermute(array, ('dp', 'core'), pairs(portion, step))  23.2 us
    all_to_all x1, starting transfers between devices, body(): lax.all_to_all(lanes, ('z', 'core'), split_axis=0, concat_axis=0, tiled=T...  17 us
    all_to_all x1, blocking collectives, body(): rows = lax.all_to_all(rows, 'dp', split_axis=0, concat_axis=0, tiled=True)  12.8 us
    all_to_all x1, waiting for transfers between devices, body(): lax.all_to_all(lanes, 'dp', split_axis=0, concat_axis=0, tiled=True)  10.1 us
    ppermute x8, waiting for transfers between devices, exchange(): return lax.ppermute(array, ('dp', 'core'), pairs(portion, step))  8.87 us
    all_to_all x1, starting transfers between devices, body(): lax.all_to_all(packed, 'dp', split_axis=0, concat_axis=0, tiled=True)  7.6 us
    all_to_all x1, waiting for transfers between devices, body(): lax.all_to_all(lanes, ('z', 'core'), split_axis=0, concat_axis=0, tiled=T...  4.25 us
    all_to_all x1, starting transfers between devices, body(): lax.all_to_all(lanes, 'dp', split_axis=0, concat_axis=0, tiled=True)  4.08 us
  transfers between devices with their start and end apart: 11, of which 6 were waited for; matrix products, arithmetic and copies ran while one was open for 1% of the time, Pallas kernels for 10%

profile of v12, /device:TPU:1, one launch (start us, length us, event | category | flops | bytes accessed | tf_op | source)
XLA Modules:
  0.0 109.1 jit_solution(10825001605436746515)
XLA Ops:
  0.0 0.0 copy-start.6
  0.0 2.2 %shard_map.73 = bf16[16,2,72,128]{3,2,1,0:T(8,128)(2,1)} custom-call(f32[2,512,512]{2,1,0:T(8,128)} %bitcast.12), custom_call_target="tpu_custom_call" | custom-call | bytes 3145728 | tf_op jit(solution)/shard_map/pallas_call | solution.py:419
  2.2 7.6 %all-to-all-start = ((bf16[16,2,72,128]{3,2,1,0:T(8,128)(2,1)}), bf16[16,2,72,128]{3,2,1,0:T(8,128)(2,1)S(1)}, u32[]{:S(2)}, u32[]{:S(2)}) async-start(bf16[16,2,72,128]{3,2,1,0:T(8,128)(2,1)} %shard_map.73), calls=%async_computation | async-start | bytes 1179648 | tf_op jit(solution)/shard_map/all_to_all | solution.py:433
  9.8 3.5 %shard_map.74 = (bf16[3,256,512]{2,1,0:T(8,128)(2,1)}, bf16[3,256,512]{2,1,0:T(8,128)(2,1)}, bf16[3,256,512]{2,1,0:T(8,128)(2,1)}, bf16[3,256,512]{2,1,0:T(8,128)(2,1)}) custom-call(s32[384]{0:T(512)} %constant.54.clone.table, bf16[5,512,512]{2,1,0:T(8,128)(2,1)} %bitcast.11), custom_call_target="tpu_custom_call" | custom-call | bytes 3145728 | tf_op jit(solution)/shard_map/pallas_call | solution.py:340
  13.4 4.5 %collective-permute-start = (bf16[3,256,512]{2,1,0:T(8,128)(2,1)}, bf16[3,256,512]{2,1,0:T(8,128)(2,1)S(1)}, u32[]{:S(2)}, u32[]{:S(2)}) collective-permute-start(bf16[3,256,512]{2,1,0:T(8,128)(2,1)} %get-tuple-element.22), channel_id=1, source_target_pairs={{0,128},{1,385},{32,160},{33,417},{64,192},{65,449},{96,224},{97,4... | collective-permute-start | bytes 2359304 | tf_op jit(solution)/shard_map/ppermute | solution.py:335
  17.8 3.1 %collective-permute-start.3 = (bf16[3,256,512]{2,1,0:T(8,128)(2,1)}, bf16[3,256,512]{2,1,0:T(8,128)(2,1)S(1)}, u32[]{:S(2)}, u32[]{:S(2)}) collective-permute-start(bf16[3,256,512]{2,1,0:T(8,128)(2,1)} %get-tuple-element.23), channel_id=1, source_target_pairs={{0,96},{1,33},{32,64},{33,1},{64,32},{65,97},{96,0},{97,65},{128,2... | collective-permute-start | bytes 2359304 | tf_op jit(solution)/shard_map/ppermute | solution.py:335
  21.0 0.0 copy-done.6
  21.0 0.1 reduce_max.14
  21.1 0.1 reduce_max.18
  21.2 0.2 convert_reduce_fusion
  21.4 0.0 all-to-all-done
  21.4 0.0 copy-start.2
  21.4 1.4 %shard_map.75 = bf16[32,72,128]{2,1,0:T(8,128)(2,1)} custom-call(s32[32]{0:T(128)S(1)} %compare_select_fusion.1.table, bf16[32,72,128]{2,1,0:T(8,128)(2,1)S(1)} %bitcast.9), custom_call_target="tpu_custom_call" | custom-call | flops 33333334016 | bytes 4194304 | tf_op jit(solution)/shard_map/pallas_call | solution.py:183
  22.9 17.0 %all-to-all-start.1 = ((bf16[32,72,128]{2,1,0:T(8,128)(2,1)}), bf16[32,72,128]{2,1,0:T(8,128)(2,1)S(1)}, u32[]{:S(2)}, u32[]{:S(2)}) async-start(bf16[32,72,128]{2,1,0:T(8,128)(2,1)} %shard_map.75), calls=%async_computation.1 | async-start | bytes 1179648 | tf_op jit(solution)/shard_map/all_to_all | solution.py:438
  39.9 0.0 collective-permute-done.got
  39.9 0.0 copy-start.4
  39.9 0.9 copy-done.4
  40.8 0.0 copy-done.2
  40.8 0.0 copy-start.3
  40.8 1.1 %copy-done.3 = bf16[3,256,512]{2,1,0:T(8,128)(2,1)S(1)} copy-done((bf16[3,256,512]{2,1,0:T(8,128)(2,1)S(1)}, bf16[3,256,512]{2,1,0:T(8,128)(2,1)}, u32[]{:S(2)}) %copy-start.3) | copy-done | bytes 786456
  41.9 0.0 copy-start.5
  41.9 1.1 %copy-done.5 = bf16[3,256,512]{2,1,0:T(8,128)(2,1)S(1)} copy-done((bf16[3,256,512]{2,1,0:T(8,128)(2,1)S(1)}, bf16[3,256,512]{2,1,0:T(8,128)(2,1)}, u32[]{:S(2)}) %copy-start.5) | copy-done | bytes 786456
  43.1 0.0 copy-start
  43.1 0.0 copy-start.1
  43.1 0.8 shard_map.77
  43.9 0.0 copy-start.7
  43.9 2.2 %collective-permute-start.1 = (bf16[2,256,512]{2,1,0:T(8,128)(2,1)S(1)}, bf16[2,256,512]{2,1,0:T(8,128)(2,1)S(1)}, u32[]{:S(2)}, u32[]{:S(2)}) collective-permute-start(bf16[2,256,512]{2,1,0:T(8,128)(2,1)S(1)} %get-tuple-element.27), channel_id=1, source_target_pairs={{0,384},{1,129},{32,416},{33,161},{64,448},{65,193},{96,480},{97,2... | collective-permute-start | bytes 1572872 | tf_op jit(solution)/shard_map/ppermute | solution.py:335
  46.1 0.0 collective-permute-done.3.got
  46.1 0.0 copy-done
  46.1 1.5 %shard_map.80 = (bf16[2,256,512]{2,1,0:T(8,128)(2,1)}, bf16[2,256,512]{2,1,0:T(8,128)(2,1)S(1)}) custom-call(s32[256]{0:T(256)S(1)} %copy-done.2, bf16[3,256,512]{2,1,0:T(8,128)(2,1)S(1)} %copy-done, bf16[3,256,512]{2,1,0:T(8,128)(2,1)S(1)} %collective-permute-done.3.got), custom_call_target="tpu_custom_call" | custom-call | bytes 2097152 | tf_op jit(solution)/shard_map/pallas_call | solution.py:359
  47.6 1.9 %collective-permute-start.4 = (bf16[2,256,512]{2,1,0:T(8,128)(2,1)}, bf16[2,256,512]{2,1,0:T(8,128)(2,1)S(1)}, u32[]{:S(2)}, u32[]{:S(2)}) collective-permute-start(bf16[2,256,512]{2,1,0:T(8,128)(2,1)} %get-tuple-element.33), channel_id=1, source_target_pairs={{0,32},{1,97},{32,0},{33,65},{64,96},{65,33},{96,64},{97,1},{128,1... | collective-permute-start | bytes 1572872 | tf_op jit(solution)/shard_map/ppermute | solution.py:335
  49.6 0.1 copy.9
  49.7 0.1 reshape.16
  49.8 4.3 %collective-permute-done.1.got = bf16[2,256,512]{2,1,0:T(8,128)(2,1)S(1)} collective-permute-done((bf16[2,256,512]{2,1,0:T(8,128)(2,1)S(1)}, bf16[2,256,512]{2,1,0:T(8,128)(2,1)S(1)}, u32[]{:S(2)}, u32[]{:S(2)}) %collective-permute-start.1) | collective-permute-done | bytes 524320 | tf_op jit(solution)/shard_map/ppermute | solution.py:335
  54.1 0.0 copy-done.1
  54.1 0.7 shard_map.78
  54.8 2.2 %collective-permute-start.2 = (bf16[256,512]{1,0:T(8,128)(2,1)S(1)}, bf16[256,512]{1,0:T(8,128)(2,1)S(1)}, u32[]{:S(2)}, u32[]{:S(2)}) collective-permute-start(bf16[256,512]{1,0:T(8,128)(2,1)S(1)} %get-tuple-element.29), channel_id=1, source_target_pairs={{0,32},{1,97},{32,0},{33,65},{64,96},{65,33},{96,64},{97,1},{128,1... | collective-permute-start | bytes 786440 | tf_op jit(solution)/shard_map/ppermute | solution.py:335
  57.0 2.3 %collective-permute-done.4.got = bf16[2,256,512]{2,1,0:T(8,128)(2,1)S(1)} collective-permute-done((bf16[2,256,512]{2,1,0:T(8,128)(2,1)}, bf16[2,256,512]{2,1,0:T(8,128)(2,1)S(1)}, u32[]{:S(2)}, u32[]{:S(2)}) %collective-permute-start.4) | collective-permute-done | bytes 524320 | tf_op jit(solution)/shard_map/ppermute | solution.py:335
  59.3 0.7 shard_map.81
  60.0 3.1 %collective-permute-start.5 = (bf16[256,512]{1,0:T(8,128)(2,1)S(1)}, bf16[256,512]{1,0:T(8,128)(2,1)S(1)}, u32[]{:S(2)}, u32[]{:S(2)}) collective-permute-start(bf16[256,512]{1,0:T(8,128)(2,1)S(1)} %get-tuple-element.35), channel_id=1, source_target_pairs={{0,384},{1,129},{32,416},{33,161},{64,448},{65,193},{96,480},{97,2... | collective-permute-start | bytes 786440 | tf_op jit(solution)/shard_map/ppermute | solution.py:335
  63.1 0.0 copy-done.7
  63.1 0.3 collective-permute-done.2.got
  63.4 0.1 shard_map.79.a
  63.5 1.9 %collective-permute-start.6 = (bf16[256,512]{1,0:T(8,128)(2,1)S(1)}, bf16[256,512]{1,0:T(8,128)(2,1)S(1)}, u32[]{:S(2)}, u32[]{:S(2)}) collective-permute-start(bf16[256,512]{1,0:T(8,128)(2,1)S(1)} %shard_map.79.a), channel_id=1, source_target_pairs={{0,96},{1,33},{32,64},{33,1},{64,32},{65,97},{96,0},{97,65},{128,2... | collective-permute-start | bytes 786440 | tf_op jit(solution)/shard_map/ppermute | solution.py:335
  65.4 1.9 %collective-permute-done.5.got = bf16[256,512]{1,0:T(8,128)(2,1)S(1)} collective-permute-done((bf16[256,512]{1,0:T(8,128)(2,1)S(1)}, bf16[256,512]{1,0:T(8,128)(2,1)S(1)}, u32[]{:S(2)}, u32[]{:S(2)}) %collective-permute-start.5) | collective-permute-done | bytes 262176 | tf_op jit(solution)/shard_map/ppermute | solution.py:335
  67.4 0.1 shard_map.82.b
  67.4 4.3 %collective-permute-start.7 = (bf16[256,512]{1,0:T(8,128)(2,1)S(1)}, bf16[256,512]{1,0:T(8,128)(2,1)S(1)}, u32[]{:S(2)}, u32[]{:S(2)}) collective-permute-start(bf16[256,512]{1,0:T(8,128)(2,1)S(1)} %shard_map.82.b), channel_id=1, source_target_pairs={{0,128},{1,385},{32,160},{33,417},{64,192},{65,449},{96,224},{97,4... | collective-permute-start | bytes 786440 | tf_op jit(solution)/shard_map/ppermute | solution.py:335
  71.8 0.2 select_reduce_fusion.table
  71.9 4.2 %all-to-all-done.1.source = bf16[32,72,128]{2,1,0:T(8,128)(2,1)S(1)} async-done(((bf16[32,72,128]{2,1,0:T(8,128)(2,1)}), bf16[32,72,128]{2,1,0:T(8,128)(2,1)S(1)}, u32[]{:S(2)}, u32[]{:S(2)}) %all-to-all-start.1) | async-done | bytes 589856 | tf_op jit(solution)/shard_map/all_to_all | solution.py:438
  76.2 1.4 %shard_map.76 = bf16[32,72,128]{2,1,0:T(8,128)(2,1)} custom-call(s32[32]{0:T(128)S(1)} %select_reduce_fusion.table, bf16[32,72,128]{2,1,0:T(8,128)(2,1)S(1)} %all-to-all-done.1.source), custom_call_target="tpu_custom_call" | custom-call | bytes 4194304 | tf_op jit(solution)/shard_map/pallas_call | solution.py:183
  77.6 4.1 %all-to-all-start.2 = ((bf16[16,2,72,128]{3,2,1,0:T(8,128)(2,1)}), bf16[16,2,72,128]{3,2,1,0:T(8,128)(2,1)S(1)}, u32[]{:S(2)}, u32[]{:S(2)}) async-start(bf16[16,2,72,128]{3,2,1,0:T(8,128)(2,1)} %bitcast.5), calls=%async_computation.2 | async-start | bytes 1179648 | tf_op jit(solution)/shard_map/all_to_all | solution.py:441
  81.7 0.0 collective-permute-done.6.r0
  81.7 0.0 collective-permute-done.7.r1
  81.7 0.8 shard_map.83
  82.5 10.1 %all-to-all-done.2.chunks = bf16[16,2,72,128]{3,2,1,0:T(8,128)(2,1)S(1)} async-done(((bf16[16,2,72,128]{3,2,1,0:T(8,128)(2,1)}), bf16[16,2,72,128]{3,2,1,0:T(8,128)(2,1)S(1)}, u32[]{:S(2)}, u32[]{:S(2)}) %all-to-all-start.2) | async-done | bytes 589856 | tf_op jit(solution)/shard_map/all_to_all | solution.py:441
  92.6 3.0 %shard_map.84 = bf16[512,512]{1,0:T(8,128)(2,1)S(1)} custom-call(bf16[16,2,72,128]{3,2,1,0:T(8,128)(2,1)S(1)} %all-to-all-done.2.chunks, bf16[512,512]{1,0:T(8,128)(2,1)S(1)} %get-tuple-element.36.gradient, bf16[512,512]{1,0:T(8,128)(2,1)S(1)} %get-tuple-element.37.left, bf16[512,512]{1,0:T(8,128)(2,1)S(1)} %get-tuple-element.38.right), custom_call_target="tpu_custom_call" | custom-call | flops 2147483648 | bytes 6291456 | tf_op jit(solution)/shard_map/pallas_call | solution.py:444
  95.6 12.8 %all_to_all.20.source = bf16[16,32,512]{2,1,0:T(8,128)(2,1)S(1)} all-to-all(bf16[16,32,512]{2,1,0:T(8,128)(2,1)S(1)} %bitcast.10), channel_id=1, replica_groups=mesh['dp'=16,'z'=16,'core'=2] {'dp'}, dimensions={0} | all-to-all | bytes 1048576 | tf_op jit(solution)/shard_map/all_to_all | solution.py:458
  108.4 0.7 shard_map.85
  (6 shorter events, 0.1 us)
Async XLA Ops:
  0.0 21.0 %copy-start.6 = (s32[160,2]{0,1:T(2,128)S(1)}, s32[160,2]{0,1:T(2,128)}, u32[]{:S(2)}) copy-start(s32[160,2]{0,1:T(2,128)} %param.9) | copy-start | bytes 3844
  2.2 19.2 %all-to-all-start = ((bf16[16,2,72,128]{3,2,1,0:T(8,128)(2,1)}), bf16[16,2,72,128]{3,2,1,0:T(8,128)(2,1)S(1)}, u32[]{:S(2)}, u32[]{:S(2)}) async-start(bf16[16,2,72,128]{3,2,1,0:T(8,128)(2,1)} %shard_map.73), calls=%async_computation | async-start | bytes 1179648 | tf_op jit(solution)/shard_map/all_to_all | solution.py:433
  13.4 26.6 %collective-permute-start = (bf16[3,256,512]{2,1,0:T(8,128)(2,1)}, bf16[3,256,512]{2,1,0:T(8,128)(2,1)S(1)}, u32[]{:S(2)}, u32[]{:S(2)}) collective-permute-start(bf16[3,256,512]{2,1,0:T(8,128)(2,1)} %get-tuple-element.22), channel_id=1, source_target_pairs={{0,128},{1,385},{32,160},{33,417},{64,192},{65,449},{96,224},{97,4... | collective-permute-start | bytes 2359304 | tf_op jit(solution)/shard_map/ppermute | solution.py:335
  17.8 28.3 %collective-permute-start.3 = (bf16[3,256,512]{2,1,0:T(8,128)(2,1)}, bf16[3,256,512]{2,1,0:T(8,128)(2,1)S(1)}, u32[]{:S(2)}, u32[]{:S(2)}) collective-permute-start(bf16[3,256,512]{2,1,0:T(8,128)(2,1)} %get-tuple-element.23), channel_id=1, source_target_pairs={{0,96},{1,33},{32,64},{33,1},{64,32},{65,97},{96,0},{97,65},{128,2... | collective-permute-start | bytes 2359304 | tf_op jit(solution)/shard_map/ppermute | solution.py:335
  21.4 19.4 %copy-start.2 = (s32[256]{0:T(256)S(1)}, s32[256]{0:T(256)}, u32[]{:S(2)}) copy-start(s32[256]{0:T(256)} %constant.55.clone.table) | copy-start | bytes 3076
  22.9 53.3 %all-to-all-start.1 = ((bf16[32,72,128]{2,1,0:T(8,128)(2,1)}), bf16[32,72,128]{2,1,0:T(8,128)(2,1)S(1)}, u32[]{:S(2)}, u32[]{:S(2)}) async-start(bf16[32,72,128]{2,1,0:T(8,128)(2,1)} %shard_map.75), calls=%async_computation.1 | async-start | bytes 1179648 | tf_op jit(solution)/shard_map/all_to_all | solution.py:438
  39.9 0.9 copy-start.4
  40.8 1.1 %copy-start.3 = (bf16[3,256,512]{2,1,0:T(8,128)(2,1)S(1)}, bf16[3,256,512]{2,1,0:T(8,128)(2,1)}, u32[]{:S(2)}) copy-start(bf16[3,256,512]{2,1,0:T(8,128)(2,1)} %get-tuple-element.25.kept) | copy-start | bytes 2359300
  41.9 1.1 %copy-start.5 = (bf16[3,256,512]{2,1,0:T(8,128)(2,1)S(1)}, bf16[3,256,512]{2,1,0:T(8,128)(2,1)}, u32[]{:S(2)}) copy-start(bf16[3,256,512]{2,1,0:T(8,128)(2,1)} %copy-done.4) | copy-start | bytes 2359300
  43.1 3.0 %copy-start = (bf16[3,256,512]{2,1,0:T(8,128)(2,1)S(1)}, bf16[3,256,512]{2,1,0:T(8,128)(2,1)}, u32[]{:S(2)}) copy-start(bf16[3,256,512]{2,1,0:T(8,128)(2,1)} %get-tuple-element.30.kept) | copy-start | bytes 2359300
  43.1 11.0 %copy-start.1 = (s32[128]{0:T(128)S(1)}, s32[128]{0:T(128)}, u32[]{:S(2)}) copy-start(s32[128]{0:T(128)} %constant.56.clone.table) | copy-start | bytes 1540
  43.9 19.2 %copy-start.7 = (s32[2,32]{1,0:T(2,128)S(1)}, s32[2,32]{1,0:T(2,128)}, u32[]{:S(2)}) copy-start(s32[2,32]{1,0:T(2,128)} %constant.57.clone) | copy-start | bytes 772
  43.9 10.2 %collective-permute-start.1 = (bf16[2,256,512]{2,1,0:T(8,128)(2,1)S(1)}, bf16[2,256,512]{2,1,0:T(8,128)(2,1)S(1)}, u32[]{:S(2)}, u32[]{:S(2)}) collective-permute-start(bf16[2,256,512]{2,1,0:T(8,128)(2,1)S(1)} %get-tuple-element.27), channel_id=1, source_target_pairs={{0,384},{1,129},{32,416},{33,161},{64,448},{65,193},{96,480},{97,2... | collective-permute-start | bytes 1572872 | tf_op jit(solution)/shard_map/ppermute | solution.py:335
  47.6 11.6 %collective-permute-start.4 = (bf16[2,256,512]{2,1,0:T(8,128)(2,1)}, bf16[2,256,512]{2,1,0:T(8,128)(2,1)S(1)}, u32[]{:S(2)}, u32[]{:S(2)}) collective-permute-start(bf16[2,256,512]{2,1,0:T(8,128)(2,1)} %get-tuple-element.33), channel_id=1, source_target_pairs={{0,32},{1,97},{32,0},{33,65},{64,96},{65,33},{96,64},{97,1},{128,1... | collective-permute-start | bytes 1572872 | tf_op jit(solution)/shard_map/ppermute | solution.py:335
  54.8 8.6 %collective-permute-start.2 = (bf16[256,512]{1,0:T(8,128)(2,1)S(1)}, bf16[256,512]{1,0:T(8,128)(2,1)S(1)}, u32[]{:S(2)}, u32[]{:S(2)}) collective-permute-start(bf16[256,512]{1,0:T(8,128)(2,1)S(1)} %get-tuple-element.29), channel_id=1, source_target_pairs={{0,32},{1,97},{32,0},{33,65},{64,96},{65,33},{96,64},{97,1},{128,1... | collective-permute-start | bytes 786440 | tf_op jit(solution)/shard_map/ppermute | solution.py:335
  60.0 7.4 %collective-permute-start.5 = (bf16[256,512]{1,0:T(8,128)(2,1)S(1)}, bf16[256,512]{1,0:T(8,128)(2,1)S(1)}, u32[]{:S(2)}, u32[]{:S(2)}) collective-permute-start(bf16[256,512]{1,0:T(8,128)(2,1)S(1)} %get-tuple-element.35), channel_id=1, source_target_pairs={{0,384},{1,129},{32,416},{33,161},{64,448},{65,193},{96,480},{97,2... | collective-permute-start | bytes 786440 | tf_op jit(solution)/shard_map/ppermute | solution.py:335
  63.5 18.2 %collective-permute-start.6 = (bf16[256,512]{1,0:T(8,128)(2,1)S(1)}, bf16[256,512]{1,0:T(8,128)(2,1)S(1)}, u32[]{:S(2)}, u32[]{:S(2)}) collective-permute-start(bf16[256,512]{1,0:T(8,128)(2,1)S(1)} %shard_map.79.a), channel_id=1, source_target_pairs={{0,96},{1,33},{32,64},{33,1},{64,32},{65,97},{96,0},{97,65},{128,2... | collective-permute-start | bytes 786440 | tf_op jit(solution)/shard_map/ppermute | solution.py:335
  67.4 14.3 %collective-permute-start.7 = (bf16[256,512]{1,0:T(8,128)(2,1)S(1)}, bf16[256,512]{1,0:T(8,128)(2,1)S(1)}, u32[]{:S(2)}, u32[]{:S(2)}) collective-permute-start(bf16[256,512]{1,0:T(8,128)(2,1)S(1)} %shard_map.82.b), channel_id=1, source_target_pairs={{0,128},{1,385},{32,160},{33,417},{64,192},{65,449},{96,224},{97,4... | collective-permute-start | bytes 786440 | tf_op jit(solution)/shard_map/ppermute | solution.py:335
  77.6 15.0 %all-to-all-start.2 = ((bf16[16,2,72,128]{3,2,1,0:T(8,128)(2,1)}), bf16[16,2,72,128]{3,2,1,0:T(8,128)(2,1)S(1)}, u32[]{:S(2)}, u32[]{:S(2)}) async-start(bf16[16,2,72,128]{3,2,1,0:T(8,128)(2,1)} %bitcast.5), calls=%async_computation.2 | async-start | bytes 1179648 | tf_op jit(solution)/shard_map/all_to_all | solution.py:441

commit v13 on v11

--- a/solution.py
+++ b/solution.py
@@ -383,7 +383,7 @@
         in_specs=[VMEM] * 4,
         out_specs=[VMEM] * 3,
         compiler_params=params(16),
-        cost_estimate=cost(35 * 10**8, 4 * small),
+        cost_estimate=cost(2 * 10**9, 4 * small),
     )(*sent, *got)
 
 

time: 111 us -> 115 us (1.036); the launches traced: 109 us -> 115 us
  waiting for transfers between devices: 23.3 us -> 29.2 us
  local copies, waits for them, and re-layouts: 3.46 us -> 0.33 us
  blocking collectives: 12.8 us -> 15.1 us
    all_to_all x1, waiting for transfers between devices: 4.25 us -> 17.2 us  [body(): lax.all_to_all(lanes, ('z', 'core'), split_axis=0, concat_axis=0, tiled=T...]
    all_to_all x1, waiting for transfers between devices: 10.1 us -> 0.01 us  [body(): lax.all_to_all(lanes, 'dp', split_axis=0, concat_axis=0, tiled=True)]
    unnamed x17 -> x13, local copies, waits for them, and re-layouts: 3.28 us -> 0.14 us
    ppermute x8, waiting for transfers between devices: 8.87 us -> 12 us  [exchange(): return lax.ppermute(array, ('dp', 'core'), pairs(portion, step))]
    all_to_all x1, blocking collectives: 12.8 us -> 15.1 us  [body(): rows = lax.all_to_all(rows, 'dp', split_axis=0, concat_axis=0, tiled=True)]
  transfers between devices with their start and end apart: 11 -> 11, of which waited for: 6 -> 5; matrix products, arithmetic and copies ran while one was open for 1% -> 1% of each run, Pallas kernels for 10% -> 9%
where the time goes in v13:
time: 115 us
  starting transfers between devices  53 us (46%)
  waiting for transfers between devices  29.2 us (25%)
  Pallas kernels  16.2 us (14%)
  blocking collectives  15.1 us (13%)
    ppermute x8, starting transfers between devices, exchange(): return lax.ppermute(array, ('dp', 'core'), pairs(portion, step))  24.2 us
    all_to_all x1, waiting for transfers between devices, body(): lax.all_to_all(lanes, ('z', 'core'), split_axis=0, concat_axis=0, tiled=T...  17.2 us
    all_to_all x1, starting transfers between devices, body(): lax.all_to_all(lanes, ('z', 'core'), split_axis=0, concat_axis=0, tiled=T...  17 us
    all_to_all x1, blocking collectives, body(): rows = lax.all_to_all(rows, 'dp', split_axis=0, concat_axis=0, tiled=True)  15.1 us
    ppermute x8, waiting for transfers between devices, exchange(): return lax.ppermute(array, ('dp', 'core'), pairs(portion, step))  12 us
    all_to_all x1, starting transfers between devices, body(): lax.all_to_all(packed, 'dp', split_axis=0, concat_axis=0, tiled=True)  7.6 us
    all_to_all x1, starting transfers between devices, body(): lax.all_to_all(lanes, 'dp', split_axis=0, concat_axis=0, tiled=True)  4.08 us
    pallas_call x1, Pallas kernels, first_sent(): pl.pallas_call(choose_kernel, out_shape=[shape(3, n // 2, order_n)] * 4,...  3.61 us
  transfers between devices with their start and end apart: 11, of which 5 were waited for; matrix products, arithmetic and copies ran while one was open for 1% of the time, Pallas kernels for 9%

profile of v13, /device:TPU:1, one launch (start us, length us, event | category | flops | bytes accessed | tf_op | source)
XLA Modules:
  0.0 114.7 jit_solution(9580184999568298998)
XLA Ops:
  0.0 0.0 copy-start.4
  0.0 2.2 %shard_map.73 = bf16[16,2,72,128]{3,2,1,0:T(8,128)(2,1)} custom-call(f32[2,512,512]{2,1,0:T(8,128)} %bitcast.12), custom_call_target="tpu_custom_call" | custom-call | bytes 3145728 | tf_op jit(solution)/shard_map/pallas_call | solution.py:413
  2.2 7.6 %all-to-all-start = ((bf16[16,2,72,128]{3,2,1,0:T(8,128)(2,1)}), bf16[16,2,72,128]{3,2,1,0:T(8,128)(2,1)S(1)}, u32[]{:S(2)}, u32[]{:S(2)}) async-start(bf16[16,2,72,128]{3,2,1,0:T(8,128)(2,1)} %shard_map.73), calls=%async_computation | async-start | bytes 1179648 | tf_op jit(solution)/shard_map/all_to_all | solution.py:427
  9.8 3.6 %shard_map.74 = (bf16[3,256,512]{2,1,0:T(8,128)(2,1)}, bf16[3,256,512]{2,1,0:T(8,128)(2,1)}, bf16[3,256,512]{2,1,0:T(8,128)(2,1)}, bf16[3,256,512]{2,1,0:T(8,128)(2,1)}) custom-call(s32[384]{0:T(512)} %constant.54.clone.table, bf16[5,512,512]{2,1,0:T(8,128)(2,1)} %bitcast.11), custom_call_target="tpu_custom_call" | custom-call | bytes 3145728 | tf_op jit(solution)/shard_map/pallas_call | solution.py:335
  13.4 4.5 %collective-permute-start = (bf16[3,256,512]{2,1,0:T(8,128)(2,1)}, bf16[3,256,512]{2,1,0:T(8,128)(2,1)S(1)}, u32[]{:S(2)}, u32[]{:S(2)}) collective-permute-start(bf16[3,256,512]{2,1,0:T(8,128)(2,1)} %get-tuple-element.22), channel_id=1, source_target_pairs={{0,128},{1,385},{32,160},{33,417},{64,192},{65,449},{96,224},{97,4... | collective-permute-start | bytes 2359304 | tf_op jit(solution)/shard_map/ppermute | solution.py:330
  17.9 3.1 %collective-permute-start.3 = (bf16[3,256,512]{2,1,0:T(8,128)(2,1)}, bf16[3,256,512]{2,1,0:T(8,128)(2,1)S(1)}, u32[]{:S(2)}, u32[]{:S(2)}) collective-permute-start(bf16[3,256,512]{2,1,0:T(8,128)(2,1)} %get-tuple-element.23), channel_id=1, source_target_pairs={{0,96},{1,33},{32,64},{33,1},{64,32},{65,97},{96,0},{97,65},{128,2... | collective-permute-start | bytes 2359304 | tf_op jit(solution)/shard_map/ppermute | solution.py:330
  21.0 0.0 copy-done.4
  21.0 0.1 copy.9
  21.2 0.1 reduce_max.14
  21.3 0.1 reshape.16
  21.3 0.1 reduce_max.18
  21.5 0.2 convert_reduce_fusion
  21.7 0.0 all-to-all-done
  21.7 0.0 copy-start.2
  21.7 0.0 copy-start.3
  21.7 1.4 %shard_map.75 = bf16[32,72,128]{2,1,0:T(8,128)(2,1)} custom-call(s32[32]{0:T(128)S(1)} %compare_select_fusion.1.table, bf16[32,72,128]{2,1,0:T(8,128)(2,1)S(1)} %bitcast.9), custom_call_target="tpu_custom_call" | custom-call | flops 33333334016 | bytes 4194304 | tf_op jit(solution)/shard_map/pallas_call | solution.py:178
  23.1 17.0 %all-to-all-start.1 = ((bf16[32,72,128]{2,1,0:T(8,128)(2,1)}), bf16[32,72,128]{2,1,0:T(8,128)(2,1)S(1)}, u32[]{:S(2)}, u32[]{:S(2)}) async-start(bf16[32,72,128]{2,1,0:T(8,128)(2,1)} %shard_map.75), calls=%async_computation.1 | async-start | bytes 1179648 | tf_op jit(solution)/shard_map/all_to_all | solution.py:432
  40.2 0.0 collective-permute-done.got
  40.2 0.0 copy-done.2
  40.2 0.0 copy-done.3
  40.2 0.0 copy-start
  40.2 0.0 copy-start.5
  40.2 0.0 copy-start.1
  40.2 0.8 shard_map.77
  41.0 2.2 %collective-permute-start.1 = (bf16[2,256,512]{2,1,0:T(8,128)(2,1)S(1)}, bf16[2,256,512]{2,1,0:T(8,128)(2,1)S(1)}, u32[]{:S(2)}, u32[]{:S(2)}) collective-permute-start(bf16[2,256,512]{2,1,0:T(8,128)(2,1)S(1)} %get-tuple-element.27), channel_id=1, source_target_pairs={{0,384},{1,129},{32,416},{33,161},{64,448},{65,193},{96,480},{97,2... | collective-permute-start | bytes 1572872 | tf_op jit(solution)/shard_map/ppermute | solution.py:330
  43.2 0.0 collective-permute-done.3.got
  43.2 0.0 copy-done
  43.3 0.8 shard_map.80
  44.1 1.9 %collective-permute-start.4 = (bf16[2,256,512]{2,1,0:T(8,128)(2,1)S(1)}, bf16[2,256,512]{2,1,0:T(8,128)(2,1)S(1)}, u32[]{:S(2)}, u32[]{:S(2)}) collective-permute-start(bf16[2,256,512]{2,1,0:T(8,128)(2,1)S(1)} %get-tuple-element.33), channel_id=1, source_target_pairs={{0,32},{1,97},{32,0},{33,65},{64,96},{65,33},{96,64},{97,1},{128,1... | collective-permute-start | bytes 1572872 | tf_op jit(solution)/shard_map/ppermute | solution.py:330
  46.0 0.0 copy-done.5
  46.0 5.2 %collective-permute-done.1.got = bf16[2,256,512]{2,1,0:T(8,128)(2,1)S(1)} collective-permute-done((bf16[2,256,512]{2,1,0:T(8,128)(2,1)S(1)}, bf16[2,256,512]{2,1,0:T(8,128)(2,1)S(1)}, u32[]{:S(2)}, u32[]{:S(2)}) %collective-permute-start.1) | collective-permute-done | bytes 524320 | tf_op jit(solution)/shard_map/ppermute | solution.py:330
  51.3 0.0 copy-done.1
  51.3 0.7 shard_map.78
  51.9 2.2 %collective-permute-start.2 = (bf16[256,512]{1,0:T(8,128)(2,1)S(1)}, bf16[256,512]{1,0:T(8,128)(2,1)S(1)}, u32[]{:S(2)}, u32[]{:S(2)}) collective-permute-start(bf16[256,512]{1,0:T(8,128)(2,1)S(1)} %get-tuple-element.29), channel_id=1, source_target_pairs={{0,32},{1,97},{32,0},{33,65},{64,96},{65,33},{96,64},{97,1},{128,1... | collective-permute-start | bytes 786440 | tf_op jit(solution)/shard_map/ppermute | solution.py:330
  54.1 1.4 %collective-permute-done.4.got = bf16[2,256,512]{2,1,0:T(8,128)(2,1)S(1)} collective-permute-done((bf16[2,256,512]{2,1,0:T(8,128)(2,1)S(1)}, bf16[2,256,512]{2,1,0:T(8,128)(2,1)S(1)}, u32[]{:S(2)}, u32[]{:S(2)}) %collective-permute-start.4) | collective-permute-done | bytes 524320 | tf_op jit(solution)/shard_map/ppermute | solution.py:330
  55.5 0.7 shard_map.81
  56.2 2.8 %collective-permute-start.5 = (bf16[256,512]{1,0:T(8,128)(2,1)S(1)}, bf16[256,512]{1,0:T(8,128)(2,1)S(1)}, u32[]{:S(2)}, u32[]{:S(2)}) collective-permute-start(bf16[256,512]{1,0:T(8,128)(2,1)S(1)} %get-tuple-element.35), channel_id=1, source_target_pairs={{0,384},{1,129},{32,416},{33,161},{64,448},{65,193},{96,480},{97,2... | collective-permute-start | bytes 786440 | tf_op jit(solution)/shard_map/ppermute | solution.py:330
  59.0 0.2 select_reduce_fusion.table
  59.2 17.2 %all-to-all-done.1.source = bf16[32,72,128]{2,1,0:T(8,128)(2,1)S(1)} async-done(((bf16[32,72,128]{2,1,0:T(8,128)(2,1)}), bf16[32,72,128]{2,1,0:T(8,128)(2,1)S(1)}, u32[]{:S(2)}, u32[]{:S(2)}) %all-to-all-start.1) | async-done | bytes 589856 | tf_op jit(solution)/shard_map/all_to_all | solution.py:432
  76.4 1.4 %shard_map.76 = bf16[32,72,128]{2,1,0:T(8,128)(2,1)} custom-call(s32[32]{0:T(128)S(1)} %select_reduce_fusion.table, bf16[32,72,128]{2,1,0:T(8,128)(2,1)S(1)} %all-to-all-done.1.source), custom_call_target="tpu_custom_call" | custom-call | bytes 4194304 | tf_op jit(solution)/shard_map/pallas_call | solution.py:178
  77.9 4.1 %all-to-all-start.2 = ((bf16[16,2,72,128]{3,2,1,0:T(8,128)(2,1)}), bf16[16,2,72,128]{3,2,1,0:T(8,128)(2,1)S(1)}, u32[]{:S(2)}, u32[]{:S(2)}) async-start(bf16[16,2,72,128]{3,2,1,0:T(8,128)(2,1)} %bitcast.5), calls=%async_computation.2 | async-start | bytes 1179648 | tf_op jit(solution)/shard_map/all_to_all | solution.py:435
  81.9 0.0 collective-permute-done.2.got
  82.0 0.1 shard_map.79.a
  82.0 3.3 %collective-permute-start.6 = (bf16[256,512]{1,0:T(8,128)(2,1)S(1)}, bf16[256,512]{1,0:T(8,128)(2,1)S(1)}, u32[]{:S(2)}, u32[]{:S(2)}) collective-permute-start(bf16[256,512]{1,0:T(8,128)(2,1)S(1)} %shard_map.79.a), channel_id=1, source_target_pairs={{0,96},{1,33},{32,64},{33,1},{64,32},{65,97},{96,0},{97,65},{128,2... | collective-permute-start | bytes 786440 | tf_op jit(solution)/shard_map/ppermute | solution.py:330
  85.3 0.0 collective-permute-done.5.got
  85.3 0.1 shard_map.82.b
  85.4 4.3 %collective-permute-start.7 = (bf16[256,512]{1,0:T(8,128)(2,1)S(1)}, bf16[256,512]{1,0:T(8,128)(2,1)S(1)}, u32[]{:S(2)}, u32[]{:S(2)}) collective-permute-start(bf16[256,512]{1,0:T(8,128)(2,1)S(1)} %shard_map.82.b), channel_id=1, source_target_pairs={{0,128},{1,385},{32,160},{33,417},{64,192},{65,449},{96,224},{97,4... | collective-permute-start | bytes 786440 | tf_op jit(solution)/shard_map/ppermute | solution.py:330
  89.7 4.6 %collective-permute-done.6.r0 = bf16[256,512]{1,0:T(8,128)(2,1)S(1)} collective-permute-done((bf16[256,512]{1,0:T(8,128)(2,1)S(1)}, bf16[256,512]{1,0:T(8,128)(2,1)S(1)}, u32[]{:S(2)}, u32[]{:S(2)}) %collective-permute-start.6) | collective-permute-done | bytes 262176 | tf_op jit(solution)/shard_map/ppermute | solution.py:330
  94.3 0.8 collective-permute-done.7.r1
  95.1 0.8 shard_map.83
  95.9 0.0 all-to-all-done.2.chunks
  95.9 3.0 %shard_map.84 = bf16[512,512]{1,0:T(8,128)(2,1)S(1)} custom-call(bf16[16,2,72,128]{3,2,1,0:T(8,128)(2,1)S(1)} %all-to-all-done.2.chunks, bf16[512,512]{1,0:T(8,128)(2,1)S(1)} %get-tuple-element.36.gradient, bf16[512,512]{1,0:T(8,128)(2,1)S(1)} %get-tuple-element.37.left, bf16[512,512]{1,0:T(8,128)(2,1)S(1)} %get-tuple-element.38.right), custom_call_target="tpu_custom_call" | custom-call | flops 2147483648 | bytes 6291456 | tf_op jit(solution)/shard_map/pallas_call | solution.py:438
  98.9 15.1 %all_to_all.20.source = bf16[16,32,512]{2,1,0:T(8,128)(2,1)S(1)} all-to-all(bf16[16,32,512]{2,1,0:T(8,128)(2,1)S(1)} %bitcast.10), channel_id=1, replica_groups=mesh['dp'=16,'z'=16,'core'=2] {'dp'}, dimensions={0} | all-to-all | bytes 1048576 | tf_op jit(solution)/shard_map/all_to_all | solution.py:452
  114.0 0.7 shard_map.85
  (6 shorter events, 0.1 us)
Async XLA Ops:
  0.0 21.0 %copy-start.4 = (s32[160,2]{0,1:T(2,128)S(1)}, s32[160,2]{0,1:T(2,128)}, u32[]{:S(2)}) copy-start(s32[160,2]{0,1:T(2,128)} %param.9) | copy-start | bytes 3844
  2.2 19.5 %all-to-all-start = ((bf16[16,2,72,128]{3,2,1,0:T(8,128)(2,1)}), bf16[16,2,72,128]{3,2,1,0:T(8,128)(2,1)S(1)}, u32[]{:S(2)}, u32[]{:S(2)}) async-start(bf16[16,2,72,128]{3,2,1,0:T(8,128)(2,1)} %shard_map.73), calls=%async_computation | async-start | bytes 1179648 | tf_op jit(solution)/shard_map/all_to_all | solution.py:427
  13.4 26.8 %collective-permute-start = (bf16[3,256,512]{2,1,0:T(8,128)(2,1)}, bf16[3,256,512]{2,1,0:T(8,128)(2,1)S(1)}, u32[]{:S(2)}, u32[]{:S(2)}) collective-permute-start(bf16[3,256,512]{2,1,0:T(8,128)(2,1)} %get-tuple-element.22), channel_id=1, source_target_pairs={{0,128},{1,385},{32,160},{33,417},{64,192},{65,449},{96,224},{97,4... | collective-permute-start | bytes 2359304 | tf_op jit(solution)/shard_map/ppermute | solution.py:330
  17.9 25.4 %collective-permute-start.3 = (bf16[3,256,512]{2,1,0:T(8,128)(2,1)}, bf16[3,256,512]{2,1,0:T(8,128)(2,1)S(1)}, u32[]{:S(2)}, u32[]{:S(2)}) collective-permute-start(bf16[3,256,512]{2,1,0:T(8,128)(2,1)} %get-tuple-element.23), channel_id=1, source_target_pairs={{0,96},{1,33},{32,64},{33,1},{64,32},{65,97},{96,0},{97,65},{128,2... | collective-permute-start | bytes 2359304 | tf_op jit(solution)/shard_map/ppermute | solution.py:330
  21.7 18.5 %copy-start.2 = (s32[256]{0:T(256)S(1)}, s32[256]{0:T(256)}, u32[]{:S(2)}) copy-start(s32[256]{0:T(256)} %constant.55.clone.table) | copy-start | bytes 3076
  21.7 18.5 %copy-start.3 = (bf16[3,256,512]{2,1,0:T(8,128)(2,1)S(1)}, bf16[3,256,512]{2,1,0:T(8,128)(2,1)}, u32[]{:S(2)}) copy-start(bf16[3,256,512]{2,1,0:T(8,128)(2,1)} %get-tuple-element.25.kept) | copy-start | bytes 2359300
  23.1 53.3 %all-to-all-start.1 = ((bf16[32,72,128]{2,1,0:T(8,128)(2,1)}), bf16[32,72,128]{2,1,0:T(8,128)(2,1)S(1)}, u32[]{:S(2)}, u32[]{:S(2)}) async-start(bf16[32,72,128]{2,1,0:T(8,128)(2,1)} %shard_map.75), calls=%async_computation.1 | async-start | bytes 1179648 | tf_op jit(solution)/shard_map/all_to_all | solution.py:432
  40.2 3.1 %copy-start = (bf16[3,256,512]{2,1,0:T(8,128)(2,1)S(1)}, bf16[3,256,512]{2,1,0:T(8,128)(2,1)}, u32[]{:S(2)}) copy-start(bf16[3,256,512]{2,1,0:T(8,128)(2,1)} %get-tuple-element.30.kept) | copy-start | bytes 2359300
  40.2 5.8 %copy-start.5 = (s32[2,32]{1,0:T(2,128)S(1)}, s32[2,32]{1,0:T(2,128)}, u32[]{:S(2)}) copy-start(s32[2,32]{1,0:T(2,128)} %constant.57.clone) | copy-start | bytes 772
  40.2 11.0 %copy-start.1 = (s32[128]{0:T(128)S(1)}, s32[128]{0:T(128)}, u32[]{:S(2)}) copy-start(s32[128]{0:T(128)} %constant.56.clone.table) | copy-start | bytes 1540
  41.0 10.2 %collective-permute-start.1 = (bf16[2,256,512]{2,1,0:T(8,128)(2,1)S(1)}, bf16[2,256,512]{2,1,0:T(8,128)(2,1)S(1)}, u32[]{:S(2)}, u32[]{:S(2)}) collective-permute-start(bf16[2,256,512]{2,1,0:T(8,128)(2,1)S(1)} %get-tuple-element.27), channel_id=1, source_target_pairs={{0,384},{1,129},{32,416},{33,161},{64,448},{65,193},{96,480},{97,2... | collective-permute-start | bytes 1572872 | tf_op jit(solution)/shard_map/ppermute | solution.py:330
  44.1 11.4 %collective-permute-start.4 = (bf16[2,256,512]{2,1,0:T(8,128)(2,1)S(1)}, bf16[2,256,512]{2,1,0:T(8,128)(2,1)S(1)}, u32[]{:S(2)}, u32[]{:S(2)}) collective-permute-start(bf16[2,256,512]{2,1,0:T(8,128)(2,1)S(1)} %get-tuple-element.33), channel_id=1, source_target_pairs={{0,32},{1,97},{32,0},{33,65},{64,96},{65,33},{96,64},{97,1},{128,1... | collective-permute-start | bytes 1572872 | tf_op jit(solution)/shard_map/ppermute | solution.py:330
  51.9 30.0 %collective-permute-start.2 = (bf16[256,512]{1,0:T(8,128)(2,1)S(1)}, bf16[256,512]{1,0:T(8,128)(2,1)S(1)}, u32[]{:S(2)}, u32[]{:S(2)}) collective-permute-start(bf16[256,512]{1,0:T(8,128)(2,1)S(1)} %get-tuple-element.29), channel_id=1, source_target_pairs={{0,32},{1,97},{32,0},{33,65},{64,96},{65,33},{96,64},{97,1},{128,1... | collective-permute-start | bytes 786440 | tf_op jit(solution)/shard_map/ppermute | solution.py:330
  56.2 29.1 %collective-permute-start.5 = (bf16[256,512]{1,0:T(8,128)(2,1)S(1)}, bf16[256,512]{1,0:T(8,128)(2,1)S(1)}, u32[]{:S(2)}, u32[]{:S(2)}) collective-permute-start(bf16[256,512]{1,0:T(8,128)(2,1)S(1)} %get-tuple-element.35), channel_id=1, source_target_pairs={{0,384},{1,129},{32,416},{33,161},{64,448},{65,193},{96,480},{97,2... | collective-permute-start | bytes 786440 | tf_op jit(solution)/shard_map/ppermute | solution.py:330
  77.9 18.0 %all-to-all-start.2 = ((bf16[16,2,72,128]{3,2,1,0:T(8,128)(2,1)}), bf16[16,2,72,128]{3,2,1,0:T(8,128)(2,1)S(1)}, u32[]{:S(2)}, u32[]{:S(2)}) async-start(bf16[16,2,72,128]{3,2,1,0:T(8,128)(2,1)} %bitcast.5), calls=%async_computation.2 | async-start | bytes 1179648 | tf_op jit(solution)/shard_map/all_to_all | solution.py:435
  82.0 12.3 %collective-permute-start.6 = (bf16[256,512]{1,0:T(8,128)(2,1)S(1)}, bf16[256,512]{1,0:T(8,128)(2,1)S(1)}, u32[]{:S(2)}, u32[]{:S(2)}) collective-permute-start(bf16[256,512]{1,0:T(8,128)(2,1)S(1)} %shard_map.79.a), channel_id=1, source_target_pairs={{0,96},{1,33},{32,64},{33,1},{64,32},{65,97},{96,0},{97,65},{128,2... | collective-permute-start | bytes 786440 | tf_op jit(solution)/shard_map/ppermute | solution.py:330
  85.4 9.7 %collective-permute-start.7 = (bf16[256,512]{1,0:T(8,128)(2,1)S(1)}, bf16[256,512]{1,0:T(8,128)(2,1)S(1)}, u32[]{:S(2)}, u32[]{:S(2)}) collective-permute-start(bf16[256,512]{1,0:T(8,128)(2,1)S(1)} %shard_map.82.b), channel_id=1, source_target_pairs={{0,128},{1,385},{32,160},{33,417},{64,192},{65,449},{96,224},{97,4... | collective-permute-start | bytes 786440 | tf_op jit(solution)/shard_map/ppermute | solution.py:330
